TPU v7x, 32 devices: a whole 2x2x4 slice. The times are simulated.
32 devices in a mesh: grp: 2 (over y), node: 4 (over z), head: 4 (over x, core).
Axes of the slice: x: 2, y: 2, z: 4, core: 2. Of those that a mesh axis runs over, the one named last changes fastest.
Arguments:
- queries: bfloat16 [2048, 1024], P(('grp', 'node', 'head')), parts along dimension 0, may hold values from -8 to 8
- key_rows: bfloat16 [2048, 1024], P(('grp', 'node', 'head')), parts along dimension 0, may hold values from -8 to 8
- value_rows: bfloat16 [2048, 1024], P(('grp', 'node', 'head')), parts along dimension 0, may hold values from -6 to 6
- out_grads: bfloat16 [2048, 1024], P(('grp', 'node', 'head')), parts along dimension 0, may hold values from -6 to 6
- neighbours: int32 [16, 8], P('grp'), parts along dimension 0, may hold values from 0 to 7, as said below
Outputs:
- attended: bfloat16 [2048, 1024], P(('grp', 'node', 'head')), parts along dimension 0
- query_grad: bfloat16 [2048, 1024], P(('grp', 'node', 'head')), parts along dimension 0
- key_grad: bfloat16 [2048, 1024], P(('grp', 'node', 'head')), parts along dimension 0
- value_grad: bfloat16 [2048, 1024], P(('grp', 'node', 'head')), parts along dimension 0
There are 2 independent parts, one for each index of `grp`. A program takes and returns all parts, laid end to end along the dimension named above; each array names one. Nothing has to cross between parts.
Inputs may be any that keep to these rules, and one draw needn't show every extreme that they name: `neighbours`: the owner of patch p is p // 2. Every listed neighbour of a patch has an owner at distance at most 1 from the patch's owner. The patches of one owner together list exactly 1 distinct patches of each other owner within distance 1 that exists, and none of any other owner.
All inputs are finite; a program needn't handle non-finite values.
Results may differ from a plain program's by a relative error of at most 0.012.
Values may be sent and summed in bfloat16 or wider, within the bound.
No kernel may reach another device: no remote copies, remote signals or barrier semaphores. Data moves between devices by JAX's collectives and lax.ppermute only.
A program may use at most 64 MiB of HBM per device.

v0:
```python
import math

import jax
import jax.numpy as jnp
from jax import lax
from jax.sharding import PartitionSpec as P

HEAD_DIM = 64
PATCH = 128
NBRS = 8
RADIUS = 1


def from_behind(block, axis, distance):
    devices = range(lax.axis_size(axis))
    route = [(i - distance, i) for i in devices if i - distance in devices]
    return lax.ppermute(block, axis, route)


def attend_block(query_blk, grad_blk, key_blk, value_blk):
    score_scale = HEAD_DIM ** (-0.5)
    scores = (
        jnp.einsum("bqhd,bkhd->bhqk", query_blk, key_blk, preferred_element_type=jnp.float32)
        * score_scale
    )
    row_max = jnp.max(scores, -1, keepdims=True)
    exp_scores = jnp.exp(scores - row_max)
    weights = exp_scores / jnp.sum(exp_scores, -1, keepdims=True)
    weights_low = weights.astype(jnp.bfloat16)
    mixed = jnp.einsum(
        "bhqk,bkhd->bqhd", weights_low, value_blk, preferred_element_type=jnp.float32
    )
    grad_weights = jnp.einsum(
        "bqhd,bkhd->bhqk", grad_blk, value_blk, preferred_element_type=jnp.float32
    )
    row_dots = jnp.transpose(jnp.sum(grad_blk.astype(jnp.float32) * mixed, -1), (0, 2, 1))[
        ..., None
    ]
    grad_scores = (weights * (grad_weights - row_dots)).astype(jnp.bfloat16)
    query_grad = (
        jnp.einsum("bhqk,bkhd->bqhd", grad_scores, key_blk, preferred_element_type=jnp.float32)
        * score_scale
    ).astype(jnp.bfloat16)
    key_grad = (
        jnp.einsum("bhqk,bqhd->bkhd", grad_scores, query_blk, preferred_element_type=jnp.float32)
        * score_scale
    )
    value_grad = jnp.einsum(
        "bhqk,bqhd->bkhd", weights_low, grad_blk, preferred_element_type=jnp.float32
    )
    return (mixed.astype(jnp.bfloat16), query_grad, key_grad, value_grad)


def shards(queries, key_rows, value_rows, out_grads, neighbours):
    head_query, head_key, head_value, head_grad = (
        lax.all_to_all(queries, "head", split_axis=1, concat_axis=0, tiled=True),
        lax.all_to_all(key_rows, "head", split_axis=1, concat_axis=0, tiled=True),
        lax.all_to_all(value_rows, "head", split_axis=1, concat_axis=0, tiled=True),
        lax.all_to_all(out_grads, "head", split_axis=1, concat_axis=0, tiled=True),
    )
    row_count, feat_width = head_query.shape
    local_count = row_count // PATCH
    groups = feat_width // HEAD_DIM
    device = lax.axis_index("node")
    local_pairs = jnp.concatenate([head_key, head_value], 1).reshape(
        local_count, PATCH, 2 * feat_width
    )
    my_lists = lax.dynamic_slice_in_dim(neighbours, device * local_count, local_count, 0)
    offsets = list(range(-RADIUS, 0)) + list(range(1, RADIUS + 1))
    local_ids = jnp.arange(local_count, dtype=jnp.int32)
    pieces = []
    for offset in range(-RADIUS, RADIUS + 1):
        if offset == 0:
            pieces.append(local_pairs)
        else:
            pieces.append(from_behind(local_pairs, "node", -offset))
    key_pool = jnp.concatenate(pieces, 0)
    window_start = (device - RADIUS) * local_count
    key_index = jnp.concatenate(
        [(local_ids + RADIUS * local_count)[:, None], my_lists - window_start], 1
    )
    block = math.gcd(local_count, max(1, 512 // PATCH))
    block_count = local_count // block
    span = (NBRS + 1) * PATCH

    def one_block(grad_pool, inputs):
        query_blk, grad_blk, index_blk = inputs
        flat_index = index_blk.reshape(-1)
        taken = jnp.take(key_pool, flat_index, axis=0).reshape(block, span, 2, groups, HEAD_DIM)
        mixed, query_grad, key_grad, value_grad = attend_block(
            query_blk, grad_blk, taken[:, :, 0], taken[:, :, 1]
        )
        contrib = jnp.stack([key_grad, value_grad], 2).reshape(
            block * (NBRS + 1), PATCH, 2 * feat_width
        )
        grad_pool = grad_pool.at[flat_index].add(contrib)
        return (grad_pool, (mixed, query_grad))

    inputs = (
        head_query.reshape(block_count, block, PATCH, groups, HEAD_DIM),
        head_grad.reshape(block_count, block, PATCH, groups, HEAD_DIM),
        key_index.reshape(block_count, block, NBRS + 1),
    )
    grad_pool, (mixed_all, qgrad_all) = lax.scan(
        one_block, jnp.zeros(key_pool.shape, jnp.float32), inputs
    )
    local_grad = grad_pool[RADIUS * local_count : (RADIUS + 1) * local_count]
    for offset in offsets:
        start_row = (offset + RADIUS) * local_count
        slab = grad_pool[start_row : start_row + local_count]
        local_grad = local_grad + from_behind(slab.astype(jnp.bfloat16), "node", offset).astype(
            slab.dtype
        )
    flat_grad = local_grad.reshape(row_count, 2 * feat_width)
    key_out = flat_grad[:, :feat_width].astype(jnp.bfloat16)
    value_out = flat_grad[:, feat_width:].astype(jnp.bfloat16)
    mixed_out = mixed_all.reshape(row_count, feat_width)
    query_out = qgrad_all.reshape(row_count, feat_width)
    return (
        lax.all_to_all(mixed_out, "head", split_axis=0, concat_axis=1, tiled=True),
        lax.all_to_all(query_out, "head", split_axis=0, concat_axis=1, tiled=True),
        lax.all_to_all(key_out, "head", split_axis=0, concat_axis=1, tiled=True),
        lax.all_to_all(value_out, "head", split_axis=0, concat_axis=1, tiled=True),
    )


def solution(mesh):
    in_specs = (
        P(("grp", "node", "head"), None),
        P(("grp", "node", "head"), None),
        P(("grp", "node", "head"), None),
        P(("grp", "node", "head"), None),
        P("grp", None),
    )
    out_specs = (
        P(("grp", "node", "head"), None),
        P(("grp", "node", "head"), None),
        P(("grp", "node", "head"), None),
        P(("grp", "node", "head"), None),
    )
    return jax.shard_map(shards, mesh=mesh, in_specs=in_specs, out_specs=out_specs, check_vma=False)
```

profile of v0, /device:TPU:0, one launch (start us, length us, event | category | flops | bytes accessed | tf_op | source)
XLA Modules:
  0.0 137.4 jit_solution(383944772927640221)
XLA Ops:
  0.6 1.6 %copy.100 = bf16[8,4,8,256]{3,2,0,1:T(8,128)(2,1)} copy(bf16[8,4,8,256]{3,2,1,0:T(8,128)(2,1)} %bitcast.109) | data formatting | bytes 262144 | tf_op jit(solution)/shard_map/all_to_all | solution.py:57
  2.2 4.2 %all-to-all-start = ((bf16[64,4,256]{2,0,1:T(8,128)(2,1)}), bf16[64,4,256]{2,0,1:T(8,128)(2,1)S(1)}, u32[]{:S(2)}, u32[]{:S(2)}) async-start(bf16[64,4,256]{2,0,1:T(8,128)(2,1)} %bitcast.93), calls=%async_computation | async-start | bytes 262144 | tf_op jit(solution)/shard_map/all_to_all | solution.py:57
  6.4 1.6 %copy.99 = bf16[8,4,8,256]{3,2,0,1:T(8,128)(2,1)} copy(bf16[8,4,8,256]{3,2,1,0:T(8,128)(2,1)} %bitcast.110) | data formatting | bytes 262144 | tf_op jit(solution)/shard_map/all_to_all | solution.py:58
  8.0 0.7 dynamic-slice_subtract_fusion
  8.8 2.3 %all-to-all-done = bf16[64,4,256]{2,0,1:T(8,128)(2,1)S(1)} async-done(((bf16[64,4,256]{2,0,1:T(8,128)(2,1)}), bf16[64,4,256]{2,0,1:T(8,128)(2,1)S(1)}, u32[]{:S(2)}, u32[]{:S(2)}) %all-to-all-start) | async-done | bytes 131104 | tf_op jit(solution)/shard_map/all_to_all | solution.py:57
  11.0 3.3 %all-to-all-start.1 = ((bf16[64,4,256]{2,0,1:T(8,128)(2,1)}), bf16[64,4,256]{2,0,1:T(8,128)(2,1)S(1)}, u32[]{:S(2)}, u32[]{:S(2)}) async-start(bf16[64,4,256]{2,0,1:T(8,128)(2,1)} %bitcast.92), calls=%async_computation.1 | async-start | bytes 262144 | tf_op jit(solution)/shard_map/all_to_all | solution.py:58
  14.5 1.6 %copy.98 = bf16[8,4,8,256]{3,2,0,1:T(8,128)(2,1)} copy(bf16[8,4,8,256]{3,2,1,0:T(8,128)(2,1)} %bitcast.111) | data formatting | bytes 262144 | tf_op jit(solution)/shard_map/all_to_all | solution.py:56
  16.1 2.9 %all-to-all-done.1 = bf16[64,4,256]{2,0,1:T(8,128)(2,1)S(1)} async-done(((bf16[64,4,256]{2,0,1:T(8,128)(2,1)}), bf16[64,4,256]{2,0,1:T(8,128)(2,1)S(1)}, u32[]{:S(2)}, u32[]{:S(2)}) %all-to-all-start.1) | async-done | bytes 131104 | tf_op jit(solution)/shard_map/all_to_all | solution.py:58
  19.0 3.3 %all-to-all-start.2 = ((bf16[64,4,256]{2,0,1:T(8,128)(2,1)}), bf16[64,4,256]{2,0,1:T(8,128)(2,1)S(1)}, u32[]{:S(2)}, u32[]{:S(2)}) async-start(bf16[64,4,256]{2,0,1:T(8,128)(2,1)} %bitcast.91), calls=%async_computation.2 | async-start | bytes 262144 | tf_op jit(solution)/shard_map/all_to_all | solution.py:56
  22.3 1.3 collective-permute-start.1
  23.6 4.7 %collective-permute-start = (bf16[2,128,512]{2,1,0:T(8,128)(2,1)S(1)}, bf16[2,128,512]{2,1,0:T(8,128)(2,1)S(1)}, u32[]{:S(2)}, u32[]{:S(2)}) collective-permute-start(bf16[2,128,512]{2,1,0:T(8,128)(2,1)S(1)} %pad_maximum_fusion.2), channel_id=1, source_target_pairs={{0,4},{4,8},{8,12},{1,5},{5,9},{9,13},{2,6},{6,10},{10,14},{3,7},{... | collective-permute-start | bytes 786440 | tf_op jit(solution)/shard_map/ppermute | solution.py:17
  28.3 1.6 %copy.97 = bf16[8,4,8,256]{3,2,0,1:T(8,128)(2,1)} copy(bf16[8,4,8,256]{3,2,1,0:T(8,128)(2,1)} %bitcast.112) | data formatting | bytes 262144 | tf_op jit(solution)/shard_map/all_to_all | solution.py:59
  29.9 3.3 %all-to-all-start.4 = ((bf16[64,4,256]{2,0,1:T(8,128)(2,1)}), bf16[64,4,256]{2,0,1:T(8,128)(2,1)S(1)}, u32[]{:S(2)}, u32[]{:S(2)}) async-start(bf16[64,4,256]{2,0,1:T(8,128)(2,1)} %bitcast.90), calls=%async_computation.4 | async-start | bytes 262144 | tf_op jit(solution)/shard_map/all_to_all | solution.py:59
  33.6 4.3 %all-to-all-done.4 = bf16[64,4,256]{2,0,1:T(8,128)(2,1)S(1)} async-done(((bf16[64,4,256]{2,0,1:T(8,128)(2,1)}), bf16[64,4,256]{2,0,1:T(8,128)(2,1)S(1)}, u32[]{:S(2)}, u32[]{:S(2)}) %all-to-all-start.4) | async-done | bytes 131104 | tf_op jit(solution)/shard_map/all_to_all | solution.py:59
  38.3 0.7 gather_fusion
  39.0 4.3 %reshape.134 = bf16[2,1152,2,4,64]{4,3,2,1,0:T(4,128)(2,1)} reshape(bf16[18,128,512]{2,1,0:T(8,128)(2,1)S(1)} %gather_fusion) | data formatting | bytes 4718592 | tf_op jit(solution)/shard_map/while/body/eval_jaxpr/jit(_take)/gather | solution.py:89
  43.3 6.8 %copy.55 = bf16[2,1152,2,4,64]{1,4,3,0,2:T(8,128)(2,1)S(1)} copy(bf16[2,1152,2,4,64]{4,3,2,1,0:T(4,128)(2,1)} %reshape.134) | data formatting | bytes 4718592 | tf_op jit(solution)/shard_map/while/body/eval_jaxpr/jit(_take)/gather | solution.py:89
  50.0 1.6 %broadcast_select_fusion = bf16[2,1152,2,4,64]{1,4,3,0,2:T(8,128)(2,1)} fusion(bf16[2,1152,2,4,64]{1,4,3,0,2:T(8,128)(2,1)S(1)} %copy.55, pred[2,1152]{1,0:T(4,128)(4,1)S(1)} %bitcast.117), kind=kLoop, calls=%fused_computation.16 | loop fusion | flops 1179648 | bytes 4720896 | tf_op jit(solution)/shard_map/while/body/eval_jaxpr/jit(_take)/select_n | solution.py:89
  51.7 5.1 %exponential_reduce_fusion = (f32[2,4,128]{2,1,0:T(4,128)S(1)}, f32[2,4,128,1152]{2,3,1,0:T(8,128)}) fusion(bf16[2,128,4,64]{1,3,2,0:T(8,128)(2,1)S(1)} %copy.57, bf16[2,1152,2,4,64]{1,4,3,0,2:T(8,128)(2,1)} %broadcast_select_fusion), kind=kOutput, calls=%fused_computation.12 | convolution fusion | flops 154535040 | bytes 6033408 | tf_op jit(solution)/shard_map/while/body/eval_jaxpr/sub | solution.py:27
  56.8 3.1 %fusion.5 = bf16[2,4,128,1152]{2,3,1,0:T(8,128)(2,1)S(1)} fusion(f32[2,4,128]{2,1,0:T(4,128)S(1)} %get-tuple-element.36, f32[2,4,128,1152]{2,3,1,0:T(8,128)} %get-tuple-element.37), kind=kLoop, calls=%fused_computation.17 | loop fusion | flops 2359296 | bytes 7081984 | tf_op jit(solution)/shard_map/while/body/eval_jaxpr/convert_element_type | solution.py:29
  59.9 0.6 multiply_reduce_fusion
  60.5 1.0 convolution_bitcast_fusion
  61.6 1.4 %fusion.2 = bf16[2,4,128,1152]{2,3,1,0:T(8,128)(2,1)S(1)} fusion(bf16[2,128,4,64]{1,3,2,0:T(8,128)(2,1)S(1)} %copy.62, f32[2,4,128]{2,1,0:T(4,128)S(1)} %bitcast.118, f32[2,4,128]{2,1,0:T(4,128)S(1)} %get-tuple-element.36, f32[2,4,128,1152]{2,3,1,0:T(8,128)S(1)} %bitcast.96, bf16[2,1152,2,4,64]{1,4,3,0,2:T(8,128)(2,1)S(1)} %copy-done), kind=kOutput, calls=%fused_computation.8 | convolution fusion | flops 155713536 | bytes 8396800 | tf_op jit(solution)/shard_map/while/body/eval_jaxpr/bqhd,bkhd->bhqk/dot_general | solution.py:33
  63.0 1.4 %copy-done.2 = bf16[2,4,128,1152]{2,3,1,0:T(8,128)(2,1)} copy-done((bf16[2,4,128,1152]{2,3,1,0:T(8,128)(2,1)}, bf16[2,4,128,1152]{2,3,1,0:T(8,128)(2,1)S(1)}, u32[]{:S(2)}) %copy-start.2) | copy-done | bytes 2359320
  64.4 1.0 fusion.4
  65.4 2.6 %pad_maximum_fusion = f32[2,1152,2,4,64]{1,4,3,0,2:T(8,128)} fusion(f32[2,1152,1,4,64]{1,4,3,0,2:T(8,128)S(1)} %convolution_bitcast_fusion, f32[2,1152,1,4,64]{1,4,3,0,2:T(8,128)S(1)} %fusion.4), kind=kLoop, calls=%fused_computation.6 | loop fusion | flops 1179648 | bytes 9437184 | tf_op jit(solution)/shard_map/while/body/eval_jaxpr/stack | solution.py:93
  68.0 9.6 %copy.81 = f32[2,1152,2,4,64]{4,3,2,1,0:T(4,128)} copy(f32[2,1152,2,4,64]{1,4,3,0,2:T(8,128)} %pad_maximum_fusion) | data formatting | bytes 9437184 | tf_op jit(solution)/shard_map/while/body/eval_jaxpr/reshape | solution.py:93
  77.6 10.3 %reshape.135 = f32[18,128,512]{2,1,0:T(8,128)} reshape(f32[2,1152,2,4,64]{4,3,2,1,0:T(4,128)} %copy.81) | data formatting | bytes 9437184 | tf_op jit(solution)/shard_map/while/body/eval_jaxpr/reshape | solution.py:93
  88.0 8.3 %scatter_fusion = f32[6,128,512]{2,1,0:T(8,128)S(1)} fusion(f32[6,128,512]{2,1,0:T(8,128)S(1)} %broadcast_in_dim.37, s32[18]{0:T(128)S(1)} %fusion.10, f32[18,128,512]{2,1,0:T(8,128)} %reshape.135), kind=kCustom, calls=%fused_computation.1 | custom fusion | flops 1179648 | bytes 14155848 | tf_op jit(solution)/shard_map/while/body/eval_jaxpr/scatter-add | solution.py:96
  96.5 1.4 %collective-permute-start.2 = (bf16[2,128,512]{2,1,0:T(8,128)(2,1)S(1)}, bf16[2,128,512]{2,1,0:T(8,128)(2,1)S(1)}, u32[]{:S(2)}, u32[]{:S(2)}) collective-permute-start(bf16[2,128,512]{2,1,0:T(8,128)(2,1)S(1)} %get-tuple-element.22), channel_id=1, source_target_pairs={{4,0},{8,4},{12,8},{5,1},{9,5},{13,9},{6,2},{10,6},{14,10},{7,3},{... | collective-permute-start | bytes 786440 | tf_op jit(solution)/shard_map/ppermute | solution.py:17
  98.0 4.6 %collective-permute-start.3 = (bf16[2,128,512]{2,1,0:T(8,128)(2,1)S(1)}, bf16[2,128,512]{2,1,0:T(8,128)(2,1)S(1)}, u32[]{:S(2)}, u32[]{:S(2)}) collective-permute-start(bf16[2,128,512]{2,1,0:T(8,128)(2,1)S(1)} %get-tuple-element.23), channel_id=1, source_target_pairs={{0,4},{4,8},{8,12},{1,5},{5,9},{9,13},{2,6},{6,10},{10,14},{3,7},{... | collective-permute-start | bytes 786440 | tf_op jit(solution)/shard_map/ppermute | solution.py:17
  102.5 2.3 %fusion.7 = bf16[2,128,4,64]{1,3,2,0:T(8,128)(2,1)S(1)} fusion(bf16[2,4,128,1152]{2,3,1,0:T(8,128)(2,1)} %copy-done.2, bf16[2,1152,2,4,64]{1,4,3,0,2:T(8,128)(2,1)S(1)} %copy-done.1), kind=kOutput, calls=%fused_computation.23 | convolution fusion | flops 151126016 | bytes 3670016 | tf_op jit(solution)/shard_map/while/body/eval_jaxpr/bhqk,bkhd->bqhd/dot_general | solution.py:41
  104.8 0.2 copy.65
  105.0 0.9 all_to_all.120
  105.9 3.3 %all-to-all-start.5 = ((bf16[4,64,256]{2,1,0:T(8,128)(2,1)}), bf16[4,64,256]{2,1,0:T(8,128)(2,1)S(1)}, u32[]{:S(2)}, u32[]{:S(2)}) async-start(bf16[4,64,256]{2,1,0:T(8,128)(2,1)} %all_to_all.120), calls=%async_computation.5 | async-start | bytes 262144 | tf_op jit(solution)/shard_map/all_to_all | solution.py:121
  109.2 0.2 copy.59
  109.4 0.9 all_to_all.113
  110.4 3.4 %all-to-all-done.5 = bf16[4,64,256]{2,1,0:T(8,128)(2,1)S(1)} async-done(((bf16[4,64,256]{2,1,0:T(8,128)(2,1)}), bf16[4,64,256]{2,1,0:T(8,128)(2,1)S(1)}, u32[]{:S(2)}, u32[]{:S(2)}) %all-to-all-start.5) | async-done | bytes 131104 | tf_op jit(solution)/shard_map/all_to_all | solution.py:121
  113.8 3.3 %all-to-all-start.3 = ((bf16[4,64,256]{2,1,0:T(8,128)(2,1)}), bf16[4,64,256]{2,1,0:T(8,128)(2,1)S(1)}, u32[]{:S(2)}, u32[]{:S(2)}) async-start(bf16[4,64,256]{2,1,0:T(8,128)(2,1)} %all_to_all.113), calls=%async_computation.3 | async-start | bytes 262144 | tf_op jit(solution)/shard_map/all_to_all | solution.py:120
  117.2 0.7 fusion.13
  117.8 3.9 %all-to-all-done.3 = bf16[4,64,256]{2,1,0:T(8,128)(2,1)S(1)} async-done(((bf16[4,64,256]{2,1,0:T(8,128)(2,1)}), bf16[4,64,256]{2,1,0:T(8,128)(2,1)S(1)}, u32[]{:S(2)}, u32[]{:S(2)}) %all-to-all-start.3) | async-done | bytes 131104 | tf_op jit(solution)/shard_map/all_to_all | solution.py:120
  121.8 7.0 %all_to_all.140 = bf16[4,64,256]{2,1,0:T(8,128)(2,1)S(1)} all-to-all(bf16[4,64,256]{2,1,0:T(8,128)(2,1)S(1)} %bitcast.108), channel_id=1, replica_groups=mesh['grp'=2,'node'=4,'head'=4] {'head'}, dimensions={0} | all-to-all | bytes 262144 | tf_op jit(solution)/shard_map/all_to_all | solution.py:122
  128.8 3.3 %all-to-all-start.7 = ((bf16[4,64,256]{2,1,0:T(8,128)(2,1)}), bf16[4,64,256]{2,1,0:T(8,128)(2,1)S(1)}, u32[]{:S(2)}, u32[]{:S(2)}) async-start(bf16[4,64,256]{2,1,0:T(8,128)(2,1)} %bitcast.23), calls=%async_computation.7 | async-start | bytes 262144 | tf_op jit(solution)/shard_map/all_to_all | solution.py:123
  132.1 0.7 copy.88
  132.8 0.7 copy.87
  133.4 0.7 copy.89
  134.1 2.6 %all-to-all-done.7 = bf16[4,64,256]{2,1,0:T(8,128)(2,1)S(1)} async-done(((bf16[4,64,256]{2,1,0:T(8,128)(2,1)}), bf16[4,64,256]{2,1,0:T(8,128)(2,1)S(1)}, u32[]{:S(2)}, u32[]{:S(2)}) %all-to-all-start.7) | async-done | bytes 131104 | tf_op jit(solution)/shard_map/all_to_all | solution.py:123
  136.7 0.7 copy.90
  (32 shorter events, 1.4 us)
Async XLA Ops:
  2.2 8.8 %all-to-all-start = ((bf16[64,4,256]{2,0,1:T(8,128)(2,1)}), bf16[64,4,256]{2,0,1:T(8,128)(2,1)S(1)}, u32[]{:S(2)}, u32[]{:S(2)}) async-start(bf16[64,4,256]{2,0,1:T(8,128)(2,1)} %bitcast.93), calls=%async_computation | async-start | bytes 262144 | tf_op jit(solution)/shard_map/all_to_all | solution.py:57
  11.0 7.9 %all-to-all-start.1 = ((bf16[64,4,256]{2,0,1:T(8,128)(2,1)}), bf16[64,4,256]{2,0,1:T(8,128)(2,1)S(1)}, u32[]{:S(2)}, u32[]{:S(2)}) async-start(bf16[64,4,256]{2,0,1:T(8,128)(2,1)} %bitcast.92), calls=%async_computation.1 | async-start | bytes 262144 | tf_op jit(solution)/shard_map/all_to_all | solution.py:58
  19.0 10.9 %all-to-all-start.2 = ((bf16[64,4,256]{2,0,1:T(8,128)(2,1)}), bf16[64,4,256]{2,0,1:T(8,128)(2,1)S(1)}, u32[]{:S(2)}, u32[]{:S(2)}) async-start(bf16[64,4,256]{2,0,1:T(8,128)(2,1)} %bitcast.91), calls=%async_computation.2 | async-start | bytes 262144 | tf_op jit(solution)/shard_map/all_to_all | solution.py:56
  22.3 15.8 %collective-permute-start.1 = (bf16[2,128,512]{2,1,0:T(8,128)(2,1)S(1)}, bf16[2,128,512]{2,1,0:T(8,128)(2,1)S(1)}, u32[]{:S(2)}, u32[]{:S(2)}) collective-permute-start(bf16[2,128,512]{2,1,0:T(8,128)(2,1)S(1)} %pad_maximum_fusion.2), channel_id=1, source_target_pairs={{4,0},{8,4},{12,8},{5,1},{9,5},{13,9},{6,2},{10,6},{14,10},{7,3},{... | collective-permute-start | bytes 786440 | tf_op jit(solution)/shard_map/ppermute | solution.py:17
  23.6 14.5 %collective-permute-start = (bf16[2,128,512]{2,1,0:T(8,128)(2,1)S(1)}, bf16[2,128,512]{2,1,0:T(8,128)(2,1)S(1)}, u32[]{:S(2)}, u32[]{:S(2)}) collective-permute-start(bf16[2,128,512]{2,1,0:T(8,128)(2,1)S(1)} %pad_maximum_fusion.2), channel_id=1, source_target_pairs={{0,4},{4,8},{8,12},{1,5},{5,9},{9,13},{2,6},{6,10},{10,14},{3,7},{... | collective-permute-start | bytes 786440 | tf_op jit(solution)/shard_map/ppermute | solution.py:17
  29.9 7.9 %all-to-all-start.4 = ((bf16[64,4,256]{2,0,1:T(8,128)(2,1)}), bf16[64,4,256]{2,0,1:T(8,128)(2,1)S(1)}, u32[]{:S(2)}, u32[]{:S(2)}) async-start(bf16[64,4,256]{2,0,1:T(8,128)(2,1)} %bitcast.90), calls=%async_computation.4 | async-start | bytes 262144 | tf_op jit(solution)/shard_map/all_to_all | solution.py:59
  56.8 3.1 %copy-start = (bf16[2,1152,2,4,64]{1,4,3,0,2:T(8,128)(2,1)S(1)}, bf16[2,1152,2,4,64]{1,4,3,0,2:T(8,128)(2,1)}, u32[]{:S(2)}) copy-start(bf16[2,1152,2,4,64]{1,4,3,0,2:T(8,128)(2,1)} %broadcast_select_fusion) | copy-start | bytes 7077892
  56.8 4.7 %slice-start = ((s8[4718592]{0:T(1024)(128)(4,1)}), s8[4194304]{0:T(1024)(128)(4,1)S(1)}, s32[]{:S(2)}) async-start(s8[4718592]{0:T(1024)(128)(4,1)} %bitcast.95), calls=%async_computation.8 | async-start | bytes 8388608
  59.9 1.6 %slice-start.1 = ((s8[4718592]{0:T(1024)(128)(4,1)}), s8[524288]{0:T(1024)(128)(4,1)S(1)}, s32[]{:S(2)}) async-start(s8[4718592]{0:T(1024)(128)(4,1)} %bitcast.95), calls=%async_computation.9 | async-start | bytes 1048576
  63.0 1.4 %copy-start.2 = (bf16[2,4,128,1152]{2,3,1,0:T(8,128)(2,1)}, bf16[2,4,128,1152]{2,3,1,0:T(8,128)(2,1)S(1)}, u32[]{:S(2)}) copy-start(bf16[2,4,128,1152]{2,3,1,0:T(8,128)(2,1)S(1)} %fusion.2) | copy-start | bytes 7077892
  96.4 6.2 %copy-start.1 = (bf16[2,1152,2,4,64]{1,4,3,0,2:T(8,128)(2,1)S(1)}, bf16[2,1152,2,4,64]{1,4,3,0,2:T(8,128)(2,1)}, u32[]{:S(2)}) copy-start(bf16[2,1152,2,4,64]{1,4,3,0,2:T(8,128)(2,1)} %broadcast_select_fusion) | copy-start | bytes 7077892
  96.5 13.8 %collective-permute-start.2 = (bf16[2,128,512]{2,1,0:T(8,128)(2,1)S(1)}, bf16[2,128,512]{2,1,0:T(8,128)(2,1)S(1)}, u32[]{:S(2)}, u32[]{:S(2)}) collective-permute-start(bf16[2,128,512]{2,1,0:T(8,128)(2,1)S(1)} %get-tuple-element.22), channel_id=1, source_target_pairs={{4,0},{8,4},{12,8},{5,1},{9,5},{13,9},{6,2},{10,6},{14,10},{7,3},{... | collective-permute-start | bytes 786440 | tf_op jit(solution)/shard_map/ppermute | solution.py:17
  98.0 12.3 %collective-permute-start.3 = (bf16[2,128,512]{2,1,0:T(8,128)(2,1)S(1)}, bf16[2,128,512]{2,1,0:T(8,128)(2,1)S(1)}, u32[]{:S(2)}, u32[]{:S(2)}) collective-permute-start(bf16[2,128,512]{2,1,0:T(8,128)(2,1)S(1)} %get-tuple-element.23), channel_id=1, source_target_pairs={{0,4},{4,8},{8,12},{1,5},{5,9},{9,13},{2,6},{6,10},{10,14},{3,7},{... | collective-permute-start | bytes 786440 | tf_op jit(solution)/shard_map/ppermute | solution.py:17
  105.9 7.9 %all-to-all-start.5 = ((bf16[4,64,256]{2,1,0:T(8,128)(2,1)}), bf16[4,64,256]{2,1,0:T(8,128)(2,1)S(1)}, u32[]{:S(2)}, u32[]{:S(2)}) async-start(bf16[4,64,256]{2,1,0:T(8,128)(2,1)} %all_to_all.120), calls=%async_computation.5 | async-start | bytes 262144 | tf_op jit(solution)/shard_map/all_to_all | solution.py:121
  113.8 7.9 %all-to-all-start.3 = ((bf16[4,64,256]{2,1,0:T(8,128)(2,1)}), bf16[4,64,256]{2,1,0:T(8,128)(2,1)S(1)}, u32[]{:S(2)}, u32[]{:S(2)}) async-start(bf16[4,64,256]{2,1,0:T(8,128)(2,1)} %all_to_all.113), calls=%async_computation.3 | async-start | bytes 262144 | tf_op jit(solution)/shard_map/all_to_all | solution.py:120
  128.8 7.9 %all-to-all-start.7 = ((bf16[4,64,256]{2,1,0:T(8,128)(2,1)}), bf16[4,64,256]{2,1,0:T(8,128)(2,1)S(1)}, u32[]{:S(2)}, u32[]{:S(2)}) async-start(bf16[4,64,256]{2,1,0:T(8,128)(2,1)} %bitcast.23), calls=%async_computation.7 | async-start | bytes 262144 | tf_op jit(solution)/shard_map/all_to_all | solution.py:123
where the time goes:
time: 139 us; the launch traced here: 137 us
  local copies, waits for them, and re-layouts  45.8 us (33%)
  starting transfers between devices  36.1 us (26%)
  waiting for transfers between devices  19.3 us (14%)
  other arithmetic  16.7 us (12%)
  matrix products  11.4 us (8%)
  blocking collectives  7.01 us (5%)
    reshape x2, local copies, waits for them, and re-layouts, one_block(): jnp.stack([key_grad, value_grad], 2)  19.9 us
    ppermute x4, starting transfers between devices, from_behind(): return lax.ppermute(block, axis, route)  11.9 us
    gather x3, local copies, waits for them, and re-layouts, one_block(): jnp.take(key_pool, flat_index, axis=0)  11.8 us
    scatter-add x1, other arithmetic, one_block(): grad_pool = grad_pool.at[flat_index].add(contrib)  8.31 us
    all_to_all x1, blocking collectives, shards(): lax.all_to_all(key_out, 'head', split_axis=0, concat_axis=1, tiled=True)  7.01 us
    sub x1, matrix products, attend_block(): exp_scores = jnp.exp(scores - row_max)  5.13 us
    all_to_all x1, waiting for transfers between devices, shards(): lax.all_to_all(out_grads, 'head', split_axis=1, concat_axis=0, tiled=True)  4.26 us
    all_to_all x1, starting transfers between devices, shards(): lax.all_to_all(key_rows, 'head', split_axis=1, concat_axis=0, tiled=True)  4.21 us
  transfers between devices with their start and end apart: 11, of which 6 were waited for; matrix products, arithmetic and copies ran while one was open for 9% of the time, Pallas kernels for 0%

commit v1 on v0

v1 whole, which is shorter than its diff:
```python
import functools
import math

import jax
import jax.numpy as jnp
from jax import lax
from jax.experimental import pallas as pl
from jax.experimental.pallas import tpu as pltpu
from jax.sharding import PartitionSpec as P

HEAD_DIM = 64
NEVER = -1e30
VMEM = pl.BlockSpec(memory_space=pltpu.VMEM)
SMEM = pl.BlockSpec(memory_space=pltpu.SMEM)
ANY = pl.BlockSpec(memory_space=pl.ANY)
NT = (((1,), (1,)), ((), ()))


def dot(left, right, dims=(((1,), (0,)), ((), ()))):
    return lax.dot_general(left, right, dims, preferred_element_type=jnp.float32)


def partners(node, owners):
    odd = lax.rem(node, 2)
    return node + 1 - 2 * odd, node - 1 + 2 * odd


def pair_routes(owners):
    first = [(i, i ^ 1 if i ^ 1 < owners else i) for i in range(owners)]
    other = [i - 1 + 2 * (i % 2) for i in range(owners)]
    second = [(i, j if 0 <= j < owners else i) for i, j in enumerate(other)]
    return first, second


def wanted(nbr_ref, partner, node, local_count, owners):
    inside = jnp.logical_and(partner >= 0, partner < owners)
    row = jnp.where(inside, partner, 0) * local_count
    found = jnp.int32(0)
    for p in range(local_count):
        for j in range(nbr_ref.shape[1]):
            entry = nbr_ref[row + p, j] - node * local_count
            mine = jnp.logical_and(entry >= 0, entry < local_count)
            found = jnp.where(jnp.logical_and(inside, mine), entry, found)
    return found


def pack_kernel(heads, width, one_ref, two_ref, *refs):
    outs, sem = refs[:heads], refs[heads]
    me = lax.axis_index("head")
    copies = []
    for d in range(heads):
        cols = pl.ds(pl.multiple_of((me ^ d) * width, width), width)
        for a, ref in enumerate((one_ref, two_ref)):
            copies.append(pltpu.make_async_copy(ref.at[:, cols], outs[d].at[a], sem.at[2 * d + a]))
    for copy in copies:
        copy.start()
    for copy in copies:
        copy.wait()


def unpack_kernel(heads, width, *refs):
    blocks, outs, sem = refs[:heads], refs[heads : heads + 2], refs[heads + 2]
    me = lax.axis_index("head")
    copies = []
    for d in range(heads):
        cols = pl.ds(pl.multiple_of((me ^ d) * width, width), width)
        for a, ref in enumerate(outs):
            copies.append(pltpu.make_async_copy(blocks[d].at[a], ref.at[:, cols], sem.at[2 * d + a]))
    for copy in copies:
        copy.start()
    for copy in copies:
        copy.wait()


def pick_kernel(heads, owners, local_count, nbr_ref, *refs):
    blocks, outs = refs[:heads], refs[heads:]
    rows = blocks[0].shape[1]
    per_patch = outs[0].shape[1] // rows
    me, node = lax.axis_index("head"), lax.axis_index("node")
    for out, partner in zip(outs, partners(node, owners)):
        chosen = wanted(nbr_ref, partner, node, local_count, owners)
        for t in range(per_patch):
            slot = me ^ (chosen * per_patch + t)
            value = blocks[0][...]
            for d in range(1, heads):
                value = jnp.where(slot == d, blocks[d][...], value)
            out[:, t * rows : (t + 1) * rows, :] = value


def attend_kernel(heads, owners, local_count, nbr_ref, *refs):
    kv, qg, far = refs[:heads], refs[heads : 2 * heads], refs[2 * heads : 2 * heads + 2]
    outs = refs[2 * heads + 2 :]
    mq_out, near_out, far_out = outs[:heads], outs[heads : 2 * heads], outs[2 * heads : 2 * heads + 2]
    w_all, ds_all = outs[2 * heads + 2 :]
    rows, width = kv[0].shape[1:]
    patch = far[0].shape[1]
    queries = heads * rows
    groups = width // HEAD_DIM
    me, node = lax.axis_index("head"), lax.axis_index("node")
    pair = partners(node, owners)

    own = [[jnp.int32(p == k) for k in range(local_count)] for p in range(local_count)]
    out_of = [[jnp.int32(0), jnp.int32(0)] for _ in range(local_count)]
    for p in range(local_count):
        for j in range(nbr_ref.shape[1]):
            entry = nbr_ref[node * local_count + p, j]
            for k in range(local_count):
                own[p][k] += jnp.where(entry == node * local_count + k, 1, 0)
            for s in range(2):
                start = pair[s] * local_count
                inside = jnp.logical_and(entry >= start, entry < start + local_count)
                out_of[p][s] += jnp.where(inside, 1, 0)

    def choose(index, values):
        value = values[0]
        for i in range(1, len(values)):
            value = jnp.where(index == i, values[i], value)
        return value

    patch_of = [((me ^ d) * rows) // patch for d in range(heads)]
    lane_block = lax.broadcasted_iota(jnp.int32, (1, queries), 1) // rows
    key_counts = []
    for d in range(heads):
        key_counts.append(
            [choose(patch_of[e], [choose(patch_of[d], own[p]) for p in range(local_count)]) for e in range(heads)]
        )
    for s in range(2):
        key_counts.append([choose(patch_of[e], [out_of[p][s] for p in range(local_count)]) for e in range(heads)])
    biases = []
    for counts in key_counts:
        row = jnp.zeros((1, queries), jnp.float32)
        for e in range(heads):
            row = jnp.where(lane_block == e, counts[e].astype(jnp.float32), row)
        biases.append(jnp.where(row > 0.5, jnp.log(jnp.maximum(row, 1.0)) * (1 / math.log(2)), NEVER))
    sizes = [rows] * heads + [patch, patch]
    bias = jnp.concatenate([jnp.broadcast_to(b, (n, queries)) for b, n in zip(biases, sizes)], 0)

    keys = jnp.concatenate([r[0] for r in kv] + [r[0] for r in far], 0)
    values = jnp.concatenate([r[1] for r in kv] + [r[1] for r in far], 0)
    query = jnp.concatenate([r[0] for r in qg], 0)
    grad = jnp.concatenate([r[1] for r in qg], 0)
    keys_t, values_t = keys.T, values.T
    lane_head = lax.broadcasted_iota(jnp.int32, (1, width), 1) // HEAD_DIM
    scale = HEAD_DIM**-0.5
    mixed_t, qgrad_t, query_h, grad_h = [], [], [], []
    for head in range(groups):
        feats = slice(head * HEAD_DIM, (head + 1) * HEAD_DIM)
        lanes = slice(head * queries, (head + 1) * queries)
        query_h.append(jnp.where(lane_head == head, query, jnp.zeros_like(query)))
        grad_h.append(jnp.where(lane_head == head, grad, jnp.zeros_like(grad)))
        scores = dot(keys, query_h[head], NT) * (scale / math.log(2)) + bias
        weights = jnp.exp2(scores - jnp.max(scores, 0, keepdims=True))
        weights = weights * (1.0 / jnp.sum(weights, 0, keepdims=True))
        weights_low = weights.astype(jnp.bfloat16)
        grad_weights = dot(values, grad_h[head], NT)
        row_dots = jnp.sum(weights * grad_weights, 0, keepdims=True)
        grad_scores = (weights * (grad_weights - row_dots)).astype(jnp.bfloat16)
        w_all[:, lanes] = weights_low
        ds_all[:, lanes] = grad_scores
        mixed_t.append(dot(values_t[feats], weights_low))
        qgrad_t.append(dot(keys_t[feats], grad_scores) * scale)
    mixed = jnp.concatenate(mixed_t, 0).T.astype(jnp.bfloat16)
    qgrad = jnp.concatenate(qgrad_t, 0).T.astype(jnp.bfloat16)
    key_grad = dot(ds_all[...], jnp.concatenate(query_h, 0)) * scale
    value_grad = dot(w_all[...], jnp.concatenate(grad_h, 0))
    for d in range(heads):
        span = slice(d * rows, (d + 1) * rows)
        mq_out[d][0], mq_out[d][1] = mixed[span], qgrad[span]
        near_out[d][0], near_out[d][1] = key_grad[span], value_grad[span]
    for s in range(2):
        span = slice(queries + s * patch, queries + (s + 1) * patch)
        far_out[s][0], far_out[s][1] = key_grad[span].astype(jnp.bfloat16), value_grad[span].astype(jnp.bfloat16)


def merge_kernel(heads, owners, local_count, nbr_ref, *refs):
    near, back, outs = refs[:heads], refs[heads : heads + 2], refs[heads + 2 :]
    rows = near[0].shape[1]
    per_patch = back[0].shape[1] // rows
    me, node = lax.axis_index("head"), lax.axis_index("node")
    chosen = [wanted(nbr_ref, partner, node, local_count, owners) for partner in partners(node, owners)]
    for d in range(heads):
        total = near[d][...]
        for s in range(2):
            slot = me ^ d
            for t in range(per_patch):
                hit = slot == chosen[s] * per_patch + t
                term = back[s][:, t * rows : (t + 1) * rows, :].astype(jnp.float32)
                total = total + jnp.where(hit, term, 0.0)
        outs[d][...] = total.astype(jnp.bfloat16)


def exchange(blocks):
    heads = len(blocks)
    return [blocks[0]] + [
        lax.ppermute(blocks[d], "head", [(i, i ^ d) for i in range(heads)]) for d in range(1, heads)
    ]


def shards(queries, key_rows, value_rows, out_grads, neighbours):
    rows, features = queries.shape
    heads, owners = lax.axis_size("head"), lax.axis_size("node")
    width = features // heads
    local_count = neighbours.shape[0] // owners
    patch = rows * heads // local_count
    low = jnp.bfloat16
    block = jax.ShapeDtypeStruct((2, rows, width), low)
    wide = jax.ShapeDtypeStruct((2, rows, width), jnp.float32)
    slab = jax.ShapeDtypeStruct((2, patch, width), low)
    sems = [pltpu.SemaphoreType.DMA((2 * heads,))]
    routes = pair_routes(owners)

    def pack(one, two):
        return pl.pallas_call(
            functools.partial(pack_kernel, heads, width),
            out_shape=[block] * heads,
            in_specs=[ANY] * 2,
            out_specs=[ANY] * heads,
            scratch_shapes=sems,
            name="pack",
        )(one, two)

    def unpack(blocks):
        return pl.pallas_call(
            functools.partial(unpack_kernel, heads, width),
            out_shape=[jax.ShapeDtypeStruct((rows, features), low)] * 2,
            in_specs=[ANY] * heads,
            out_specs=[ANY] * 2,
            scratch_shapes=sems,
            name="unpack",
        )(*blocks)

    kv = exchange(pack(key_rows, value_rows))
    qg = exchange(pack(queries, out_grads))
    picked = pl.pallas_call(
        functools.partial(pick_kernel, heads, owners, local_count),
        out_shape=[slab] * 2,
        in_specs=[SMEM] + [VMEM] * heads,
        out_specs=[VMEM] * 2,
        name="pick",
    )(neighbours, *kv)
    far = [lax.ppermute(p, "node", r) for p, r in zip(picked, routes)]
    results = pl.pallas_call(
        functools.partial(attend_kernel, heads, owners, local_count),
        out_shape=[block] * heads + [wide] * heads + [slab] * 2,
        in_specs=[SMEM] + [VMEM] * (2 * heads + 2),
        out_specs=[VMEM] * (2 * heads + 2),
        scratch_shapes=[
            pltpu.VMEM((heads * rows + 2 * patch, width // HEAD_DIM * heads * rows), low),
            pltpu.VMEM((heads * rows + 2 * patch, width // HEAD_DIM * heads * rows), low),
        ],
        name="attend",
        compiler_params=pltpu.CompilerParams(vmem_limit_bytes=32 * 1024 * 1024),
    )(neighbours, *kv, *qg, *far)
    mq, near, far_grads = results[:heads], results[heads : 2 * heads], results[2 * heads :]
    back = [lax.ppermute(p, "node", r) for p, r in zip(far_grads, routes)]
    merged = pl.pallas_call(
        functools.partial(merge_kernel, heads, owners, local_count),
        out_shape=[block] * heads,
        in_specs=[SMEM] + [VMEM] * (heads + 2),
        out_specs=[VMEM] * heads,
        name="merge",
    )(neighbours, *near, *back)
    mixed, query_grad = unpack(exchange(mq))
    key_grad, value_grad = unpack(exchange(merged))
    return mixed, query_grad, key_grad, value_grad


def solution(mesh):
    rows = P(("grp", "node", "head"), None)
    return jax.shard_map(
        shards,
        mesh=mesh,
        in_specs=(rows, rows, rows, rows, P("grp", None)),
        out_specs=(rows, rows, rows, rows),
        check_vma=False,
    )
```

time: 139 us -> 78.7 us (0.57)
  Pallas kernels: 0 us -> 44 us
  local copies, waits for them, and re-layouts: 45.8 us -> 6.67 us
  starting transfers between devices: 36.1 us -> 16.3 us
  other arithmetic: 16.7 us -> 0 us
  matrix products: 11.4 us -> 0 us
  waiting for transfers between devices: 19.3 us -> 9.47 us
  blocking collectives: 7.01 us -> 0 us
    pallas_call x0 -> x7, Pallas kernels: none -> 44 us  [the longest x2 18.2 us: pack(): pl.pallas_call(functools.partial(pack_kernel, heads, width), out_shape=[b...]
    all_to_all x7 -> x0, starting transfers between devices: 24.2 us -> none  [the longest x1 4.21 us: shards(): lax.all_to_all(key_rows, 'head', split_axis=1, concat_axis=0, tiled=True)]
    reshape x3 -> x0, local copies, waits for them, and re-layouts: 19.9 us -> none  [the longest x2 19.9 us: one_block(): jnp.stack([key_grad, value_grad], 2)]
    all_to_all x7 -> x0, waiting for transfers between devices: 19.3 us -> none  [the longest x1 4.26 us: shards(): lax.all_to_all(out_grads, 'head', split_axis=1, concat_axis=0, tiled=True)]
    gather x3 -> x0, local copies, waits for them, and re-layouts: 11.8 us -> none  [one_block(): jnp.take(key_pool, flat_index, axis=0)]
    all_to_all x10 -> x0, local copies, waits for them, and re-layouts: 10.7 us -> none  [the longest x1 1.57 us: shards(): lax.all_to_all(out_grads, 'head', split_axis=1, concat_axis=0, tiled=True)]
    ppermute x4 -> x16, waiting for transfers between devices: 0.01 us -> 9.47 us  [the longest x12 8.29 us: exchange(): lax.ppermute(blocks[d], 'head', [(i, i ^ d) for i in range(heads)])]
    scatter-add x1 -> x0, other arithmetic: 8.31 us -> none  [one_block(): grad_pool = grad_pool.at[flat_index].add(contrib)]
  transfers between devices with their start and end apart: 11 -> 16, of which waited for: 6 -> 5; matrix products, arithmetic and copies ran while one was open for 9% -> 0% of each run, Pallas kernels for 0% -> 26%
where the time goes in v1:
time: 78.7 us; the launch traced here: 77.3 us
  Pallas kernels  44 us (56%)
  starting transfers between devices  16.3 us (21%)
  waiting for transfers between devices  9.47 us (12%)
  local copies, waits for them, and re-layouts  6.67 us (8%)
  between operations  0.84 us (1%)
    pallas_call x2, Pallas kernels, pack(): pl.pallas_call(functools.partial(pack_kernel, heads, width), out_shape=[b...  18.2 us
    pallas_call x2, Pallas kernels, unpack(): pl.pallas_call(functools.partial(unpack_kernel, heads, width), out_shape=...  18.2 us
    ppermute x12, starting transfers between devices, exchange(): lax.ppermute(blocks[d], 'head', [(i, i ^ d) for i in range(heads)])  8.88 us
    ppermute x12, waiting for transfers between devices, exchange(): lax.ppermute(blocks[d], 'head', [(i, i ^ d) for i in range(heads)])  8.29 us
    unnamed x44, local copies, waits for them, and re-layouts  6.67 us
    ppermute x2, starting transfers between devices, shards(): back = [lax.ppermute(p, 'node', r) for p, r in zip(far_grads, routes)]  4.17 us
    pallas_call x1, Pallas kernels, shards(): pl.pallas_call(functools.partial(attend_kernel, heads, owners, local_coun...  3.68 us
    ppermute x2, starting transfers between devices, shards(): far = [lax.ppermute(p, 'node', r) for p, r in zip(picked, routes)]  3.27 us
  transfers between devices with their start and end apart: 16, of which 5 were waited for; matrix products, arithmetic and copies ran while one was open for 0% of the time, Pallas kernels for 26%

profile of v1, /device:TPU:0, one launch (start us, length us, event | category | flops | bytes accessed | tf_op | source)
XLA Modules:
  0.0 77.3 jit_solution(15940217641748049588)
XLA Ops:
  0.6 9.1 %pack.2 = (bf16[2,64,256]{2,1,0:T(8,128)(2,1)}, bf16[2,64,256]{2,1,0:T(8,128)(2,1)}, bf16[2,64,256]{2,1,0:T(8,128)(2,1)}, bf16[2,64,256]{2,1,0:T(8,128)(2,1)}) custom-call(bf16[64,1024]{1,0:T(8,128)(2,1)} %one_ref.2, bf16[64,1024]{1,0:T(8,128)(2,1)} %two_ref.2), custom_call_target="tpu_custom_call" | custom-call | tf_op jit(solution)/shard_map/pack/pallas_call | solution.py:213
  9.8 0.5 collective-permute-start
  10.3 2.6 %collective-permute-start.1 = (bf16[2,64,256]{2,1,0:T(8,128)(2,1)}, bf16[2,64,256]{2,1,0:T(8,128)(2,1)S(1)}, u32[]{:S(2)}, u32[]{:S(2)}) collective-permute-start(bf16[2,64,256]{2,1,0:T(8,128)(2,1)} %get-tuple-element.34), channel_id=1, source_target_pairs={{0,2},{1,3},{2,0},{3,1},{4,6},{5,7},{6,4},{7,5},{8,10},{9,11},{10,... | collective-permute-start | bytes 196616 | tf_op jit(solution)/shard_map/ppermute | solution.py:195
  12.8 0.1 collective-permute-start.2
  12.9 2.8 %collective-permute-done.1.refs_2_ = bf16[2,64,256]{2,1,0:T(8,128)(2,1)S(1)} collective-permute-done((bf16[2,64,256]{2,1,0:T(8,128)(2,1)}, bf16[2,64,256]{2,1,0:T(8,128)(2,1)S(1)}, u32[]{:S(2)}, u32[]{:S(2)}) %collective-permute-start.1) | collective-permute-done | bytes 65568 | tf_op jit(solution)/shard_map/ppermute | solution.py:195
  15.7 1.4 %collective-permute-done.2.refs_3_ = bf16[2,64,256]{2,1,0:T(8,128)(2,1)S(1)} collective-permute-done((bf16[2,64,256]{2,1,0:T(8,128)(2,1)}, bf16[2,64,256]{2,1,0:T(8,128)(2,1)S(1)}, u32[]{:S(2)}, u32[]{:S(2)}) %collective-permute-start.2) | collective-permute-done | bytes 65568 | tf_op jit(solution)/shard_map/ppermute | solution.py:195
  17.2 0.6 copy-done.5
  17.8 1.7 %pick.1 = (bf16[2,128,256]{2,1,0:T(8,128)(2,1)}, bf16[2,128,256]{2,1,0:T(8,128)(2,1)}) custom-call(s32[8,8]{1,0:T(8,128)} %nbr_ref.5, bf16[2,64,256]{2,1,0:T(8,128)(2,1)} %get-tuple-element.32.refs_0_, bf16[2,64,256]{2,1,0:T(8,128)(2,1)} %copy-done.1, bf16[2,64,256]{2,1,0:T(8,128)(2,1)} %copy-done.3, bf16[2,64,256]{2,1,0:T(8,128)(2,1)} %copy-done.5), custom_call_target="tpu_custom_call" | custom-call | tf_op jit(solution)/shard_map/pick/pallas_call | solution.py:234
  19.6 1.6 %collective-permute-start.6 = (bf16[2,128,256]{2,1,0:T(8,128)(2,1)}, bf16[2,128,256]{2,1,0:T(8,128)(2,1)S(1)}, u32[]{:S(2)}, u32[]{:S(2)}) collective-permute-start(bf16[2,128,256]{2,1,0:T(8,128)(2,1)} %get-tuple-element.40), channel_id=1, source_target_pairs={{0,4},{4,0},{8,12},{12,8},{1,5},{5,1},{9,13},{13,9},{2,6},{6,2},{1... | collective-permute-start | bytes 393224 | tf_op jit(solution)/shard_map/ppermute | solution.py:241
  21.1 1.7 %collective-permute-start.7 = (bf16[2,128,256]{2,1,0:T(8,128)(2,1)}, bf16[2,128,256]{2,1,0:T(8,128)(2,1)S(1)}, u32[]{:S(2)}, u32[]{:S(2)}) collective-permute-start(bf16[2,128,256]{2,1,0:T(8,128)(2,1)} %get-tuple-element.41), channel_id=1, source_target_pairs={{0,0},{4,8},{8,4},{12,12},{1,1},{5,9},{9,5},{13,13},{2,2},{6,10},{... | collective-permute-start | bytes 393224 | tf_op jit(solution)/shard_map/ppermute | solution.py:241
  22.8 9.1 %pack.3 = (bf16[2,64,256]{2,1,0:T(8,128)(2,1)}, bf16[2,64,256]{2,1,0:T(8,128)(2,1)}, bf16[2,64,256]{2,1,0:T(8,128)(2,1)}, bf16[2,64,256]{2,1,0:T(8,128)(2,1)}) custom-call(bf16[64,1024]{1,0:T(8,128)(2,1)} %one_ref.3, bf16[64,1024]{1,0:T(8,128)(2,1)} %two_ref.3), custom_call_target="tpu_custom_call" | custom-call | tf_op jit(solution)/shard_map/pack/pallas_call | solution.py:213
  32.0 0.0 copy-start.13
  32.0 0.1 collective-permute-start.3
  32.1 1.3 %collective-permute-start.4 = (bf16[2,64,256]{2,1,0:T(8,128)(2,1)}, bf16[2,64,256]{2,1,0:T(8,128)(2,1)S(1)}, u32[]{:S(2)}, u32[]{:S(2)}) collective-permute-start(bf16[2,64,256]{2,1,0:T(8,128)(2,1)} %get-tuple-element.38), channel_id=1, source_target_pairs={{0,2},{1,3},{2,0},{3,1},{4,6},{5,7},{6,4},{7,5},{8,10},{9,11},{10,... | collective-permute-start | bytes 196616 | tf_op jit(solution)/shard_map/ppermute | solution.py:195
  33.4 0.5 collective-permute-start.5
  33.9 0.0 collective-permute-done.3.refs_5_
  33.9 3.1 %collective-permute-done.4.refs_6_ = bf16[2,64,256]{2,1,0:T(8,128)(2,1)S(1)} collective-permute-done((bf16[2,64,256]{2,1,0:T(8,128)(2,1)}, bf16[2,64,256]{2,1,0:T(8,128)(2,1)S(1)}, u32[]{:S(2)}, u32[]{:S(2)}) %collective-permute-start.4) | collective-permute-done | bytes 65568 | tf_op jit(solution)/shard_map/ppermute | solution.py:195
  37.0 0.9 %collective-permute-done.5.refs_7_ = bf16[2,64,256]{2,1,0:T(8,128)(2,1)S(1)} collective-permute-done((bf16[2,64,256]{2,1,0:T(8,128)(2,1)}, bf16[2,64,256]{2,1,0:T(8,128)(2,1)S(1)}, u32[]{:S(2)}, u32[]{:S(2)}) %collective-permute-start.5) | collective-permute-done | bytes 65568 | tf_op jit(solution)/shard_map/ppermute | solution.py:195
  37.9 0.0 collective-permute-done.6.refs_8_
  37.9 0.0 collective-permute-done.7.refs_9_
  38.0 0.8 %copy-done.11 = bf16[2,64,256]{2,1,0:T(8,128)(2,1)S(1)} copy-done((bf16[2,64,256]{2,1,0:T(8,128)(2,1)S(1)}, bf16[2,64,256]{2,1,0:T(8,128)(2,1)}, u32[]{:S(2)}) %copy-start.11) | copy-done | bytes 65560
  38.8 3.7 %attend.1 = (bf16[2,64,256]{2,1,0:T(8,128)(2,1)S(1)}, bf16[2,64,256]{2,1,0:T(8,128)(2,1)S(1)}, bf16[2,64,256]{2,1,0:T(8,128)(2,1)S(1)}, bf16[2,64,256]{2,1,0:T(8...) custom-call(s32[8,8]{1,0:T(8,128)S(1)} %copy-done.13, ...), custom_call_target="tpu_custom_call" | custom-call | tf_op jit(solution)/shard_map/attend/pallas_call | solution.py:242
  42.5 0.0 copy-start.7
  42.5 0.6 copy-done.7
  43.2 0.7 copy-done.8
  43.8 0.7 copy-done.9
  44.5 0.7 copy-done.10
  45.1 0.6 copy-done.12
  45.7 3.5 %collective-permute-start.11 = (bf16[2,128,256]{2,1,0:T(8,128)(2,1)S(1)}, bf16[2,128,256]{2,1,0:T(8,128)(2,1)S(1)}, u32[]{:S(2)}, u32[]{:S(2)}) collective-permute-start(bf16[2,128,256]{2,1,0:T(8,128)(2,1)S(1)} %get-tuple-element.52), channel_id=1, source_target_pairs={{0,4},{4,0},{8,12},{12,8},{1,5},{5,1},{9,13},{13,9},{2,6},{6,2},{1... | collective-permute-start | bytes 393224 | tf_op jit(solution)/shard_map/ppermute | solution.py:255
  49.3 0.7 collective-permute-start.12
  49.9 0.1 collective-permute-start.8
  50.0 1.1 %collective-permute-start.9 = (bf16[2,64,256]{2,1,0:T(8,128)(2,1)S(1)}, bf16[2,64,256]{2,1,0:T(8,128)(2,1)S(1)}, u32[]{:S(2)}, u32[]{:S(2)}) collective-permute-start(bf16[2,64,256]{2,1,0:T(8,128)(2,1)S(1)} %get-tuple-element.44), channel_id=1, source_target_pairs={{0,2},{1,3},{2,0},{3,1},{4,6},{5,7},{6,4},{7,5},{8,10},{9,11},{10,... | collective-permute-start | bytes 196616 | tf_op jit(solution)/shard_map/ppermute | solution.py:195
  51.1 0.7 collective-permute-start.10
  51.9 1.2 %collective-permute-done.11.refs_4_ = bf16[2,128,256]{2,1,0:T(8,128)(2,1)S(1)} collective-permute-done((bf16[2,128,256]{2,1,0:T(8,128)(2,1)S(1)}, bf16[2,128,256]{2,1,0:T(8,128)(2,1)S(1)}, u32[]{:S(2)}, u32[]{:S(2)}) %collective-permute-start.11) | collective-permute-done | bytes 131104 | tf_op jit(solution)/shard_map/ppermute | solution.py:255
  53.0 0.6 copy-done.14
  53.7 0.0 copy-done.15
  53.7 2.2 %merge.1 = (bf16[2,64,256]{2,1,0:T(8,128)(2,1)}, bf16[2,64,256]{2,1,0:T(8,128)(2,1)}, bf16[2,64,256]{2,1,0:T(8,128)(2,1)}, bf16[2,64,256]{2,1,0:T(8,128)(2,1)}) custom-call(s32[8,8]{1,0:T(8,128)} %nbr_ref.5, f32[2,64,256]{2,1,0:T(8,128)} %copy-done.7, f32[2,64,256]{2,1,0:T(8,128)} %copy-done.8, f32[2,64,256]{2,1,0:T(8,128)} %copy-done.9, ...), custom_call_target="tpu_custom_call" | custom-call | tf_op jit(solution)/shard_map/merge/pallas_call | solution.py:256
  55.9 1.2 %collective-permute-start.14 = (bf16[2,64,256]{2,1,0:T(8,128)(2,1)}, bf16[2,64,256]{2,1,0:T(8,128)(2,1)S(1)}, u32[]{:S(2)}, u32[]{:S(2)}) collective-permute-start(bf16[2,64,256]{2,1,0:T(8,128)(2,1)} %get-tuple-element.56), channel_id=1, source_target_pairs={{0,2},{1,3},{2,0},{3,1},{4,6},{5,7},{6,4},{7,5},{8,10},{9,11},{10,... | collective-permute-start | bytes 196616 | tf_op jit(solution)/shard_map/ppermute | solution.py:195
  57.1 0.6 collective-permute-start.15
  57.8 0.0 collective-permute-done.9.refs_2_
  57.8 0.0 collective-permute-done.10.refs_3_
  57.8 0.6 copy-done.17
  58.4 0.0 copy-done.18
  58.4 9.1 %unpack.2 = (bf16[64,1024]{1,0:T(8,128)(2,1)}, bf16[64,1024]{1,0:T(8,128)(2,1)}) custom-call(bf16[2,64,256]{2,1,0:T(8,128)(2,1)} %copy-done.12, bf16[2,64,256]{2,1,0:T(8,128)(2,1)} %copy-done.16, bf16[2,64,256]{2,1,0:T(8,128)(2,1)} %copy-done.17, bf16[2,64,256]{2,1,0:T(8,128)(2,1)} %copy-done.18), custom_call_target="tpu_custom_call" | custom-call | tf_op jit(solution)/shard_map/unpack/pallas_call | solution.py:223
  67.6 0.6 copy-done.19
  68.2 0.0 copy-done.20
  68.2 0.0 copy-done.21
  68.2 9.1 %unpack.3 = (bf16[64,1024]{1,0:T(8,128)(2,1)}, bf16[64,1024]{1,0:T(8,128)(2,1)}) custom-call(bf16[2,64,256]{2,1,0:T(8,128)(2,1)} %get-tuple-element.54.refs_0_, bf16[2,64,256]{2,1,0:T(8,128)(2,1)} %copy-done.19, bf16[2,64,256]{2,1,0:T(8,128)(2,1)} %copy-done.20, bf16[2,64,256]{2,1,0:T(8,128)(2,1)} %copy-done.21), custom_call_target="tpu_custom_call" | custom-call | tf_op jit(solution)/shard_map/unpack/pallas_call | solution.py:223
  (35 shorter events, 0.1 us)
Async XLA Ops:
  9.8 3.2 %collective-permute-start = (bf16[2,64,256]{2,1,0:T(8,128)(2,1)}, bf16[2,64,256]{2,1,0:T(8,128)(2,1)S(1)}, u32[]{:S(2)}, u32[]{:S(2)}) collective-permute-start(bf16[2,64,256]{2,1,0:T(8,128)(2,1)} %get-tuple-element.33), channel_id=1, source_target_pairs={{0,1},{1,0},{2,3},{3,2},{4,5},{5,4},{6,7},{7,6},{8,9},{9,8},{10,11... | collective-permute-start | bytes 196616 | tf_op jit(solution)/shard_map/ppermute | solution.py:195
  10.3 5.5 %collective-permute-start.1 = (bf16[2,64,256]{2,1,0:T(8,128)(2,1)}, bf16[2,64,256]{2,1,0:T(8,128)(2,1)S(1)}, u32[]{:S(2)}, u32[]{:S(2)}) collective-permute-start(bf16[2,64,256]{2,1,0:T(8,128)(2,1)} %get-tuple-element.34), channel_id=1, source_target_pairs={{0,2},{1,3},{2,0},{3,1},{4,6},{5,7},{6,4},{7,5},{8,10},{9,11},{10,... | collective-permute-start | bytes 196616 | tf_op jit(solution)/shard_map/ppermute | solution.py:195
  12.8 4.3 %collective-permute-start.2 = (bf16[2,64,256]{2,1,0:T(8,128)(2,1)}, bf16[2,64,256]{2,1,0:T(8,128)(2,1)S(1)}, u32[]{:S(2)}, u32[]{:S(2)}) collective-permute-start(bf16[2,64,256]{2,1,0:T(8,128)(2,1)} %get-tuple-element.35), channel_id=1, source_target_pairs={{0,3},{1,2},{2,1},{3,0},{4,7},{5,6},{6,5},{7,4},{8,11},{9,10},{10,... | collective-permute-start | bytes 196616 | tf_op jit(solution)/shard_map/ppermute | solution.py:195
  12.9 4.3 %copy-start.1 = (bf16[2,64,256]{2,1,0:T(8,128)(2,1)}, bf16[2,64,256]{2,1,0:T(8,128)(2,1)S(1)}, u32[]{:S(2)}) copy-start(bf16[2,64,256]{2,1,0:T(8,128)(2,1)S(1)} %collective-permute-done.refs_1_) | copy-start | bytes 196612
  15.7 1.5 %copy-start.3 = (bf16[2,64,256]{2,1,0:T(8,128)(2,1)}, bf16[2,64,256]{2,1,0:T(8,128)(2,1)S(1)}, u32[]{:S(2)}) copy-start(bf16[2,64,256]{2,1,0:T(8,128)(2,1)S(1)} %collective-permute-done.1.refs_2_) | copy-start | bytes 196612
  17.2 0.6 copy-start.5
  19.6 18.4 %collective-permute-start.6 = (bf16[2,128,256]{2,1,0:T(8,128)(2,1)}, bf16[2,128,256]{2,1,0:T(8,128)(2,1)S(1)}, u32[]{:S(2)}, u32[]{:S(2)}) collective-permute-start(bf16[2,128,256]{2,1,0:T(8,128)(2,1)} %get-tuple-element.40), channel_id=1, source_target_pairs={{0,4},{4,0},{8,12},{12,8},{1,5},{5,1},{9,13},{13,9},{2,6},{6,2},{1... | collective-permute-start | bytes 393224 | tf_op jit(solution)/shard_map/ppermute | solution.py:241
  21.1 16.8 %copy-start = (bf16[2,64,256]{2,1,0:T(8,128)(2,1)S(1)}, bf16[2,64,256]{2,1,0:T(8,128)(2,1)}, u32[]{:S(2)}) copy-start(bf16[2,64,256]{2,1,0:T(8,128)(2,1)} %get-tuple-element.32.refs_0_) | copy-start | bytes 196612
  21.1 16.8 %copy-start.2 = (bf16[2,64,256]{2,1,0:T(8,128)(2,1)S(1)}, bf16[2,64,256]{2,1,0:T(8,128)(2,1)}, u32[]{:S(2)}) copy-start(bf16[2,64,256]{2,1,0:T(8,128)(2,1)} %copy-done.1) | copy-start | bytes 196612
  21.1 16.8 %copy-start.4 = (bf16[2,64,256]{2,1,0:T(8,128)(2,1)S(1)}, bf16[2,64,256]{2,1,0:T(8,128)(2,1)}, u32[]{:S(2)}) copy-start(bf16[2,64,256]{2,1,0:T(8,128)(2,1)} %copy-done.3) | copy-start | bytes 196612
  21.1 16.8 %copy-start.6 = (bf16[2,64,256]{2,1,0:T(8,128)(2,1)S(1)}, bf16[2,64,256]{2,1,0:T(8,128)(2,1)}, u32[]{:S(2)}) copy-start(bf16[2,64,256]{2,1,0:T(8,128)(2,1)} %copy-done.5) | copy-start | bytes 196612
  21.1 16.8 %collective-permute-start.7 = (bf16[2,128,256]{2,1,0:T(8,128)(2,1)}, bf16[2,128,256]{2,1,0:T(8,128)(2,1)S(1)}, u32[]{:S(2)}, u32[]{:S(2)}) collective-permute-start(bf16[2,128,256]{2,1,0:T(8,128)(2,1)} %get-tuple-element.41), channel_id=1, source_target_pairs={{0,0},{4,8},{8,4},{12,12},{1,1},{5,9},{9,5},{13,13},{2,2},{6,10},{... | collective-permute-start | bytes 393224 | tf_op jit(solution)/shard_map/ppermute | solution.py:241
  32.0 6.0 %copy-start.13 = (s32[8,8]{1,0:T(8,128)S(1)}, s32[8,8]{1,0:T(8,128)}, u32[]{:S(2)}) copy-start(s32[8,8]{1,0:T(8,128)} %nbr_ref.5) | copy-start | bytes 772
  32.0 1.9 %collective-permute-start.3 = (bf16[2,64,256]{2,1,0:T(8,128)(2,1)}, bf16[2,64,256]{2,1,0:T(8,128)(2,1)S(1)}, u32[]{:S(2)}, u32[]{:S(2)}) collective-permute-start(bf16[2,64,256]{2,1,0:T(8,128)(2,1)} %get-tuple-element.37), channel_id=1, source_target_pairs={{0,1},{1,0},{2,3},{3,2},{4,5},{5,4},{6,7},{7,6},{8,9},{9,8},{10,11... | collective-permute-start | bytes 196616 | tf_op jit(solution)/shard_map/ppermute | solution.py:195
  32.1 5.0 %collective-permute-start.4 = (bf16[2,64,256]{2,1,0:T(8,128)(2,1)}, bf16[2,64,256]{2,1,0:T(8,128)(2,1)S(1)}, u32[]{:S(2)}, u32[]{:S(2)}) collective-permute-start(bf16[2,64,256]{2,1,0:T(8,128)(2,1)} %get-tuple-element.38), channel_id=1, source_target_pairs={{0,2},{1,3},{2,0},{3,1},{4,6},{5,7},{6,4},{7,5},{8,10},{9,11},{10,... | collective-permute-start | bytes 196616 | tf_op jit(solution)/shard_map/ppermute | solution.py:195
  33.4 4.5 %collective-permute-start.5 = (bf16[2,64,256]{2,1,0:T(8,128)(2,1)}, bf16[2,64,256]{2,1,0:T(8,128)(2,1)S(1)}, u32[]{:S(2)}, u32[]{:S(2)}) collective-permute-start(bf16[2,64,256]{2,1,0:T(8,128)(2,1)} %get-tuple-element.39), channel_id=1, source_target_pairs={{0,3},{1,2},{2,1},{3,0},{4,7},{5,6},{6,5},{7,4},{8,11},{9,10},{10,... | collective-permute-start | bytes 196616 | tf_op jit(solution)/shard_map/ppermute | solution.py:195
  38.0 0.8 %copy-start.11 = (bf16[2,64,256]{2,1,0:T(8,128)(2,1)S(1)}, bf16[2,64,256]{2,1,0:T(8,128)(2,1)}, u32[]{:S(2)}) copy-start(bf16[2,64,256]{2,1,0:T(8,128)(2,1)} %get-tuple-element.36.refs_4_) | copy-start | bytes 196612
  42.5 0.7 copy-start.7
  43.2 0.7 copy-start.8
  43.8 0.7 copy-start.9
  44.5 0.7 copy-start.10
  45.1 0.6 copy-start.12
  45.7 7.3 %collective-permute-start.11 = (bf16[2,128,256]{2,1,0:T(8,128)(2,1)S(1)}, bf16[2,128,256]{2,1,0:T(8,128)(2,1)S(1)}, u32[]{:S(2)}, u32[]{:S(2)}) collective-permute-start(bf16[2,128,256]{2,1,0:T(8,128)(2,1)S(1)} %get-tuple-element.52), channel_id=1, source_target_pairs={{0,4},{4,0},{8,12},{12,8},{1,5},{5,1},{9,13},{13,9},{2,6},{6,2},{1... | collective-permute-start | bytes 393224 | tf_op jit(solution)/shard_map/ppermute | solution.py:255
  49.3 3.8 %collective-permute-start.12 = (bf16[2,128,256]{2,1,0:T(8,128)(2,1)S(1)}, bf16[2,128,256]{2,1,0:T(8,128)(2,1)S(1)}, u32[]{:S(2)}, u32[]{:S(2)}) collective-permute-start(bf16[2,128,256]{2,1,0:T(8,128)(2,1)S(1)} %get-tuple-element.53), channel_id=1, source_target_pairs={{0,0},{4,8},{8,4},{12,12},{1,1},{5,9},{9,5},{13,13},{2,2},{6,10},{... | collective-permute-start | bytes 393224 | tf_op jit(solution)/shard_map/ppermute | solution.py:255
  49.9 7.2 %collective-permute-start.8 = (bf16[2,64,256]{2,1,0:T(8,128)(2,1)S(1)}, bf16[2,64,256]{2,1,0:T(8,128)(2,1)S(1)}, u32[]{:S(2)}, u32[]{:S(2)}) collective-permute-start(bf16[2,64,256]{2,1,0:T(8,128)(2,1)S(1)} %get-tuple-element.43), channel_id=1, source_target_pairs={{0,1},{1,0},{2,3},{3,2},{4,5},{5,4},{6,7},{7,6},{8,9},{9,8},{10,11... | collective-permute-start | bytes 196616 | tf_op jit(solution)/shard_map/ppermute | solution.py:195
  50.0 7.8 %collective-permute-start.9 = (bf16[2,64,256]{2,1,0:T(8,128)(2,1)S(1)}, bf16[2,64,256]{2,1,0:T(8,128)(2,1)S(1)}, u32[]{:S(2)}, u32[]{:S(2)}) collective-permute-start(bf16[2,64,256]{2,1,0:T(8,128)(2,1)S(1)} %get-tuple-element.44), channel_id=1, source_target_pairs={{0,2},{1,3},{2,0},{3,1},{4,6},{5,7},{6,4},{7,5},{8,10},{9,11},{10,... | collective-permute-start | bytes 196616 | tf_op jit(solution)/shard_map/ppermute | solution.py:195
  51.1 6.6 %collective-permute-start.10 = (bf16[2,64,256]{2,1,0:T(8,128)(2,1)S(1)}, bf16[2,64,256]{2,1,0:T(8,128)(2,1)S(1)}, u32[]{:S(2)}, u32[]{:S(2)}) collective-permute-start(bf16[2,64,256]{2,1,0:T(8,128)(2,1)S(1)} %get-tuple-element.45), channel_id=1, source_target_pairs={{0,3},{1,2},{2,1},{3,0},{4,7},{5,6},{6,5},{7,4},{8,11},{9,10},{10,... | collective-permute-start | bytes 196616 | tf_op jit(solution)/shard_map/ppermute | solution.py:195
  53.0 0.7 copy-start.14
  53.0 0.7 copy-start.15
  55.9 11.6 %collective-permute-start.13 = (bf16[2,64,256]{2,1,0:T(8,128)(2,1)}, bf16[2,64,256]{2,1,0:T(8,128)(2,1)S(1)}, u32[]{:S(2)}, u32[]{:S(2)}) collective-permute-start(bf16[2,64,256]{2,1,0:T(8,128)(2,1)} %get-tuple-element.55), channel_id=1, source_target_pairs={{0,1},{1,0},{2,3},{3,2},{4,5},{5,4},{6,7},{7,6},{8,9},{9,8},{10,11... | collective-permute-start | bytes 196616 | tf_op jit(solution)/shard_map/ppermute | solution.py:195
  55.9 11.7 %collective-permute-start.14 = (bf16[2,64,256]{2,1,0:T(8,128)(2,1)}, bf16[2,64,256]{2,1,0:T(8,128)(2,1)S(1)}, u32[]{:S(2)}, u32[]{:S(2)}) collective-permute-start(bf16[2,64,256]{2,1,0:T(8,128)(2,1)} %get-tuple-element.56), channel_id=1, source_target_pairs={{0,2},{1,3},{2,0},{3,1},{4,6},{5,7},{6,4},{7,5},{8,10},{9,11},{10,... | collective-permute-start | bytes 196616 | tf_op jit(solution)/shard_map/ppermute | solution.py:195
  57.1 0.6 copy-start.16
  57.1 10.4 %collective-permute-start.15 = (bf16[2,64,256]{2,1,0:T(8,128)(2,1)}, bf16[2,64,256]{2,1,0:T(8,128)(2,1)S(1)}, u32[]{:S(2)}, u32[]{:S(2)}) collective-permute-start(bf16[2,64,256]{2,1,0:T(8,128)(2,1)} %get-tuple-element.57), channel_id=1, source_target_pairs={{0,3},{1,2},{2,1},{3,0},{4,7},{5,6},{6,5},{7,4},{8,11},{9,10},{10,... | collective-permute-start | bytes 196616 | tf_op jit(solution)/shard_map/ppermute | solution.py:195
  57.8 0.6 copy-start.17
  57.8 0.6 copy-start.18
  67.5 0.6 copy-start.19
  67.6 0.7 copy-start.20
  67.6 0.6 copy-start.21

commit v2 on v1

--- a/solution.py
+++ b/solution.py
@@ -12,7 +12,7 @@
 NEVER = -1e30
 VMEM = pl.BlockSpec(memory_space=pltpu.VMEM)
 SMEM = pl.BlockSpec(memory_space=pltpu.SMEM)
-ANY = pl.BlockSpec(memory_space=pl.ANY)
+SMALL = pltpu.CompilerParams(vmem_limit_bytes=8 * 1024 * 1024)
 NT = (((1,), (1,)), ((), ()))
 
 
@@ -44,32 +44,20 @@
     return found
 
 
-def pack_kernel(heads, width, one_ref, two_ref, *refs):
-    outs, sem = refs[:heads], refs[heads]
+def pack_kernel(heads, width, one_ref, two_ref, *outs):
     me = lax.axis_index("head")
-    copies = []
-    for d in range(heads):
+    for d, out in enumerate(outs):
         cols = pl.ds(pl.multiple_of((me ^ d) * width, width), width)
-        for a, ref in enumerate((one_ref, two_ref)):
-            copies.append(pltpu.make_async_copy(ref.at[:, cols], outs[d].at[a], sem.at[2 * d + a]))
-    for copy in copies:
-        copy.start()
-    for copy in copies:
-        copy.wait()
+        out[0], out[1] = one_ref[:, cols], two_ref[:, cols]
 
 
 def unpack_kernel(heads, width, *refs):
-    blocks, outs, sem = refs[:heads], refs[heads : heads + 2], refs[heads + 2]
+    blocks, outs = refs[:heads], refs[heads:]
     me = lax.axis_index("head")
-    copies = []
-    for d in range(heads):
+    for d, block in enumerate(blocks):
         cols = pl.ds(pl.multiple_of((me ^ d) * width, width), width)
-        for a, ref in enumerate(outs):
-            copies.append(pltpu.make_async_copy(blocks[d].at[a], ref.at[:, cols], sem.at[2 * d + a]))
-    for copy in copies:
-        copy.start()
-    for copy in copies:
-        copy.wait()
+        for a, out in enumerate(outs):
+            out[:, cols] = block[a]
 
 
 def pick_kernel(heads, owners, local_count, nbr_ref, *refs):
@@ -206,27 +194,26 @@
     block = jax.ShapeDtypeStruct((2, rows, width), low)
     wide = jax.ShapeDtypeStruct((2, rows, width), jnp.float32)
     slab = jax.ShapeDtypeStruct((2, patch, width), low)
-    sems = [pltpu.SemaphoreType.DMA((2 * heads,))]
     routes = pair_routes(owners)
 
     def pack(one, two):
         return pl.pallas_call(
             functools.partial(pack_kernel, heads, width),
             out_shape=[block] * heads,
-            in_specs=[ANY] * 2,
-            out_specs=[ANY] * heads,
-            scratch_shapes=sems,
+            in_specs=[VMEM] * 2,
+            out_specs=[VMEM] * heads,
             name="pack",
+            compiler_params=SMALL,
         )(one, two)
 
     def unpack(blocks):
         return pl.pallas_call(
             functools.partial(unpack_kernel, heads, width),
             out_shape=[jax.ShapeDtypeStruct((rows, features), low)] * 2,
-            in_specs=[ANY] * heads,
-            out_specs=[ANY] * 2,
-            scratch_shapes=sems,
+            in_specs=[VMEM] * heads,
+            out_specs=[VMEM] * 2,
             name="unpack",
+            compiler_params=SMALL,
         )(*blocks)
 
     kv = exchange(pack(key_rows, value_rows))
@@ -237,6 +224,7 @@
         in_specs=[SMEM] + [VMEM] * heads,
         out_specs=[VMEM] * 2,
         name="pick",
+        compiler_params=SMALL,
     )(neighbours, *kv)
     far = [lax.ppermute(p, "node", r) for p, r in zip(picked, routes)]
     results = pl.pallas_call(
@@ -249,7 +237,7 @@
             pltpu.VMEM((heads * rows + 2 * patch, width // HEAD_DIM * heads * rows), low),
         ],
         name="attend",
-        compiler_params=pltpu.CompilerParams(vmem_limit_bytes=32 * 1024 * 1024),
+        compiler_params=pltpu.CompilerParams(vmem_limit_bytes=24 * 1024 * 1024),
     )(neighbours, *kv, *qg, *far)
     mq, near, far_grads = results[:heads], results[heads : 2 * heads], results[2 * heads :]
     back = [lax.ppermute(p, "node", r) for p, r in zip(far_grads, routes)]
@@ -259,6 +247,7 @@
         in_specs=[SMEM] + [VMEM] * (heads + 2),
         out_specs=[VMEM] * heads,
         name="merge",
+        compiler_params=SMALL,
     )(neighbours, *near, *back)
     mixed, query_grad = unpack(exchange(mq))
     key_grad, value_grad = unpack(exchange(merged))

time: 78.7 us -> 38.9 us (0.49)
  the two profiles are of different devices: /device:TPU:0 before, /device:TPU:9 now
where the time goes in v2:
time: 38.9 us; the launch traced here: 38.8 us
  starting transfers between devices  16.9 us (43%)
  waiting for transfers between devices  12.5 us (32%)
  Pallas kernels  6.86 us (18%)
  local copies, waits for them, and re-layouts  1.81 us (5%)
  between operations  0.73 us (2%)
    ppermute x12, starting transfers between devices, exchange(): lax.ppermute(blocks[d], 'head', [(i, i ^ d) for i in range(heads)])  10.3 us
    ppermute x12, waiting for transfers between devices, exchange(): lax.ppermute(blocks[d], 'head', [(i, i ^ d) for i in range(heads)])  10 us
    ppermute x2, starting transfers between devices, shards(): far = [lax.ppermute(p, 'node', r) for p, r in zip(picked, routes)]  4.55 us
    pallas_call x1, Pallas kernels, shards(): pl.pallas_call(functools.partial(attend_kernel, heads, owners, local_coun...  3.7 us
    ppermute x2, waiting for transfers between devices, shards(): back = [lax.ppermute(p, 'node', r) for p, r in zip(far_grads, routes)]  2.44 us
    ppermute x2, starting transfers between devices, shards(): back = [lax.ppermute(p, 'node', r) for p, r in zip(far_grads, routes)]  1.99 us
    unnamed x10, local copies, waits for them, and re-layouts  1.81 us
    pallas_call x2, Pallas kernels, unpack(): pl.pallas_call(functools.partial(unpack_kernel, heads, width), out_shape=...  1.45 us
  transfers between devices with their start and end apart: 16, of which 8 were waited for; matrix products, arithmetic and copies ran while one was open for 0% of the time, Pallas kernels for 4%

profile of v2, /device:TPU:9, one launch (start us, length us, event | category | flops | bytes accessed | tf_op | source)
XLA Modules:
  0.0 38.8 jit_solution(15078454104677690457)
XLA Ops:
  0.6 0.0 copy-start
  0.6 0.9 %copy-done = bf16[64,1024]{1,0:T(8,128)(2,1)S(1)} copy-done((bf16[64,1024]{1,0:T(8,128)(2,1)S(1)}, bf16[64,1024]{1,0:T(8,128)(2,1)}, u32[]{:S(2)}) %copy-start) | copy-done | bytes 131096
  1.5 0.0 copy-start.1
  1.5 0.9 %copy-done.1 = bf16[64,1024]{1,0:T(8,128)(2,1)S(1)} copy-done((bf16[64,1024]{1,0:T(8,128)(2,1)S(1)}, bf16[64,1024]{1,0:T(8,128)(2,1)}, u32[]{:S(2)}) %copy-start.1) | copy-done | bytes 131096
  2.5 0.0 copy-start.4
  2.5 0.7 %collective-permute-start = (bf16[2,64,256]{2,1,0:T(8,128)(2,1)S(1)}, bf16[2,64,256]{2,1,0:T(8,128)(2,1)S(1)}, u32[]{:S(2)}, u32[]{:S(2)}) collective-permute-start(bf16[2,64,256]{2,1,0:T(8,128)(2,1)S(1)} %get-tuple-element.33), channel_id=1, source_target_pairs={{0,1},{1,0},{2,3},{3,2},{4,5},{5,4},{6,7},{7,6},{8,9},{9,8},{10,11... | collective-permute-start | bytes 196616 | tf_op jit(solution)/shard_map/ppermute | solution.py:183
  3.2 1.2 %collective-permute-start.1 = (bf16[2,64,256]{2,1,0:T(8,128)(2,1)S(1)}, bf16[2,64,256]{2,1,0:T(8,128)(2,1)S(1)}, u32[]{:S(2)}, u32[]{:S(2)}) collective-permute-start(bf16[2,64,256]{2,1,0:T(8,128)(2,1)S(1)} %get-tuple-element.34), channel_id=1, source_target_pairs={{0,2},{1,3},{2,0},{3,1},{4,6},{5,7},{6,4},{7,5},{8,10},{9,11},{10,... | collective-permute-start | bytes 196616 | tf_op jit(solution)/shard_map/ppermute | solution.py:183
  4.5 0.5 %collective-permute-start.2 = (bf16[2,64,256]{2,1,0:T(8,128)(2,1)S(1)}, bf16[2,64,256]{2,1,0:T(8,128)(2,1)S(1)}, u32[]{:S(2)}, u32[]{:S(2)}) collective-permute-start(bf16[2,64,256]{2,1,0:T(8,128)(2,1)S(1)} %get-tuple-element.35), channel_id=1, source_target_pairs={{0,3},{1,2},{2,1},{3,0},{4,7},{5,6},{6,5},{7,4},{8,11},{9,10},{10,... | collective-permute-start | bytes 196616 | tf_op jit(solution)/shard_map/ppermute | solution.py:183
  4.9 0.0 collective-permute-done.refs_1_
  4.9 2.0 %collective-permute-done.1.refs_2_ = bf16[2,64,256]{2,1,0:T(8,128)(2,1)S(1)} collective-permute-done((bf16[2,64,256]{2,1,0:T(8,128)(2,1)S(1)}, bf16[2,64,256]{2,1,0:T(8,128)(2,1)S(1)}, u32[]{:S(2)}, u32[]{:S(2)}) %collective-permute-start.1) | collective-permute-done | bytes 65568 | tf_op jit(solution)/shard_map/ppermute | solution.py:183
  6.9 1.6 %collective-permute-done.2.refs_3_ = bf16[2,64,256]{2,1,0:T(8,128)(2,1)S(1)} collective-permute-done((bf16[2,64,256]{2,1,0:T(8,128)(2,1)S(1)}, bf16[2,64,256]{2,1,0:T(8,128)(2,1)S(1)}, u32[]{:S(2)}, u32[]{:S(2)}) %collective-permute-start.2) | collective-permute-done | bytes 65568 | tf_op jit(solution)/shard_map/ppermute | solution.py:183
  8.5 0.0 copy-done.4
  8.5 0.0 copy-start.2
  8.5 0.0 copy-start.3
  8.5 0.7 %pick.1 = (bf16[2,128,256]{2,1,0:T(8,128)(2,1)S(1)}, bf16[2,128,256]{2,1,0:T(8,128)(2,1)S(1)}) custom-call(s32[8,8]{1,0:T(8,128)S(1)} %copy-done.4, bf16[2,64,256]{2,1,0:T(8,128)(2,1)S(1)} %get-tuple-element.32.refs_0_, bf16[2,64,256]{2,1,0:T(8,128)(2,1)S(1)} %collective-permute-done.refs_1_, bf16[2,64,256]{2,1,0:T(8,128)(2,1)S(1)} %collective-permute-done.1.refs_2_, ...), custom_call_target="tpu_custom_call" | custom-call | tf_op jit(solution)/shard_map/pick/pallas_call | solution.py:221
  9.2 0.2 collective-permute-start.6
  9.5 4.3 %collective-permute-start.7 = (bf16[2,128,256]{2,1,0:T(8,128)(2,1)S(1)}, bf16[2,128,256]{2,1,0:T(8,128)(2,1)S(1)}, u32[]{:S(2)}, u32[]{:S(2)}) collective-permute-start(bf16[2,128,256]{2,1,0:T(8,128)(2,1)S(1)} %get-tuple-element.41), channel_id=1, source_target_pairs={{0,0},{4,8},{8,4},{12,12},{1,1},{5,9},{9,5},{13,13},{2,2},{6,10},{... | collective-permute-start | bytes 393224 | tf_op jit(solution)/shard_map/ppermute | solution.py:229
  13.8 0.0 copy-done.2
  13.8 0.0 copy-done.3
  13.9 1.0 %collective-permute-start.3 = (bf16[2,64,256]{2,1,0:T(8,128)(2,1)S(1)}, bf16[2,64,256]{2,1,0:T(8,128)(2,1)S(1)}, u32[]{:S(2)}, u32[]{:S(2)}) collective-permute-start(bf16[2,64,256]{2,1,0:T(8,128)(2,1)S(1)} %get-tuple-element.37), channel_id=1, source_target_pairs={{0,1},{1,0},{2,3},{3,2},{4,5},{5,4},{6,7},{7,6},{8,9},{9,8},{10,11... | collective-permute-start | bytes 196616 | tf_op jit(solution)/shard_map/ppermute | solution.py:183
  14.8 1.1 %collective-permute-start.4 = (bf16[2,64,256]{2,1,0:T(8,128)(2,1)S(1)}, bf16[2,64,256]{2,1,0:T(8,128)(2,1)S(1)}, u32[]{:S(2)}, u32[]{:S(2)}) collective-permute-start(bf16[2,64,256]{2,1,0:T(8,128)(2,1)S(1)} %get-tuple-element.38), channel_id=1, source_target_pairs={{0,2},{1,3},{2,0},{3,1},{4,6},{5,7},{6,4},{7,5},{8,10},{9,11},{10,... | collective-permute-start | bytes 196616 | tf_op jit(solution)/shard_map/ppermute | solution.py:183
  15.9 0.6 %collective-permute-start.5 = (bf16[2,64,256]{2,1,0:T(8,128)(2,1)S(1)}, bf16[2,64,256]{2,1,0:T(8,128)(2,1)S(1)}, u32[]{:S(2)}, u32[]{:S(2)}) collective-permute-start(bf16[2,64,256]{2,1,0:T(8,128)(2,1)S(1)} %get-tuple-element.39), channel_id=1, source_target_pairs={{0,3},{1,2},{2,1},{3,0},{4,7},{5,6},{6,5},{7,4},{8,11},{9,10},{10,... | collective-permute-start | bytes 196616 | tf_op jit(solution)/shard_map/ppermute | solution.py:183
  16.6 0.0 collective-permute-done.3.refs_5_
  16.6 2.0 %collective-permute-done.4.refs_6_ = bf16[2,64,256]{2,1,0:T(8,128)(2,1)S(1)} collective-permute-done((bf16[2,64,256]{2,1,0:T(8,128)(2,1)S(1)}, bf16[2,64,256]{2,1,0:T(8,128)(2,1)S(1)}, u32[]{:S(2)}, u32[]{:S(2)}) %collective-permute-start.4) | collective-permute-done | bytes 65568 | tf_op jit(solution)/shard_map/ppermute | solution.py:183
  18.5 1.6 %collective-permute-done.5.refs_7_ = bf16[2,64,256]{2,1,0:T(8,128)(2,1)S(1)} collective-permute-done((bf16[2,64,256]{2,1,0:T(8,128)(2,1)S(1)}, bf16[2,64,256]{2,1,0:T(8,128)(2,1)S(1)}, u32[]{:S(2)}, u32[]{:S(2)}) %collective-permute-start.5) | collective-permute-done | bytes 65568 | tf_op jit(solution)/shard_map/ppermute | solution.py:183
  20.1 0.0 collective-permute-done.6.refs_8_
  20.1 0.0 collective-permute-done.7.refs_9_
  20.1 3.7 %attend.1 = (bf16[2,64,256]{2,1,0:T(8,128)(2,1)S(1)}, bf16[2,64,256]{2,1,0:T(8,128)(2,1)S(1)}, bf16[2,64,256]{2,1,0:T(8,128)(2,1)S(1)}, bf16[2,64,256]{2,1,0:T(8...) custom-call(s32[8,8]{1,0:T(8,128)S(1)} %copy-done.4, ...), custom_call_target="tpu_custom_call" | custom-call | tf_op jit(solution)/shard_map/attend/pallas_call | solution.py:230
  23.9 0.1 collective-permute-start.11
  23.9 1.9 %collective-permute-start.12 = (bf16[2,128,256]{2,1,0:T(8,128)(2,1)S(1)}, bf16[2,128,256]{2,1,0:T(8,128)(2,1)S(1)}, u32[]{:S(2)}, u32[]{:S(2)}) collective-permute-start(bf16[2,128,256]{2,1,0:T(8,128)(2,1)S(1)} %get-tuple-element.53), channel_id=1, source_target_pairs={{0,0},{4,8},{8,4},{12,12},{1,1},{5,9},{9,5},{13,13},{2,2},{6,10},{... | collective-permute-start | bytes 393224 | tf_op jit(solution)/shard_map/ppermute | solution.py:243
  25.9 0.5 %collective-permute-start.8 = (bf16[2,64,256]{2,1,0:T(8,128)(2,1)S(1)}, bf16[2,64,256]{2,1,0:T(8,128)(2,1)S(1)}, u32[]{:S(2)}, u32[]{:S(2)}) collective-permute-start(bf16[2,64,256]{2,1,0:T(8,128)(2,1)S(1)} %get-tuple-element.43), channel_id=1, source_target_pairs={{0,1},{1,0},{2,3},{3,2},{4,5},{5,4},{6,7},{7,6},{8,9},{9,8},{10,11... | collective-permute-start | bytes 196616 | tf_op jit(solution)/shard_map/ppermute | solution.py:183
  26.3 0.8 %collective-permute-start.9 = (bf16[2,64,256]{2,1,0:T(8,128)(2,1)S(1)}, bf16[2,64,256]{2,1,0:T(8,128)(2,1)S(1)}, u32[]{:S(2)}, u32[]{:S(2)}) collective-permute-start(bf16[2,64,256]{2,1,0:T(8,128)(2,1)S(1)} %get-tuple-element.44), channel_id=1, source_target_pairs={{0,2},{1,3},{2,0},{3,1},{4,6},{5,7},{6,4},{7,5},{8,10},{9,11},{10,... | collective-permute-start | bytes 196616 | tf_op jit(solution)/shard_map/ppermute | solution.py:183
  27.2 0.9 %collective-permute-start.10 = (bf16[2,64,256]{2,1,0:T(8,128)(2,1)S(1)}, bf16[2,64,256]{2,1,0:T(8,128)(2,1)S(1)}, u32[]{:S(2)}, u32[]{:S(2)}) collective-permute-start(bf16[2,64,256]{2,1,0:T(8,128)(2,1)S(1)} %get-tuple-element.45), channel_id=1, source_target_pairs={{0,3},{1,2},{2,1},{3,0},{4,7},{5,6},{6,5},{7,4},{8,11},{9,10},{10,... | collective-permute-start | bytes 196616 | tf_op jit(solution)/shard_map/ppermute | solution.py:183
  28.1 0.5 %collective-permute-done.11.refs_4_ = bf16[2,128,256]{2,1,0:T(8,128)(2,1)S(1)} collective-permute-done((bf16[2,128,256]{2,1,0:T(8,128)(2,1)S(1)}, bf16[2,128,256]{2,1,0:T(8,128)(2,1)S(1)}, u32[]{:S(2)}, u32[]{:S(2)}) %collective-permute-start.11) | collective-permute-done | bytes 131104 | tf_op jit(solution)/shard_map/ppermute | solution.py:243
  28.6 1.9 %collective-permute-done.12.refs_5_ = bf16[2,128,256]{2,1,0:T(8,128)(2,1)S(1)} collective-permute-done((bf16[2,128,256]{2,1,0:T(8,128)(2,1)S(1)}, bf16[2,128,256]{2,1,0:T(8,128)(2,1)S(1)}, u32[]{:S(2)}, u32[]{:S(2)}) %collective-permute-start.12) | collective-permute-done | bytes 131104 | tf_op jit(solution)/shard_map/ppermute | solution.py:243
  30.5 0.9 %merge.1 = (bf16[2,64,256]{2,1,0:T(8,128)(2,1)S(1)}, bf16[2,64,256]{2,1,0:T(8,128)(2,1)S(1)}, bf16[2,64,256]{2,1,0:T(8,128)(2,1)S(1)}, bf16[2,64,256]{2,1,0:T(8,128)(2,1)S(1)}) custom-call(s32[8,8]{1,0:T(8,128)S(1)} %copy-done.4, f32[2,64,256]{2,1,0:T(8,128)S(1)} %get-tuple-element.48.refs_0_, f32[2,64,256]{2,1,0:T(8,128)S(1)} %get-tuple-element.49.refs_1_, ...), custom_call_target="tpu_custom_call" | custom-call | tf_op jit(solution)/shard_map/merge/pallas_call | solution.py:244
  31.4 1.3 %collective-permute-start.13 = (bf16[2,64,256]{2,1,0:T(8,128)(2,1)S(1)}, bf16[2,64,256]{2,1,0:T(8,128)(2,1)S(1)}, u32[]{:S(2)}, u32[]{:S(2)}) collective-permute-start(bf16[2,64,256]{2,1,0:T(8,128)(2,1)S(1)} %get-tuple-element.55), channel_id=1, source_target_pairs={{0,1},{1,0},{2,3},{3,2},{4,5},{5,4},{6,7},{7,6},{8,9},{9,8},{10,11... | collective-permute-start | bytes 196616 | tf_op jit(solution)/shard_map/ppermute | solution.py:183
  32.7 1.0 %collective-permute-start.14 = (bf16[2,64,256]{2,1,0:T(8,128)(2,1)S(1)}, bf16[2,64,256]{2,1,0:T(8,128)(2,1)S(1)}, u32[]{:S(2)}, u32[]{:S(2)}) collective-permute-start(bf16[2,64,256]{2,1,0:T(8,128)(2,1)S(1)} %get-tuple-element.56), channel_id=1, source_target_pairs={{0,2},{1,3},{2,0},{3,1},{4,6},{5,7},{6,4},{7,5},{8,10},{9,11},{10,... | collective-permute-start | bytes 196616 | tf_op jit(solution)/shard_map/ppermute | solution.py:183
  33.7 0.0 collective-permute-done.8.refs_1_
  33.7 0.7 %collective-permute-start.15 = (bf16[2,64,256]{2,1,0:T(8,128)(2,1)S(1)}, bf16[2,64,256]{2,1,0:T(8,128)(2,1)S(1)}, u32[]{:S(2)}, u32[]{:S(2)}) collective-permute-start(bf16[2,64,256]{2,1,0:T(8,128)(2,1)S(1)} %get-tuple-element.57), channel_id=1, source_target_pairs={{0,3},{1,2},{2,1},{3,0},{4,7},{5,6},{6,5},{7,4},{8,11},{9,10},{10,... | collective-permute-start | bytes 196616 | tf_op jit(solution)/shard_map/ppermute | solution.py:183
  34.4 0.0 collective-permute-done.9.refs_2_
  34.4 0.0 collective-permute-done.10.refs_3_
  34.4 0.7 %unpack.2 = (bf16[64,1024]{1,0:T(8,128)(2,1)}, bf16[64,1024]{1,0:T(8,128)(2,1)}) custom-call(bf16[2,64,256]{2,1,0:T(8,128)(2,1)S(1)} %get-tuple-element.42.refs_0_, bf16[2,64,256]{2,1,0:T(8,128)(2,1)S(1)} %collective-permute-done.8.refs_1_, bf16[2,64,256]{2,1,0:T(8,128)(2,1)S(1)} %collective-permute-done.9.refs_2_, ...), custom_call_target="tpu_custom_call" | custom-call | tf_op jit(solution)/shard_map/unpack/pallas_call | solution.py:210
  35.2 0.0 collective-permute-done.13.refs_1_
  35.2 1.2 %collective-permute-done.14.refs_2_ = bf16[2,64,256]{2,1,0:T(8,128)(2,1)S(1)} collective-permute-done((bf16[2,64,256]{2,1,0:T(8,128)(2,1)S(1)}, bf16[2,64,256]{2,1,0:T(8,128)(2,1)S(1)}, u32[]{:S(2)}, u32[]{:S(2)}) %collective-permute-start.14) | collective-permute-done | bytes 65568 | tf_op jit(solution)/shard_map/ppermute | solution.py:183
  36.4 1.7 %collective-permute-done.15.refs_3_ = bf16[2,64,256]{2,1,0:T(8,128)(2,1)S(1)} collective-permute-done((bf16[2,64,256]{2,1,0:T(8,128)(2,1)S(1)}, bf16[2,64,256]{2,1,0:T(8,128)(2,1)S(1)}, u32[]{:S(2)}, u32[]{:S(2)}) %collective-permute-start.15) | collective-permute-done | bytes 65568 | tf_op jit(solution)/shard_map/ppermute | solution.py:183
  38.0 0.7 %unpack.3 = (bf16[64,1024]{1,0:T(8,128)(2,1)}, bf16[64,1024]{1,0:T(8,128)(2,1)}) custom-call(bf16[2,64,256]{2,1,0:T(8,128)(2,1)S(1)} %get-tuple-element.54.refs_0_, bf16[2,64,256]{2,1,0:T(8,128)(2,1)S(1)} %collective-permute-done.13.refs_1_, bf16[2,64,256]{2,1,0:T(8,128)(2,1)S(1)} %collective-permute-done.14.refs_2_, ...), custom_call_target="tpu_custom_call" | custom-call | tf_op jit(solution)/shard_map/unpack/pallas_call | solution.py:210
  (2 shorter events, 0.1 us)
Async XLA Ops:
  0.6 0.9 %copy-start = (bf16[64,1024]{1,0:T(8,128)(2,1)S(1)}, bf16[64,1024]{1,0:T(8,128)(2,1)}, u32[]{:S(2)}) copy-start(bf16[64,1024]{1,0:T(8,128)(2,1)} %one_ref.2) | copy-start | bytes 393220
  1.5 0.9 %copy-start.1 = (bf16[64,1024]{1,0:T(8,128)(2,1)S(1)}, bf16[64,1024]{1,0:T(8,128)(2,1)}, u32[]{:S(2)}) copy-start(bf16[64,1024]{1,0:T(8,128)(2,1)} %two_ref.2) | copy-start | bytes 393220
  2.5 6.0 %copy-start.4 = (s32[8,8]{1,0:T(8,128)S(1)}, s32[8,8]{1,0:T(8,128)}, u32[]{:S(2)}) copy-start(s32[8,8]{1,0:T(8,128)} %nbr_ref.5) | copy-start | bytes 772
  2.5 2.5 %collective-permute-start = (bf16[2,64,256]{2,1,0:T(8,128)(2,1)S(1)}, bf16[2,64,256]{2,1,0:T(8,128)(2,1)S(1)}, u32[]{:S(2)}, u32[]{:S(2)}) collective-permute-start(bf16[2,64,256]{2,1,0:T(8,128)(2,1)S(1)} %get-tuple-element.33), channel_id=1, source_target_pairs={{0,1},{1,0},{2,3},{3,2},{4,5},{5,4},{6,7},{7,6},{8,9},{9,8},{10,11... | collective-permute-start | bytes 196616 | tf_op jit(solution)/shard_map/ppermute | solution.py:183
  3.2 3.7 %collective-permute-start.1 = (bf16[2,64,256]{2,1,0:T(8,128)(2,1)S(1)}, bf16[2,64,256]{2,1,0:T(8,128)(2,1)S(1)}, u32[]{:S(2)}, u32[]{:S(2)}) collective-permute-start(bf16[2,64,256]{2,1,0:T(8,128)(2,1)S(1)} %get-tuple-element.34), channel_id=1, source_target_pairs={{0,2},{1,3},{2,0},{3,1},{4,6},{5,7},{6,4},{7,5},{8,10},{9,11},{10,... | collective-permute-start | bytes 196616 | tf_op jit(solution)/shard_map/ppermute | solution.py:183
  4.5 4.0 %collective-permute-start.2 = (bf16[2,64,256]{2,1,0:T(8,128)(2,1)S(1)}, bf16[2,64,256]{2,1,0:T(8,128)(2,1)S(1)}, u32[]{:S(2)}, u32[]{:S(2)}) collective-permute-start(bf16[2,64,256]{2,1,0:T(8,128)(2,1)S(1)} %get-tuple-element.35), channel_id=1, source_target_pairs={{0,3},{1,2},{2,1},{3,0},{4,7},{5,6},{6,5},{7,4},{8,11},{9,10},{10,... | collective-permute-start | bytes 196616 | tf_op jit(solution)/shard_map/ppermute | solution.py:183
  8.5 5.3 %copy-start.2 = (bf16[64,1024]{1,0:T(8,128)(2,1)S(1)}, bf16[64,1024]{1,0:T(8,128)(2,1)}, u32[]{:S(2)}) copy-start(bf16[64,1024]{1,0:T(8,128)(2,1)} %one_ref.3) | copy-start | bytes 393220
  8.5 5.3 %copy-start.3 = (bf16[64,1024]{1,0:T(8,128)(2,1)S(1)}, bf16[64,1024]{1,0:T(8,128)(2,1)}, u32[]{:S(2)}) copy-start(bf16[64,1024]{1,0:T(8,128)(2,1)} %two_ref.3) | copy-start | bytes 393220
  9.2 10.9 %collective-permute-start.6 = (bf16[2,128,256]{2,1,0:T(8,128)(2,1)S(1)}, bf16[2,128,256]{2,1,0:T(8,128)(2,1)S(1)}, u32[]{:S(2)}, u32[]{:S(2)}) collective-permute-start(bf16[2,128,256]{2,1,0:T(8,128)(2,1)S(1)} %get-tuple-element.40), channel_id=1, source_target_pairs={{0,4},{4,0},{8,12},{12,8},{1,5},{5,1},{9,13},{13,9},{2,6},{6,2},{1... | collective-permute-start | bytes 393224 | tf_op jit(solution)/shard_map/ppermute | solution.py:229
  9.5 10.7 %collective-permute-start.7 = (bf16[2,128,256]{2,1,0:T(8,128)(2,1)S(1)}, bf16[2,128,256]{2,1,0:T(8,128)(2,1)S(1)}, u32[]{:S(2)}, u32[]{:S(2)}) collective-permute-start(bf16[2,128,256]{2,1,0:T(8,128)(2,1)S(1)} %get-tuple-element.41), channel_id=1, source_target_pairs={{0,0},{4,8},{8,4},{12,12},{1,1},{5,9},{9,5},{13,13},{2,2},{6,10},{... | collective-permute-start | bytes 393224 | tf_op jit(solution)/shard_map/ppermute | solution.py:229
  13.9 2.7 %collective-permute-start.3 = (bf16[2,64,256]{2,1,0:T(8,128)(2,1)S(1)}, bf16[2,64,256]{2,1,0:T(8,128)(2,1)S(1)}, u32[]{:S(2)}, u32[]{:S(2)}) collective-permute-start(bf16[2,64,256]{2,1,0:T(8,128)(2,1)S(1)} %get-tuple-element.37), channel_id=1, source_target_pairs={{0,1},{1,0},{2,3},{3,2},{4,5},{5,4},{6,7},{7,6},{8,9},{9,8},{10,11... | collective-permute-start | bytes 196616 | tf_op jit(solution)/shard_map/ppermute | solution.py:183
  14.8 3.7 %collective-permute-start.4 = (bf16[2,64,256]{2,1,0:T(8,128)(2,1)S(1)}, bf16[2,64,256]{2,1,0:T(8,128)(2,1)S(1)}, u32[]{:S(2)}, u32[]{:S(2)}) collective-permute-start(bf16[2,64,256]{2,1,0:T(8,128)(2,1)S(1)} %get-tuple-element.38), channel_id=1, source_target_pairs={{0,2},{1,3},{2,0},{3,1},{4,6},{5,7},{6,4},{7,5},{8,10},{9,11},{10,... | collective-permute-start | bytes 196616 | tf_op jit(solution)/shard_map/ppermute | solution.py:183
  15.9 4.2 %collective-permute-start.5 = (bf16[2,64,256]{2,1,0:T(8,128)(2,1)S(1)}, bf16[2,64,256]{2,1,0:T(8,128)(2,1)S(1)}, u32[]{:S(2)}, u32[]{:S(2)}) collective-permute-start(bf16[2,64,256]{2,1,0:T(8,128)(2,1)S(1)} %get-tuple-element.39), channel_id=1, source_target_pairs={{0,3},{1,2},{2,1},{3,0},{4,7},{5,6},{6,5},{7,4},{8,11},{9,10},{10,... | collective-permute-start | bytes 196616 | tf_op jit(solution)/shard_map/ppermute | solution.py:183
  23.9 4.7 %collective-permute-start.11 = (bf16[2,128,256]{2,1,0:T(8,128)(2,1)S(1)}, bf16[2,128,256]{2,1,0:T(8,128)(2,1)S(1)}, u32[]{:S(2)}, u32[]{:S(2)}) collective-permute-start(bf16[2,128,256]{2,1,0:T(8,128)(2,1)S(1)} %get-tuple-element.52), channel_id=1, source_target_pairs={{0,4},{4,0},{8,12},{12,8},{1,5},{5,1},{9,13},{13,9},{2,6},{6,2},{1... | collective-permute-start | bytes 393224 | tf_op jit(solution)/shard_map/ppermute | solution.py:243
  23.9 6.6 %collective-permute-start.12 = (bf16[2,128,256]{2,1,0:T(8,128)(2,1)S(1)}, bf16[2,128,256]{2,1,0:T(8,128)(2,1)S(1)}, u32[]{:S(2)}, u32[]{:S(2)}) collective-permute-start(bf16[2,128,256]{2,1,0:T(8,128)(2,1)S(1)} %get-tuple-element.53), channel_id=1, source_target_pairs={{0,0},{4,8},{8,4},{12,12},{1,1},{5,9},{9,5},{13,13},{2,2},{6,10},{... | collective-permute-start | bytes 393224 | tf_op jit(solution)/shard_map/ppermute | solution.py:243
  25.9 7.9 %collective-permute-start.8 = (bf16[2,64,256]{2,1,0:T(8,128)(2,1)S(1)}, bf16[2,64,256]{2,1,0:T(8,128)(2,1)S(1)}, u32[]{:S(2)}, u32[]{:S(2)}) collective-permute-start(bf16[2,64,256]{2,1,0:T(8,128)(2,1)S(1)} %get-tuple-element.43), channel_id=1, source_target_pairs={{0,1},{1,0},{2,3},{3,2},{4,5},{5,4},{6,7},{7,6},{8,9},{9,8},{10,11... | collective-permute-start | bytes 196616 | tf_op jit(solution)/shard_map/ppermute | solution.py:183
  26.3 8.1 %collective-permute-start.9 = (bf16[2,64,256]{2,1,0:T(8,128)(2,1)S(1)}, bf16[2,64,256]{2,1,0:T(8,128)(2,1)S(1)}, u32[]{:S(2)}, u32[]{:S(2)}) collective-permute-start(bf16[2,64,256]{2,1,0:T(8,128)(2,1)S(1)} %get-tuple-element.44), channel_id=1, source_target_pairs={{0,2},{1,3},{2,0},{3,1},{4,6},{5,7},{6,4},{7,5},{8,10},{9,11},{10,... | collective-permute-start | bytes 196616 | tf_op jit(solution)/shard_map/ppermute | solution.py:183
  27.2 7.3 %collective-permute-start.10 = (bf16[2,64,256]{2,1,0:T(8,128)(2,1)S(1)}, bf16[2,64,256]{2,1,0:T(8,128)(2,1)S(1)}, u32[]{:S(2)}, u32[]{:S(2)}) collective-permute-start(bf16[2,64,256]{2,1,0:T(8,128)(2,1)S(1)} %get-tuple-element.45), channel_id=1, source_target_pairs={{0,3},{1,2},{2,1},{3,0},{4,7},{5,6},{6,5},{7,4},{8,11},{9,10},{10,... | collective-permute-start | bytes 196616 | tf_op jit(solution)/shard_map/ppermute | solution.py:183
  31.4 3.7 %collective-permute-start.13 = (bf16[2,64,256]{2,1,0:T(8,128)(2,1)S(1)}, bf16[2,64,256]{2,1,0:T(8,128)(2,1)S(1)}, u32[]{:S(2)}, u32[]{:S(2)}) collective-permute-start(bf16[2,64,256]{2,1,0:T(8,128)(2,1)S(1)} %get-tuple-element.55), channel_id=1, source_target_pairs={{0,1},{1,0},{2,3},{3,2},{4,5},{5,4},{6,7},{7,6},{8,9},{9,8},{10,11... | collective-permute-start | bytes 196616 | tf_op jit(solution)/shard_map/ppermute | solution.py:183
  32.7 3.7 %collective-permute-start.14 = (bf16[2,64,256]{2,1,0:T(8,128)(2,1)S(1)}, bf16[2,64,256]{2,1,0:T(8,128)(2,1)S(1)}, u32[]{:S(2)}, u32[]{:S(2)}) collective-permute-start(bf16[2,64,256]{2,1,0:T(8,128)(2,1)S(1)} %get-tuple-element.56), channel_id=1, source_target_pairs={{0,2},{1,3},{2,0},{3,1},{4,6},{5,7},{6,4},{7,5},{8,10},{9,11},{10,... | collective-permute-start | bytes 196616 | tf_op jit(solution)/shard_map/ppermute | solution.py:183
  33.7 4.3 %collective-permute-start.15 = (bf16[2,64,256]{2,1,0:T(8,128)(2,1)S(1)}, bf16[2,64,256]{2,1,0:T(8,128)(2,1)S(1)}, u32[]{:S(2)}, u32[]{:S(2)}) collective-permute-start(bf16[2,64,256]{2,1,0:T(8,128)(2,1)S(1)} %get-tuple-element.57), channel_id=1, source_target_pairs={{0,3},{1,2},{2,1},{3,0},{4,7},{5,6},{6,5},{7,4},{8,11},{9,10},{10,... | collective-permute-start | bytes 196616 | tf_op jit(solution)/shard_map/ppermute | solution.py:183

commit v3 on v2

v3 whole, which is shorter than its diff:
```python
import functools
import math

import jax
import jax.numpy as jnp
from jax import lax
from jax.experimental import pallas as pl
from jax.experimental.pallas import tpu as pltpu
from jax.sharding import PartitionSpec as P

HEAD_DIM = 64
NEVER = -1e30
LOW = jnp.bfloat16
VMEM = pl.BlockSpec(memory_space=pltpu.VMEM)
SMEM = pl.BlockSpec(memory_space=pltpu.SMEM)
NT = (((1,), (1,)), ((), ()))


def dot(left, right, dims=(((1,), (0,)), ((), ()))):
    return lax.dot_general(left, right, dims, preferred_element_type=jnp.float32)


def call(kernel, name, outs, *args, limit=8, scratch=(), cost=None, specs=None):
    return pl.pallas_call(
        kernel,
        out_shape=outs,
        in_specs=specs or [VMEM] * len(args),
        out_specs=[VMEM] * len(outs),
        scratch_shapes=scratch,
        name=name,
        cost_estimate=cost,
        compiler_params=pltpu.CompilerParams(vmem_limit_bytes=limit * 1024 * 1024),
    )(*args)


def pair_routes(owners, heads):
    routes = []
    for step in (1, -1):
        route = []
        for n in range(owners):
            other = n + step * (1 - 2 * (n % 2))
            for h in range(heads):
                target = other * heads + h if 0 <= other < owners else n * heads + (h ^ 1)
                route.append((n * heads + h, target))
        routes.append(route)
    return routes


def prep_kernel(heads, owners, local_count, per_patch, rows, nbr_ref, after_ref, bias_ref, slot_ref):
    me, node = lax.axis_index("head"), lax.axis_index("node")
    odd = lax.rem(node, 2)
    pair = (node + 1 - 2 * odd, node - 1 + 2 * odd)
    queries = heads * rows
    own = [[jnp.int32(p == k) for k in range(local_count)] for p in range(local_count)]
    out_of = [[jnp.int32(0), jnp.int32(0)] for _ in range(local_count)]
    for p in range(local_count):
        for j in range(nbr_ref.shape[1]):
            entry = nbr_ref[node * local_count + p, j]
            for k in range(local_count):
                own[p][k] += jnp.where(entry == node * local_count + k, 1, 0)
            for s in range(2):
                start = pair[s] * local_count
                inside = jnp.logical_and(entry >= start, entry < start + local_count)
                out_of[p][s] += jnp.where(inside, 1, 0)

    def choose(index, values):
        value = values[0]
        for i in range(1, len(values)):
            value = jnp.where(index == i, values[i], value)
        return value

    patch_of = [(me ^ d) // per_patch for d in range(heads)]
    counts = [
        [choose(patch_of[e], [choose(patch_of[d], own[p]) for p in range(local_count)]) for e in range(heads)]
        for d in range(heads)
    ]
    for s in range(2):
        counts.append([choose(patch_of[e], [out_of[p][s] for p in range(local_count)]) for e in range(heads)])
    lane_block = lax.broadcasted_iota(jnp.int32, (1, queries), 1) // rows
    for b, row_counts in enumerate(counts):
        row = jnp.zeros((1, queries), jnp.float32)
        for e in range(heads):
            row = jnp.where(lane_block == e, row_counts[e].astype(jnp.float32), row)
        row = jnp.where(row > 0.5, jnp.log(jnp.maximum(row, 1.0)) * (1 / math.log(2)), NEVER)
        bias_ref[b : b + 1, :] = row
    for s in range(2):
        inside = jnp.logical_and(pair[s] >= 0, pair[s] < owners)
        first = jnp.where(inside, pair[s], 0) * local_count
        chosen = jnp.int32(0)
        for p in range(local_count):
            for j in range(nbr_ref.shape[1]):
                entry = nbr_ref[first + p, j] - node * local_count
                mine = jnp.logical_and(entry >= 0, entry < local_count)
                chosen = jnp.where(jnp.logical_and(inside, mine), entry, chosen)
        for t in range(per_patch):
            slot = me ^ (chosen * per_patch + t)
            slot_ref[s * per_patch + t : s * per_patch + t + 1, :] = jnp.full((1, slot_ref.shape[1]), slot)


def pack_kernel(heads, keys, both_ref, one_peer, two_peer, *refs):
    me = lax.axis_index("head")
    outs = refs[-len(keys) :]
    width = outs[0].shape[-1]
    for out, pairs in zip(outs, keys):
        for i, (u, w) in enumerate(pairs):
            one, two = (one_peer, two_peer) if u else (both_ref.at[0], both_ref.at[1])
            cols = pl.ds(pl.multiple_of((me ^ w) * width, width), width)
            out[i, 0], out[i, 1] = one[:, cols], two[:, cols]


def gather_kernel(places, *refs):
    for i, (a, j) in enumerate(places):
        refs[-1][i] = refs[a][j]


def pick_kernel(heads, places, slot_ref, *refs):
    arrays, outs = refs[:-2], refs[-2:]
    rows = arrays[0].shape[2]
    per_patch = outs[0].shape[1] // rows
    blocks = [arrays[a][j].astype(jnp.float32) for a, j in places]
    for s, out in enumerate(outs):
        for t in range(per_patch):
            slot = slot_ref[s * per_patch + t : s * per_patch + t + 1, :]
            value = blocks[0]
            for d in range(1, heads):
                value = jnp.where((slot == d)[None], blocks[d], value)
            out[:, t * rows : (t + 1) * rows, :] = value.astype(LOW)


def attend_kernel(heads, places, count, bias_ref, *refs):
    kv_arrays, qg_arrays, far, outs = refs[:count], refs[count : 2 * count], refs[2 * count : 2 * count + 2], refs[2 * count + 2 :]
    mq_kept, mq_sent, near_out, far_a, far_b, w_all, ds_all = outs
    kv = [kv_arrays[a].at[j] for a, j in places]
    qg = [qg_arrays[a].at[j] for a, j in places]
    rows, width = kv[0].shape[1:]
    patch = far[0].shape[1]
    queries = heads * rows
    groups = width // HEAD_DIM
    sizes = [rows] * heads + [patch, patch]
    bias = jnp.concatenate(
        [jnp.broadcast_to(bias_ref[b : b + 1, :], (n, queries)) for b, n in enumerate(sizes)], 0
    )
    keys = jnp.concatenate([r[0] for r in kv] + [r[0] for r in far], 0)
    values = jnp.concatenate([r[1] for r in kv] + [r[1] for r in far], 0)
    query = jnp.concatenate([r[0] for r in qg], 0)
    grad = jnp.concatenate([r[1] for r in qg], 0)
    keys_t, values_t = keys.T, values.T
    lane_head = lax.broadcasted_iota(jnp.int32, (1, width), 1) // HEAD_DIM
    scale = HEAD_DIM**-0.5
    mixed_t, qgrad_t, query_h, grad_h = [], [], [], []
    for head in range(groups):
        feats = slice(head * HEAD_DIM, (head + 1) * HEAD_DIM)
        lanes = slice(head * queries, (head + 1) * queries)
        query_h.append(jnp.where(lane_head == head, query, jnp.zeros_like(query)))
        grad_h.append(jnp.where(lane_head == head, grad, jnp.zeros_like(grad)))
        scores = dot(keys, query_h[head], NT) * (scale / math.log(2)) + bias
        weights = jnp.exp2(scores - jnp.max(scores, 0, keepdims=True))
        weights = weights * (1.0 / jnp.sum(weights, 0, keepdims=True))
        weights_low = weights.astype(LOW)
        grad_weights = dot(values, grad_h[head], NT)
        row_dots = jnp.sum(weights * grad_weights, 0, keepdims=True)
        grad_scores = (weights * (grad_weights - row_dots)).astype(LOW)
        w_all[:, lanes] = weights_low
        ds_all[:, lanes] = grad_scores
        mixed_t.append(dot(values_t[feats], weights_low))
        qgrad_t.append(dot(keys_t[feats], grad_scores) * scale)
    mixed = jnp.concatenate(mixed_t, 0).T.astype(LOW)
    qgrad = jnp.concatenate(qgrad_t, 0).T.astype(LOW)
    key_grad = dot(ds_all[...], jnp.concatenate(query_h, 0)) * scale
    value_grad = dot(w_all[...], jnp.concatenate(grad_h, 0))
    for d in range(heads):
        span = slice(d * rows, (d + 1) * rows)
        out = (mq_sent if d % 2 else mq_kept).at[d // 2]
        out[0], out[1] = mixed[span], qgrad[span]
        near_out[d, 0], near_out[d, 1] = key_grad[span], value_grad[span]
    for s, out in enumerate((far_a, far_b)):
        span = slice(queries + s * patch, queries + (s + 1) * patch)
        out[0], out[1] = key_grad[span].astype(LOW), value_grad[span].astype(LOW)


def merge_kernel(heads, slot_ref, near, back_a, back_b, kept, sent):
    rows = near.shape[2]
    per_patch = back_a.shape[1] // rows
    for d in range(heads):
        total = near[d]
        for s, back in enumerate((back_a, back_b)):
            for t in range(per_patch):
                slot = slot_ref[s * per_patch + t : s * per_patch + t + 1, :]
                term = back[:, t * rows : (t + 1) * rows, :].astype(jnp.float32)
                total = total + jnp.where((slot == d)[None], term, 0.0)
        (sent if d % 2 else kept)[d // 2] = total.astype(LOW)


def unpack_kernel(heads, places, *refs):
    arrays, outs = refs[:-2], refs[-2:]
    width = arrays[0].shape[-1]
    me = lax.axis_index("head")
    for d, (a, j) in enumerate(places):
        cols = pl.ds(pl.multiple_of((me ^ d) * width, width), width)
        outs[0][:, cols], outs[1][:, cols] = arrays[a][j, 0], arrays[a][j, 1]


def swap(array, bit):
    heads = lax.axis_size("head")
    return lax.ppermute(array, "head", [(i, i ^ bit) for i in range(heads)])


def regroup(arrays, places):
    shape = jax.ShapeDtypeStruct((len(places),) + arrays[0].shape[1:], LOW)
    return call(functools.partial(gather_kernel, places), "regroup", [shape], *arrays)[0]


def exchange(heads, bit, arrays, held, outgoing, going):
    while True:
        arrays.append(swap(outgoing, bit))
        for i, (u, w) in enumerate(going):
            held[(u + bit, w - bit)] = (len(arrays) - 1, i)
        bit *= 2
        if bit >= heads:
            return arrays, [held[(d, 0)] for d in range(heads)]
        going = sorted(k for k in held if k[1] & bit)
        outgoing = regroup(arrays, [held.pop(k) for k in going])


def gather_in(heads, one, two, block, *after):
    one_peer, two_peer = swap(one, 1), swap(two, 1)
    both = lax.optimization_barrier(jnp.concatenate([one, two], 0)).reshape((2,) + one.shape)
    keys = [[(u, w) for u in range(2) for w in range(0, heads, 2) if bool(w & 2) == b] for b in (False, True)]
    shapes = [jax.ShapeDtypeStruct((len(k),) + block, LOW) for k in keys]
    kept, sent = call(functools.partial(pack_kernel, heads, keys), "pack", shapes, both, one_peer, two_peer, *after)
    held = {k: (0, i) for i, k in enumerate(keys[0])}
    return exchange(heads, 2, [kept], held, sent, keys[1])


def scatter_out(heads, kept, sent):
    held = {(0, w): (0, w // 2) for w in range(0, heads, 2)}
    return exchange(heads, 1, [kept], held, sent, [(0, w) for w in range(1, heads, 2)])


def shards(queries, key_rows, value_rows, out_grads, neighbours):
    rows, features = queries.shape
    heads, owners = lax.axis_size("head"), lax.axis_size("node")
    width = features // heads
    local_count = neighbours.shape[0] // owners
    per_patch = heads // local_count
    patch = rows * per_patch
    half = jax.ShapeDtypeStruct((heads // 2, 2, rows, width), LOW)
    near_shape = jax.ShapeDtypeStruct((heads, 2, rows, width), jnp.float32)
    slab = jax.ShapeDtypeStruct((2, patch, width), LOW)
    whole = jax.ShapeDtypeStruct((rows, features), LOW)
    routes = pair_routes(owners, heads)
    span = heads * rows + 2 * patch
    lanes = width // HEAD_DIM * heads * rows

    kv, places = gather_in(heads, key_rows, value_rows, (2, rows, width))
    bias, slots = call(
        functools.partial(prep_kernel, heads, owners, local_count, per_patch, rows),
        "prep",
        [
            jax.ShapeDtypeStruct((heads + 2, heads * rows), jnp.float32),
            jax.ShapeDtypeStruct((2 * per_patch, width), jnp.int32),
        ],
        neighbours,
        kv[0],
        specs=[SMEM, VMEM],
    )
    qg, _ = gather_in(heads, queries, out_grads, (2, rows, width), slots)
    picked = call(functools.partial(pick_kernel, heads, places), "pick", [slab] * 2, slots, *kv)
    far = [lax.ppermute(p, ("node", "head"), r) for p, r in zip(picked, routes)]
    mq_kept, mq_sent, near, *far_grads = call(
        functools.partial(attend_kernel, heads, places, len(kv)),
        "attend",
        [half, half, near_shape, slab, slab],
        bias,
        *kv,
        *qg,
        *far,
        limit=24,
        scratch=[pltpu.VMEM((span, lanes), LOW)] * 2,
    )
    back = [lax.ppermute(p, ("node", "head"), r) for p, r in zip(far_grads, routes)]
    mq, _ = scatter_out(heads, mq_kept, mq_sent)
    merged = call(functools.partial(merge_kernel, heads), "merge", [half] * 2, slots, near, *back)
    kv_grads, out_places = scatter_out(heads, *merged)
    unpack = functools.partial(unpack_kernel, heads, out_places)
    mixed, query_grad = call(unpack, "unpack", [whole] * 2, *mq)
    key_grad, value_grad = call(unpack, "unpack", [whole] * 2, *kv_grads)
    return mixed, query_grad, key_grad, value_grad


def solution(mesh):
    rows = P(("grp", "node", "head"), None)
    return jax.shard_map(
        shards,
        mesh=mesh,
        in_specs=(rows, rows, rows, rows, P("grp", None)),
        out_specs=(rows, rows, rows, rows),
        check_vma=False,
    )
```

time: 38.9 us -> 33.8 us (0.87)
  the two profiles are of different devices: /device:TPU:9 before, /device:TPU:0 now
where the time goes in v3:
time: 33.8 us; the launch traced here: 33.6 us
  starting transfers between devices  13.6 us (40%)
  waiting for transfers between devices  11.8 us (35%)
  Pallas kernels  5.85 us (17%)
  other arithmetic  1 us (3%)
  between operations  0.76 us (2%)
  local copies, waits for them, and re-layouts  0.68 us (2%)
    ppermute x10, starting transfers between devices, swap(): return lax.ppermute(array, 'head', [(i, i ^ bit) for i in range(heads)])  8.65 us
    ppermute x10, waiting for transfers between devices, swap(): return lax.ppermute(array, 'head', [(i, i ^ bit) for i in range(heads)])  7.32 us
    pallas_call x10, Pallas kernels, call(): pl.pallas_call(kernel, out_shape=outs, in_specs=specs or [VMEM] * len(arg...  5.85 us
    ppermute x2, starting transfers between devices, shards(): lax.ppermute(p, ('node', 'head'), r)  3.02 us
    ppermute x2, waiting for transfers between devices, shards(): lax.ppermute(p, ('node', 'head'), r)  2.44 us
    ppermute x2, waiting for transfers between devices, shards(): far = [lax.ppermute(p, ('node', 'head'), r) for p, r in zip(picked, routes)]  2 us
    ppermute x2, starting transfers between devices, shards(): far = [lax.ppermute(p, ('node', 'head'), r) for p, r in zip(picked, routes)]  1.89 us
    concatenate x2, other arithmetic, gather_in(): jnp.concatenate([one, two], 0)  1 us
  transfers between devices with their start and end apart: 14, of which 6 were waited for; matrix products, arithmetic and copies ran while one was open for 3% of the time, Pallas kernels for 6%

profile of v3, /device:TPU:0, one launch (start us, length us, event | category | flops | bytes accessed | tf_op | source)
XLA Modules:
  0.0 33.6 jit_solution(2733711605081951697)
XLA Ops:
  0.6 0.5 %collective-permute-start = (bf16[64,1024]{1,0:T(8,128)(2,1)}, bf16[64,1024]{1,0:T(8,128)(2,1)S(1)}, u32[]{:S(2)}, u32[]{:S(2)}) collective-permute-start(bf16[64,1024]{1,0:T(8,128)(2,1)} %param.6), channel_id=1, source_target_pairs={{0,1},{1,0},{2,3},{3,2},{4,5},{5,4},{6,7},{7,6},{8,9},{9,8},{10,11... | collective-permute-start | bytes 393224 | tf_op jit(solution)/shard_map/ppermute | solution.py:205
  1.1 0.1 collective-permute-start.1
  1.2 0.4 %collective-permute-start.3 = (bf16[64,1024]{1,0:T(8,128)(2,1)}, bf16[64,1024]{1,0:T(8,128)(2,1)S(1)}, u32[]{:S(2)}, u32[]{:S(2)}) collective-permute-start(bf16[64,1024]{1,0:T(8,128)(2,1)} %param.5), channel_id=1, source_target_pairs={{0,1},{1,0},{2,3},{3,2},{4,5},{5,4},{6,7},{7,6},{8,9},{9,8},{10,11... | collective-permute-start | bytes 393224 | tf_op jit(solution)/shard_map/ppermute | solution.py:205
  1.7 0.1 collective-permute-start.4
  1.7 1.0 %pad_maximum_fusion = bf16[128,1024]{1,0:T(8,128)(2,1)S(1)} fusion(bf16[64,1024]{1,0:T(8,128)(2,1)} %param.7, bf16[64,1024]{1,0:T(8,128)(2,1)} %param.6), kind=kLoop, calls=%fused_computation | loop fusion | flops 524288 | bytes 524288 | tf_op jit(solution)/shard_map/concatenate | solution.py:227
  2.7 0.0 collective-permute-done.one_peer
  2.7 0.0 collective-permute-done.1.two_peer
  2.7 0.0 copy-start.1
  2.8 0.0 copy-start.2
  2.8 3.0 %collective-permute-start.2 = (bf16[2,2,64,256]{3,2,1,0:T(8,128)(2,1)S(1)}, bf16[2,2,64,256]{3,2,1,0:T(8,128)(2,1)S(1)}, u32[]{:S(2)}, u32[]{:S(2)}) collective-permute-start(bf16[2,2,64,256]{3,2,1,0:T(8,128)(2,1)S(1)} %get-tuple-element.25), channel_id=1, source_target_pairs={{0,2},{1,3},{2,0},{3,1},{4,6},{5,7},{6,4},{7,5},{8,10},{9,11},{10,... | collective-permute-start | bytes 393224 | tf_op jit(solution)/shard_map/ppermute | solution.py:205
  5.8 0.0 copy-done.1
  5.8 0.0 copy-done.2
  5.8 0.0 copy-start
  5.8 0.7 %copy-done = s32[8,8]{1,0:T(8,128)S(1)} copy-done((s32[8,8]{1,0:T(8,128)S(1)}, s32[8,8]{1,0:T(8,128)}, u32[]{:S(2)}) %copy-start) | copy-done | bytes 280
  6.5 0.8 %prep.1 = (f32[6,256]{1,0:T(8,128)S(1)}, s32[4,256]{1,0:T(4,128)S(1)}) custom-call(s32[8,8]{1,0:T(8,128)S(1)} %copy-done, bf16[2,2,64,256]{3,2,1,0:T(8,128)(2,1)S(1)} %get-tuple-element.23.after_ref.refs_0_), custom_call_target="tpu_custom_call" | custom-call | tf_op jit(solution)/shard_map/prep/pallas_call | solution.py:24
  7.3 0.0 collective-permute-done.3.one_peer
  7.4 0.0 collective-permute-done.4.two_peer
  7.4 0.9 %collective-permute-start.5 = (bf16[2,2,64,256]{3,2,1,0:T(8,128)(2,1)S(1)}, bf16[2,2,64,256]{3,2,1,0:T(8,128)(2,1)S(1)}, u32[]{:S(2)}, u32[]{:S(2)}) collective-permute-start(bf16[2,2,64,256]{3,2,1,0:T(8,128)(2,1)S(1)} %get-tuple-element.28), channel_id=1, source_target_pairs={{0,2},{1,3},{2,0},{3,1},{4,6},{5,7},{6,4},{7,5},{8,10},{9,11},{10,... | collective-permute-start | bytes 393224 | tf_op jit(solution)/shard_map/ppermute | solution.py:205
  8.3 1.2 %collective-permute-done.2.refs_1_ = bf16[2,2,64,256]{3,2,1,0:T(8,128)(2,1)S(1)} collective-permute-done((bf16[2,2,64,256]{3,2,1,0:T(8,128)(2,1)S(1)}, bf16[2,2,64,256]{3,2,1,0:T(8,128)(2,1)S(1)}, u32[]{:S(2)}, u32[]{:S(2)}) %collective-permute-start.2) | collective-permute-done | bytes 131104 | tf_op jit(solution)/shard_map/ppermute | solution.py:205
  9.5 0.1 pick.1
  9.7 1.9 %collective-permute-start.6 = (bf16[2,128,256]{2,1,0:T(8,128)(2,1)S(1)}, bf16[2,128,256]{2,1,0:T(8,128)(2,1)S(1)}, u32[]{:S(2)}, u32[]{:S(2)}) collective-permute-start(bf16[2,128,256]{2,1,0:T(8,128)(2,1)S(1)} %get-tuple-element.29), channel_id=1, source_target_pairs={{0,4},{1,5},{2,6},{3,7},{4,0},{5,1},{6,2},{7,3},{8,12},{9,13},{10,... | collective-permute-start | bytes 393224 | tf_op jit(solution)/shard_map/ppermute | solution.py:269
  11.5 0.0 collective-permute-start.7
  11.5 1.1 %collective-permute-done.5.refs_3_ = bf16[2,2,64,256]{3,2,1,0:T(8,128)(2,1)S(1)} collective-permute-done((bf16[2,2,64,256]{3,2,1,0:T(8,128)(2,1)S(1)}, bf16[2,2,64,256]{3,2,1,0:T(8,128)(2,1)S(1)}, u32[]{:S(2)}, u32[]{:S(2)}) %collective-permute-start.5) | collective-permute-done | bytes 131104 | tf_op jit(solution)/shard_map/ppermute | solution.py:205
  12.7 2.0 %collective-permute-done.6.refs_4_ = bf16[2,128,256]{2,1,0:T(8,128)(2,1)S(1)} collective-permute-done((bf16[2,128,256]{2,1,0:T(8,128)(2,1)S(1)}, bf16[2,128,256]{2,1,0:T(8,128)(2,1)S(1)}, u32[]{:S(2)}, u32[]{:S(2)}) %collective-permute-start.6) | collective-permute-done | bytes 131104 | tf_op jit(solution)/shard_map/ppermute | solution.py:269
  14.7 0.0 collective-permute-done.7.refs_5_
  14.7 3.1 %attend.1 = (bf16[2,2,64,256]{3,2,1,0:T(8,128)(2,1)S(1)}, bf16[2,2,64,256]{3,2,1,0:T(8,128)(2,1)S(1)}, f32[4,2,64,256]{3,2,1,0:T(8,128)S(1)}, bf16[2,128,256]{2,1,0:T(8,128)(2,1)S(1)}, bf16[2,128,256]{2,1,0:T(8,128)(2,1)S(1)}) custom-call(f32[6,256]{1,0:T(8,128)S(1)} %get-tuple-element.24.bias_ref, ...), custom_call_target="tpu_custom_call" | custom-call | tf_op jit(solution)/shard_map/attend/pallas_call | solution.py:24
  17.8 3.0 %collective-permute-start.10 = (bf16[2,128,256]{2,1,0:T(8,128)(2,1)S(1)}, bf16[2,128,256]{2,1,0:T(8,128)(2,1)S(1)}, u32[]{:S(2)}, u32[]{:S(2)}) collective-permute-start(bf16[2,128,256]{2,1,0:T(8,128)(2,1)S(1)} %get-tuple-element.36), channel_id=1, source_target_pairs={{0,4},{1,5},{2,6},{3,7},{4,0},{5,1},{6,2},{7,3},{8,12},{9,13},{10,... | collective-permute-start | bytes 393224 | tf_op jit(solution)/shard_map/ppermute | solution.py:281
  20.8 0.0 collective-permute-start.11
  20.8 0.5 %collective-permute-start.8 = (bf16[2,2,64,256]{3,2,1,0:T(8,128)(2,1)S(1)}, bf16[2,2,64,256]{3,2,1,0:T(8,128)(2,1)S(1)}, u32[]{:S(2)}, u32[]{:S(2)}) collective-permute-start(bf16[2,2,64,256]{3,2,1,0:T(8,128)(2,1)S(1)} %get-tuple-element.32), channel_id=1, source_target_pairs={{0,1},{1,0},{2,3},{3,2},{4,5},{5,4},{6,7},{7,6},{8,9},{9,8},{10,11... | collective-permute-start | bytes 393224 | tf_op jit(solution)/shard_map/ppermute | solution.py:205
  21.3 2.4 %collective-permute-done.10.back_a = bf16[2,128,256]{2,1,0:T(8,128)(2,1)S(1)} collective-permute-done((bf16[2,128,256]{2,1,0:T(8,128)(2,1)S(1)}, bf16[2,128,256]{2,1,0:T(8,128)(2,1)S(1)}, u32[]{:S(2)}, u32[]{:S(2)}) %collective-permute-start.10) | collective-permute-done | bytes 131104 | tf_op jit(solution)/shard_map/ppermute | solution.py:281
  23.8 0.0 collective-permute-done.11.back_b
  23.8 0.2 merge.1
  24.0 0.1 collective-permute-start.12
  24.1 0.0 collective-permute-done.8.refs_1_
  24.1 1.8 %collective-permute-start.9 = (bf16[2,2,64,256]{3,2,1,0:T(8,128)(2,1)S(1)}, bf16[2,2,64,256]{3,2,1,0:T(8,128)(2,1)S(1)}, u32[]{:S(2)}, u32[]{:S(2)}) collective-permute-start(bf16[2,2,64,256]{3,2,1,0:T(8,128)(2,1)S(1)} %regroup.2), channel_id=1, source_target_pairs={{0,2},{1,3},{2,0},{3,1},{4,6},{5,7},{6,4},{7,5},{8,10},{9,11},{10,... | collective-permute-start | bytes 393224 | tf_op jit(solution)/shard_map/ppermute | solution.py:205
  25.9 0.0 collective-permute-done.12.refs_1_
  25.9 1.3 %collective-permute-start.13 = (bf16[2,2,64,256]{3,2,1,0:T(8,128)(2,1)S(1)}, bf16[2,2,64,256]{3,2,1,0:T(8,128)(2,1)S(1)}, u32[]{:S(2)}, u32[]{:S(2)}) collective-permute-start(bf16[2,2,64,256]{3,2,1,0:T(8,128)(2,1)S(1)} %regroup.3), channel_id=1, source_target_pairs={{0,2},{1,3},{2,0},{3,1},{4,6},{5,7},{6,4},{7,5},{8,10},{9,11},{10,... | collective-permute-start | bytes 393224 | tf_op jit(solution)/shard_map/ppermute | solution.py:205
  27.2 3.2 %collective-permute-done.9.refs_2_ = bf16[2,2,64,256]{3,2,1,0:T(8,128)(2,1)S(1)} collective-permute-done((bf16[2,2,64,256]{3,2,1,0:T(8,128)(2,1)S(1)}, bf16[2,2,64,256]{3,2,1,0:T(8,128)(2,1)S(1)}, u32[]{:S(2)}, u32[]{:S(2)}) %collective-permute-start.9) | collective-permute-done | bytes 131104 | tf_op jit(solution)/shard_map/ppermute | solution.py:205
  30.5 0.7 %unpack.2 = (bf16[64,1024]{1,0:T(8,128)(2,1)}, bf16[64,1024]{1,0:T(8,128)(2,1)}) custom-call(bf16[2,2,64,256]{3,2,1,0:T(8,128)(2,1)S(1)} %get-tuple-element.31.refs_0_, bf16[2,2,64,256]{3,2,1,0:T(8,128)(2,1)S(1)} %collective-permute-done.8.refs_1_, bf16[2,2,64,256]{3,2,1,0:T(8,128)(2,1)S(1)} %collective-permute-done.9.refs_2_), custom_call_target="tpu_custom_call" | custom-call | tf_op jit(solution)/shard_map/unpack/pallas_call | solution.py:24
  31.2 1.7 %collective-permute-done.13.refs_2_ = bf16[2,2,64,256]{3,2,1,0:T(8,128)(2,1)S(1)} collective-permute-done((bf16[2,2,64,256]{3,2,1,0:T(8,128)(2,1)S(1)}, bf16[2,2,64,256]{3,2,1,0:T(8,128)(2,1)S(1)}, u32[]{:S(2)}, u32[]{:S(2)}) %collective-permute-start.13) | collective-permute-done | bytes 131104 | tf_op jit(solution)/shard_map/ppermute | solution.py:205
  32.9 0.7 %unpack.3 = (bf16[64,1024]{1,0:T(8,128)(2,1)}, bf16[64,1024]{1,0:T(8,128)(2,1)}) custom-call(bf16[2,2,64,256]{3,2,1,0:T(8,128)(2,1)S(1)} %get-tuple-element.38.refs_0_, bf16[2,2,64,256]{3,2,1,0:T(8,128)(2,1)S(1)} %collective-permute-done.12.refs_1_, bf16[2,2,64,256]{3,2,1,0:T(8,128)(2,1)S(1)} %collective-permute-done.13.refs_2_), custom_call_target="tpu_custom_call" | custom-call | tf_op jit(solution)/shard_map/unpack/pallas_call | solution.py:24
  (5 shorter events, 0.1 us)
Async XLA Ops:
  0.6 2.1 %collective-permute-start = (bf16[64,1024]{1,0:T(8,128)(2,1)}, bf16[64,1024]{1,0:T(8,128)(2,1)S(1)}, u32[]{:S(2)}, u32[]{:S(2)}) collective-permute-start(bf16[64,1024]{1,0:T(8,128)(2,1)} %param.6), channel_id=1, source_target_pairs={{0,1},{1,0},{2,3},{3,2},{4,5},{5,4},{6,7},{7,6},{8,9},{9,8},{10,11... | collective-permute-start | bytes 393224 | tf_op jit(solution)/shard_map/ppermute | solution.py:205
  1.1 1.6 %collective-permute-start.1 = (bf16[64,1024]{1,0:T(8,128)(2,1)}, bf16[64,1024]{1,0:T(8,128)(2,1)S(1)}, u32[]{:S(2)}, u32[]{:S(2)}) collective-permute-start(bf16[64,1024]{1,0:T(8,128)(2,1)} %param.7), channel_id=1, source_target_pairs={{0,1},{1,0},{2,3},{3,2},{4,5},{5,4},{6,7},{7,6},{8,9},{9,8},{10,11... | collective-permute-start | bytes 393224 | tf_op jit(solution)/shard_map/ppermute | solution.py:205
  1.2 6.1 %collective-permute-start.3 = (bf16[64,1024]{1,0:T(8,128)(2,1)}, bf16[64,1024]{1,0:T(8,128)(2,1)S(1)}, u32[]{:S(2)}, u32[]{:S(2)}) collective-permute-start(bf16[64,1024]{1,0:T(8,128)(2,1)} %param.5), channel_id=1, source_target_pairs={{0,1},{1,0},{2,3},{3,2},{4,5},{5,4},{6,7},{7,6},{8,9},{9,8},{10,11... | collective-permute-start | bytes 393224 | tf_op jit(solution)/shard_map/ppermute | solution.py:205
  1.7 5.7 %collective-permute-start.4 = (bf16[64,1024]{1,0:T(8,128)(2,1)}, bf16[64,1024]{1,0:T(8,128)(2,1)S(1)}, u32[]{:S(2)}, u32[]{:S(2)}) collective-permute-start(bf16[64,1024]{1,0:T(8,128)(2,1)} %param.8), channel_id=1, source_target_pairs={{0,1},{1,0},{2,3},{3,2},{4,5},{5,4},{6,7},{7,6},{8,9},{9,8},{10,11... | collective-permute-start | bytes 393224 | tf_op jit(solution)/shard_map/ppermute | solution.py:205
  2.7 3.1 %copy-start.1 = (bf16[64,1024]{1,0:T(8,128)(2,1)S(1)}, bf16[64,1024]{1,0:T(8,128)(2,1)}, u32[]{:S(2)}) copy-start(bf16[64,1024]{1,0:T(8,128)(2,1)} %param.5) | copy-start | bytes 393220
  2.8 3.1 %copy-start.2 = (bf16[64,1024]{1,0:T(8,128)(2,1)S(1)}, bf16[64,1024]{1,0:T(8,128)(2,1)}, u32[]{:S(2)}) copy-start(bf16[64,1024]{1,0:T(8,128)(2,1)} %param.8) | copy-start | bytes 393220
  2.8 6.7 %collective-permute-start.2 = (bf16[2,2,64,256]{3,2,1,0:T(8,128)(2,1)S(1)}, bf16[2,2,64,256]{3,2,1,0:T(8,128)(2,1)S(1)}, u32[]{:S(2)}, u32[]{:S(2)}) collective-permute-start(bf16[2,2,64,256]{3,2,1,0:T(8,128)(2,1)S(1)} %get-tuple-element.25), channel_id=1, source_target_pairs={{0,2},{1,3},{2,0},{3,1},{4,6},{5,7},{6,4},{7,5},{8,10},{9,11},{10,... | collective-permute-start | bytes 393224 | tf_op jit(solution)/shard_map/ppermute | solution.py:205
  5.8 0.7 %copy-start = (s32[8,8]{1,0:T(8,128)S(1)}, s32[8,8]{1,0:T(8,128)}, u32[]{:S(2)}) copy-start(s32[8,8]{1,0:T(8,128)} %nbr_ref.1) | copy-start | bytes 772
  7.4 5.3 %collective-permute-start.5 = (bf16[2,2,64,256]{3,2,1,0:T(8,128)(2,1)S(1)}, bf16[2,2,64,256]{3,2,1,0:T(8,128)(2,1)S(1)}, u32[]{:S(2)}, u32[]{:S(2)}) collective-permute-start(bf16[2,2,64,256]{3,2,1,0:T(8,128)(2,1)S(1)} %get-tuple-element.28), channel_id=1, source_target_pairs={{0,2},{1,3},{2,0},{3,1},{4,6},{5,7},{6,4},{7,5},{8,10},{9,11},{10,... | collective-permute-start | bytes 393224 | tf_op jit(solution)/shard_map/ppermute | solution.py:205
  9.7 5.0 %collective-permute-start.6 = (bf16[2,128,256]{2,1,0:T(8,128)(2,1)S(1)}, bf16[2,128,256]{2,1,0:T(8,128)(2,1)S(1)}, u32[]{:S(2)}, u32[]{:S(2)}) collective-permute-start(bf16[2,128,256]{2,1,0:T(8,128)(2,1)S(1)} %get-tuple-element.29), channel_id=1, source_target_pairs={{0,4},{1,5},{2,6},{3,7},{4,0},{5,1},{6,2},{7,3},{8,12},{9,13},{10,... | collective-permute-start | bytes 393224 | tf_op jit(solution)/shard_map/ppermute | solution.py:269
  11.5 3.1 %collective-permute-start.7 = (bf16[2,128,256]{2,1,0:T(8,128)(2,1)S(1)}, bf16[2,128,256]{2,1,0:T(8,128)(2,1)S(1)}, u32[]{:S(2)}, u32[]{:S(2)}) collective-permute-start(bf16[2,128,256]{2,1,0:T(8,128)(2,1)S(1)} %get-tuple-element.30), channel_id=1, source_target_pairs={{0,1},{1,0},{2,3},{3,2},{4,8},{5,9},{6,10},{7,11},{8,4},{9,5},{10,... | collective-permute-start | bytes 393224 | tf_op jit(solution)/shard_map/ppermute | solution.py:269
  17.8 6.0 %collective-permute-start.10 = (bf16[2,128,256]{2,1,0:T(8,128)(2,1)S(1)}, bf16[2,128,256]{2,1,0:T(8,128)(2,1)S(1)}, u32[]{:S(2)}, u32[]{:S(2)}) collective-permute-start(bf16[2,128,256]{2,1,0:T(8,128)(2,1)S(1)} %get-tuple-element.36), channel_id=1, source_target_pairs={{0,4},{1,5},{2,6},{3,7},{4,0},{5,1},{6,2},{7,3},{8,12},{9,13},{10,... | collective-permute-start | bytes 393224 | tf_op jit(solution)/shard_map/ppermute | solution.py:281
  20.8 3.0 %collective-permute-start.11 = (bf16[2,128,256]{2,1,0:T(8,128)(2,1)S(1)}, bf16[2,128,256]{2,1,0:T(8,128)(2,1)S(1)}, u32[]{:S(2)}, u32[]{:S(2)}) collective-permute-start(bf16[2,128,256]{2,1,0:T(8,128)(2,1)S(1)} %get-tuple-element.37), channel_id=1, source_target_pairs={{0,1},{1,0},{2,3},{3,2},{4,8},{5,9},{6,10},{7,11},{8,4},{9,5},{10,... | collective-permute-start | bytes 393224 | tf_op jit(solution)/shard_map/ppermute | solution.py:281
  20.8 3.3 %collective-permute-start.8 = (bf16[2,2,64,256]{3,2,1,0:T(8,128)(2,1)S(1)}, bf16[2,2,64,256]{3,2,1,0:T(8,128)(2,1)S(1)}, u32[]{:S(2)}, u32[]{:S(2)}) collective-permute-start(bf16[2,2,64,256]{3,2,1,0:T(8,128)(2,1)S(1)} %get-tuple-element.32), channel_id=1, source_target_pairs={{0,1},{1,0},{2,3},{3,2},{4,5},{5,4},{6,7},{7,6},{8,9},{9,8},{10,11... | collective-permute-start | bytes 393224 | tf_op jit(solution)/shard_map/ppermute | solution.py:205
  24.0 1.9 %collective-permute-start.12 = (bf16[2,2,64,256]{3,2,1,0:T(8,128)(2,1)S(1)}, bf16[2,2,64,256]{3,2,1,0:T(8,128)(2,1)S(1)}, u32[]{:S(2)}, u32[]{:S(2)}) collective-permute-start(bf16[2,2,64,256]{3,2,1,0:T(8,128)(2,1)S(1)} %get-tuple-element.39), channel_id=1, source_target_pairs={{0,1},{1,0},{2,3},{3,2},{4,5},{5,4},{6,7},{7,6},{8,9},{9,8},{10,11... | collective-permute-start | bytes 393224 | tf_op jit(solution)/shard_map/ppermute | solution.py:205
  24.1 6.4 %collective-permute-start.9 = (bf16[2,2,64,256]{3,2,1,0:T(8,128)(2,1)S(1)}, bf16[2,2,64,256]{3,2,1,0:T(8,128)(2,1)S(1)}, u32[]{:S(2)}, u32[]{:S(2)}) collective-permute-start(bf16[2,2,64,256]{3,2,1,0:T(8,128)(2,1)S(1)} %regroup.2), channel_id=1, source_target_pairs={{0,2},{1,3},{2,0},{3,1},{4,6},{5,7},{6,4},{7,5},{8,10},{9,11},{10,... | collective-permute-start | bytes 393224 | tf_op jit(solution)/shard_map/ppermute | solution.py:205
  25.9 7.0 %collective-permute-start.13 = (bf16[2,2,64,256]{3,2,1,0:T(8,128)(2,1)S(1)}, bf16[2,2,64,256]{3,2,1,0:T(8,128)(2,1)S(1)}, u32[]{:S(2)}, u32[]{:S(2)}) collective-permute-start(bf16[2,2,64,256]{3,2,1,0:T(8,128)(2,1)S(1)} %regroup.3), channel_id=1, source_target_pairs={{0,2},{1,3},{2,0},{3,1},{4,6},{5,7},{6,4},{7,5},{8,10},{9,11},{10,... | collective-permute-start | bytes 393224 | tf_op jit(solution)/shard_map/ppermute | solution.py:205

commit v4 on v3

--- a/solution.py
+++ b/solution.py
@@ -31,6 +31,14 @@
         cost_estimate=cost,
         compiler_params=pltpu.CompilerParams(vmem_limit_bytes=limit * 1024 * 1024),
     )(*args)
+
+
+def all_bits(heads):
+    return [1 << i for i in range(heads.bit_length() - 1)]
+
+
+def split_at(heads, bit):
+    return [w for w in range(heads) if not w & bit], [w for w in range(heads) if w & bit]
 
 
 def pair_routes(owners, heads):
@@ -170,7 +178,8 @@
     value_grad = dot(w_all[...], jnp.concatenate(grad_h, 0))
     for d in range(heads):
         span = slice(d * rows, (d + 1) * rows)
-        out = (mq_sent if d % 2 else mq_kept).at[d // 2]
+        stay, go = split_at(heads, heads // 2)
+        out = mq_kept.at[stay.index(d)] if d in stay else mq_sent.at[go.index(d)]
         out[0], out[1] = mixed[span], qgrad[span]
         near_out[d, 0], near_out[d, 1] = key_grad[span], value_grad[span]
     for s, out in enumerate((far_a, far_b)):
@@ -188,7 +197,11 @@
                 slot = slot_ref[s * per_patch + t : s * per_patch + t + 1, :]
                 term = back[:, t * rows : (t + 1) * rows, :].astype(jnp.float32)
                 total = total + jnp.where((slot == d)[None], term, 0.0)
-        (sent if d % 2 else kept)[d // 2] = total.astype(LOW)
+        stay, go = split_at(heads, heads // 2)
+        if d in stay:
+            kept[stay.index(d)] = total.astype(LOW)
+        else:
+            sent[go.index(d)] = total.astype(LOW)
 
 
 def unpack_kernel(heads, places, *refs):
@@ -210,16 +223,15 @@
     return call(functools.partial(gather_kernel, places), "regroup", [shape], *arrays)[0]
 
 
-def exchange(heads, bit, arrays, held, outgoing, going):
-    while True:
+def exchange(bits, arrays, held, outgoing, going):
+    for i, bit in enumerate(bits):
+        if i:
+            going = sorted(k for k in held if k[1] & bit)
+            outgoing = regroup(arrays, [held.pop(k) for k in going])
         arrays.append(swap(outgoing, bit))
-        for i, (u, w) in enumerate(going):
-            held[(u + bit, w - bit)] = (len(arrays) - 1, i)
-        bit *= 2
-        if bit >= heads:
-            return arrays, [held[(d, 0)] for d in range(heads)]
-        going = sorted(k for k in held if k[1] & bit)
-        outgoing = regroup(arrays, [held.pop(k) for k in going])
+        for j, (u, w) in enumerate(going):
+            held[(u + bit, w - bit)] = (len(arrays) - 1, j)
+    return arrays, [held[(d, 0)] for d in range(lax.axis_size("head"))]
 
 
 def gather_in(heads, one, two, block, *after):
@@ -229,12 +241,12 @@
     shapes = [jax.ShapeDtypeStruct((len(k),) + block, LOW) for k in keys]
     kept, sent = call(functools.partial(pack_kernel, heads, keys), "pack", shapes, both, one_peer, two_peer, *after)
     held = {k: (0, i) for i, k in enumerate(keys[0])}
-    return exchange(heads, 2, [kept], held, sent, keys[1])
-
-
-def scatter_out(heads, kept, sent):
-    held = {(0, w): (0, w // 2) for w in range(0, heads, 2)}
-    return exchange(heads, 1, [kept], held, sent, [(0, w) for w in range(1, heads, 2)])
+    return exchange(all_bits(heads)[1:], [kept], held, sent, keys[1])
+
+
+def scatter_out(heads, bits, kept, sent):
+    stay, go = split_at(heads, bits[0])
+    return exchange(bits, [kept], {(0, w): (0, i) for i, w in enumerate(stay)}, sent, [(0, w) for w in go])
 
 
 def shards(queries, key_rows, value_rows, out_grads, neighbours):
@@ -279,12 +291,12 @@
         scratch=[pltpu.VMEM((span, lanes), LOW)] * 2,
     )
     back = [lax.ppermute(p, ("node", "head"), r) for p, r in zip(far_grads, routes)]
-    mq, _ = scatter_out(heads, mq_kept, mq_sent)
+    mq, mq_places = scatter_out(heads, all_bits(heads)[::-1], mq_kept, mq_sent)
     merged = call(functools.partial(merge_kernel, heads), "merge", [half] * 2, slots, near, *back)
-    kv_grads, out_places = scatter_out(heads, *merged)
-    unpack = functools.partial(unpack_kernel, heads, out_places)
-    mixed, query_grad = call(unpack, "unpack", [whole] * 2, *mq)
-    key_grad, value_grad = call(unpack, "unpack", [whole] * 2, *kv_grads)
+    kv_grads, kv_places = scatter_out(heads, all_bits(heads)[::-1], *merged)
+    unpack = functools.partial(unpack_kernel, heads)
+    mixed, query_grad = call(functools.partial(unpack, mq_places), "unpack", [whole] * 2, *mq)
+    key_grad, value_grad = call(functools.partial(unpack, kv_places), "unpack", [whole] * 2, *kv_grads)
     return mixed, query_grad, key_grad, value_grad
 
 

time: 33.8 us -> 31.9 us (0.944)
  waiting for transfers between devices: 11.8 us -> 9.85 us
    ppermute x2, waiting for transfers between devices: 2.44 us -> 1.22 us  [shards(): lax.ppermute(p, ('node', 'head'), r)]
    ppermute x10, waiting for transfers between devices: 7.32 us -> 6.62 us  [swap(): return lax.ppermute(array, 'head', [(i, i ^ bit) for i in range(heads)])]
  transfers between devices with their start and end apart: 14 -> 14, of which waited for: 6 -> 7; matrix products, arithmetic and copies ran while one was open for 3% -> 3% of each run, Pallas kernels for 6% -> 6%
where the time goes in v4:
time: 31.9 us; the launch traced here: 31.7 us
  starting transfers between devices  13.5 us (42%)
  waiting for transfers between devices  9.85 us (31%)
  Pallas kernels  5.85 us (18%)
  other arithmetic  1 us (3%)
  between operations  0.77 us (2%)
  local copies, waits for them, and re-layouts  0.68 us (2%)
    ppermute x10, starting transfers between devices, swap(): return lax.ppermute(array, 'head', [(i, i ^ bit) for i in range(heads)])  8.63 us
    ppermute x10, waiting for transfers between devices, swap(): return lax.ppermute(array, 'head', [(i, i ^ bit) for i in range(heads)])  6.62 us
    pallas_call x10, Pallas kernels, call(): pl.pallas_call(kernel, out_shape=outs, in_specs=specs or [VMEM] * len(arg...  5.85 us
    ppermute x2, starting transfers between devices, shards(): lax.ppermute(p, ('node', 'head'), r)  3.02 us
    ppermute x2, waiting for transfers between devices, shards(): far = [lax.ppermute(p, ('node', 'head'), r) for p, r in zip(picked, routes)]  2 us
    ppermute x2, starting transfers between devices, shards(): far = [lax.ppermute(p, ('node', 'head'), r) for p, r in zip(picked, routes)]  1.89 us
    ppermute x2, waiting for transfers between devices, shards(): lax.ppermute(p, ('node', 'head'), r)  1.22 us
    concatenate x2, other arithmetic, gather_in(): jnp.concatenate([one, two], 0)  1 us
  transfers between devices with their start and end apart: 14, of which 7 were waited for; matrix products, arithmetic and copies ran while one was open for 3% of the time, Pallas kernels for 6%

profile of v4, /device:TPU:0, one launch (start us, length us, event | category | flops | bytes accessed | tf_op | source)
XLA Modules:
  0.0 31.7 jit_solution(17278359653649699746)
XLA Ops:
  0.6 0.5 %collective-permute-start = (bf16[64,1024]{1,0:T(8,128)(2,1)}, bf16[64,1024]{1,0:T(8,128)(2,1)S(1)}, u32[]{:S(2)}, u32[]{:S(2)}) collective-permute-start(bf16[64,1024]{1,0:T(8,128)(2,1)} %param.6), channel_id=1, source_target_pairs={{0,1},{1,0},{2,3},{3,2},{4,5},{5,4},{6,7},{7,6},{8,9},{9,8},{10,11... | collective-permute-start | bytes 393224 | tf_op jit(solution)/shard_map/ppermute | solution.py:218
  1.1 0.1 collective-permute-start.1
  1.2 0.4 %collective-permute-start.3 = (bf16[64,1024]{1,0:T(8,128)(2,1)}, bf16[64,1024]{1,0:T(8,128)(2,1)S(1)}, u32[]{:S(2)}, u32[]{:S(2)}) collective-permute-start(bf16[64,1024]{1,0:T(8,128)(2,1)} %param.5), channel_id=1, source_target_pairs={{0,1},{1,0},{2,3},{3,2},{4,5},{5,4},{6,7},{7,6},{8,9},{9,8},{10,11... | collective-permute-start | bytes 393224 | tf_op jit(solution)/shard_map/ppermute | solution.py:218
  1.7 0.1 collective-permute-start.4
  1.7 1.0 %pad_maximum_fusion = bf16[128,1024]{1,0:T(8,128)(2,1)S(1)} fusion(bf16[64,1024]{1,0:T(8,128)(2,1)} %param.7, bf16[64,1024]{1,0:T(8,128)(2,1)} %param.6), kind=kLoop, calls=%fused_computation | loop fusion | flops 524288 | bytes 524288 | tf_op jit(solution)/shard_map/concatenate | solution.py:239
  2.7 0.0 collective-permute-done.one_peer
  2.7 0.0 collective-permute-done.1.two_peer
  2.7 0.0 copy-start.1
  2.8 0.0 copy-start.2
  2.8 3.0 %collective-permute-start.2 = (bf16[2,2,64,256]{3,2,1,0:T(8,128)(2,1)S(1)}, bf16[2,2,64,256]{3,2,1,0:T(8,128)(2,1)S(1)}, u32[]{:S(2)}, u32[]{:S(2)}) collective-permute-start(bf16[2,2,64,256]{3,2,1,0:T(8,128)(2,1)S(1)} %get-tuple-element.25), channel_id=1, source_target_pairs={{0,2},{1,3},{2,0},{3,1},{4,6},{5,7},{6,4},{7,5},{8,10},{9,11},{10,... | collective-permute-start | bytes 393224 | tf_op jit(solution)/shard_map/ppermute | solution.py:218
  5.8 0.0 copy-done.1
  5.8 0.0 copy-done.2
  5.8 0.0 copy-start
  5.8 0.7 %copy-done = s32[8,8]{1,0:T(8,128)S(1)} copy-done((s32[8,8]{1,0:T(8,128)S(1)}, s32[8,8]{1,0:T(8,128)}, u32[]{:S(2)}) %copy-start) | copy-done | bytes 280
  6.5 0.8 %prep.1 = (f32[6,256]{1,0:T(8,128)S(1)}, s32[4,256]{1,0:T(4,128)S(1)}) custom-call(s32[8,8]{1,0:T(8,128)S(1)} %copy-done, bf16[2,2,64,256]{3,2,1,0:T(8,128)(2,1)S(1)} %get-tuple-element.23.after_ref.refs_0_), custom_call_target="tpu_custom_call" | custom-call | tf_op jit(solution)/shard_map/prep/pallas_call | solution.py:24
  7.3 0.0 collective-permute-done.3.one_peer
  7.4 0.0 collective-permute-done.4.two_peer
  7.4 0.9 %collective-permute-start.5 = (bf16[2,2,64,256]{3,2,1,0:T(8,128)(2,1)S(1)}, bf16[2,2,64,256]{3,2,1,0:T(8,128)(2,1)S(1)}, u32[]{:S(2)}, u32[]{:S(2)}) collective-permute-start(bf16[2,2,64,256]{3,2,1,0:T(8,128)(2,1)S(1)} %get-tuple-element.28), channel_id=1, source_target_pairs={{0,2},{1,3},{2,0},{3,1},{4,6},{5,7},{6,4},{7,5},{8,10},{9,11},{10,... | collective-permute-start | bytes 393224 | tf_op jit(solution)/shard_map/ppermute | solution.py:218
  8.3 1.2 %collective-permute-done.2.refs_1_ = bf16[2,2,64,256]{3,2,1,0:T(8,128)(2,1)S(1)} collective-permute-done((bf16[2,2,64,256]{3,2,1,0:T(8,128)(2,1)S(1)}, bf16[2,2,64,256]{3,2,1,0:T(8,128)(2,1)S(1)}, u32[]{:S(2)}, u32[]{:S(2)}) %collective-permute-start.2) | collective-permute-done | bytes 131104 | tf_op jit(solution)/shard_map/ppermute | solution.py:218
  9.5 0.1 pick.1
  9.7 1.9 %collective-permute-start.6 = (bf16[2,128,256]{2,1,0:T(8,128)(2,1)S(1)}, bf16[2,128,256]{2,1,0:T(8,128)(2,1)S(1)}, u32[]{:S(2)}, u32[]{:S(2)}) collective-permute-start(bf16[2,128,256]{2,1,0:T(8,128)(2,1)S(1)} %get-tuple-element.29), channel_id=1, source_target_pairs={{0,4},{1,5},{2,6},{3,7},{4,0},{5,1},{6,2},{7,3},{8,12},{9,13},{10,... | collective-permute-start | bytes 393224 | tf_op jit(solution)/shard_map/ppermute | solution.py:281
  11.5 0.0 collective-permute-start.7
  11.5 1.1 %collective-permute-done.5.refs_3_ = bf16[2,2,64,256]{3,2,1,0:T(8,128)(2,1)S(1)} collective-permute-done((bf16[2,2,64,256]{3,2,1,0:T(8,128)(2,1)S(1)}, bf16[2,2,64,256]{3,2,1,0:T(8,128)(2,1)S(1)}, u32[]{:S(2)}, u32[]{:S(2)}) %collective-permute-start.5) | collective-permute-done | bytes 131104 | tf_op jit(solution)/shard_map/ppermute | solution.py:218
  12.7 2.0 %collective-permute-done.6.refs_4_ = bf16[2,128,256]{2,1,0:T(8,128)(2,1)S(1)} collective-permute-done((bf16[2,128,256]{2,1,0:T(8,128)(2,1)S(1)}, bf16[2,128,256]{2,1,0:T(8,128)(2,1)S(1)}, u32[]{:S(2)}, u32[]{:S(2)}) %collective-permute-start.6) | collective-permute-done | bytes 131104 | tf_op jit(solution)/shard_map/ppermute | solution.py:281
  14.7 0.0 collective-permute-done.7.refs_5_
  14.7 3.1 %attend.1 = (bf16[2,2,64,256]{3,2,1,0:T(8,128)(2,1)S(1)}, bf16[2,2,64,256]{3,2,1,0:T(8,128)(2,1)S(1)}, f32[4,2,64,256]{3,2,1,0:T(8,128)S(1)}, bf16[2,128,256]{2,1,0:T(8,128)(2,1)S(1)}, bf16[2,128,256]{2,1,0:T(8,128)(2,1)S(1)}) custom-call(f32[6,256]{1,0:T(8,128)S(1)} %get-tuple-element.24.bias_ref, ...), custom_call_target="tpu_custom_call" | custom-call | tf_op jit(solution)/shard_map/attend/pallas_call | solution.py:24
  17.8 3.0 %collective-permute-start.10 = (bf16[2,128,256]{2,1,0:T(8,128)(2,1)S(1)}, bf16[2,128,256]{2,1,0:T(8,128)(2,1)S(1)}, u32[]{:S(2)}, u32[]{:S(2)}) collective-permute-start(bf16[2,128,256]{2,1,0:T(8,128)(2,1)S(1)} %get-tuple-element.36), channel_id=1, source_target_pairs={{0,4},{1,5},{2,6},{3,7},{4,0},{5,1},{6,2},{7,3},{8,12},{9,13},{10,... | collective-permute-start | bytes 393224 | tf_op jit(solution)/shard_map/ppermute | solution.py:293
  20.8 0.0 collective-permute-start.11
  20.8 1.7 %collective-permute-start.8 = (bf16[2,2,64,256]{3,2,1,0:T(8,128)(2,1)S(1)}, bf16[2,2,64,256]{3,2,1,0:T(8,128)(2,1)S(1)}, u32[]{:S(2)}, u32[]{:S(2)}) collective-permute-start(bf16[2,2,64,256]{3,2,1,0:T(8,128)(2,1)S(1)} %get-tuple-element.32), channel_id=1, source_target_pairs={{0,2},{1,3},{2,0},{3,1},{4,6},{5,7},{6,4},{7,5},{8,10},{9,11},{10,... | collective-permute-start | bytes 393224 | tf_op jit(solution)/shard_map/ppermute | solution.py:218
  22.6 1.2 %collective-permute-done.10.back_a = bf16[2,128,256]{2,1,0:T(8,128)(2,1)S(1)} collective-permute-done((bf16[2,128,256]{2,1,0:T(8,128)(2,1)S(1)}, bf16[2,128,256]{2,1,0:T(8,128)(2,1)S(1)}, u32[]{:S(2)}, u32[]{:S(2)}) %collective-permute-start.10) | collective-permute-done | bytes 131104 | tf_op jit(solution)/shard_map/ppermute | solution.py:293
  23.8 0.0 collective-permute-done.11.back_b
  23.8 0.2 merge.1
  24.0 1.8 %collective-permute-start.12 = (bf16[2,2,64,256]{3,2,1,0:T(8,128)(2,1)S(1)}, bf16[2,2,64,256]{3,2,1,0:T(8,128)(2,1)S(1)}, u32[]{:S(2)}, u32[]{:S(2)}) collective-permute-start(bf16[2,2,64,256]{3,2,1,0:T(8,128)(2,1)S(1)} %get-tuple-element.39), channel_id=1, source_target_pairs={{0,2},{1,3},{2,0},{3,1},{4,6},{5,7},{6,4},{7,5},{8,10},{9,11},{10,... | collective-permute-start | bytes 393224 | tf_op jit(solution)/shard_map/ppermute | solution.py:218
  25.8 1.3 %collective-permute-done.8.refs_1_ = bf16[2,2,64,256]{3,2,1,0:T(8,128)(2,1)S(1)} collective-permute-done((bf16[2,2,64,256]{3,2,1,0:T(8,128)(2,1)S(1)}, bf16[2,2,64,256]{3,2,1,0:T(8,128)(2,1)S(1)}, u32[]{:S(2)}, u32[]{:S(2)}) %collective-permute-start.8) | collective-permute-done | bytes 131104 | tf_op jit(solution)/shard_map/ppermute | solution.py:218
  27.1 0.1 collective-permute-start.9
  27.2 2.3 %collective-permute-done.12.refs_1_ = bf16[2,2,64,256]{3,2,1,0:T(8,128)(2,1)S(1)} collective-permute-done((bf16[2,2,64,256]{3,2,1,0:T(8,128)(2,1)S(1)}, bf16[2,2,64,256]{3,2,1,0:T(8,128)(2,1)S(1)}, u32[]{:S(2)}, u32[]{:S(2)}) %collective-permute-start.12) | collective-permute-done | bytes 131104 | tf_op jit(solution)/shard_map/ppermute | solution.py:218
  29.6 0.1 collective-permute-start.13
  29.6 0.0 collective-permute-done.9.refs_2_
  29.6 0.7 %unpack.2 = (bf16[64,1024]{1,0:T(8,128)(2,1)}, bf16[64,1024]{1,0:T(8,128)(2,1)}) custom-call(bf16[2,2,64,256]{3,2,1,0:T(8,128)(2,1)S(1)} %get-tuple-element.31.refs_0_, bf16[2,2,64,256]{3,2,1,0:T(8,128)(2,1)S(1)} %collective-permute-done.8.refs_1_, bf16[2,2,64,256]{3,2,1,0:T(8,128)(2,1)S(1)} %collective-permute-done.9.refs_2_), custom_call_target="tpu_custom_call" | custom-call | tf_op jit(solution)/shard_map/unpack/pallas_call | solution.py:24
  30.4 0.6 %collective-permute-done.13.refs_2_ = bf16[2,2,64,256]{3,2,1,0:T(8,128)(2,1)S(1)} collective-permute-done((bf16[2,2,64,256]{3,2,1,0:T(8,128)(2,1)S(1)}, bf16[2,2,64,256]{3,2,1,0:T(8,128)(2,1)S(1)}, u32[]{:S(2)}, u32[]{:S(2)}) %collective-permute-start.13) | collective-permute-done | bytes 131104 | tf_op jit(solution)/shard_map/ppermute | solution.py:218
  31.0 0.7 %unpack.3 = (bf16[64,1024]{1,0:T(8,128)(2,1)}, bf16[64,1024]{1,0:T(8,128)(2,1)}) custom-call(bf16[2,2,64,256]{3,2,1,0:T(8,128)(2,1)S(1)} %get-tuple-element.38.refs_0_, bf16[2,2,64,256]{3,2,1,0:T(8,128)(2,1)S(1)} %collective-permute-done.12.refs_1_, bf16[2,2,64,256]{3,2,1,0:T(8,128)(2,1)S(1)} %collective-permute-done.13.refs_2_), custom_call_target="tpu_custom_call" | custom-call | tf_op jit(solution)/shard_map/unpack/pallas_call | solution.py:24
  (5 shorter events, 0.1 us)
Async XLA Ops:
  0.6 2.1 %collective-permute-start = (bf16[64,1024]{1,0:T(8,128)(2,1)}, bf16[64,1024]{1,0:T(8,128)(2,1)S(1)}, u32[]{:S(2)}, u32[]{:S(2)}) collective-permute-start(bf16[64,1024]{1,0:T(8,128)(2,1)} %param.6), channel_id=1, source_target_pairs={{0,1},{1,0},{2,3},{3,2},{4,5},{5,4},{6,7},{7,6},{8,9},{9,8},{10,11... | collective-permute-start | bytes 393224 | tf_op jit(solution)/shard_map/ppermute | solution.py:218
  1.1 1.6 %collective-permute-start.1 = (bf16[64,1024]{1,0:T(8,128)(2,1)}, bf16[64,1024]{1,0:T(8,128)(2,1)S(1)}, u32[]{:S(2)}, u32[]{:S(2)}) collective-permute-start(bf16[64,1024]{1,0:T(8,128)(2,1)} %param.7), channel_id=1, source_target_pairs={{0,1},{1,0},{2,3},{3,2},{4,5},{5,4},{6,7},{7,6},{8,9},{9,8},{10,11... | collective-permute-start | bytes 393224 | tf_op jit(solution)/shard_map/ppermute | solution.py:218
  1.2 6.1 %collective-permute-start.3 = (bf16[64,1024]{1,0:T(8,128)(2,1)}, bf16[64,1024]{1,0:T(8,128)(2,1)S(1)}, u32[]{:S(2)}, u32[]{:S(2)}) collective-permute-start(bf16[64,1024]{1,0:T(8,128)(2,1)} %param.5), channel_id=1, source_target_pairs={{0,1},{1,0},{2,3},{3,2},{4,5},{5,4},{6,7},{7,6},{8,9},{9,8},{10,11... | collective-permute-start | bytes 393224 | tf_op jit(solution)/shard_map/ppermute | solution.py:218
  1.7 5.7 %collective-permute-start.4 = (bf16[64,1024]{1,0:T(8,128)(2,1)}, bf16[64,1024]{1,0:T(8,128)(2,1)S(1)}, u32[]{:S(2)}, u32[]{:S(2)}) collective-permute-start(bf16[64,1024]{1,0:T(8,128)(2,1)} %param.8), channel_id=1, source_target_pairs={{0,1},{1,0},{2,3},{3,2},{4,5},{5,4},{6,7},{7,6},{8,9},{9,8},{10,11... | collective-permute-start | bytes 393224 | tf_op jit(solution)/shard_map/ppermute | solution.py:218
  2.7 3.1 %copy-start.1 = (bf16[64,1024]{1,0:T(8,128)(2,1)S(1)}, bf16[64,1024]{1,0:T(8,128)(2,1)}, u32[]{:S(2)}) copy-start(bf16[64,1024]{1,0:T(8,128)(2,1)} %param.5) | copy-start | bytes 393220
  2.8 3.1 %copy-start.2 = (bf16[64,1024]{1,0:T(8,128)(2,1)S(1)}, bf16[64,1024]{1,0:T(8,128)(2,1)}, u32[]{:S(2)}) copy-start(bf16[64,1024]{1,0:T(8,128)(2,1)} %param.8) | copy-start | bytes 393220
  2.8 6.7 %collective-permute-start.2 = (bf16[2,2,64,256]{3,2,1,0:T(8,128)(2,1)S(1)}, bf16[2,2,64,256]{3,2,1,0:T(8,128)(2,1)S(1)}, u32[]{:S(2)}, u32[]{:S(2)}) collective-permute-start(bf16[2,2,64,256]{3,2,1,0:T(8,128)(2,1)S(1)} %get-tuple-element.25), channel_id=1, source_target_pairs={{0,2},{1,3},{2,0},{3,1},{4,6},{5,7},{6,4},{7,5},{8,10},{9,11},{10,... | collective-permute-start | bytes 393224 | tf_op jit(solution)/shard_map/ppermute | solution.py:218
  5.8 0.7 %copy-start = (s32[8,8]{1,0:T(8,128)S(1)}, s32[8,8]{1,0:T(8,128)}, u32[]{:S(2)}) copy-start(s32[8,8]{1,0:T(8,128)} %nbr_ref.1) | copy-start | bytes 772
  7.4 5.3 %collective-permute-start.5 = (bf16[2,2,64,256]{3,2,1,0:T(8,128)(2,1)S(1)}, bf16[2,2,64,256]{3,2,1,0:T(8,128)(2,1)S(1)}, u32[]{:S(2)}, u32[]{:S(2)}) collective-permute-start(bf16[2,2,64,256]{3,2,1,0:T(8,128)(2,1)S(1)} %get-tuple-element.28), channel_id=1, source_target_pairs={{0,2},{1,3},{2,0},{3,1},{4,6},{5,7},{6,4},{7,5},{8,10},{9,11},{10,... | collective-permute-start | bytes 393224 | tf_op jit(solution)/shard_map/ppermute | solution.py:218
  9.7 5.0 %collective-permute-start.6 = (bf16[2,128,256]{2,1,0:T(8,128)(2,1)S(1)}, bf16[2,128,256]{2,1,0:T(8,128)(2,1)S(1)}, u32[]{:S(2)}, u32[]{:S(2)}) collective-permute-start(bf16[2,128,256]{2,1,0:T(8,128)(2,1)S(1)} %get-tuple-element.29), channel_id=1, source_target_pairs={{0,4},{1,5},{2,6},{3,7},{4,0},{5,1},{6,2},{7,3},{8,12},{9,13},{10,... | collective-permute-start | bytes 393224 | tf_op jit(solution)/shard_map/ppermute | solution.py:281
  11.5 3.1 %collective-permute-start.7 = (bf16[2,128,256]{2,1,0:T(8,128)(2,1)S(1)}, bf16[2,128,256]{2,1,0:T(8,128)(2,1)S(1)}, u32[]{:S(2)}, u32[]{:S(2)}) collective-permute-start(bf16[2,128,256]{2,1,0:T(8,128)(2,1)S(1)} %get-tuple-element.30), channel_id=1, source_target_pairs={{0,1},{1,0},{2,3},{3,2},{4,8},{5,9},{6,10},{7,11},{8,4},{9,5},{10,... | collective-permute-start | bytes 393224 | tf_op jit(solution)/shard_map/ppermute | solution.py:281
  17.8 6.0 %collective-permute-start.10 = (bf16[2,128,256]{2,1,0:T(8,128)(2,1)S(1)}, bf16[2,128,256]{2,1,0:T(8,128)(2,1)S(1)}, u32[]{:S(2)}, u32[]{:S(2)}) collective-permute-start(bf16[2,128,256]{2,1,0:T(8,128)(2,1)S(1)} %get-tuple-element.36), channel_id=1, source_target_pairs={{0,4},{1,5},{2,6},{3,7},{4,0},{5,1},{6,2},{7,3},{8,12},{9,13},{10,... | collective-permute-start | bytes 393224 | tf_op jit(solution)/shard_map/ppermute | solution.py:293
  20.8 3.0 %collective-permute-start.11 = (bf16[2,128,256]{2,1,0:T(8,128)(2,1)S(1)}, bf16[2,128,256]{2,1,0:T(8,128)(2,1)S(1)}, u32[]{:S(2)}, u32[]{:S(2)}) collective-permute-start(bf16[2,128,256]{2,1,0:T(8,128)(2,1)S(1)} %get-tuple-element.37), channel_id=1, source_target_pairs={{0,1},{1,0},{2,3},{3,2},{4,8},{5,9},{6,10},{7,11},{8,4},{9,5},{10,... | collective-permute-start | bytes 393224 | tf_op jit(solution)/shard_map/ppermute | solution.py:293
  20.8 6.3 %collective-permute-start.8 = (bf16[2,2,64,256]{3,2,1,0:T(8,128)(2,1)S(1)}, bf16[2,2,64,256]{3,2,1,0:T(8,128)(2,1)S(1)}, u32[]{:S(2)}, u32[]{:S(2)}) collective-permute-start(bf16[2,2,64,256]{3,2,1,0:T(8,128)(2,1)S(1)} %get-tuple-element.32), channel_id=1, source_target_pairs={{0,2},{1,3},{2,0},{3,1},{4,6},{5,7},{6,4},{7,5},{8,10},{9,11},{10,... | collective-permute-start | bytes 393224 | tf_op jit(solution)/shard_map/ppermute | solution.py:218
  24.0 5.5 %collective-permute-start.12 = (bf16[2,2,64,256]{3,2,1,0:T(8,128)(2,1)S(1)}, bf16[2,2,64,256]{3,2,1,0:T(8,128)(2,1)S(1)}, u32[]{:S(2)}, u32[]{:S(2)}) collective-permute-start(bf16[2,2,64,256]{3,2,1,0:T(8,128)(2,1)S(1)} %get-tuple-element.39), channel_id=1, source_target_pairs={{0,2},{1,3},{2,0},{3,1},{4,6},{5,7},{6,4},{7,5},{8,10},{9,11},{10,... | collective-permute-start | bytes 393224 | tf_op jit(solution)/shard_map/ppermute | solution.py:218
  27.1 2.5 %collective-permute-start.9 = (bf16[2,2,64,256]{3,2,1,0:T(8,128)(2,1)S(1)}, bf16[2,2,64,256]{3,2,1,0:T(8,128)(2,1)S(1)}, u32[]{:S(2)}, u32[]{:S(2)}) collective-permute-start(bf16[2,2,64,256]{3,2,1,0:T(8,128)(2,1)S(1)} %regroup.2), channel_id=1, source_target_pairs={{0,1},{1,0},{2,3},{3,2},{4,5},{5,4},{6,7},{7,6},{8,9},{9,8},{10,11... | collective-permute-start | bytes 393224 | tf_op jit(solution)/shard_map/ppermute | solution.py:218
  29.6 1.4 %collective-permute-start.13 = (bf16[2,2,64,256]{3,2,1,0:T(8,128)(2,1)S(1)}, bf16[2,2,64,256]{3,2,1,0:T(8,128)(2,1)S(1)}, u32[]{:S(2)}, u32[]{:S(2)}) collective-permute-start(bf16[2,2,64,256]{3,2,1,0:T(8,128)(2,1)S(1)} %regroup.3), channel_id=1, source_target_pairs={{0,1},{1,0},{2,3},{3,2},{4,5},{5,4},{6,7},{7,6},{8,9},{9,8},{10,11... | collective-permute-start | bytes 393224 | tf_op jit(solution)/shard_map/ppermute | solution.py:218

commit v5 on v3

v5 whole, which is shorter than its diff:
```python
import functools
import math

import jax
import jax.numpy as jnp
from jax import lax
from jax.experimental import pallas as pl
from jax.experimental.pallas import tpu as pltpu
from jax.sharding import PartitionSpec as P

HEAD_DIM = 64
NEVER = -1e30
SCORE_SCALE = HEAD_DIM**-0.5 / math.log(2)
LOW = jnp.bfloat16
VMEM = pl.BlockSpec(memory_space=pltpu.VMEM)
SMEM = pl.BlockSpec(memory_space=pltpu.SMEM)
NT = (((1,), (1,)), ((), ()))


def dot(left, right, dims=(((1,), (0,)), ((), ()))):
    return lax.dot_general(left, right, dims, preferred_element_type=jnp.float32)


def call(kernel, name, outs, *args, limit=8, scratch=(), cost=None, specs=None):
    return pl.pallas_call(
        kernel,
        out_shape=outs,
        in_specs=specs or [VMEM] * len(args),
        out_specs=[VMEM] * len(outs),
        scratch_shapes=scratch,
        name=name,
        cost_estimate=cost,
        compiler_params=pltpu.CompilerParams(vmem_limit_bytes=limit * 1024 * 1024),
    )(*args)


def pair_routes(owners, heads):
    routes = []
    for step in (1, -1):
        route = []
        for n in range(owners):
            other = n + step * (1 - 2 * (n % 2))
            for h in range(heads):
                target = other * heads + h if 0 <= other < owners else n * heads + (h ^ 1)
                route.append((n * heads + h, target))
        routes.append(route)
    return routes


def prep_kernel(heads, owners, local_count, per_patch, rows, nbr_ref, after_ref, bias_ref, slot_ref):
    me, node = lax.axis_index("head"), lax.axis_index("node")
    odd = lax.rem(node, 2)
    pair = (node + 1 - 2 * odd, node - 1 + 2 * odd)
    queries = heads * rows
    own = [[jnp.int32(p == k) for k in range(local_count)] for p in range(local_count)]
    out_of = [[jnp.int32(0), jnp.int32(0)] for _ in range(local_count)]
    for p in range(local_count):
        for j in range(nbr_ref.shape[1]):
            entry = nbr_ref[node * local_count + p, j]
            for k in range(local_count):
                own[p][k] += jnp.where(entry == node * local_count + k, 1, 0)
            for s in range(2):
                start = pair[s] * local_count
                inside = jnp.logical_and(entry >= start, entry < start + local_count)
                out_of[p][s] += jnp.where(inside, 1, 0)

    def choose(index, values):
        value = values[0]
        for i in range(1, len(values)):
            value = jnp.where(index == i, values[i], value)
        return value

    patch_of = [(me ^ d) // per_patch for d in range(heads)]
    counts = [
        [choose(patch_of[e], [choose(patch_of[d], own[p]) for p in range(local_count)]) for e in range(heads)]
        for d in range(heads)
    ]
    for s in range(2):
        counts.append([choose(patch_of[e], [out_of[p][s] for p in range(local_count)]) for e in range(heads)])
    lane_block = lax.broadcasted_iota(jnp.int32, (1, queries), 1) // rows
    for b, row_counts in enumerate(counts):
        row = jnp.zeros((1, queries), jnp.float32)
        for e in range(heads):
            row = jnp.where(lane_block == e, row_counts[e].astype(jnp.float32), row)
        row = jnp.where(row > 0.5, jnp.log(jnp.maximum(row, 1.0)) * (1 / math.log(2)), NEVER)
        bias_ref[b : b + 1, :] = row
    for s in range(2):
        inside = jnp.logical_and(pair[s] >= 0, pair[s] < owners)
        first = jnp.where(inside, pair[s], 0) * local_count
        chosen = jnp.int32(0)
        for p in range(local_count):
            for j in range(nbr_ref.shape[1]):
                entry = nbr_ref[first + p, j] - node * local_count
                mine = jnp.logical_and(entry >= 0, entry < local_count)
                chosen = jnp.where(jnp.logical_and(inside, mine), entry, chosen)
        for t in range(per_patch):
            slot = me ^ (chosen * per_patch + t)
            slot_ref[s * per_patch + t : s * per_patch + t + 1, :] = jnp.full((1, slot_ref.shape[1]), slot)


def pack_kernel(heads, joint, *refs):
    one, two = (refs[0].at[0], refs[0].at[1]) if joint else refs[:2]
    me = lax.axis_index("head")
    width = refs[-1].shape[-1]
    for d, out in enumerate(refs[-heads:]):
        cols = pl.ds(pl.multiple_of((me ^ d) * width, width), width)
        out[0, 0], out[0, 1] = one[:, cols], two[:, cols]


def pick_kernel(heads, places, slot_ref, *refs):
    arrays, outs = refs[:-2], refs[-2:]
    rows = arrays[0].shape[2]
    per_patch = outs[0].shape[1] // rows
    blocks = [arrays[a][j].astype(jnp.float32) for a, j in places]
    for s, out in enumerate(outs):
        for t in range(per_patch):
            slot = slot_ref[s * per_patch + t : s * per_patch + t + 1, :]
            value = blocks[0]
            for d in range(1, heads):
                value = jnp.where((slot == d)[None], blocks[d], value)
            out[:, t * rows : (t + 1) * rows, :] = value.astype(LOW)


def masked(rows, groups):
    head_of = lax.broadcasted_iota(jnp.int32, (1, rows.shape[1]), 1) // HEAD_DIM
    return [jnp.where(head_of == head, rows, jnp.zeros_like(rows)) for head in range(groups)]


def spread(bias_ref, first, sizes):
    queries = bias_ref.shape[1]
    rows = [jnp.broadcast_to(bias_ref[first + i : first + i + 1, :], (n, queries)) for i, n in enumerate(sizes)]
    return jnp.concatenate(rows, 0)


def joined(arrays, places, which):
    return jnp.concatenate([arrays[a][j, which] for a, j in places], 0)


def near_kernel(heads, places, count, bias_ref, *refs):
    kv, qg, (exps_ref, gw_ref, stat_ref) = refs[:count], refs[count : 2 * count], refs[2 * count :]
    rows, width = kv[0].shape[2:]
    queries = heads * rows
    groups = width // HEAD_DIM
    bias = spread(bias_ref, 0, [rows] * heads)
    keys, values = joined(kv, places, 0), joined(kv, places, 1)
    query_h, grad_h = masked(joined(qg, places, 0), groups), masked(joined(qg, places, 1), groups)
    for head in range(groups):
        lanes = slice(head * queries, (head + 1) * queries)
        scores = dot(keys, query_h[head], NT) * SCORE_SCALE + bias
        top = jnp.max(scores, 0, keepdims=True)
        exps = jnp.exp2(scores - top)
        grad_weights = dot(values, grad_h[head], NT)
        exps_ref[:, lanes] = exps
        gw_ref[:, lanes] = grad_weights
        stat_ref[0:1, lanes] = top
        stat_ref[1:2, lanes] = jnp.sum(exps, 0, keepdims=True)
        stat_ref[2:3, lanes] = jnp.sum(exps * grad_weights, 0, keepdims=True)


def far_kernel(heads, places, count, bias_ref, stat_ref, *refs):
    qg, far, (w_ref, ds_ref, final_ref, far_a, far_b) = refs[:count], refs[count : count + 2], refs[count + 2 :]
    patch, width = far[0].shape[1:]
    queries = bias_ref.shape[1]
    groups = width // HEAD_DIM
    bias = spread(bias_ref, heads, [patch, patch])
    keys, values = jnp.concatenate([r[0] for r in far], 0), jnp.concatenate([r[1] for r in far], 0)
    query_h, grad_h = masked(joined(qg, places, 0), groups), masked(joined(qg, places, 1), groups)
    for head in range(groups):
        lanes = slice(head * queries, (head + 1) * queries)
        near_top = stat_ref[0:1, lanes]
        scores = dot(keys, query_h[head], NT) * SCORE_SCALE + bias
        top = jnp.maximum(near_top, jnp.max(scores, 0, keepdims=True))
        exps = jnp.exp2(scores - top)
        shrink = jnp.exp2(near_top - top)
        grad_weights = dot(values, grad_h[head], NT)
        part = 1.0 / (shrink * stat_ref[1:2, lanes] + jnp.sum(exps, 0, keepdims=True))
        weights = exps * part
        shrink = shrink * part
        row_dots = shrink * stat_ref[2:3, lanes] + jnp.sum(weights * grad_weights, 0, keepdims=True)
        w_ref[:, lanes] = weights.astype(LOW)
        ds_ref[:, lanes] = (weights * (grad_weights - row_dots)).astype(LOW)
        final_ref[0:1, lanes] = shrink
        final_ref[1:2, lanes] = row_dots
    key_grad = dot(ds_ref[...], jnp.concatenate(query_h, 0)) * HEAD_DIM**-0.5
    value_grad = dot(w_ref[...], jnp.concatenate(grad_h, 0))
    for s, out in enumerate((far_a, far_b)):
        span = slice(s * patch, (s + 1) * patch)
        out[0], out[1] = key_grad[span].astype(LOW), value_grad[span].astype(LOW)


def rest_kernel(heads, places, count, final_ref, exps_ref, gw_ref, far_w_ref, far_ds_ref, *refs):
    kv, qg, far = refs[:count], refs[count : 2 * count], refs[2 * count : 2 * count + 2]
    mq_out, (near_out, w_ref, ds_ref) = refs[2 * count + 2 : -3], refs[-3:]
    rows, width = kv[0].shape[2:]
    queries = heads * rows
    groups = width // HEAD_DIM
    scale = HEAD_DIM**-0.5
    keys_t, values_t = joined(kv, places, 0).T, joined(kv, places, 1).T
    far_keys_t = jnp.concatenate([r[0] for r in far], 0).T
    far_values_t = jnp.concatenate([r[1] for r in far], 0).T
    query_h, grad_h = masked(joined(qg, places, 0), groups), masked(joined(qg, places, 1), groups)
    mixed_t, qgrad_t = [], []
    for head in range(groups):
        feats = slice(head * HEAD_DIM, (head + 1) * HEAD_DIM)
        lanes = slice(head * queries, (head + 1) * queries)
        weights = exps_ref[:, lanes] * final_ref[0:1, lanes]
        low = weights.astype(LOW)
        grad_scores = (weights * (gw_ref[:, lanes] - final_ref[1:2, lanes])).astype(LOW)
        w_ref[:, lanes] = low
        ds_ref[:, lanes] = grad_scores
        mixed_t.append(dot(values_t[feats], low) + dot(far_values_t[feats], far_w_ref[:, lanes]))
        qgrad_t.append((dot(keys_t[feats], grad_scores) + dot(far_keys_t[feats], far_ds_ref[:, lanes])) * scale)
    mixed = jnp.concatenate(mixed_t, 0).T.astype(LOW)
    qgrad = jnp.concatenate(qgrad_t, 0).T.astype(LOW)
    key_grad = dot(ds_ref[...], jnp.concatenate(query_h, 0)) * scale
    value_grad = dot(w_ref[...], jnp.concatenate(grad_h, 0))
    for d in range(heads):
        span = slice(d * rows, (d + 1) * rows)
        mq_out[d][0, 0], mq_out[d][0, 1] = mixed[span], qgrad[span]
        near_out[d, 0], near_out[d, 1] = key_grad[span], value_grad[span]


def merge_kernel(heads, slot_ref, near, back_a, back_b, *outs):
    rows = near.shape[2]
    per_patch = back_a.shape[1] // rows
    for d in range(heads):
        total = near[d]
        for s, back in enumerate((back_a, back_b)):
            for t in range(per_patch):
                slot = slot_ref[s * per_patch + t : s * per_patch + t + 1, :]
                term = back[:, t * rows : (t + 1) * rows, :].astype(jnp.float32)
                total = total + jnp.where((slot == d)[None], term, 0.0)
        outs[d][0] = total.astype(LOW)


def unpack_kernel(heads, places, *refs):
    arrays, outs = refs[:-2], refs[-2:]
    width = arrays[0].shape[-1]
    me = lax.axis_index("head")
    for d, (a, j) in enumerate(places):
        cols = pl.ds(pl.multiple_of((me ^ d) * width, width), width)
        outs[0][:, cols], outs[1][:, cols] = arrays[a][j, 0], arrays[a][j, 1]


def exchange(blocks):
    heads = len(blocks)
    got = list(blocks)
    for d in sorted(range(1, heads), key=lambda d: (-(d >> 1), d)):
        got[d] = lax.ppermute(blocks[d], "head", [(i, i ^ d) for i in range(heads)])
    return got


def gather_in(heads, one, two, joint, block, *after):
    own = [one, two]
    if joint:
        own = [lax.optimization_barrier(jnp.concatenate(own, 0)).reshape((2,) + one.shape)]
    return exchange(call(functools.partial(pack_kernel, heads, joint), "pack", [block] * heads, *own, *after))


def shards(queries, key_rows, value_rows, out_grads, neighbours):
    rows, features = queries.shape
    heads, owners = lax.axis_size("head"), lax.axis_size("node")
    width = features // heads
    local_count = neighbours.shape[0] // owners
    per_patch = heads // local_count
    patch = rows * per_patch
    block = jax.ShapeDtypeStruct((1, 2, rows, width), LOW)
    places = [(d, 0) for d in range(heads)]
    near_shape = jax.ShapeDtypeStruct((heads, 2, rows, width), jnp.float32)
    slab = jax.ShapeDtypeStruct((2, patch, width), LOW)
    whole = jax.ShapeDtypeStruct((rows, features), LOW)
    routes = pair_routes(owners, heads)

    kv = gather_in(heads, key_rows, value_rows, True, block)
    bias, slots = call(
        functools.partial(prep_kernel, heads, owners, local_count, per_patch, rows),
        "prep",
        [
            jax.ShapeDtypeStruct((heads + 2, heads * rows), jnp.float32),
            jax.ShapeDtypeStruct((2 * per_patch, width), jnp.int32),
        ],
        neighbours,
        kv[0],
        specs=[SMEM, VMEM],
    )
    qg = gather_in(heads, queries, out_grads, False, block, slots)
    picked = call(functools.partial(pick_kernel, heads, places), "pick", [slab] * 2, slots, *kv)
    far = [lax.ppermute(p, ("node", "head"), r) for p, r in zip(picked, routes)]
    lanes = width // HEAD_DIM * heads * rows
    own, other = heads * rows, 2 * patch
    work = pl.CostEstimate(flops=1500000000, bytes_accessed=1, transcendentals=0)

    def table(height, kind=jnp.float32):
        return jax.ShapeDtypeStruct((height, lanes), kind)

    exps, grad_weights, stats = call(
        functools.partial(near_kernel, heads, places, len(kv)),
        "near",
        [table(own), table(own), table(3)],
        bias,
        *kv,
        *qg,
        cost=work,
    )
    far_w, far_ds, final, *far_grads = call(
        functools.partial(far_kernel, heads, places, len(kv)),
        "far",
        [table(other, LOW), table(other, LOW), table(2), slab, slab],
        bias,
        stats,
        *qg,
        *far,
        cost=work,
    )
    *mq, near = call(
        functools.partial(rest_kernel, heads, places, len(kv)),
        "rest",
        [block] * heads + [near_shape],
        final,
        exps,
        grad_weights,
        far_w,
        far_ds,
        *kv,
        *qg,
        *far,
        scratch=[pltpu.VMEM((own, lanes), LOW)] * 2,
        cost=work,
    )
    back = [lax.ppermute(p, ("node", "head"), r) for p, r in zip(far_grads, routes)]
    mq = exchange(mq)
    kv_grads = exchange(call(functools.partial(merge_kernel, heads), "merge", [block] * heads, slots, near, *back))
    unpack = functools.partial(unpack_kernel, heads, places)
    mixed, query_grad = call(unpack, "unpack", [whole] * 2, *mq)
    key_grad, value_grad = call(unpack, "unpack", [whole] * 2, *kv_grads)
    return mixed, query_grad, key_grad, value_grad


def solution(mesh):
    rows = P(("grp", "node", "head"), None)
    return jax.shard_map(
        shards,
        mesh=mesh,
        in_specs=(rows, rows, rows, rows, P("grp", None)),
        out_specs=(rows, rows, rows, rows),
        check_vma=False,
    )
```

time: 33.8 us -> 29.2 us (0.86)
  waiting for transfers between devices: 11.8 us -> 8.42 us
  local copies, waits for them, and re-layouts: 0.68 us -> 0.02 us
  Pallas kernels: 5.85 us -> 5.35 us
    ppermute x2, waiting for transfers between devices: 2.44 us -> 0.14 us  [shards(): lax.ppermute(p, ('node', 'head'), r)]
    ppermute x10 -> x12, waiting for transfers between devices: 7.32 us -> 6.3 us  [exchange(): got[d] = lax.ppermute(blocks[d], 'head', [(i, i ^ d) for i in range(heads)])]
    ppermute x10 -> x12, starting transfers between devices: 8.65 us -> 9.43 us  [exchange(): got[d] = lax.ppermute(blocks[d], 'head', [(i, i ^ d) for i in range(heads)])]
    unnamed x6, local copies, waits for them, and re-layouts: 0.68 us -> 0.02 us
    ppermute x2, starting transfers between devices: 3.02 us -> 2.49 us  [shards(): lax.ppermute(p, ('node', 'head'), r)]
    pallas_call x10, Pallas kernels: 5.85 us -> 5.35 us  [call(): pl.pallas_call(kernel, out_shape=outs, in_specs=specs or [VMEM] * len(arg...]
    concatenate x2 -> x1, other arithmetic: 1 us -> 0.99 us  [gather_in(): jnp.concatenate(own, 0)]
  transfers between devices with their start and end apart: 14 -> 16, of which waited for: 6 -> 8; matrix products, arithmetic and copies ran while one was open for 3% -> 0% of each run, Pallas kernels for 6% -> 12%
where the time goes in v5:
time: 29.2 us; the launch traced here: 29.1 us
  starting transfers between devices  13.6 us (47%)
  waiting for transfers between devices  8.42 us (29%)
  Pallas kernels  5.35 us (18%)
  other arithmetic  0.99 us (3%)
  between operations  0.74 us (3%)
    ppermute x12, starting transfers between devices, exchange(): got[d] = lax.ppermute(blocks[d], 'head', [(i, i ^ d) for i in range(heads)])  9.43 us
    ppermute x12, waiting for transfers between devices, exchange(): got[d] = lax.ppermute(blocks[d], 'head', [(i, i ^ d) for i in range(heads)])  6.3 us
    pallas_call x10, Pallas kernels, call(): pl.pallas_call(kernel, out_shape=outs, in_specs=specs or [VMEM] * len(arg...  5.35 us
    ppermute x2, starting transfers between devices, shards(): lax.ppermute(p, ('node', 'head'), r)  2.49 us
    ppermute x2, waiting for transfers between devices, shards(): far = [lax.ppermute(p, ('node', 'head'), r) for p, r in zip(picked, routes)]  1.99 us
    ppermute x2, starting transfers between devices, shards(): far = [lax.ppermute(p, ('node', 'head'), r) for p, r in zip(picked, routes)]  1.64 us
    concatenate x1, other arithmetic, gather_in(): jnp.concatenate(own, 0)  0.99 us
  transfers between devices with their start and end apart: 16, of which 8 were waited for; matrix products, arithmetic and copies ran while one was open for 0% of the time, Pallas kernels for 12%

profile of v5, /device:TPU:0, one launch (start us, length us, event | category | flops | bytes accessed | tf_op | source)
XLA Modules:
  0.0 29.1 jit_solution(17136988102898183807)
XLA Ops:
  0.6 1.0 %pad_maximum_fusion = bf16[128,1024]{1,0:T(8,128)(2,1)S(1)} fusion(bf16[64,1024]{1,0:T(8,128)(2,1)} %param.7, bf16[64,1024]{1,0:T(8,128)(2,1)} %param.6), kind=kLoop, calls=%fused_computation | loop fusion | flops 524288 | bytes 524288 | tf_op jit(solution)/shard_map/concatenate | solution.py:256
  1.6 0.0 copy-start
  1.6 0.0 copy-start.1
  1.7 0.0 copy-start.2
  1.7 0.5 %collective-permute-start = (bf16[1,2,64,256]{3,2,1,0:T(8,128)(2,1)S(1)}, bf16[1,2,64,256]{3,2,1,0:T(8,128)(2,1)S(1)}, u32[]{:S(2)}, u32[]{:S(2)}) collective-permute-start(bf16[1,2,64,256]{3,2,1,0:T(8,128)(2,1)S(1)} %get-tuple-element.39), channel_id=1, source_target_pairs={{0,1},{1,0},{2,3},{3,2},{4,5},{5,4},{6,7},{7,6},{8,9},{9,8},{10,11... | collective-permute-start | bytes 196616 | tf_op jit(solution)/shard_map/ppermute | solution.py:249
  2.2 2.6 %collective-permute-start.1 = (bf16[1,2,64,256]{3,2,1,0:T(8,128)(2,1)S(1)}, bf16[1,2,64,256]{3,2,1,0:T(8,128)(2,1)S(1)}, u32[]{:S(2)}, u32[]{:S(2)}) collective-permute-start(bf16[1,2,64,256]{3,2,1,0:T(8,128)(2,1)S(1)} %get-tuple-element.40), channel_id=1, source_target_pairs={{0,2},{1,3},{2,0},{3,1},{4,6},{5,7},{6,4},{7,5},{8,10},{9,11},{10,... | collective-permute-start | bytes 196616 | tf_op jit(solution)/shard_map/ppermute | solution.py:249
  4.8 0.1 collective-permute-start.2
  4.9 0.0 copy-done.2
  4.9 0.8 %prep.1 = (f32[6,256]{1,0:T(8,128)S(1)}, s32[4,256]{1,0:T(4,128)S(1)}) custom-call(s32[8,8]{1,0:T(8,128)S(1)} %copy-done.2, bf16[1,2,64,256]{3,2,1,0:T(8,128)(2,1)S(1)} %get-tuple-element.37.after_ref.refs_0_), custom_call_target="tpu_custom_call" | custom-call | tf_op jit(solution)/shard_map/prep/pallas_call | solution.py:25
  5.7 0.0 copy-done
  5.7 0.0 copy-done.1
  5.8 0.2 collective-permute-start.3
  6.0 1.9 %collective-permute-start.4 = (bf16[1,2,64,256]{3,2,1,0:T(8,128)(2,1)S(1)}, bf16[1,2,64,256]{3,2,1,0:T(8,128)(2,1)S(1)}, u32[]{:S(2)}, u32[]{:S(2)}) collective-permute-start(bf16[1,2,64,256]{3,2,1,0:T(8,128)(2,1)S(1)} %get-tuple-element.45), channel_id=1, source_target_pairs={{0,2},{1,3},{2,0},{3,1},{4,6},{5,7},{6,4},{7,5},{8,10},{9,11},{10,... | collective-permute-start | bytes 196616 | tf_op jit(solution)/shard_map/ppermute | solution.py:249
  7.9 0.0 collective-permute-done.refs_1_
  7.9 0.0 collective-permute-start.5
  7.9 0.0 collective-permute-done.1.refs_2_
  7.9 0.9 %collective-permute-done.2.refs_3_ = bf16[1,2,64,256]{3,2,1,0:T(8,128)(2,1)S(1)} collective-permute-done((bf16[1,2,64,256]{3,2,1,0:T(8,128)(2,1)S(1)}, bf16[1,2,64,256]{3,2,1,0:T(8,128)(2,1)S(1)}, u32[]{:S(2)}, u32[]{:S(2)}) %collective-permute-start.2) | collective-permute-done | bytes 65568 | tf_op jit(solution)/shard_map/ppermute | solution.py:249
  8.8 0.1 pick.1
  8.9 1.6 %collective-permute-start.6 = (bf16[2,128,256]{2,1,0:T(8,128)(2,1)S(1)}, bf16[2,128,256]{2,1,0:T(8,128)(2,1)S(1)}, u32[]{:S(2)}, u32[]{:S(2)}) collective-permute-start(bf16[2,128,256]{2,1,0:T(8,128)(2,1)S(1)} %get-tuple-element.48), channel_id=1, source_target_pairs={{0,4},{1,5},{2,6},{3,7},{4,0},{5,1},{6,2},{7,3},{8,12},{9,13},{10,... | collective-permute-start | bytes 393224 | tf_op jit(solution)/shard_map/ppermute | solution.py:288
  10.6 0.0 collective-permute-start.7
  10.6 0.0 collective-permute-done.3.refs_5_.refs_1_
  10.6 0.0 collective-permute-done.4.refs_6_.refs_2_
  10.6 1.7 %collective-permute-done.5.refs_7_.refs_3_ = bf16[1,2,64,256]{3,2,1,0:T(8,128)(2,1)S(1)} collective-permute-done((bf16[1,2,64,256]{3,2,1,0:T(8,128)(2,1)S(1)}, bf16[1,2,64,256]{3,2,1,0:T(8,128)(2,1)S(1)}, u32[]{:S(2)}, u32[]{:S(2)}) %collective-permute-start.5) | collective-permute-done | bytes 65568 | tf_op jit(solution)/shard_map/ppermute | solution.py:249
  12.3 0.6 %near.1 = (f32[256,1024]{1,0:T(8,128)S(1)}, f32[256,1024]{1,0:T(8,128)S(1)}, f32[3,1024]{1,0:T(4,128)S(1)}) custom-call(f32[6,256]{1,0:T(8,128)S(1)} %get-tuple-element.38.bias_ref, bf16[1,2,64,256]{3,2,1,0:T(8,128)(2,1)S(1)} %get-tuple-element.37.after_ref.refs_0_, bf16[1,2,64,256]{3,2,1,0:T(8,128)(2,1)S(1)} %collective-permute-done.refs_1_, ...), custom_call_target="tpu_custom_call" | custom-call | flops 1500000000 | bytes 1 | tf_op jit(solution)/shard_map/near/pallas_call | solution.py:25
  12.9 2.0 %collective-permute-done.6.refs_4_.refs_8_ = bf16[2,128,256]{2,1,0:T(8,128)(2,1)S(1)} collective-permute-done((bf16[2,128,256]{2,1,0:T(8,128)(2,1)S(1)}, bf16[2,128,256]{2,1,0:T(8,128)(2,1)S(1)}, u32[]{:S(2)}, u32[]{:S(2)}) %collective-permute-start.6) | collective-permute-done | bytes 131104 | tf_op jit(solution)/shard_map/ppermute | solution.py:288
  14.9 0.0 collective-permute-done.7.refs_5_.refs_9_
  14.9 1.2 %far.1 = (bf16[256,1024]{1,0:T(8,128)(2,1)S(1)}, bf16[256,1024]{1,0:T(8,128)(2,1)S(1)}, f32[2,1024]{1,0:T(2,128)S(1)}, bf16[2,128,256]{2,1,0:T(8,128)(2,1)S(1)}, bf16[2,128,256]{2,1,0:T(8,128)(2,1)S(1)}) custom-call(f32[6,256]{1,0:T(8,128)S(1)} %get-tuple-element.38.bias_ref, f32[3,1024]{1,0:T(4,128)S(1)} %get-tuple-element.47.stat_ref, ...), custom_call_target="tpu_custom_call" | custom-call | flops 1500000000 | bytes 1 | tf_op jit(solution)/shard_map/far/pallas_call | solution.py:25
  16.1 2.5 %collective-permute-start.11 = (bf16[2,128,256]{2,1,0:T(8,128)(2,1)S(1)}, bf16[2,128,256]{2,1,0:T(8,128)(2,1)S(1)}, u32[]{:S(2)}, u32[]{:S(2)}) collective-permute-start(bf16[2,128,256]{2,1,0:T(8,128)(2,1)S(1)} %get-tuple-element.62), channel_id=1, source_target_pairs={{0,4},{1,5},{2,6},{3,7},{4,0},{5,1},{6,2},{7,3},{8,12},{9,13},{10,... | collective-permute-start | bytes 393224 | tf_op jit(solution)/shard_map/ppermute | solution.py:330
  18.6 0.0 collective-permute-start.12
  18.6 0.8 %rest.1 = (bf16[1,2,64,256]{3,2,1,0:T(8,128)(2,1)S(1)}, bf16[1,2,64,256]{3,2,1,0:T(8,128)(2,1)S(1)}, bf16[1,2,64,256]{3,2,1,0:T(8,128)(2,1)S(1)}, bf16[1,2,64,25...) custom-call(f32[2,1024]{1,0:T(2,128)S(1)} %get-tuple-element.50.final_ref, f32[256,1024]{1,0:T(8,128)S(1)} %get-tuple-element.51.exps_ref, ...), custom_call_target="tpu_custom_call" | custom-call | flops 1500000000 | bytes 1 | tf_op jit(solution)/shard_map/rest/pallas_call | solution.py:25
  19.4 0.6 %collective-permute-start.8 = (bf16[1,2,64,256]{3,2,1,0:T(8,128)(2,1)S(1)}, bf16[1,2,64,256]{3,2,1,0:T(8,128)(2,1)S(1)}, u32[]{:S(2)}, u32[]{:S(2)}) collective-permute-start(bf16[1,2,64,256]{3,2,1,0:T(8,128)(2,1)S(1)} %get-tuple-element.56), channel_id=1, source_target_pairs={{0,1},{1,0},{2,3},{3,2},{4,5},{5,4},{6,7},{7,6},{8,9},{9,8},{10,11... | collective-permute-start | bytes 196616 | tf_op jit(solution)/shard_map/ppermute | solution.py:249
  20.0 1.5 %collective-permute-start.9 = (bf16[1,2,64,256]{3,2,1,0:T(8,128)(2,1)S(1)}, bf16[1,2,64,256]{3,2,1,0:T(8,128)(2,1)S(1)}, u32[]{:S(2)}, u32[]{:S(2)}) collective-permute-start(bf16[1,2,64,256]{3,2,1,0:T(8,128)(2,1)S(1)} %get-tuple-element.57), channel_id=1, source_target_pairs={{0,2},{1,3},{2,0},{3,1},{4,6},{5,7},{6,4},{7,5},{8,10},{9,11},{10,... | collective-permute-start | bytes 196616 | tf_op jit(solution)/shard_map/ppermute | solution.py:249
  21.4 0.0 collective-permute-start.10
  21.4 0.1 collective-permute-done.11.back_a
  21.6 0.0 collective-permute-done.12.back_b
  21.6 0.2 merge.1
  21.8 0.6 %collective-permute-start.13 = (bf16[1,2,64,256]{3,2,1,0:T(8,128)(2,1)S(1)}, bf16[1,2,64,256]{3,2,1,0:T(8,128)(2,1)S(1)}, u32[]{:S(2)}, u32[]{:S(2)}) collective-permute-start(bf16[1,2,64,256]{3,2,1,0:T(8,128)(2,1)S(1)} %get-tuple-element.65), channel_id=1, source_target_pairs={{0,1},{1,0},{2,3},{3,2},{4,5},{5,4},{6,7},{7,6},{8,9},{9,8},{10,11... | collective-permute-start | bytes 196616 | tf_op jit(solution)/shard_map/ppermute | solution.py:249
  22.4 1.5 %collective-permute-start.14 = (bf16[1,2,64,256]{3,2,1,0:T(8,128)(2,1)S(1)}, bf16[1,2,64,256]{3,2,1,0:T(8,128)(2,1)S(1)}, u32[]{:S(2)}, u32[]{:S(2)}) collective-permute-start(bf16[1,2,64,256]{3,2,1,0:T(8,128)(2,1)S(1)} %get-tuple-element.66), channel_id=1, source_target_pairs={{0,2},{1,3},{2,0},{3,1},{4,6},{5,7},{6,4},{7,5},{8,10},{9,11},{10,... | collective-permute-start | bytes 196616 | tf_op jit(solution)/shard_map/ppermute | solution.py:249
  23.9 0.0 collective-permute-done.8.refs_1_
  23.9 0.0 collective-permute-start.15
  23.9 0.3 %collective-permute-done.9.refs_2_ = bf16[1,2,64,256]{3,2,1,0:T(8,128)(2,1)S(1)} collective-permute-done((bf16[1,2,64,256]{3,2,1,0:T(8,128)(2,1)S(1)}, bf16[1,2,64,256]{3,2,1,0:T(8,128)(2,1)S(1)}, u32[]{:S(2)}, u32[]{:S(2)}) %collective-permute-start.9) | collective-permute-done | bytes 65568 | tf_op jit(solution)/shard_map/ppermute | solution.py:249
  24.2 1.6 %collective-permute-done.10.refs_3_ = bf16[1,2,64,256]{3,2,1,0:T(8,128)(2,1)S(1)} collective-permute-done((bf16[1,2,64,256]{3,2,1,0:T(8,128)(2,1)S(1)}, bf16[1,2,64,256]{3,2,1,0:T(8,128)(2,1)S(1)}, u32[]{:S(2)}, u32[]{:S(2)}) %collective-permute-start.10) | collective-permute-done | bytes 65568 | tf_op jit(solution)/shard_map/ppermute | solution.py:249
  25.8 0.7 %unpack.2 = (bf16[64,1024]{1,0:T(8,128)(2,1)}, bf16[64,1024]{1,0:T(8,128)(2,1)}) custom-call(bf16[1,2,64,256]{3,2,1,0:T(8,128)(2,1)S(1)} %get-tuple-element.55.refs_0_, bf16[1,2,64,256]{3,2,1,0:T(8,128)(2,1)S(1)} %collective-permute-done.8.refs_1_, bf16[1,2,64,256]{3,2,1,0:T(8,128)(2,1)S(1)} %collective-permute-done.9.refs_2_, ...), custom_call_target="tpu_custom_call" | custom-call | tf_op jit(solution)/shard_map/unpack/pallas_call | solution.py:25
  26.5 0.0 collective-permute-done.13.refs_1_
  26.5 0.9 %collective-permute-done.14.refs_2_ = bf16[1,2,64,256]{3,2,1,0:T(8,128)(2,1)S(1)} collective-permute-done((bf16[1,2,64,256]{3,2,1,0:T(8,128)(2,1)S(1)}, bf16[1,2,64,256]{3,2,1,0:T(8,128)(2,1)S(1)}, u32[]{:S(2)}, u32[]{:S(2)}) %collective-permute-start.14) | collective-permute-done | bytes 65568 | tf_op jit(solution)/shard_map/ppermute | solution.py:249
  27.4 0.9 %collective-permute-done.15.refs_3_ = bf16[1,2,64,256]{3,2,1,0:T(8,128)(2,1)S(1)} collective-permute-done((bf16[1,2,64,256]{3,2,1,0:T(8,128)(2,1)S(1)}, bf16[1,2,64,256]{3,2,1,0:T(8,128)(2,1)S(1)}, u32[]{:S(2)}, u32[]{:S(2)}) %collective-permute-start.15) | collective-permute-done | bytes 65568 | tf_op jit(solution)/shard_map/ppermute | solution.py:249
  28.4 0.7 %unpack.3 = (bf16[64,1024]{1,0:T(8,128)(2,1)}, bf16[64,1024]{1,0:T(8,128)(2,1)}) custom-call(bf16[1,2,64,256]{3,2,1,0:T(8,128)(2,1)S(1)} %get-tuple-element.64.refs_0_, bf16[1,2,64,256]{3,2,1,0:T(8,128)(2,1)S(1)} %collective-permute-done.13.refs_1_, bf16[1,2,64,256]{3,2,1,0:T(8,128)(2,1)S(1)} %collective-permute-done.14.refs_2_, ...), custom_call_target="tpu_custom_call" | custom-call | tf_op jit(solution)/shard_map/unpack/pallas_call | solution.py:25
  (2 shorter events, 0.1 us)
Async XLA Ops:
  1.6 4.1 %copy-start = (bf16[64,1024]{1,0:T(8,128)(2,1)S(1)}, bf16[64,1024]{1,0:T(8,128)(2,1)}, u32[]{:S(2)}) copy-start(bf16[64,1024]{1,0:T(8,128)(2,1)} %refs_0_.1) | copy-start | bytes 393220
  1.6 4.1 %copy-start.1 = (bf16[64,1024]{1,0:T(8,128)(2,1)S(1)}, bf16[64,1024]{1,0:T(8,128)(2,1)}, u32[]{:S(2)}) copy-start(bf16[64,1024]{1,0:T(8,128)(2,1)} %refs_1_.1) | copy-start | bytes 393220
  1.7 3.2 %copy-start.2 = (s32[8,8]{1,0:T(8,128)S(1)}, s32[8,8]{1,0:T(8,128)}, u32[]{:S(2)}) copy-start(s32[8,8]{1,0:T(8,128)} %nbr_ref.1) | copy-start | bytes 772
  1.7 6.2 %collective-permute-start = (bf16[1,2,64,256]{3,2,1,0:T(8,128)(2,1)S(1)}, bf16[1,2,64,256]{3,2,1,0:T(8,128)(2,1)S(1)}, u32[]{:S(2)}, u32[]{:S(2)}) collective-permute-start(bf16[1,2,64,256]{3,2,1,0:T(8,128)(2,1)S(1)} %get-tuple-element.39), channel_id=1, source_target_pairs={{0,1},{1,0},{2,3},{3,2},{4,5},{5,4},{6,7},{7,6},{8,9},{9,8},{10,11... | collective-permute-start | bytes 196616 | tf_op jit(solution)/shard_map/ppermute | solution.py:249
  2.2 5.7 %collective-permute-start.1 = (bf16[1,2,64,256]{3,2,1,0:T(8,128)(2,1)S(1)}, bf16[1,2,64,256]{3,2,1,0:T(8,128)(2,1)S(1)}, u32[]{:S(2)}, u32[]{:S(2)}) collective-permute-start(bf16[1,2,64,256]{3,2,1,0:T(8,128)(2,1)S(1)} %get-tuple-element.40), channel_id=1, source_target_pairs={{0,2},{1,3},{2,0},{3,1},{4,6},{5,7},{6,4},{7,5},{8,10},{9,11},{10,... | collective-permute-start | bytes 196616 | tf_op jit(solution)/shard_map/ppermute | solution.py:249
  4.8 4.0 %collective-permute-start.2 = (bf16[1,2,64,256]{3,2,1,0:T(8,128)(2,1)S(1)}, bf16[1,2,64,256]{3,2,1,0:T(8,128)(2,1)S(1)}, u32[]{:S(2)}, u32[]{:S(2)}) collective-permute-start(bf16[1,2,64,256]{3,2,1,0:T(8,128)(2,1)S(1)} %get-tuple-element.41), channel_id=1, source_target_pairs={{0,3},{1,2},{2,1},{3,0},{4,7},{5,6},{6,5},{7,4},{8,11},{9,10},{10,... | collective-permute-start | bytes 196616 | tf_op jit(solution)/shard_map/ppermute | solution.py:249
  5.8 4.8 %collective-permute-start.3 = (bf16[1,2,64,256]{3,2,1,0:T(8,128)(2,1)S(1)}, bf16[1,2,64,256]{3,2,1,0:T(8,128)(2,1)S(1)}, u32[]{:S(2)}, u32[]{:S(2)}) collective-permute-start(bf16[1,2,64,256]{3,2,1,0:T(8,128)(2,1)S(1)} %get-tuple-element.44), channel_id=1, source_target_pairs={{0,1},{1,0},{2,3},{3,2},{4,5},{5,4},{6,7},{7,6},{8,9},{9,8},{10,11... | collective-permute-start | bytes 196616 | tf_op jit(solution)/shard_map/ppermute | solution.py:249
  6.0 4.6 %collective-permute-start.4 = (bf16[1,2,64,256]{3,2,1,0:T(8,128)(2,1)S(1)}, bf16[1,2,64,256]{3,2,1,0:T(8,128)(2,1)S(1)}, u32[]{:S(2)}, u32[]{:S(2)}) collective-permute-start(bf16[1,2,64,256]{3,2,1,0:T(8,128)(2,1)S(1)} %get-tuple-element.45), channel_id=1, source_target_pairs={{0,2},{1,3},{2,0},{3,1},{4,6},{5,7},{6,4},{7,5},{8,10},{9,11},{10,... | collective-permute-start | bytes 196616 | tf_op jit(solution)/shard_map/ppermute | solution.py:249
  7.9 4.3 %collective-permute-start.5 = (bf16[1,2,64,256]{3,2,1,0:T(8,128)(2,1)S(1)}, bf16[1,2,64,256]{3,2,1,0:T(8,128)(2,1)S(1)}, u32[]{:S(2)}, u32[]{:S(2)}) collective-permute-start(bf16[1,2,64,256]{3,2,1,0:T(8,128)(2,1)S(1)} %get-tuple-element.46), channel_id=1, source_target_pairs={{0,3},{1,2},{2,1},{3,0},{4,7},{5,6},{6,5},{7,4},{8,11},{9,10},{10,... | collective-permute-start | bytes 196616 | tf_op jit(solution)/shard_map/ppermute | solution.py:249
  8.9 5.9 %collective-permute-start.6 = (bf16[2,128,256]{2,1,0:T(8,128)(2,1)S(1)}, bf16[2,128,256]{2,1,0:T(8,128)(2,1)S(1)}, u32[]{:S(2)}, u32[]{:S(2)}) collective-permute-start(bf16[2,128,256]{2,1,0:T(8,128)(2,1)S(1)} %get-tuple-element.48), channel_id=1, source_target_pairs={{0,4},{1,5},{2,6},{3,7},{4,0},{5,1},{6,2},{7,3},{8,12},{9,13},{10,... | collective-permute-start | bytes 393224 | tf_op jit(solution)/shard_map/ppermute | solution.py:288
  10.6 4.3 %collective-permute-start.7 = (bf16[2,128,256]{2,1,0:T(8,128)(2,1)S(1)}, bf16[2,128,256]{2,1,0:T(8,128)(2,1)S(1)}, u32[]{:S(2)}, u32[]{:S(2)}) collective-permute-start(bf16[2,128,256]{2,1,0:T(8,128)(2,1)S(1)} %get-tuple-element.49), channel_id=1, source_target_pairs={{0,1},{1,0},{2,3},{3,2},{4,8},{5,9},{6,10},{7,11},{8,4},{9,5},{10,... | collective-permute-start | bytes 393224 | tf_op jit(solution)/shard_map/ppermute | solution.py:288
  16.1 5.5 %collective-permute-start.11 = (bf16[2,128,256]{2,1,0:T(8,128)(2,1)S(1)}, bf16[2,128,256]{2,1,0:T(8,128)(2,1)S(1)}, u32[]{:S(2)}, u32[]{:S(2)}) collective-permute-start(bf16[2,128,256]{2,1,0:T(8,128)(2,1)S(1)} %get-tuple-element.62), channel_id=1, source_target_pairs={{0,4},{1,5},{2,6},{3,7},{4,0},{5,1},{6,2},{7,3},{8,12},{9,13},{10,... | collective-permute-start | bytes 393224 | tf_op jit(solution)/shard_map/ppermute | solution.py:330
  18.6 3.0 %collective-permute-start.12 = (bf16[2,128,256]{2,1,0:T(8,128)(2,1)S(1)}, bf16[2,128,256]{2,1,0:T(8,128)(2,1)S(1)}, u32[]{:S(2)}, u32[]{:S(2)}) collective-permute-start(bf16[2,128,256]{2,1,0:T(8,128)(2,1)S(1)} %get-tuple-element.63), channel_id=1, source_target_pairs={{0,1},{1,0},{2,3},{3,2},{4,8},{5,9},{6,10},{7,11},{8,4},{9,5},{10,... | collective-permute-start | bytes 393224 | tf_op jit(solution)/shard_map/ppermute | solution.py:330
  19.4 4.5 %collective-permute-start.8 = (bf16[1,2,64,256]{3,2,1,0:T(8,128)(2,1)S(1)}, bf16[1,2,64,256]{3,2,1,0:T(8,128)(2,1)S(1)}, u32[]{:S(2)}, u32[]{:S(2)}) collective-permute-start(bf16[1,2,64,256]{3,2,1,0:T(8,128)(2,1)S(1)} %get-tuple-element.56), channel_id=1, source_target_pairs={{0,1},{1,0},{2,3},{3,2},{4,5},{5,4},{6,7},{7,6},{8,9},{9,8},{10,11... | collective-permute-start | bytes 196616 | tf_op jit(solution)/shard_map/ppermute | solution.py:249
  20.0 4.3 %collective-permute-start.9 = (bf16[1,2,64,256]{3,2,1,0:T(8,128)(2,1)S(1)}, bf16[1,2,64,256]{3,2,1,0:T(8,128)(2,1)S(1)}, u32[]{:S(2)}, u32[]{:S(2)}) collective-permute-start(bf16[1,2,64,256]{3,2,1,0:T(8,128)(2,1)S(1)} %get-tuple-element.57), channel_id=1, source_target_pairs={{0,2},{1,3},{2,0},{3,1},{4,6},{5,7},{6,4},{7,5},{8,10},{9,11},{10,... | collective-permute-start | bytes 196616 | tf_op jit(solution)/shard_map/ppermute | solution.py:249
  21.4 4.4 %collective-permute-start.10 = (bf16[1,2,64,256]{3,2,1,0:T(8,128)(2,1)S(1)}, bf16[1,2,64,256]{3,2,1,0:T(8,128)(2,1)S(1)}, u32[]{:S(2)}, u32[]{:S(2)}) collective-permute-start(bf16[1,2,64,256]{3,2,1,0:T(8,128)(2,1)S(1)} %get-tuple-element.58), channel_id=1, source_target_pairs={{0,3},{1,2},{2,1},{3,0},{4,7},{5,6},{6,5},{7,4},{8,11},{9,10},{10,... | collective-permute-start | bytes 196616 | tf_op jit(solution)/shard_map/ppermute | solution.py:249
  21.8 4.7 %collective-permute-start.13 = (bf16[1,2,64,256]{3,2,1,0:T(8,128)(2,1)S(1)}, bf16[1,2,64,256]{3,2,1,0:T(8,128)(2,1)S(1)}, u32[]{:S(2)}, u32[]{:S(2)}) collective-permute-start(bf16[1,2,64,256]{3,2,1,0:T(8,128)(2,1)S(1)} %get-tuple-element.65), channel_id=1, source_target_pairs={{0,1},{1,0},{2,3},{3,2},{4,5},{5,4},{6,7},{7,6},{8,9},{9,8},{10,11... | collective-permute-start | bytes 196616 | tf_op jit(solution)/shard_map/ppermute | solution.py:249
  22.4 5.0 %collective-permute-start.14 = (bf16[1,2,64,256]{3,2,1,0:T(8,128)(2,1)S(1)}, bf16[1,2,64,256]{3,2,1,0:T(8,128)(2,1)S(1)}, u32[]{:S(2)}, u32[]{:S(2)}) collective-permute-start(bf16[1,2,64,256]{3,2,1,0:T(8,128)(2,1)S(1)} %get-tuple-element.66), channel_id=1, source_target_pairs={{0,2},{1,3},{2,0},{3,1},{4,6},{5,7},{6,4},{7,5},{8,10},{9,11},{10,... | collective-permute-start | bytes 196616 | tf_op jit(solution)/shard_map/ppermute | solution.py:249
  23.9 4.5 %collective-permute-start.15 = (bf16[1,2,64,256]{3,2,1,0:T(8,128)(2,1)S(1)}, bf16[1,2,64,256]{3,2,1,0:T(8,128)(2,1)S(1)}, u32[]{:S(2)}, u32[]{:S(2)}) collective-permute-start(bf16[1,2,64,256]{3,2,1,0:T(8,128)(2,1)S(1)} %get-tuple-element.67), channel_id=1, source_target_pairs={{0,3},{1,2},{2,1},{3,0},{4,7},{5,6},{6,5},{7,4},{8,11},{9,10},{10,... | collective-permute-start | bytes 196616 | tf_op jit(solution)/shard_map/ppermute | solution.py:249

commit v6 on v5

--- a/solution.py
+++ b/solution.py
@@ -14,11 +14,10 @@
 LOW = jnp.bfloat16
 VMEM = pl.BlockSpec(memory_space=pltpu.VMEM)
 SMEM = pl.BlockSpec(memory_space=pltpu.SMEM)
-NT = (((1,), (1,)), ((), ()))
-
-
-def dot(left, right, dims=(((1,), (0,)), ((), ()))):
-    return lax.dot_general(left, right, dims, preferred_element_type=jnp.float32)
+
+
+def dot(left, right):
+    return jnp.dot(left, right, preferred_element_type=jnp.float32)
 
 
 def call(kernel, name, outs, *args, limit=8, scratch=(), cost=None, specs=None):
@@ -121,11 +120,6 @@
             out[:, t * rows : (t + 1) * rows, :] = value.astype(LOW)
 
 
-def masked(rows, groups):
-    head_of = lax.broadcasted_iota(jnp.int32, (1, rows.shape[1]), 1) // HEAD_DIM
-    return [jnp.where(head_of == head, rows, jnp.zeros_like(rows)) for head in range(groups)]
-
-
 def spread(bias_ref, first, sizes):
     queries = bias_ref.shape[1]
     rows = [jnp.broadcast_to(bias_ref[first + i : first + i + 1, :], (n, queries)) for i, n in enumerate(sizes)]
@@ -137,19 +131,29 @@
 
 
 def near_kernel(heads, places, count, bias_ref, *refs):
-    kv, qg, (exps_ref, gw_ref, stat_ref) = refs[:count], refs[count : 2 * count], refs[2 * count :]
+    kv, qg, outs = refs[:count], refs[count : 2 * count], refs[2 * count :]
+    exps_ref, gw_ref, stat_ref, *sides = outs
     rows, width = kv[0].shape[2:]
     queries = heads * rows
     groups = width // HEAD_DIM
     bias = spread(bias_ref, 0, [rows] * heads)
     keys, values = joined(kv, places, 0), joined(kv, places, 1)
-    query_h, grad_h = masked(joined(qg, places, 0), groups), masked(joined(qg, places, 1), groups)
+    lane_head = lax.broadcasted_iota(jnp.int32, (1, width), 1) // HEAD_DIM
+    for which, (down, across) in enumerate((sides[:2], sides[2:])):
+        whole = joined(qg, places, which)
+        turned = whole.T
+        across[...] = jnp.zeros_like(across)
+        for head in range(groups):
+            feats = slice(head * HEAD_DIM, (head + 1) * HEAD_DIM)
+            lanes = slice(head * queries, (head + 1) * queries)
+            down[lanes, :] = jnp.where(lane_head == head, whole, jnp.zeros_like(whole))
+            across[feats, lanes] = turned[feats]
     for head in range(groups):
         lanes = slice(head * queries, (head + 1) * queries)
-        scores = dot(keys, query_h[head], NT) * SCORE_SCALE + bias
+        scores = dot(keys, sides[1][:, lanes]) * SCORE_SCALE + bias
         top = jnp.max(scores, 0, keepdims=True)
         exps = jnp.exp2(scores - top)
-        grad_weights = dot(values, grad_h[head], NT)
+        grad_weights = dot(values, sides[3][:, lanes])
         exps_ref[:, lanes] = exps
         gw_ref[:, lanes] = grad_weights
         stat_ref[0:1, lanes] = top
@@ -157,50 +161,66 @@
         stat_ref[2:3, lanes] = jnp.sum(exps * grad_weights, 0, keepdims=True)
 
 
-def far_kernel(heads, places, count, bias_ref, stat_ref, *refs):
-    qg, far, (w_ref, ds_ref, final_ref, far_a, far_b) = refs[:count], refs[count : count + 2], refs[count + 2 :]
-    patch, width = far[0].shape[1:]
+def first_kernel(heads, bias_ref, query_across, grad_across, keys_ref, exps_ref, gw_ref, stat_ref):
     queries = bias_ref.shape[1]
-    groups = width // HEAD_DIM
-    bias = spread(bias_ref, heads, [patch, patch])
-    keys, values = jnp.concatenate([r[0] for r in far], 0), jnp.concatenate([r[1] for r in far], 0)
-    query_h, grad_h = masked(joined(qg, places, 0), groups), masked(joined(qg, places, 1), groups)
-    for head in range(groups):
+    patch, width = keys_ref.shape[1:]
+    bias = spread(bias_ref, heads, [patch])
+    for head in range(width // HEAD_DIM):
         lanes = slice(head * queries, (head + 1) * queries)
-        near_top = stat_ref[0:1, lanes]
-        scores = dot(keys, query_h[head], NT) * SCORE_SCALE + bias
-        top = jnp.maximum(near_top, jnp.max(scores, 0, keepdims=True))
+        scores = dot(keys_ref[0], query_across[:, lanes]) * SCORE_SCALE + bias
+        top = jnp.max(scores, 0, keepdims=True)
+        exps = jnp.where(bias > NEVER, jnp.exp2(scores - top), 0.0)
+        grad_weights = dot(keys_ref[1], grad_across[:, lanes])
+        exps_ref[:, lanes] = exps
+        gw_ref[:, lanes] = grad_weights
+        stat_ref[0:1, lanes] = top
+        stat_ref[1:2, lanes] = jnp.sum(exps, 0, keepdims=True)
+        stat_ref[2:3, lanes] = jnp.sum(exps * grad_weights, 0, keepdims=True)
+
+
+def far_kernel(heads, bias_ref, stat_ref, exps_ref, gw_ref, first_ref, query_down, query_across, grad_down, *refs):
+    grad_across, second_ref, w_ref, ds_ref, final_ref, far_a, far_b = refs
+    patch, width = second_ref.shape[1:]
+    queries = bias_ref.shape[1]
+    bias = spread(bias_ref, heads + 1, [patch])
+    for head in range(width // HEAD_DIM):
+        lanes = slice(head * queries, (head + 1) * queries)
+        near_top, first_top = stat_ref[0:1, lanes], first_ref[0:1, lanes]
+        scores = dot(second_ref[0], query_across[:, lanes]) * SCORE_SCALE + bias
+        top = jnp.maximum(jnp.maximum(near_top, first_top), jnp.max(scores, 0, keepdims=True))
         exps = jnp.exp2(scores - top)
-        shrink = jnp.exp2(near_top - top)
-        grad_weights = dot(values, grad_h[head], NT)
-        part = 1.0 / (shrink * stat_ref[1:2, lanes] + jnp.sum(exps, 0, keepdims=True))
+        shrink, first_shrink = jnp.exp2(near_top - top), jnp.exp2(first_top - top)
+        grad_weights = dot(second_ref[1], grad_across[:, lanes])
+        total = shrink * stat_ref[1:2, lanes] + first_shrink * first_ref[1:2, lanes]
+        part = 1.0 / (total + jnp.sum(exps, 0, keepdims=True))
         weights = exps * part
-        shrink = shrink * part
-        row_dots = shrink * stat_ref[2:3, lanes] + jnp.sum(weights * grad_weights, 0, keepdims=True)
-        w_ref[:, lanes] = weights.astype(LOW)
-        ds_ref[:, lanes] = (weights * (grad_weights - row_dots)).astype(LOW)
+        shrink, first_shrink = shrink * part, first_shrink * part
+        row_dots = shrink * stat_ref[2:3, lanes] + first_shrink * first_ref[2:3, lanes]
+        row_dots = row_dots + jnp.sum(weights * grad_weights, 0, keepdims=True)
+        w_ref[patch:, lanes] = weights.astype(LOW)
+        ds_ref[patch:, lanes] = (weights * (grad_weights - row_dots)).astype(LOW)
+        weights = exps_ref[:, lanes] * first_shrink
+        w_ref[:patch, lanes] = weights.astype(LOW)
+        ds_ref[:patch, lanes] = (weights * (gw_ref[:, lanes] - row_dots)).astype(LOW)
         final_ref[0:1, lanes] = shrink
         final_ref[1:2, lanes] = row_dots
-    key_grad = dot(ds_ref[...], jnp.concatenate(query_h, 0)) * HEAD_DIM**-0.5
-    value_grad = dot(w_ref[...], jnp.concatenate(grad_h, 0))
+    key_grad = dot(ds_ref[...], query_down[...]) * HEAD_DIM**-0.5
+    value_grad = dot(w_ref[...], grad_down[...])
     for s, out in enumerate((far_a, far_b)):
         span = slice(s * patch, (s + 1) * patch)
         out[0], out[1] = key_grad[span].astype(LOW), value_grad[span].astype(LOW)
 
 
-def rest_kernel(heads, places, count, final_ref, exps_ref, gw_ref, far_w_ref, far_ds_ref, *refs):
-    kv, qg, far = refs[:count], refs[count : 2 * count], refs[2 * count : 2 * count + 2]
-    mq_out, (near_out, w_ref, ds_ref) = refs[2 * count + 2 : -3], refs[-3:]
+def rest_kernel(heads, places, final_ref, exps_ref, gw_ref, far_w_ref, far_ds_ref, query_down, grad_down, *refs):
+    kv, far, outs = refs[:heads], refs[heads : heads + 2], refs[heads + 2 : -3]
+    near_out, w_ref, ds_ref = refs[-3:]
     rows, width = kv[0].shape[2:]
     queries = heads * rows
-    groups = width // HEAD_DIM
-    scale = HEAD_DIM**-0.5
     keys_t, values_t = joined(kv, places, 0).T, joined(kv, places, 1).T
     far_keys_t = jnp.concatenate([r[0] for r in far], 0).T
     far_values_t = jnp.concatenate([r[1] for r in far], 0).T
-    query_h, grad_h = masked(joined(qg, places, 0), groups), masked(joined(qg, places, 1), groups)
     mixed_t, qgrad_t = [], []
-    for head in range(groups):
+    for head in range(width // HEAD_DIM):
         feats = slice(head * HEAD_DIM, (head + 1) * HEAD_DIM)
         lanes = slice(head * queries, (head + 1) * queries)
         weights = exps_ref[:, lanes] * final_ref[0:1, lanes]
@@ -209,27 +229,28 @@
         w_ref[:, lanes] = low
         ds_ref[:, lanes] = grad_scores
         mixed_t.append(dot(values_t[feats], low) + dot(far_values_t[feats], far_w_ref[:, lanes]))
-        qgrad_t.append((dot(keys_t[feats], grad_scores) + dot(far_keys_t[feats], far_ds_ref[:, lanes])) * scale)
+        qgrad_t.append((dot(keys_t[feats], grad_scores) + dot(far_keys_t[feats], far_ds_ref[:, lanes])) * HEAD_DIM**-0.5)
     mixed = jnp.concatenate(mixed_t, 0).T.astype(LOW)
     qgrad = jnp.concatenate(qgrad_t, 0).T.astype(LOW)
-    key_grad = dot(ds_ref[...], jnp.concatenate(query_h, 0)) * scale
-    value_grad = dot(w_ref[...], jnp.concatenate(grad_h, 0))
-    for d in range(heads):
+    key_grad = dot(ds_ref[...], query_down[...]) * HEAD_DIM**-0.5
+    value_grad = dot(w_ref[...], grad_down[...])
+    for d, out in enumerate(outs):
         span = slice(d * rows, (d + 1) * rows)
-        mq_out[d][0, 0], mq_out[d][0, 1] = mixed[span], qgrad[span]
+        out[0, 0], out[0, 1] = mixed[span], qgrad[span]
         near_out[d, 0], near_out[d, 1] = key_grad[span], value_grad[span]
 
 
 def merge_kernel(heads, slot_ref, near, back_a, back_b, *outs):
     rows = near.shape[2]
     per_patch = back_a.shape[1] // rows
+    me = lax.axis_index("head")
     for d in range(heads):
         total = near[d]
+        part = lax.rem(me ^ d, per_patch)
         for s, back in enumerate((back_a, back_b)):
-            for t in range(per_patch):
-                slot = slot_ref[s * per_patch + t : s * per_patch + t + 1, :]
-                term = back[:, t * rows : (t + 1) * rows, :].astype(jnp.float32)
-                total = total + jnp.where((slot == d)[None], term, 0.0)
+            slot = slot_ref[pl.ds(s * per_patch + part, 1), :]
+            term = back[:, pl.ds(pl.multiple_of(part * rows, rows), rows), :].astype(jnp.float32)
+            total = total + jnp.where((slot == d)[None], term, 0.0)
         outs[d][0] = total.astype(LOW)
 
 
@@ -242,12 +263,14 @@
         outs[0][:, cols], outs[1][:, cols] = arrays[a][j, 0], arrays[a][j, 1]
 
 
+def far_first(heads):
+    return [0] + sorted(range(1, heads), key=lambda d: (-(d >> 1), d))
+
+
 def exchange(blocks):
     heads = len(blocks)
-    got = list(blocks)
-    for d in sorted(range(1, heads), key=lambda d: (-(d >> 1), d)):
-        got[d] = lax.ppermute(blocks[d], "head", [(i, i ^ d) for i in range(heads)])
-    return got
+    swaps = [[(i, i ^ d) for i in range(heads)] for d in range(heads)]
+    return [lax.ppermute(blocks[d], "head", swaps[d]) if d else blocks[0] for d in far_first(heads)]
 
 
 def gather_in(heads, one, two, joint, block, *after):
@@ -265,7 +288,7 @@
     per_patch = heads // local_count
     patch = rows * per_patch
     block = jax.ShapeDtypeStruct((1, 2, rows, width), LOW)
-    places = [(d, 0) for d in range(heads)]
+    places = [(far_first(heads).index(d), 0) for d in range(heads)]
     near_shape = jax.ShapeDtypeStruct((heads, 2, rows, width), jnp.float32)
     slab = jax.ShapeDtypeStruct((2, patch, width), LOW)
     whole = jax.ShapeDtypeStruct((rows, features), LOW)
@@ -293,27 +316,39 @@
     def table(height, kind=jnp.float32):
         return jax.ShapeDtypeStruct((height, lanes), kind)
 
-    exps, grad_weights, stats = call(
+    down = jax.ShapeDtypeStruct((lanes, width), LOW)
+    across = jax.ShapeDtypeStruct((width, lanes), LOW)
+    exps, grad_weights, stats, *sides = call(
         functools.partial(near_kernel, heads, places, len(kv)),
         "near",
-        [table(own), table(own), table(3)],
+        [table(own), table(own), table(3), down, across, down, across],
         bias,
         *kv,
         *qg,
         cost=work,
     )
+    first = call(
+        functools.partial(first_kernel, heads),
+        "first",
+        [table(patch), table(patch), table(3)],
+        bias,
+        sides[1],
+        sides[3],
+        far[0],
+    )
     far_w, far_ds, final, *far_grads = call(
-        functools.partial(far_kernel, heads, places, len(kv)),
+        functools.partial(far_kernel, heads),
         "far",
         [table(other, LOW), table(other, LOW), table(2), slab, slab],
         bias,
         stats,
-        *qg,
-        *far,
+        *first,
+        *sides,
+        far[1],
         cost=work,
     )
     *mq, near = call(
-        functools.partial(rest_kernel, heads, places, len(kv)),
+        functools.partial(rest_kernel, heads, places),
         "rest",
         [block] * heads + [near_shape],
         final,
@@ -321,8 +356,9 @@
         grad_weights,
         far_w,
         far_ds,
+        sides[0],
+        sides[2],
         *kv,
-        *qg,
         *far,
         scratch=[pltpu.VMEM((own, lanes), LOW)] * 2,
         cost=work,

time: 29.2 us -> 28.3 us (0.969)
  waiting for transfers between devices: 8.42 us -> 7.56 us
    ppermute x2, waiting for transfers between devices: 1.99 us -> 1.45 us  [shards(): far = [lax.ppermute(p, ('node', 'head'), r) for p, r in zip(picked, routes)]]
    pallas_call x10 -> x11, Pallas kernels: 5.35 us -> 5.41 us  [call(): pl.pallas_call(kernel, out_shape=outs, in_specs=specs or [VMEM] * len(arg...]
  transfers between devices with their start and end apart: 16 -> 16, of which waited for: 8 -> 7; matrix products, arithmetic and copies ran while one was open for 0% -> 0% of each run, Pallas kernels for 12% -> 13%
where the time goes in v6:
time: 28.3 us; the launch traced here: 28.1 us
  starting transfers between devices  13.4 us (47%)
  waiting for transfers between devices  7.56 us (27%)
  Pallas kernels  5.41 us (19%)
  other arithmetic  0.99 us (3%)
  between operations  0.75 us (3%)
    ppermute x12, starting transfers between devices, exchange(): lax.ppermute(blocks[d], 'head', swaps[d])  9.25 us
    ppermute x12, waiting for transfers between devices, exchange(): lax.ppermute(blocks[d], 'head', swaps[d])  6.1 us
    pallas_call x11, Pallas kernels, call(): pl.pallas_call(kernel, out_shape=outs, in_specs=specs or [VMEM] * len(arg...  5.41 us
    ppermute x2, starting transfers between devices, shards(): lax.ppermute(p, ('node', 'head'), r)  2.47 us
    ppermute x2, starting transfers between devices, shards(): far = [lax.ppermute(p, ('node', 'head'), r) for p, r in zip(picked, routes)]  1.7 us
    ppermute x2, waiting for transfers between devices, shards(): far = [lax.ppermute(p, ('node', 'head'), r) for p, r in zip(picked, routes)]  1.45 us
    concatenate x1, other arithmetic, gather_in(): jnp.concatenate(own, 0)  0.99 us
  transfers between devices with their start and end apart: 16, of which 7 were waited for; matrix products, arithmetic and copies ran while one was open for 0% of the time, Pallas kernels for 13%

profile of v6, /device:TPU:0, one launch (start us, length us, event | category | flops | bytes accessed | tf_op | source)
XLA Modules:
  0.0 28.1 jit_solution(8167215305830432633)
XLA Ops:
  0.6 1.0 %pad_maximum_fusion = bf16[128,1024]{1,0:T(8,128)(2,1)S(1)} fusion(bf16[64,1024]{1,0:T(8,128)(2,1)} %param.7, bf16[64,1024]{1,0:T(8,128)(2,1)} %param.6), kind=kLoop, calls=%fused_computation | loop fusion | flops 524288 | bytes 524288 | tf_op jit(solution)/shard_map/concatenate | solution.py:279
  1.6 0.0 copy-start
  1.6 0.0 copy-start.1
  1.7 0.0 copy-start.2
  1.7 3.0 %collective-permute-start = (bf16[1,2,64,256]{3,2,1,0:T(8,128)(2,1)S(1)}, bf16[1,2,64,256]{3,2,1,0:T(8,128)(2,1)S(1)}, u32[]{:S(2)}, u32[]{:S(2)}) collective-permute-start(bf16[1,2,64,256]{3,2,1,0:T(8,128)(2,1)S(1)} %get-tuple-element.46), channel_id=1, source_target_pairs={{0,2},{1,3},{2,0},{3,1},{4,6},{5,7},{6,4},{7,5},{8,10},{9,11},{10,... | collective-permute-start | bytes 196616 | tf_op jit(solution)/shard_map/ppermute | solution.py:273
  4.7 0.0 collective-permute-start.1
  4.7 0.2 collective-permute-start.2
  4.9 0.0 copy-done.2
  4.9 0.8 %prep.1 = (f32[6,256]{1,0:T(8,128)S(1)}, s32[4,256]{1,0:T(4,128)S(1)}) custom-call(s32[8,8]{1,0:T(8,128)S(1)} %copy-done.2, bf16[1,2,64,256]{3,2,1,0:T(8,128)(2,1)S(1)} %get-tuple-element.44.after_ref.refs_0_), custom_call_target="tpu_custom_call" | custom-call | tf_op jit(solution)/shard_map/prep/pallas_call | solution.py:24
  5.8 0.0 copy-done
  5.8 0.0 copy-done.1
  5.8 2.0 %collective-permute-start.3 = (bf16[1,2,64,256]{3,2,1,0:T(8,128)(2,1)S(1)}, bf16[1,2,64,256]{3,2,1,0:T(8,128)(2,1)S(1)}, u32[]{:S(2)}, u32[]{:S(2)}) collective-permute-start(bf16[1,2,64,256]{3,2,1,0:T(8,128)(2,1)S(1)} %get-tuple-element.51), channel_id=1, source_target_pairs={{0,2},{1,3},{2,0},{3,1},{4,6},{5,7},{6,4},{7,5},{8,10},{9,11},{10,... | collective-permute-start | bytes 196616 | tf_op jit(solution)/shard_map/ppermute | solution.py:273
  7.8 0.0 collective-permute-start.4
  7.8 0.0 collective-permute-done.refs_1_
  7.8 0.2 collective-permute-start.5
  8.0 0.8 %collective-permute-done.1.refs_2_ = bf16[1,2,64,256]{3,2,1,0:T(8,128)(2,1)S(1)} collective-permute-done((bf16[1,2,64,256]{3,2,1,0:T(8,128)(2,1)S(1)}, bf16[1,2,64,256]{3,2,1,0:T(8,128)(2,1)S(1)}, u32[]{:S(2)}, u32[]{:S(2)}) %collective-permute-start.1) | collective-permute-done | bytes 65568 | tf_op jit(solution)/shard_map/ppermute | solution.py:273
  8.8 0.0 collective-permute-done.2.refs_3_
  8.8 0.1 pick.1
  9.0 1.7 %collective-permute-start.6 = (bf16[2,128,256]{2,1,0:T(8,128)(2,1)S(1)}, bf16[2,128,256]{2,1,0:T(8,128)(2,1)S(1)}, u32[]{:S(2)}, u32[]{:S(2)}) collective-permute-start(bf16[2,128,256]{2,1,0:T(8,128)(2,1)S(1)} %get-tuple-element.57), channel_id=1, source_target_pairs={{0,4},{1,5},{2,6},{3,7},{4,0},{5,1},{6,2},{7,3},{8,12},{9,13},{10,... | collective-permute-start | bytes 393224 | tf_op jit(solution)/shard_map/ppermute | solution.py:311
  10.6 0.0 collective-permute-start.7
  10.6 0.0 collective-permute-done.3.refs_5_
  10.7 1.5 %collective-permute-done.4.refs_6_ = bf16[1,2,64,256]{3,2,1,0:T(8,128)(2,1)S(1)} collective-permute-done((bf16[1,2,64,256]{3,2,1,0:T(8,128)(2,1)S(1)}, bf16[1,2,64,256]{3,2,1,0:T(8,128)(2,1)S(1)}, u32[]{:S(2)}, u32[]{:S(2)}) %collective-permute-start.4) | collective-permute-done | bytes 65568 | tf_op jit(solution)/shard_map/ppermute | solution.py:273
  12.1 0.0 collective-permute-done.5.refs_7_
  12.1 0.7 %near.1 = (f32[256,1024]{1,0:T(8,128)S(1)}, f32[256,1024]{1,0:T(8,128)S(1)}, f32[3,1024]{1,0:T(4,128)S(1)}, bf16[1024,256]{1,0:T(8,128)(2,1)S(1)}, bf16[256,1024...) custom-call(f32[6,256]{1,0:T(8,128)S(1)} %get-tuple-element.45.bias_ref, ...), custom_call_target="tpu_custom_call" | custom-call | flops 1500000000 | bytes 1 | tf_op jit(solution)/shard_map/near/pallas_call | solution.py:24
  12.8 1.4 %collective-permute-done.6.keys_ref.refs_4_ = bf16[2,128,256]{2,1,0:T(8,128)(2,1)S(1)} collective-permute-done((bf16[2,128,256]{2,1,0:T(8,128)(2,1)S(1)}, bf16[2,128,256]{2,1,0:T(8,128)(2,1)S(1)}, u32[]{:S(2)}, u32[]{:S(2)}) %collective-permute-start.6) | collective-permute-done | bytes 131104 | tf_op jit(solution)/shard_map/ppermute | solution.py:311
  14.3 0.4 %first.1 = (f32[128,1024]{1,0:T(8,128)S(1)}, f32[128,1024]{1,0:T(8,128)S(1)}, f32[3,1024]{1,0:T(4,128)S(1)}) custom-call(f32[6,256]{1,0:T(8,128)S(1)} %get-tuple-element.45.bias_ref, bf16[256,1024]{1,0:T(8,128)(2,1)S(1)} %get-tuple-element.55.query_across, bf16[256,1024]{1,0:T(8,128)(2,1)S(1)} %get-tuple-element.56.grad_across.refs_0_, ...), custom_call_target="tpu_custom_call" | custom-call | tf_op jit(solution)/shard_map/first/pallas_call | solution.py:24
  14.7 0.0 collective-permute-done.7.refs_1_.refs_5_
  14.7 0.9 %far.1 = (bf16[256,1024]{1,0:T(8,128)(2,1)S(1)}, bf16[256,1024]{1,0:T(8,128)(2,1)S(1)}, f32[2,1024]{1,0:T(2,128)S(1)}, bf16[2,128,256]{2,1,0:T(8,128)(2,1)S(1)}, bf16[2,128,256]{2,1,0:T(8,128)(2,1)S(1)}) custom-call(f32[6,256]{1,0:T(8,128)S(1)} %get-tuple-element.45.bias_ref, f32[3,1024]{1,0:T(4,128)S(1)} %get-tuple-element.54.stat_ref, ...), custom_call_target="tpu_custom_call" | custom-call | flops 1500000000 | bytes 1 | tf_op jit(solution)/shard_map/far/pallas_call | solution.py:24
  15.6 2.5 %collective-permute-start.11 = (bf16[2,128,256]{2,1,0:T(8,128)(2,1)S(1)}, bf16[2,128,256]{2,1,0:T(8,128)(2,1)S(1)}, u32[]{:S(2)}, u32[]{:S(2)}) collective-permute-start(bf16[2,128,256]{2,1,0:T(8,128)(2,1)S(1)} %get-tuple-element.76), channel_id=1, source_target_pairs={{0,4},{1,5},{2,6},{3,7},{4,0},{5,1},{6,2},{7,3},{8,12},{9,13},{10,... | collective-permute-start | bytes 393224 | tf_op jit(solution)/shard_map/ppermute | solution.py:366
  18.1 0.0 collective-permute-start.12
  18.1 0.8 %rest.1 = (bf16[1,2,64,256]{3,2,1,0:T(8,128)(2,1)S(1)}, bf16[1,2,64,256]{3,2,1,0:T(8,128)(2,1)S(1)}, bf16[1,2,64,256]{3,2,1,0:T(8,128)(2,1)S(1)}, bf16[1,2,64,25...) custom-call(f32[2,1024]{1,0:T(2,128)S(1)} %get-tuple-element.64.final_ref, f32[256,1024]{1,0:T(8,128)S(1)} %get-tuple-element.65.exps_ref, ...), custom_call_target="tpu_custom_call" | custom-call | flops 1500000000 | bytes 1 | tf_op jit(solution)/shard_map/rest/pallas_call | solution.py:24
  18.9 1.4 %collective-permute-start.8 = (bf16[1,2,64,256]{3,2,1,0:T(8,128)(2,1)S(1)}, bf16[1,2,64,256]{3,2,1,0:T(8,128)(2,1)S(1)}, u32[]{:S(2)}, u32[]{:S(2)}) collective-permute-start(bf16[1,2,64,256]{3,2,1,0:T(8,128)(2,1)S(1)} %get-tuple-element.70), channel_id=1, source_target_pairs={{0,2},{1,3},{2,0},{3,1},{4,6},{5,7},{6,4},{7,5},{8,10},{9,11},{10,... | collective-permute-start | bytes 196616 | tf_op jit(solution)/shard_map/ppermute | solution.py:273
  20.3 0.5 %collective-permute-start.9 = (bf16[1,2,64,256]{3,2,1,0:T(8,128)(2,1)S(1)}, bf16[1,2,64,256]{3,2,1,0:T(8,128)(2,1)S(1)}, u32[]{:S(2)}, u32[]{:S(2)}) collective-permute-start(bf16[1,2,64,256]{3,2,1,0:T(8,128)(2,1)S(1)} %get-tuple-element.71), channel_id=1, source_target_pairs={{0,3},{1,2},{2,1},{3,0},{4,7},{5,6},{6,5},{7,4},{8,11},{9,10},{10,... | collective-permute-start | bytes 196616 | tf_op jit(solution)/shard_map/ppermute | solution.py:273
  20.8 0.3 %collective-permute-start.10 = (bf16[1,2,64,256]{3,2,1,0:T(8,128)(2,1)S(1)}, bf16[1,2,64,256]{3,2,1,0:T(8,128)(2,1)S(1)}, u32[]{:S(2)}, u32[]{:S(2)}) collective-permute-start(bf16[1,2,64,256]{3,2,1,0:T(8,128)(2,1)S(1)} %get-tuple-element.72), channel_id=1, source_target_pairs={{0,1},{1,0},{2,3},{3,2},{4,5},{5,4},{6,7},{7,6},{8,9},{9,8},{10,11... | collective-permute-start | bytes 196616 | tf_op jit(solution)/shard_map/ppermute | solution.py:273
  21.1 0.0 collective-permute-done.11.back_a
  21.1 0.0 collective-permute-done.12.back_b
  21.1 0.1 merge.1
  21.2 1.4 %collective-permute-start.13 = (bf16[1,2,64,256]{3,2,1,0:T(8,128)(2,1)S(1)}, bf16[1,2,64,256]{3,2,1,0:T(8,128)(2,1)S(1)}, u32[]{:S(2)}, u32[]{:S(2)}) collective-permute-start(bf16[1,2,64,256]{3,2,1,0:T(8,128)(2,1)S(1)} %get-tuple-element.79), channel_id=1, source_target_pairs={{0,2},{1,3},{2,0},{3,1},{4,6},{5,7},{6,4},{7,5},{8,10},{9,11},{10,... | collective-permute-start | bytes 196616 | tf_op jit(solution)/shard_map/ppermute | solution.py:273
  22.7 0.2 collective-permute-start.14
  22.9 0.8 %collective-permute-done.8.refs_1_ = bf16[1,2,64,256]{3,2,1,0:T(8,128)(2,1)S(1)} collective-permute-done((bf16[1,2,64,256]{3,2,1,0:T(8,128)(2,1)S(1)}, bf16[1,2,64,256]{3,2,1,0:T(8,128)(2,1)S(1)}, u32[]{:S(2)}, u32[]{:S(2)}) %collective-permute-start.8) | collective-permute-done | bytes 65568 | tf_op jit(solution)/shard_map/ppermute | solution.py:273
  23.6 0.0 collective-permute-start.15
  23.6 1.0 %collective-permute-done.9.refs_2_ = bf16[1,2,64,256]{3,2,1,0:T(8,128)(2,1)S(1)} collective-permute-done((bf16[1,2,64,256]{3,2,1,0:T(8,128)(2,1)S(1)}, bf16[1,2,64,256]{3,2,1,0:T(8,128)(2,1)S(1)}, u32[]{:S(2)}, u32[]{:S(2)}) %collective-permute-start.9) | collective-permute-done | bytes 65568 | tf_op jit(solution)/shard_map/ppermute | solution.py:273
  24.6 0.0 collective-permute-done.10.refs_3_
  24.6 0.7 %unpack.2 = (bf16[64,1024]{1,0:T(8,128)(2,1)}, bf16[64,1024]{1,0:T(8,128)(2,1)}) custom-call(bf16[1,2,64,256]{3,2,1,0:T(8,128)(2,1)S(1)} %get-tuple-element.69.refs_0_, bf16[1,2,64,256]{3,2,1,0:T(8,128)(2,1)S(1)} %collective-permute-done.8.refs_1_, bf16[1,2,64,256]{3,2,1,0:T(8,128)(2,1)S(1)} %collective-permute-done.9.refs_2_, ...), custom_call_target="tpu_custom_call" | custom-call | tf_op jit(solution)/shard_map/unpack/pallas_call | solution.py:24
  25.3 1.2 %collective-permute-done.13.refs_1_ = bf16[1,2,64,256]{3,2,1,0:T(8,128)(2,1)S(1)} collective-permute-done((bf16[1,2,64,256]{3,2,1,0:T(8,128)(2,1)S(1)}, bf16[1,2,64,256]{3,2,1,0:T(8,128)(2,1)S(1)}, u32[]{:S(2)}, u32[]{:S(2)}) %collective-permute-start.13) | collective-permute-done | bytes 65568 | tf_op jit(solution)/shard_map/ppermute | solution.py:273
  26.5 0.9 %collective-permute-done.14.refs_2_ = bf16[1,2,64,256]{3,2,1,0:T(8,128)(2,1)S(1)} collective-permute-done((bf16[1,2,64,256]{3,2,1,0:T(8,128)(2,1)S(1)}, bf16[1,2,64,256]{3,2,1,0:T(8,128)(2,1)S(1)}, u32[]{:S(2)}, u32[]{:S(2)}) %collective-permute-start.14) | collective-permute-done | bytes 65568 | tf_op jit(solution)/shard_map/ppermute | solution.py:273
  27.4 0.0 collective-permute-done.15.refs_3_
  27.4 0.7 %unpack.3 = (bf16[64,1024]{1,0:T(8,128)(2,1)}, bf16[64,1024]{1,0:T(8,128)(2,1)}) custom-call(bf16[1,2,64,256]{3,2,1,0:T(8,128)(2,1)S(1)} %get-tuple-element.78.refs_0_, bf16[1,2,64,256]{3,2,1,0:T(8,128)(2,1)S(1)} %collective-permute-done.13.refs_1_, bf16[1,2,64,256]{3,2,1,0:T(8,128)(2,1)S(1)} %collective-permute-done.14.refs_2_, ...), custom_call_target="tpu_custom_call" | custom-call | tf_op jit(solution)/shard_map/unpack/pallas_call | solution.py:24
  (2 shorter events, 0.1 us)
Async XLA Ops:
  1.6 4.1 %copy-start = (bf16[64,1024]{1,0:T(8,128)(2,1)S(1)}, bf16[64,1024]{1,0:T(8,128)(2,1)}, u32[]{:S(2)}) copy-start(bf16[64,1024]{1,0:T(8,128)(2,1)} %refs_0_.1) | copy-start | bytes 393220
  1.6 4.1 %copy-start.1 = (bf16[64,1024]{1,0:T(8,128)(2,1)S(1)}, bf16[64,1024]{1,0:T(8,128)(2,1)}, u32[]{:S(2)}) copy-start(bf16[64,1024]{1,0:T(8,128)(2,1)} %refs_1_.1) | copy-start | bytes 393220
  1.7 3.2 %copy-start.2 = (s32[8,8]{1,0:T(8,128)S(1)}, s32[8,8]{1,0:T(8,128)}, u32[]{:S(2)}) copy-start(s32[8,8]{1,0:T(8,128)} %nbr_ref.1) | copy-start | bytes 772
  1.7 6.1 %collective-permute-start = (bf16[1,2,64,256]{3,2,1,0:T(8,128)(2,1)S(1)}, bf16[1,2,64,256]{3,2,1,0:T(8,128)(2,1)S(1)}, u32[]{:S(2)}, u32[]{:S(2)}) collective-permute-start(bf16[1,2,64,256]{3,2,1,0:T(8,128)(2,1)S(1)} %get-tuple-element.46), channel_id=1, source_target_pairs={{0,2},{1,3},{2,0},{3,1},{4,6},{5,7},{6,4},{7,5},{8,10},{9,11},{10,... | collective-permute-start | bytes 196616 | tf_op jit(solution)/shard_map/ppermute | solution.py:273
  4.7 4.1 %collective-permute-start.1 = (bf16[1,2,64,256]{3,2,1,0:T(8,128)(2,1)S(1)}, bf16[1,2,64,256]{3,2,1,0:T(8,128)(2,1)S(1)}, u32[]{:S(2)}, u32[]{:S(2)}) collective-permute-start(bf16[1,2,64,256]{3,2,1,0:T(8,128)(2,1)S(1)} %get-tuple-element.47), channel_id=1, source_target_pairs={{0,3},{1,2},{2,1},{3,0},{4,7},{5,6},{6,5},{7,4},{8,11},{9,10},{10,... | collective-permute-start | bytes 196616 | tf_op jit(solution)/shard_map/ppermute | solution.py:273
  4.7 4.1 %collective-permute-start.2 = (bf16[1,2,64,256]{3,2,1,0:T(8,128)(2,1)S(1)}, bf16[1,2,64,256]{3,2,1,0:T(8,128)(2,1)S(1)}, u32[]{:S(2)}, u32[]{:S(2)}) collective-permute-start(bf16[1,2,64,256]{3,2,1,0:T(8,128)(2,1)S(1)} %get-tuple-element.48), channel_id=1, source_target_pairs={{0,1},{1,0},{2,3},{3,2},{4,5},{5,4},{6,7},{7,6},{8,9},{9,8},{10,11... | collective-permute-start | bytes 196616 | tf_op jit(solution)/shard_map/ppermute | solution.py:273
  5.8 4.8 %collective-permute-start.3 = (bf16[1,2,64,256]{3,2,1,0:T(8,128)(2,1)S(1)}, bf16[1,2,64,256]{3,2,1,0:T(8,128)(2,1)S(1)}, u32[]{:S(2)}, u32[]{:S(2)}) collective-permute-start(bf16[1,2,64,256]{3,2,1,0:T(8,128)(2,1)S(1)} %get-tuple-element.51), channel_id=1, source_target_pairs={{0,2},{1,3},{2,0},{3,1},{4,6},{5,7},{6,4},{7,5},{8,10},{9,11},{10,... | collective-permute-start | bytes 196616 | tf_op jit(solution)/shard_map/ppermute | solution.py:273
  7.8 4.3 %collective-permute-start.4 = (bf16[1,2,64,256]{3,2,1,0:T(8,128)(2,1)S(1)}, bf16[1,2,64,256]{3,2,1,0:T(8,128)(2,1)S(1)}, u32[]{:S(2)}, u32[]{:S(2)}) collective-permute-start(bf16[1,2,64,256]{3,2,1,0:T(8,128)(2,1)S(1)} %get-tuple-element.52), channel_id=1, source_target_pairs={{0,3},{1,2},{2,1},{3,0},{4,7},{5,6},{6,5},{7,4},{8,11},{9,10},{10,... | collective-permute-start | bytes 196616 | tf_op jit(solution)/shard_map/ppermute | solution.py:273
  7.8 4.3 %collective-permute-start.5 = (bf16[1,2,64,256]{3,2,1,0:T(8,128)(2,1)S(1)}, bf16[1,2,64,256]{3,2,1,0:T(8,128)(2,1)S(1)}, u32[]{:S(2)}, u32[]{:S(2)}) collective-permute-start(bf16[1,2,64,256]{3,2,1,0:T(8,128)(2,1)S(1)} %get-tuple-element.53), channel_id=1, source_target_pairs={{0,1},{1,0},{2,3},{3,2},{4,5},{5,4},{6,7},{7,6},{8,9},{9,8},{10,11... | collective-permute-start | bytes 196616 | tf_op jit(solution)/shard_map/ppermute | solution.py:273
  9.0 5.3 %collective-permute-start.6 = (bf16[2,128,256]{2,1,0:T(8,128)(2,1)S(1)}, bf16[2,128,256]{2,1,0:T(8,128)(2,1)S(1)}, u32[]{:S(2)}, u32[]{:S(2)}) collective-permute-start(bf16[2,128,256]{2,1,0:T(8,128)(2,1)S(1)} %get-tuple-element.57), channel_id=1, source_target_pairs={{0,4},{1,5},{2,6},{3,7},{4,0},{5,1},{6,2},{7,3},{8,12},{9,13},{10,... | collective-permute-start | bytes 393224 | tf_op jit(solution)/shard_map/ppermute | solution.py:311
  10.6 4.0 %collective-permute-start.7 = (bf16[2,128,256]{2,1,0:T(8,128)(2,1)S(1)}, bf16[2,128,256]{2,1,0:T(8,128)(2,1)S(1)}, u32[]{:S(2)}, u32[]{:S(2)}) collective-permute-start(bf16[2,128,256]{2,1,0:T(8,128)(2,1)S(1)} %get-tuple-element.63), channel_id=1, source_target_pairs={{0,1},{1,0},{2,3},{3,2},{4,8},{5,9},{6,10},{7,11},{8,4},{9,5},{10,... | collective-permute-start | bytes 393224 | tf_op jit(solution)/shard_map/ppermute | solution.py:311
  15.6 5.5 %collective-permute-start.11 = (bf16[2,128,256]{2,1,0:T(8,128)(2,1)S(1)}, bf16[2,128,256]{2,1,0:T(8,128)(2,1)S(1)}, u32[]{:S(2)}, u32[]{:S(2)}) collective-permute-start(bf16[2,128,256]{2,1,0:T(8,128)(2,1)S(1)} %get-tuple-element.76), channel_id=1, source_target_pairs={{0,4},{1,5},{2,6},{3,7},{4,0},{5,1},{6,2},{7,3},{8,12},{9,13},{10,... | collective-permute-start | bytes 393224 | tf_op jit(solution)/shard_map/ppermute | solution.py:366
  18.1 3.0 %collective-permute-start.12 = (bf16[2,128,256]{2,1,0:T(8,128)(2,1)S(1)}, bf16[2,128,256]{2,1,0:T(8,128)(2,1)S(1)}, u32[]{:S(2)}, u32[]{:S(2)}) collective-permute-start(bf16[2,128,256]{2,1,0:T(8,128)(2,1)S(1)} %get-tuple-element.77), channel_id=1, source_target_pairs={{0,1},{1,0},{2,3},{3,2},{4,8},{5,9},{6,10},{7,11},{8,4},{9,5},{10,... | collective-permute-start | bytes 393224 | tf_op jit(solution)/shard_map/ppermute | solution.py:366
  18.9 4.8 %collective-permute-start.8 = (bf16[1,2,64,256]{3,2,1,0:T(8,128)(2,1)S(1)}, bf16[1,2,64,256]{3,2,1,0:T(8,128)(2,1)S(1)}, u32[]{:S(2)}, u32[]{:S(2)}) collective-permute-start(bf16[1,2,64,256]{3,2,1,0:T(8,128)(2,1)S(1)} %get-tuple-element.70), channel_id=1, source_target_pairs={{0,2},{1,3},{2,0},{3,1},{4,6},{5,7},{6,4},{7,5},{8,10},{9,11},{10,... | collective-permute-start | bytes 196616 | tf_op jit(solution)/shard_map/ppermute | solution.py:273
  20.3 4.3 %collective-permute-start.9 = (bf16[1,2,64,256]{3,2,1,0:T(8,128)(2,1)S(1)}, bf16[1,2,64,256]{3,2,1,0:T(8,128)(2,1)S(1)}, u32[]{:S(2)}, u32[]{:S(2)}) collective-permute-start(bf16[1,2,64,256]{3,2,1,0:T(8,128)(2,1)S(1)} %get-tuple-element.71), channel_id=1, source_target_pairs={{0,3},{1,2},{2,1},{3,0},{4,7},{5,6},{6,5},{7,4},{8,11},{9,10},{10,... | collective-permute-start | bytes 196616 | tf_op jit(solution)/shard_map/ppermute | solution.py:273
  20.8 3.8 %collective-permute-start.10 = (bf16[1,2,64,256]{3,2,1,0:T(8,128)(2,1)S(1)}, bf16[1,2,64,256]{3,2,1,0:T(8,128)(2,1)S(1)}, u32[]{:S(2)}, u32[]{:S(2)}) collective-permute-start(bf16[1,2,64,256]{3,2,1,0:T(8,128)(2,1)S(1)} %get-tuple-element.72), channel_id=1, source_target_pairs={{0,1},{1,0},{2,3},{3,2},{4,5},{5,4},{6,7},{7,6},{8,9},{9,8},{10,11... | collective-permute-start | bytes 196616 | tf_op jit(solution)/shard_map/ppermute | solution.py:273
  21.2 5.3 %collective-permute-start.13 = (bf16[1,2,64,256]{3,2,1,0:T(8,128)(2,1)S(1)}, bf16[1,2,64,256]{3,2,1,0:T(8,128)(2,1)S(1)}, u32[]{:S(2)}, u32[]{:S(2)}) collective-permute-start(bf16[1,2,64,256]{3,2,1,0:T(8,128)(2,1)S(1)} %get-tuple-element.79), channel_id=1, source_target_pairs={{0,2},{1,3},{2,0},{3,1},{4,6},{5,7},{6,4},{7,5},{8,10},{9,11},{10,... | collective-permute-start | bytes 196616 | tf_op jit(solution)/shard_map/ppermute | solution.py:273
  22.7 4.8 %collective-permute-start.14 = (bf16[1,2,64,256]{3,2,1,0:T(8,128)(2,1)S(1)}, bf16[1,2,64,256]{3,2,1,0:T(8,128)(2,1)S(1)}, u32[]{:S(2)}, u32[]{:S(2)}) collective-permute-start(bf16[1,2,64,256]{3,2,1,0:T(8,128)(2,1)S(1)} %get-tuple-element.80), channel_id=1, source_target_pairs={{0,3},{1,2},{2,1},{3,0},{4,7},{5,6},{6,5},{7,4},{8,11},{9,10},{10,... | collective-permute-start | bytes 196616 | tf_op jit(solution)/shard_map/ppermute | solution.py:273
  23.6 3.8 %collective-permute-start.15 = (bf16[1,2,64,256]{3,2,1,0:T(8,128)(2,1)S(1)}, bf16[1,2,64,256]{3,2,1,0:T(8,128)(2,1)S(1)}, u32[]{:S(2)}, u32[]{:S(2)}) collective-permute-start(bf16[1,2,64,256]{3,2,1,0:T(8,128)(2,1)S(1)} %get-tuple-element.81), channel_id=1, source_target_pairs={{0,1},{1,0},{2,3},{3,2},{4,5},{5,4},{6,7},{7,6},{8,9},{9,8},{10,11... | collective-permute-start | bytes 196616 | tf_op jit(solution)/shard_map/ppermute | solution.py:273

commit v7 on v6

--- a/solution.py
+++ b/solution.py
@@ -97,8 +97,7 @@
             slot_ref[s * per_patch + t : s * per_patch + t + 1, :] = jnp.full((1, slot_ref.shape[1]), slot)
 
 
-def pack_kernel(heads, joint, *refs):
-    one, two = (refs[0].at[0], refs[0].at[1]) if joint else refs[:2]
+def pack_kernel(heads, one, two, *refs):
     me = lax.axis_index("head")
     width = refs[-1].shape[-1]
     for d, out in enumerate(refs[-heads:]):
@@ -254,6 +253,12 @@
         outs[d][0] = total.astype(LOW)
 
 
+def join_kernel(*refs):
+    count = len(refs) // 3
+    for i, out in enumerate(refs[2 * count :]):
+        out[0, 0], out[0, 1] = refs[2 * i][...], refs[2 * i + 1][...]
+
+
 def unpack_kernel(heads, places, *refs):
     arrays, outs = refs[:-2], refs[-2:]
     width = arrays[0].shape[-1]
@@ -267,17 +272,18 @@
     return [0] + sorted(range(1, heads), key=lambda d: (-(d >> 1), d))
 
 
-def exchange(blocks):
+def exchange(blocks, order):
     heads = len(blocks)
     swaps = [[(i, i ^ d) for i in range(heads)] for d in range(heads)]
-    return [lax.ppermute(blocks[d], "head", swaps[d]) if d else blocks[0] for d in far_first(heads)]
-
-
-def gather_in(heads, one, two, joint, block, *after):
-    own = [one, two]
-    if joint:
-        own = [lax.optimization_barrier(jnp.concatenate(own, 0)).reshape((2,) + one.shape)]
-    return exchange(call(functools.partial(pack_kernel, heads, joint), "pack", [block] * heads, *own, *after))
+    return [lax.ppermute(blocks[d], "head", swaps[d]) if d else blocks[0] for d in order]
+
+
+def cut(one, two, heads):
+    me = lax.axis_index("head")
+    width = one.shape[1] // heads
+    starts = [(me ^ d) * width for d in range(heads)]
+    parts = [[lax.dynamic_slice_in_dim(a, at, width, 1) for a in (one, two)] for at in starts]
+    return call(join_kernel, "join", [jax.ShapeDtypeStruct((1, 2) + parts[0][0].shape, LOW)] * heads, *sum(parts, []))
 
 
 def shards(queries, key_rows, value_rows, out_grads, neighbours):
@@ -288,13 +294,14 @@
     per_patch = heads // local_count
     patch = rows * per_patch
     block = jax.ShapeDtypeStruct((1, 2, rows, width), LOW)
-    places = [(far_first(heads).index(d), 0) for d in range(heads)]
+    order, downward = far_first(heads), [0] + list(range(heads - 1, 0, -1))
+    places = [(order.index(d), 0) for d in range(heads)]
     near_shape = jax.ShapeDtypeStruct((heads, 2, rows, width), jnp.float32)
     slab = jax.ShapeDtypeStruct((2, patch, width), LOW)
     whole = jax.ShapeDtypeStruct((rows, features), LOW)
     routes = pair_routes(owners, heads)
 
-    kv = gather_in(heads, key_rows, value_rows, True, block)
+    kv = exchange(cut(key_rows, value_rows, heads), order)
     bias, slots = call(
         functools.partial(prep_kernel, heads, owners, local_count, per_patch, rows),
         "prep",
@@ -306,7 +313,8 @@
         kv[0],
         specs=[SMEM, VMEM],
     )
-    qg = gather_in(heads, queries, out_grads, False, block, slots)
+    pack = functools.partial(pack_kernel, heads)
+    qg = exchange(call(pack, "pack", [block] * heads, queries, out_grads, slots), order)
     picked = call(functools.partial(pick_kernel, heads, places), "pick", [slab] * 2, slots, *kv)
     far = [lax.ppermute(p, ("node", "head"), r) for p, r in zip(picked, routes)]
     lanes = width // HEAD_DIM * heads * rows
@@ -364,11 +372,13 @@
         cost=work,
     )
     back = [lax.ppermute(p, ("node", "head"), r) for p, r in zip(far_grads, routes)]
-    mq = exchange(mq)
-    kv_grads = exchange(call(functools.partial(merge_kernel, heads), "merge", [block] * heads, slots, near, *back))
-    unpack = functools.partial(unpack_kernel, heads, places)
-    mixed, query_grad = call(unpack, "unpack", [whole] * 2, *mq)
-    key_grad, value_grad = call(unpack, "unpack", [whole] * 2, *kv_grads)
+    mq = exchange(mq, downward)
+    merged = call(functools.partial(merge_kernel, heads), "merge", [block] * heads, slots, near, *back)
+    kv_grads = exchange(merged, order)
+    unpack = functools.partial(unpack_kernel, heads)
+    mq_places = [(downward.index(d), 0) for d in range(heads)]
+    mixed, query_grad = call(functools.partial(unpack, mq_places), "unpack", [whole] * 2, *mq)
+    key_grad, value_grad = call(functools.partial(unpack, places), "unpack", [whole] * 2, *kv_grads)
     return mixed, query_grad, key_grad, value_grad
 
 

time: 28.3 us -> 28 us (0.989)
  other arithmetic: 0.99 us -> 0 us
  waiting for transfers between devices: 7.56 us -> 6.58 us
  local copies, waits for them, and re-layouts: 0.02 us -> 0.92 us
  starting transfers between devices: 13.4 us -> 14.1 us
    concatenate x1 -> x0, other arithmetic: 0.99 us -> none  [gather_in(): jnp.concatenate(own, 0)]
    ppermute x12, waiting for transfers between devices: 6.1 us -> 5.12 us  [exchange(): lax.ppermute(blocks[d], 'head', swaps[d])]
    dynamic_slice x0 -> x1, local copies, waits for them, and re-layouts: none -> 0.9 us  [cut(): lax.dynamic_slice_in_dim(a, at, width, 1)]
    ppermute x12, starting transfers between devices: 9.25 us -> 9.94 us  [exchange(): lax.ppermute(blocks[d], 'head', swaps[d])]
  transfers between devices with their start and end apart: 16 -> 16, of which waited for: 7 -> 6; matrix products, arithmetic and copies ran while one was open for 0% -> 0% of each run, Pallas kernels for 13% -> 13%
where the time goes in v7:
time: 28 us; the launch traced here: 27.8 us
  starting transfers between devices  14.1 us (50%)
  waiting for transfers between devices  6.58 us (24%)
  Pallas kernels  5.39 us (19%)
  local copies, waits for them, and re-layouts  0.92 us (3%)
  between operations  0.77 us (3%)
    ppermute x12, starting transfers between devices, exchange(): lax.ppermute(blocks[d], 'head', swaps[d])  9.94 us
    pallas_call x11, Pallas kernels, call(): pl.pallas_call(kernel, out_shape=outs, in_specs=specs or [VMEM] * len(arg...  5.39 us
    ppermute x12, waiting for transfers between devices, exchange(): lax.ppermute(blocks[d], 'head', swaps[d])  5.12 us
    ppermute x2, starting transfers between devices, shards(): lax.ppermute(p, ('node', 'head'), r)  2.48 us
    ppermute x2, starting transfers between devices, shards(): far = [lax.ppermute(p, ('node', 'head'), r) for p, r in zip(picked, routes)]  1.7 us
    ppermute x2, waiting for transfers between devices, shards(): far = [lax.ppermute(p, ('node', 'head'), r) for p, r in zip(picked, routes)]  1.45 us
    dynamic_slice x1, local copies, waits for them, and re-layouts, cut(): lax.dynamic_slice_in_dim(a, at, width, 1)  0.9 us
  transfers between devices with their start and end apart: 16, of which 6 were waited for; matrix products, arithmetic and copies ran while one was open for 0% of the time, Pallas kernels for 13%

profile of v7, /device:TPU:0, one launch (start us, length us, event | category | flops | bytes accessed | tf_op | source)
XLA Modules:
  0.0 27.8 jit_solution(13658720604119400696)
XLA Ops:
  0.7 0.9 %constant_dynamic-slice_fusion = (bf16[64,256]{1,0:T(8,128)(2,1)S(1)}, bf16[64,256]{1,0:T(8,128)(2,1)S(1)}, bf16[64,256]{1,0:T(8,128)(2,1)S(1)}, bf16[64,256]{1,...) fusion(bf16[64,1024]{1,0:T(8,128)(2,1)} %param.7, ...), kind=kLoop, calls=%fused_computation | loop fusion | bytes 524304 | tf_op jit(solution)/shard_map/dynamic_slice | solution.py:285
  1.6 0.0 copy-start
  1.6 0.0 copy-start.1
  1.6 0.0 copy-start.2
  1.6 3.0 %collective-permute-start = (bf16[1,2,64,256]{3,2,1,0:T(8,128)(2,1)S(1)}, bf16[1,2,64,256]{3,2,1,0:T(8,128)(2,1)S(1)}, u32[]{:S(2)}, u32[]{:S(2)}) collective-permute-start(bf16[1,2,64,256]{3,2,1,0:T(8,128)(2,1)S(1)} %get-tuple-element.46), channel_id=1, source_target_pairs={{0,2},{1,3},{2,0},{3,1},{4,6},{5,7},{6,4},{7,5},{8,10},{9,11},{10,... | collective-permute-start | bytes 196616 | tf_op jit(solution)/shard_map/ppermute | solution.py:278
  4.6 0.0 collective-permute-start.1
  4.6 0.2 collective-permute-start.2
  4.8 0.0 copy-done.2
  4.8 0.8 %prep.1 = (f32[6,256]{1,0:T(8,128)S(1)}, s32[4,256]{1,0:T(4,128)S(1)}) custom-call(s32[8,8]{1,0:T(8,128)S(1)} %copy-done.2, bf16[1,2,64,256]{3,2,1,0:T(8,128)(2,1)S(1)} %get-tuple-element.44.after_ref.refs_0_), custom_call_target="tpu_custom_call" | custom-call | tf_op jit(solution)/shard_map/prep/pallas_call | solution.py:24
  5.7 0.0 copy-done
  5.7 0.0 copy-done.1
  5.7 2.0 %collective-permute-start.3 = (bf16[1,2,64,256]{3,2,1,0:T(8,128)(2,1)S(1)}, bf16[1,2,64,256]{3,2,1,0:T(8,128)(2,1)S(1)}, u32[]{:S(2)}, u32[]{:S(2)}) collective-permute-start(bf16[1,2,64,256]{3,2,1,0:T(8,128)(2,1)S(1)} %get-tuple-element.51), channel_id=1, source_target_pairs={{0,2},{1,3},{2,0},{3,1},{4,6},{5,7},{6,4},{7,5},{8,10},{9,11},{10,... | collective-permute-start | bytes 196616 | tf_op jit(solution)/shard_map/ppermute | solution.py:278
  7.8 0.0 collective-permute-start.4
  7.8 0.0 collective-permute-done.refs_1_
  7.8 0.2 collective-permute-start.5
  8.0 0.8 %collective-permute-done.1.refs_2_ = bf16[1,2,64,256]{3,2,1,0:T(8,128)(2,1)S(1)} collective-permute-done((bf16[1,2,64,256]{3,2,1,0:T(8,128)(2,1)S(1)}, bf16[1,2,64,256]{3,2,1,0:T(8,128)(2,1)S(1)}, u32[]{:S(2)}, u32[]{:S(2)}) %collective-permute-start.1) | collective-permute-done | bytes 65568 | tf_op jit(solution)/shard_map/ppermute | solution.py:278
  8.8 0.0 collective-permute-done.2.refs_3_
  8.8 0.1 pick.1
  8.9 1.7 %collective-permute-start.6 = (bf16[2,128,256]{2,1,0:T(8,128)(2,1)S(1)}, bf16[2,128,256]{2,1,0:T(8,128)(2,1)S(1)}, u32[]{:S(2)}, u32[]{:S(2)}) collective-permute-start(bf16[2,128,256]{2,1,0:T(8,128)(2,1)S(1)} %get-tuple-element.57), channel_id=1, source_target_pairs={{0,4},{1,5},{2,6},{3,7},{4,0},{5,1},{6,2},{7,3},{8,12},{9,13},{10,... | collective-permute-start | bytes 393224 | tf_op jit(solution)/shard_map/ppermute | solution.py:319
  10.6 0.0 collective-permute-start.7
  10.6 0.0 collective-permute-done.3.refs_5_
  10.6 1.5 %collective-permute-done.4.refs_6_ = bf16[1,2,64,256]{3,2,1,0:T(8,128)(2,1)S(1)} collective-permute-done((bf16[1,2,64,256]{3,2,1,0:T(8,128)(2,1)S(1)}, bf16[1,2,64,256]{3,2,1,0:T(8,128)(2,1)S(1)}, u32[]{:S(2)}, u32[]{:S(2)}) %collective-permute-start.4) | collective-permute-done | bytes 65568 | tf_op jit(solution)/shard_map/ppermute | solution.py:278
  12.1 0.0 collective-permute-done.5.refs_7_
  12.1 0.7 %near.1 = (f32[256,1024]{1,0:T(8,128)S(1)}, f32[256,1024]{1,0:T(8,128)S(1)}, f32[3,1024]{1,0:T(4,128)S(1)}, bf16[1024,256]{1,0:T(8,128)(2,1)S(1)}, bf16[256,1024...) custom-call(f32[6,256]{1,0:T(8,128)S(1)} %get-tuple-element.45.bias_ref, ...), custom_call_target="tpu_custom_call" | custom-call | flops 1500000000 | bytes 1 | tf_op jit(solution)/shard_map/near/pallas_call | solution.py:24
  12.7 1.4 %collective-permute-done.6.keys_ref.refs_4_ = bf16[2,128,256]{2,1,0:T(8,128)(2,1)S(1)} collective-permute-done((bf16[2,128,256]{2,1,0:T(8,128)(2,1)S(1)}, bf16[2,128,256]{2,1,0:T(8,128)(2,1)S(1)}, u32[]{:S(2)}, u32[]{:S(2)}) %collective-permute-start.6) | collective-permute-done | bytes 131104 | tf_op jit(solution)/shard_map/ppermute | solution.py:319
  14.2 0.4 %first.1 = (f32[128,1024]{1,0:T(8,128)S(1)}, f32[128,1024]{1,0:T(8,128)S(1)}, f32[3,1024]{1,0:T(4,128)S(1)}) custom-call(f32[6,256]{1,0:T(8,128)S(1)} %get-tuple-element.45.bias_ref, bf16[256,1024]{1,0:T(8,128)(2,1)S(1)} %get-tuple-element.55.query_across, bf16[256,1024]{1,0:T(8,128)(2,1)S(1)} %get-tuple-element.56.grad_across.refs_0_, ...), custom_call_target="tpu_custom_call" | custom-call | tf_op jit(solution)/shard_map/first/pallas_call | solution.py:24
  14.6 0.0 collective-permute-done.7.refs_1_.refs_5_
  14.6 0.9 %far.1 = (bf16[256,1024]{1,0:T(8,128)(2,1)S(1)}, bf16[256,1024]{1,0:T(8,128)(2,1)S(1)}, f32[2,1024]{1,0:T(2,128)S(1)}, bf16[2,128,256]{2,1,0:T(8,128)(2,1)S(1)}, bf16[2,128,256]{2,1,0:T(8,128)(2,1)S(1)}) custom-call(f32[6,256]{1,0:T(8,128)S(1)} %get-tuple-element.45.bias_ref, f32[3,1024]{1,0:T(4,128)S(1)} %get-tuple-element.54.stat_ref, ...), custom_call_target="tpu_custom_call" | custom-call | flops 1500000000 | bytes 1 | tf_op jit(solution)/shard_map/far/pallas_call | solution.py:24
  15.5 2.5 %collective-permute-start.11 = (bf16[2,128,256]{2,1,0:T(8,128)(2,1)S(1)}, bf16[2,128,256]{2,1,0:T(8,128)(2,1)S(1)}, u32[]{:S(2)}, u32[]{:S(2)}) collective-permute-start(bf16[2,128,256]{2,1,0:T(8,128)(2,1)S(1)} %get-tuple-element.76), channel_id=1, source_target_pairs={{0,4},{1,5},{2,6},{3,7},{4,0},{5,1},{6,2},{7,3},{8,12},{9,13},{10,... | collective-permute-start | bytes 393224 | tf_op jit(solution)/shard_map/ppermute | solution.py:374
  18.0 0.0 collective-permute-start.12
  18.0 0.8 %rest.1 = (bf16[1,2,64,256]{3,2,1,0:T(8,128)(2,1)S(1)}, bf16[1,2,64,256]{3,2,1,0:T(8,128)(2,1)S(1)}, bf16[1,2,64,256]{3,2,1,0:T(8,128)(2,1)S(1)}, bf16[1,2,64,25...) custom-call(f32[2,1024]{1,0:T(2,128)S(1)} %get-tuple-element.64.final_ref, f32[256,1024]{1,0:T(8,128)S(1)} %get-tuple-element.65.exps_ref, ...), custom_call_target="tpu_custom_call" | custom-call | flops 1500000000 | bytes 1 | tf_op jit(solution)/shard_map/rest/pallas_call | solution.py:24
  18.8 1.5 %collective-permute-start.8 = (bf16[1,2,64,256]{3,2,1,0:T(8,128)(2,1)S(1)}, bf16[1,2,64,256]{3,2,1,0:T(8,128)(2,1)S(1)}, u32[]{:S(2)}, u32[]{:S(2)}) collective-permute-start(bf16[1,2,64,256]{3,2,1,0:T(8,128)(2,1)S(1)} %get-tuple-element.70), channel_id=1, source_target_pairs={{0,3},{1,2},{2,1},{3,0},{4,7},{5,6},{6,5},{7,4},{8,11},{9,10},{10,... | collective-permute-start | bytes 196616 | tf_op jit(solution)/shard_map/ppermute | solution.py:278
  20.3 0.7 %collective-permute-start.9 = (bf16[1,2,64,256]{3,2,1,0:T(8,128)(2,1)S(1)}, bf16[1,2,64,256]{3,2,1,0:T(8,128)(2,1)S(1)}, u32[]{:S(2)}, u32[]{:S(2)}) collective-permute-start(bf16[1,2,64,256]{3,2,1,0:T(8,128)(2,1)S(1)} %get-tuple-element.71), channel_id=1, source_target_pairs={{0,2},{1,3},{2,0},{3,1},{4,6},{5,7},{6,4},{7,5},{8,10},{9,11},{10,... | collective-permute-start | bytes 196616 | tf_op jit(solution)/shard_map/ppermute | solution.py:278
  21.0 0.0 collective-permute-start.10
  21.0 0.0 collective-permute-done.11.back_a
  21.0 0.0 collective-permute-done.12.back_b
  21.0 0.1 merge.1
  21.2 1.4 %collective-permute-start.13 = (bf16[1,2,64,256]{3,2,1,0:T(8,128)(2,1)S(1)}, bf16[1,2,64,256]{3,2,1,0:T(8,128)(2,1)S(1)}, u32[]{:S(2)}, u32[]{:S(2)}) collective-permute-start(bf16[1,2,64,256]{3,2,1,0:T(8,128)(2,1)S(1)} %get-tuple-element.79), channel_id=1, source_target_pairs={{0,2},{1,3},{2,0},{3,1},{4,6},{5,7},{6,4},{7,5},{8,10},{9,11},{10,... | collective-permute-start | bytes 196616 | tf_op jit(solution)/shard_map/ppermute | solution.py:278
  22.6 0.5 %collective-permute-start.14 = (bf16[1,2,64,256]{3,2,1,0:T(8,128)(2,1)S(1)}, bf16[1,2,64,256]{3,2,1,0:T(8,128)(2,1)S(1)}, u32[]{:S(2)}, u32[]{:S(2)}) collective-permute-start(bf16[1,2,64,256]{3,2,1,0:T(8,128)(2,1)S(1)} %get-tuple-element.80), channel_id=1, source_target_pairs={{0,3},{1,2},{2,1},{3,0},{4,7},{5,6},{6,5},{7,4},{8,11},{9,10},{10,... | collective-permute-start | bytes 196616 | tf_op jit(solution)/shard_map/ppermute | solution.py:278
  23.1 0.0 collective-permute-done.8.refs_1_
  23.1 0.4 %collective-permute-start.15 = (bf16[1,2,64,256]{3,2,1,0:T(8,128)(2,1)S(1)}, bf16[1,2,64,256]{3,2,1,0:T(8,128)(2,1)S(1)}, u32[]{:S(2)}, u32[]{:S(2)}) collective-permute-start(bf16[1,2,64,256]{3,2,1,0:T(8,128)(2,1)S(1)} %get-tuple-element.81), channel_id=1, source_target_pairs={{0,1},{1,0},{2,3},{3,2},{4,5},{5,4},{6,7},{7,6},{8,9},{9,8},{10,11... | collective-permute-start | bytes 196616 | tf_op jit(solution)/shard_map/ppermute | solution.py:278
  23.5 1.6 %collective-permute-done.9.refs_2_ = bf16[1,2,64,256]{3,2,1,0:T(8,128)(2,1)S(1)} collective-permute-done((bf16[1,2,64,256]{3,2,1,0:T(8,128)(2,1)S(1)}, bf16[1,2,64,256]{3,2,1,0:T(8,128)(2,1)S(1)}, u32[]{:S(2)}, u32[]{:S(2)}) %collective-permute-start.9) | collective-permute-done | bytes 65568 | tf_op jit(solution)/shard_map/ppermute | solution.py:278
  25.1 0.0 collective-permute-done.10.refs_3_
  25.1 0.7 %unpack.2 = (bf16[64,1024]{1,0:T(8,128)(2,1)}, bf16[64,1024]{1,0:T(8,128)(2,1)}) custom-call(bf16[1,2,64,256]{3,2,1,0:T(8,128)(2,1)S(1)} %get-tuple-element.69.refs_0_, bf16[1,2,64,256]{3,2,1,0:T(8,128)(2,1)S(1)} %collective-permute-done.8.refs_1_, bf16[1,2,64,256]{3,2,1,0:T(8,128)(2,1)S(1)} %collective-permute-done.9.refs_2_, ...), custom_call_target="tpu_custom_call" | custom-call | tf_op jit(solution)/shard_map/unpack/pallas_call | solution.py:24
  25.8 0.7 %collective-permute-done.13.refs_1_ = bf16[1,2,64,256]{3,2,1,0:T(8,128)(2,1)S(1)} collective-permute-done((bf16[1,2,64,256]{3,2,1,0:T(8,128)(2,1)S(1)}, bf16[1,2,64,256]{3,2,1,0:T(8,128)(2,1)S(1)}, u32[]{:S(2)}, u32[]{:S(2)}) %collective-permute-start.13) | collective-permute-done | bytes 65568 | tf_op jit(solution)/shard_map/ppermute | solution.py:278
  26.5 0.5 %collective-permute-done.14.refs_2_ = bf16[1,2,64,256]{3,2,1,0:T(8,128)(2,1)S(1)} collective-permute-done((bf16[1,2,64,256]{3,2,1,0:T(8,128)(2,1)S(1)}, bf16[1,2,64,256]{3,2,1,0:T(8,128)(2,1)S(1)}, u32[]{:S(2)}, u32[]{:S(2)}) %collective-permute-start.14) | collective-permute-done | bytes 65568 | tf_op jit(solution)/shard_map/ppermute | solution.py:278
  27.0 0.0 collective-permute-done.15.refs_3_
  27.0 0.7 %unpack.3 = (bf16[64,1024]{1,0:T(8,128)(2,1)}, bf16[64,1024]{1,0:T(8,128)(2,1)}) custom-call(bf16[1,2,64,256]{3,2,1,0:T(8,128)(2,1)S(1)} %get-tuple-element.78.refs_0_, bf16[1,2,64,256]{3,2,1,0:T(8,128)(2,1)S(1)} %collective-permute-done.13.refs_1_, bf16[1,2,64,256]{3,2,1,0:T(8,128)(2,1)S(1)} %collective-permute-done.14.refs_2_, ...), custom_call_target="tpu_custom_call" | custom-call | tf_op jit(solution)/shard_map/unpack/pallas_call | solution.py:24
  (2 shorter events, 0.1 us)
Async XLA Ops:
  1.6 4.1 %copy-start = (bf16[64,1024]{1,0:T(8,128)(2,1)S(1)}, bf16[64,1024]{1,0:T(8,128)(2,1)}, u32[]{:S(2)}) copy-start(bf16[64,1024]{1,0:T(8,128)(2,1)} %one.1) | copy-start | bytes 393220
  1.6 4.1 %copy-start.1 = (bf16[64,1024]{1,0:T(8,128)(2,1)S(1)}, bf16[64,1024]{1,0:T(8,128)(2,1)}, u32[]{:S(2)}) copy-start(bf16[64,1024]{1,0:T(8,128)(2,1)} %two.1) | copy-start | bytes 393220
  1.6 3.2 %copy-start.2 = (s32[8,8]{1,0:T(8,128)S(1)}, s32[8,8]{1,0:T(8,128)}, u32[]{:S(2)}) copy-start(s32[8,8]{1,0:T(8,128)} %nbr_ref.1) | copy-start | bytes 772
  1.6 6.1 %collective-permute-start = (bf16[1,2,64,256]{3,2,1,0:T(8,128)(2,1)S(1)}, bf16[1,2,64,256]{3,2,1,0:T(8,128)(2,1)S(1)}, u32[]{:S(2)}, u32[]{:S(2)}) collective-permute-start(bf16[1,2,64,256]{3,2,1,0:T(8,128)(2,1)S(1)} %get-tuple-element.46), channel_id=1, source_target_pairs={{0,2},{1,3},{2,0},{3,1},{4,6},{5,7},{6,4},{7,5},{8,10},{9,11},{10,... | collective-permute-start | bytes 196616 | tf_op jit(solution)/shard_map/ppermute | solution.py:278
  4.6 4.1 %collective-permute-start.1 = (bf16[1,2,64,256]{3,2,1,0:T(8,128)(2,1)S(1)}, bf16[1,2,64,256]{3,2,1,0:T(8,128)(2,1)S(1)}, u32[]{:S(2)}, u32[]{:S(2)}) collective-permute-start(bf16[1,2,64,256]{3,2,1,0:T(8,128)(2,1)S(1)} %get-tuple-element.47), channel_id=1, source_target_pairs={{0,3},{1,2},{2,1},{3,0},{4,7},{5,6},{6,5},{7,4},{8,11},{9,10},{10,... | collective-permute-start | bytes 196616 | tf_op jit(solution)/shard_map/ppermute | solution.py:278
  4.6 4.1 %collective-permute-start.2 = (bf16[1,2,64,256]{3,2,1,0:T(8,128)(2,1)S(1)}, bf16[1,2,64,256]{3,2,1,0:T(8,128)(2,1)S(1)}, u32[]{:S(2)}, u32[]{:S(2)}) collective-permute-start(bf16[1,2,64,256]{3,2,1,0:T(8,128)(2,1)S(1)} %get-tuple-element.48), channel_id=1, source_target_pairs={{0,1},{1,0},{2,3},{3,2},{4,5},{5,4},{6,7},{7,6},{8,9},{9,8},{10,11... | collective-permute-start | bytes 196616 | tf_op jit(solution)/shard_map/ppermute | solution.py:278
  5.7 4.8 %collective-permute-start.3 = (bf16[1,2,64,256]{3,2,1,0:T(8,128)(2,1)S(1)}, bf16[1,2,64,256]{3,2,1,0:T(8,128)(2,1)S(1)}, u32[]{:S(2)}, u32[]{:S(2)}) collective-permute-start(bf16[1,2,64,256]{3,2,1,0:T(8,128)(2,1)S(1)} %get-tuple-element.51), channel_id=1, source_target_pairs={{0,2},{1,3},{2,0},{3,1},{4,6},{5,7},{6,4},{7,5},{8,10},{9,11},{10,... | collective-permute-start | bytes 196616 | tf_op jit(solution)/shard_map/ppermute | solution.py:278
  7.8 4.3 %collective-permute-start.4 = (bf16[1,2,64,256]{3,2,1,0:T(8,128)(2,1)S(1)}, bf16[1,2,64,256]{3,2,1,0:T(8,128)(2,1)S(1)}, u32[]{:S(2)}, u32[]{:S(2)}) collective-permute-start(bf16[1,2,64,256]{3,2,1,0:T(8,128)(2,1)S(1)} %get-tuple-element.52), channel_id=1, source_target_pairs={{0,3},{1,2},{2,1},{3,0},{4,7},{5,6},{6,5},{7,4},{8,11},{9,10},{10,... | collective-permute-start | bytes 196616 | tf_op jit(solution)/shard_map/ppermute | solution.py:278
  7.8 4.3 %collective-permute-start.5 = (bf16[1,2,64,256]{3,2,1,0:T(8,128)(2,1)S(1)}, bf16[1,2,64,256]{3,2,1,0:T(8,128)(2,1)S(1)}, u32[]{:S(2)}, u32[]{:S(2)}) collective-permute-start(bf16[1,2,64,256]{3,2,1,0:T(8,128)(2,1)S(1)} %get-tuple-element.53), channel_id=1, source_target_pairs={{0,1},{1,0},{2,3},{3,2},{4,5},{5,4},{6,7},{7,6},{8,9},{9,8},{10,11... | collective-permute-start | bytes 196616 | tf_op jit(solution)/shard_map/ppermute | solution.py:278
  8.9 5.3 %collective-permute-start.6 = (bf16[2,128,256]{2,1,0:T(8,128)(2,1)S(1)}, bf16[2,128,256]{2,1,0:T(8,128)(2,1)S(1)}, u32[]{:S(2)}, u32[]{:S(2)}) collective-permute-start(bf16[2,128,256]{2,1,0:T(8,128)(2,1)S(1)} %get-tuple-element.57), channel_id=1, source_target_pairs={{0,4},{1,5},{2,6},{3,7},{4,0},{5,1},{6,2},{7,3},{8,12},{9,13},{10,... | collective-permute-start | bytes 393224 | tf_op jit(solution)/shard_map/ppermute | solution.py:319
  10.6 4.0 %collective-permute-start.7 = (bf16[2,128,256]{2,1,0:T(8,128)(2,1)S(1)}, bf16[2,128,256]{2,1,0:T(8,128)(2,1)S(1)}, u32[]{:S(2)}, u32[]{:S(2)}) collective-permute-start(bf16[2,128,256]{2,1,0:T(8,128)(2,1)S(1)} %get-tuple-element.63), channel_id=1, source_target_pairs={{0,1},{1,0},{2,3},{3,2},{4,8},{5,9},{6,10},{7,11},{8,4},{9,5},{10,... | collective-permute-start | bytes 393224 | tf_op jit(solution)/shard_map/ppermute | solution.py:319
  15.5 5.5 %collective-permute-start.11 = (bf16[2,128,256]{2,1,0:T(8,128)(2,1)S(1)}, bf16[2,128,256]{2,1,0:T(8,128)(2,1)S(1)}, u32[]{:S(2)}, u32[]{:S(2)}) collective-permute-start(bf16[2,128,256]{2,1,0:T(8,128)(2,1)S(1)} %get-tuple-element.76), channel_id=1, source_target_pairs={{0,4},{1,5},{2,6},{3,7},{4,0},{5,1},{6,2},{7,3},{8,12},{9,13},{10,... | collective-permute-start | bytes 393224 | tf_op jit(solution)/shard_map/ppermute | solution.py:374
  18.0 3.0 %collective-permute-start.12 = (bf16[2,128,256]{2,1,0:T(8,128)(2,1)S(1)}, bf16[2,128,256]{2,1,0:T(8,128)(2,1)S(1)}, u32[]{:S(2)}, u32[]{:S(2)}) collective-permute-start(bf16[2,128,256]{2,1,0:T(8,128)(2,1)S(1)} %get-tuple-element.77), channel_id=1, source_target_pairs={{0,1},{1,0},{2,3},{3,2},{4,8},{5,9},{6,10},{7,11},{8,4},{9,5},{10,... | collective-permute-start | bytes 393224 | tf_op jit(solution)/shard_map/ppermute | solution.py:374
  18.8 4.3 %collective-permute-start.8 = (bf16[1,2,64,256]{3,2,1,0:T(8,128)(2,1)S(1)}, bf16[1,2,64,256]{3,2,1,0:T(8,128)(2,1)S(1)}, u32[]{:S(2)}, u32[]{:S(2)}) collective-permute-start(bf16[1,2,64,256]{3,2,1,0:T(8,128)(2,1)S(1)} %get-tuple-element.70), channel_id=1, source_target_pairs={{0,3},{1,2},{2,1},{3,0},{4,7},{5,6},{6,5},{7,4},{8,11},{9,10},{10,... | collective-permute-start | bytes 196616 | tf_op jit(solution)/shard_map/ppermute | solution.py:278
  20.3 4.8 %collective-permute-start.9 = (bf16[1,2,64,256]{3,2,1,0:T(8,128)(2,1)S(1)}, bf16[1,2,64,256]{3,2,1,0:T(8,128)(2,1)S(1)}, u32[]{:S(2)}, u32[]{:S(2)}) collective-permute-start(bf16[1,2,64,256]{3,2,1,0:T(8,128)(2,1)S(1)} %get-tuple-element.71), channel_id=1, source_target_pairs={{0,2},{1,3},{2,0},{3,1},{4,6},{5,7},{6,4},{7,5},{8,10},{9,11},{10,... | collective-permute-start | bytes 196616 | tf_op jit(solution)/shard_map/ppermute | solution.py:278
  21.0 4.1 %collective-permute-start.10 = (bf16[1,2,64,256]{3,2,1,0:T(8,128)(2,1)S(1)}, bf16[1,2,64,256]{3,2,1,0:T(8,128)(2,1)S(1)}, u32[]{:S(2)}, u32[]{:S(2)}) collective-permute-start(bf16[1,2,64,256]{3,2,1,0:T(8,128)(2,1)S(1)} %get-tuple-element.72), channel_id=1, source_target_pairs={{0,1},{1,0},{2,3},{3,2},{4,5},{5,4},{6,7},{7,6},{8,9},{9,8},{10,11... | collective-permute-start | bytes 196616 | tf_op jit(solution)/shard_map/ppermute | solution.py:278
  21.2 5.3 %collective-permute-start.13 = (bf16[1,2,64,256]{3,2,1,0:T(8,128)(2,1)S(1)}, bf16[1,2,64,256]{3,2,1,0:T(8,128)(2,1)S(1)}, u32[]{:S(2)}, u32[]{:S(2)}) collective-permute-start(bf16[1,2,64,256]{3,2,1,0:T(8,128)(2,1)S(1)} %get-tuple-element.79), channel_id=1, source_target_pairs={{0,2},{1,3},{2,0},{3,1},{4,6},{5,7},{6,4},{7,5},{8,10},{9,11},{10,... | collective-permute-start | bytes 196616 | tf_op jit(solution)/shard_map/ppermute | solution.py:278
  22.6 4.5 %collective-permute-start.14 = (bf16[1,2,64,256]{3,2,1,0:T(8,128)(2,1)S(1)}, bf16[1,2,64,256]{3,2,1,0:T(8,128)(2,1)S(1)}, u32[]{:S(2)}, u32[]{:S(2)}) collective-permute-start(bf16[1,2,64,256]{3,2,1,0:T(8,128)(2,1)S(1)} %get-tuple-element.80), channel_id=1, source_target_pairs={{0,3},{1,2},{2,1},{3,0},{4,7},{5,6},{6,5},{7,4},{8,11},{9,10},{10,... | collective-permute-start | bytes 196616 | tf_op jit(solution)/shard_map/ppermute | solution.py:278
  23.1 4.0 %collective-permute-start.15 = (bf16[1,2,64,256]{3,2,1,0:T(8,128)(2,1)S(1)}, bf16[1,2,64,256]{3,2,1,0:T(8,128)(2,1)S(1)}, u32[]{:S(2)}, u32[]{:S(2)}) collective-permute-start(bf16[1,2,64,256]{3,2,1,0:T(8,128)(2,1)S(1)} %get-tuple-element.81), channel_id=1, source_target_pairs={{0,1},{1,0},{2,3},{3,2},{4,5},{5,4},{6,7},{7,6},{8,9},{9,8},{10,11... | collective-permute-start | bytes 196616 | tf_op jit(solution)/shard_map/ppermute | solution.py:278

commit v8 on v7

--- a/solution.py
+++ b/solution.py
@@ -33,12 +33,17 @@
     )(*args)
 
 
+def partners(node):
+    turn = 1 - 2 * (node % 2)
+    return node + turn, node - turn
+
+
 def pair_routes(owners, heads):
     routes = []
-    for step in (1, -1):
+    for step in range(2):
         route = []
         for n in range(owners):
-            other = n + step * (1 - 2 * (n % 2))
+            other = partners(n)[step]
             for h in range(heads):
                 target = other * heads + h if 0 <= other < owners else n * heads + (h ^ 1)
                 route.append((n * heads + h, target))
@@ -48,8 +53,7 @@
 
 def prep_kernel(heads, owners, local_count, per_patch, rows, nbr_ref, after_ref, bias_ref, slot_ref):
     me, node = lax.axis_index("head"), lax.axis_index("node")
-    odd = lax.rem(node, 2)
-    pair = (node + 1 - 2 * odd, node - 1 + 2 * odd)
+    pair = partners(node)
     queries = heads * rows
     own = [[jnp.int32(p == k) for k in range(local_count)] for p in range(local_count)]
     out_of = [[jnp.int32(0), jnp.int32(0)] for _ in range(local_count)]
@@ -177,37 +181,60 @@
         stat_ref[2:3, lanes] = jnp.sum(exps * grad_weights, 0, keepdims=True)
 
 
-def far_kernel(heads, bias_ref, stat_ref, exps_ref, gw_ref, first_ref, query_down, query_across, grad_down, *refs):
+def far_kernel(heads, owners, bias_ref, stat_ref, exps_ref, gw_ref, first_ref, query_down, query_across, grad_down, *refs):
     grad_across, second_ref, w_ref, ds_ref, final_ref, far_a, far_b = refs
     patch, width = second_ref.shape[1:]
     queries = bias_ref.shape[1]
-    bias = spread(bias_ref, heads + 1, [patch])
-    for head in range(width // HEAD_DIM):
-        lanes = slice(head * queries, (head + 1) * queries)
-        near_top, first_top = stat_ref[0:1, lanes], first_ref[0:1, lanes]
-        scores = dot(second_ref[0], query_across[:, lanes]) * SCORE_SCALE + bias
-        top = jnp.maximum(jnp.maximum(near_top, first_top), jnp.max(scores, 0, keepdims=True))
-        exps = jnp.exp2(scores - top)
-        shrink, first_shrink = jnp.exp2(near_top - top), jnp.exp2(first_top - top)
-        grad_weights = dot(second_ref[1], grad_across[:, lanes])
-        total = shrink * stat_ref[1:2, lanes] + first_shrink * first_ref[1:2, lanes]
-        part = 1.0 / (total + jnp.sum(exps, 0, keepdims=True))
-        weights = exps * part
-        shrink, first_shrink = shrink * part, first_shrink * part
-        row_dots = shrink * stat_ref[2:3, lanes] + first_shrink * first_ref[2:3, lanes]
-        row_dots = row_dots + jnp.sum(weights * grad_weights, 0, keepdims=True)
-        w_ref[patch:, lanes] = weights.astype(LOW)
-        ds_ref[patch:, lanes] = (weights * (grad_weights - row_dots)).astype(LOW)
-        weights = exps_ref[:, lanes] * first_shrink
-        w_ref[:patch, lanes] = weights.astype(LOW)
-        ds_ref[:patch, lanes] = (weights * (gw_ref[:, lanes] - row_dots)).astype(LOW)
-        final_ref[0:1, lanes] = shrink
-        final_ref[1:2, lanes] = row_dots
-    key_grad = dot(ds_ref[...], query_down[...]) * HEAD_DIM**-0.5
-    value_grad = dot(w_ref[...], grad_down[...])
-    for s, out in enumerate((far_a, far_b)):
-        span = slice(s * patch, (s + 1) * patch)
-        out[0], out[1] = key_grad[span].astype(LOW), value_grad[span].astype(LOW)
+    node = lax.axis_index("node")
+    other = partners(node)[1]
+    both = jnp.logical_and(other >= 0, other < owners)
+
+    def softmax(second):
+        bias = spread(bias_ref, heads + 1, [patch]) if second else None
+        for head in range(width // HEAD_DIM):
+            lanes = slice(head * queries, (head + 1) * queries)
+            near_top, first_top = stat_ref[0:1, lanes], first_ref[0:1, lanes]
+            top = jnp.maximum(near_top, first_top)
+            if second:
+                scores = dot(second_ref[0], query_across[:, lanes]) * SCORE_SCALE + bias
+                top = jnp.maximum(top, jnp.max(scores, 0, keepdims=True))
+                exps = jnp.exp2(scores - top)
+                grad_weights = dot(second_ref[1], grad_across[:, lanes])
+            shrink, first_shrink = jnp.exp2(near_top - top), jnp.exp2(first_top - top)
+            total = shrink * stat_ref[1:2, lanes] + first_shrink * first_ref[1:2, lanes]
+            if second:
+                total = total + jnp.sum(exps, 0, keepdims=True)
+            part = 1.0 / total
+            shrink, first_shrink = shrink * part, first_shrink * part
+            row_dots = shrink * stat_ref[2:3, lanes] + first_shrink * first_ref[2:3, lanes]
+            if second:
+                weights = exps * part
+                row_dots = row_dots + jnp.sum(weights * grad_weights, 0, keepdims=True)
+                w_ref[patch:, lanes] = weights.astype(LOW)
+                ds_ref[patch:, lanes] = (weights * (grad_weights - row_dots)).astype(LOW)
+            weights = exps_ref[:, lanes] * first_shrink
+            w_ref[:patch, lanes] = weights.astype(LOW)
+            ds_ref[:patch, lanes] = (weights * (gw_ref[:, lanes] - row_dots)).astype(LOW)
+            final_ref[0:1, lanes] = shrink
+            final_ref[1:2, lanes] = row_dots
+
+    @pl.when(both)
+    def _():
+        softmax(True)
+        key_grad = dot(ds_ref[...], query_down[...]) * HEAD_DIM**-0.5
+        value_grad = dot(w_ref[...], grad_down[...])
+        for s, out in enumerate((far_a, far_b)):
+            span = slice(s * patch, (s + 1) * patch)
+            out[0], out[1] = key_grad[span].astype(LOW), value_grad[span].astype(LOW)
+
+    @pl.when(jnp.logical_not(both))
+    def _():
+        softmax(False)
+        far_a[0] = (dot(ds_ref[:patch, :], query_down[...]) * HEAD_DIM**-0.5).astype(LOW)
+        far_a[1] = dot(w_ref[:patch, :], grad_down[...]).astype(LOW)
+        far_b[...] = jnp.zeros_like(far_b)
+        w_ref[patch:, :] = jnp.zeros((patch, w_ref.shape[1]), LOW)
+        ds_ref[patch:, :] = jnp.zeros((patch, ds_ref.shape[1]), LOW)
 
 
 def rest_kernel(heads, places, final_ref, exps_ref, gw_ref, far_w_ref, far_ds_ref, query_down, grad_down, *refs):
@@ -345,7 +372,7 @@
         far[0],
     )
     far_w, far_ds, final, *far_grads = call(
-        functools.partial(far_kernel, heads),
+        functools.partial(far_kernel, heads, owners),
         "far",
         [table(other, LOW), table(other, LOW), table(2), slab, slab],
         bias,

time: 28 us -> 28 us (level)
  Pallas kernels: 5.39 us -> 4.88 us
  starting transfers between devices: 14.1 us -> 14.6 us
    ppermute x2, starting transfers between devices: 2.48 us -> 3 us  [shards(): lax.ppermute(p, ('node', 'head'), r)]
    pallas_call x11, Pallas kernels: 5.39 us -> 4.88 us  [call(): pl.pallas_call(kernel, out_shape=outs, in_specs=specs or [VMEM] * len(arg...]
where the time goes in v8:
time: 28 us; the launch traced here: 27.8 us
  starting transfers between devices  14.6 us (52%)
  waiting for transfers between devices  6.58 us (24%)
  Pallas kernels  4.88 us (17%)
  local copies, waits for them, and re-layouts  0.92 us (3%)
  between operations  0.77 us (3%)
    ppermute x12, starting transfers between devices, exchange(): lax.ppermute(blocks[d], 'head', swaps[d])  9.93 us
    ppermute x12, waiting for transfers between devices, exchange(): lax.ppermute(blocks[d], 'head', swaps[d])  5.13 us
    pallas_call x11, Pallas kernels, call(): pl.pallas_call(kernel, out_shape=outs, in_specs=specs or [VMEM] * len(arg...  4.88 us
    ppermute x2, starting transfers between devices, shards(): lax.ppermute(p, ('node', 'head'), r)  3 us
    ppermute x2, starting transfers between devices, shards(): far = [lax.ppermute(p, ('node', 'head'), r) for p, r in zip(picked, routes)]  1.7 us
    ppermute x2, waiting for transfers between devices, shards(): far = [lax.ppermute(p, ('node', 'head'), r) for p, r in zip(picked, routes)]  1.45 us
    dynamic_slice x1, local copies, waits for them, and re-layouts, cut(): lax.dynamic_slice_in_dim(a, at, width, 1)  0.9 us
  transfers between devices with their start and end apart: 16, of which 6 were waited for; matrix products, arithmetic and copies ran while one was open for 0% of the time, Pallas kernels for 13%

profile of v8, /device:TPU:0, one launch (start us, length us, event | category | flops | bytes accessed | tf_op | source)
XLA Modules:
  0.0 27.8 jit_solution(12316556216997444308)
XLA Ops:
  0.7 0.9 %constant_dynamic-slice_fusion = (bf16[64,256]{1,0:T(8,128)(2,1)S(1)}, bf16[64,256]{1,0:T(8,128)(2,1)S(1)}, bf16[64,256]{1,0:T(8,128)(2,1)S(1)}, bf16[64,256]{1,...) fusion(bf16[64,1024]{1,0:T(8,128)(2,1)} %param.7, ...), kind=kLoop, calls=%fused_computation | loop fusion | bytes 524304 | tf_op jit(solution)/shard_map/dynamic_slice | solution.py:312
  1.6 0.0 copy-start
  1.6 0.0 copy-start.1
  1.6 0.0 copy-start.2
  1.6 3.0 %collective-permute-start = (bf16[1,2,64,256]{3,2,1,0:T(8,128)(2,1)S(1)}, bf16[1,2,64,256]{3,2,1,0:T(8,128)(2,1)S(1)}, u32[]{:S(2)}, u32[]{:S(2)}) collective-permute-start(bf16[1,2,64,256]{3,2,1,0:T(8,128)(2,1)S(1)} %get-tuple-element.46), channel_id=1, source_target_pairs={{0,2},{1,3},{2,0},{3,1},{4,6},{5,7},{6,4},{7,5},{8,10},{9,11},{10,... | collective-permute-start | bytes 196616 | tf_op jit(solution)/shard_map/ppermute | solution.py:305
  4.6 0.0 collective-permute-start.1
  4.6 0.2 collective-permute-start.2
  4.8 0.0 copy-done.2
  4.8 0.8 %prep.1 = (f32[6,256]{1,0:T(8,128)S(1)}, s32[4,256]{1,0:T(4,128)S(1)}) custom-call(s32[8,8]{1,0:T(8,128)S(1)} %copy-done.2, bf16[1,2,64,256]{3,2,1,0:T(8,128)(2,1)S(1)} %get-tuple-element.44.after_ref.refs_0_), custom_call_target="tpu_custom_call" | custom-call | tf_op jit(solution)/shard_map/prep/pallas_call | solution.py:24
  5.7 0.0 copy-done
  5.7 0.0 copy-done.1
  5.7 2.0 %collective-permute-start.3 = (bf16[1,2,64,256]{3,2,1,0:T(8,128)(2,1)S(1)}, bf16[1,2,64,256]{3,2,1,0:T(8,128)(2,1)S(1)}, u32[]{:S(2)}, u32[]{:S(2)}) collective-permute-start(bf16[1,2,64,256]{3,2,1,0:T(8,128)(2,1)S(1)} %get-tuple-element.51), channel_id=1, source_target_pairs={{0,2},{1,3},{2,0},{3,1},{4,6},{5,7},{6,4},{7,5},{8,10},{9,11},{10,... | collective-permute-start | bytes 196616 | tf_op jit(solution)/shard_map/ppermute | solution.py:305
  7.8 0.0 collective-permute-start.4
  7.8 0.0 collective-permute-done.refs_1_
  7.8 0.2 collective-permute-start.5
  8.0 0.8 %collective-permute-done.1.refs_2_ = bf16[1,2,64,256]{3,2,1,0:T(8,128)(2,1)S(1)} collective-permute-done((bf16[1,2,64,256]{3,2,1,0:T(8,128)(2,1)S(1)}, bf16[1,2,64,256]{3,2,1,0:T(8,128)(2,1)S(1)}, u32[]{:S(2)}, u32[]{:S(2)}) %collective-permute-start.1) | collective-permute-done | bytes 65568 | tf_op jit(solution)/shard_map/ppermute | solution.py:305
  8.8 0.0 collective-permute-done.2.refs_3_
  8.8 0.1 pick.1
  8.9 1.7 %collective-permute-start.6 = (bf16[2,128,256]{2,1,0:T(8,128)(2,1)S(1)}, bf16[2,128,256]{2,1,0:T(8,128)(2,1)S(1)}, u32[]{:S(2)}, u32[]{:S(2)}) collective-permute-start(bf16[2,128,256]{2,1,0:T(8,128)(2,1)S(1)} %get-tuple-element.57), channel_id=1, source_target_pairs={{0,4},{1,5},{2,6},{3,7},{4,0},{5,1},{6,2},{7,3},{8,12},{9,13},{10,... | collective-permute-start | bytes 393224 | tf_op jit(solution)/shard_map/ppermute | solution.py:346
  10.6 0.0 collective-permute-start.7
  10.6 0.0 collective-permute-done.3.refs_5_
  10.6 1.5 %collective-permute-done.4.refs_6_ = bf16[1,2,64,256]{3,2,1,0:T(8,128)(2,1)S(1)} collective-permute-done((bf16[1,2,64,256]{3,2,1,0:T(8,128)(2,1)S(1)}, bf16[1,2,64,256]{3,2,1,0:T(8,128)(2,1)S(1)}, u32[]{:S(2)}, u32[]{:S(2)}) %collective-permute-start.4) | collective-permute-done | bytes 65568 | tf_op jit(solution)/shard_map/ppermute | solution.py:305
  12.1 0.0 collective-permute-done.5.refs_7_
  12.1 0.7 %near.1 = (f32[256,1024]{1,0:T(8,128)S(1)}, f32[256,1024]{1,0:T(8,128)S(1)}, f32[3,1024]{1,0:T(4,128)S(1)}, bf16[1024,256]{1,0:T(8,128)(2,1)S(1)}, bf16[256,1024...) custom-call(f32[6,256]{1,0:T(8,128)S(1)} %get-tuple-element.45.bias_ref, ...), custom_call_target="tpu_custom_call" | custom-call | flops 1500000000 | bytes 1 | tf_op jit(solution)/shard_map/near/pallas_call | solution.py:24
  12.7 1.4 %collective-permute-done.6.keys_ref.refs_4_ = bf16[2,128,256]{2,1,0:T(8,128)(2,1)S(1)} collective-permute-done((bf16[2,128,256]{2,1,0:T(8,128)(2,1)S(1)}, bf16[2,128,256]{2,1,0:T(8,128)(2,1)S(1)}, u32[]{:S(2)}, u32[]{:S(2)}) %collective-permute-start.6) | collective-permute-done | bytes 131104 | tf_op jit(solution)/shard_map/ppermute | solution.py:346
  14.2 0.4 %first.1 = (f32[128,1024]{1,0:T(8,128)S(1)}, f32[128,1024]{1,0:T(8,128)S(1)}, f32[3,1024]{1,0:T(4,128)S(1)}) custom-call(f32[6,256]{1,0:T(8,128)S(1)} %get-tuple-element.45.bias_ref, bf16[256,1024]{1,0:T(8,128)(2,1)S(1)} %get-tuple-element.55.query_across, bf16[256,1024]{1,0:T(8,128)(2,1)S(1)} %get-tuple-element.56.grad_across.refs_0_, ...), custom_call_target="tpu_custom_call" | custom-call | tf_op jit(solution)/shard_map/first/pallas_call | solution.py:24
  14.6 0.0 collective-permute-done.7.refs_1_.refs_5_
  14.6 0.4 %far.1 = (bf16[256,1024]{1,0:T(8,128)(2,1)S(1)}, bf16[256,1024]{1,0:T(8,128)(2,1)S(1)}, f32[2,1024]{1,0:T(2,128)S(1)}, bf16[2,128,256]{2,1,0:T(8,128)(2,1)S(1)}, bf16[2,128,256]{2,1,0:T(8,128)(2,1)S(1)}) custom-call(f32[6,256]{1,0:T(8,128)S(1)} %get-tuple-element.45.bias_ref, f32[3,1024]{1,0:T(4,128)S(1)} %get-tuple-element.54.stat_ref, ...), custom_call_target="tpu_custom_call" | custom-call | flops 1500000000 | bytes 1 | tf_op jit(solution)/shard_map/far/pallas_call | solution.py:24
  15.0 3.0 %collective-permute-start.11 = (bf16[2,128,256]{2,1,0:T(8,128)(2,1)S(1)}, bf16[2,128,256]{2,1,0:T(8,128)(2,1)S(1)}, u32[]{:S(2)}, u32[]{:S(2)}) collective-permute-start(bf16[2,128,256]{2,1,0:T(8,128)(2,1)S(1)} %get-tuple-element.76), channel_id=1, source_target_pairs={{0,4},{1,5},{2,6},{3,7},{4,0},{5,1},{6,2},{7,3},{8,12},{9,13},{10,... | collective-permute-start | bytes 393224 | tf_op jit(solution)/shard_map/ppermute | solution.py:401
  18.0 0.0 collective-permute-start.12
  18.0 0.8 %rest.1 = (bf16[1,2,64,256]{3,2,1,0:T(8,128)(2,1)S(1)}, bf16[1,2,64,256]{3,2,1,0:T(8,128)(2,1)S(1)}, bf16[1,2,64,256]{3,2,1,0:T(8,128)(2,1)S(1)}, bf16[1,2,64,25...) custom-call(f32[2,1024]{1,0:T(2,128)S(1)} %get-tuple-element.64.final_ref, f32[256,1024]{1,0:T(8,128)S(1)} %get-tuple-element.65.exps_ref, ...), custom_call_target="tpu_custom_call" | custom-call | flops 1500000000 | bytes 1 | tf_op jit(solution)/shard_map/rest/pallas_call | solution.py:24
  18.8 1.5 %collective-permute-start.8 = (bf16[1,2,64,256]{3,2,1,0:T(8,128)(2,1)S(1)}, bf16[1,2,64,256]{3,2,1,0:T(8,128)(2,1)S(1)}, u32[]{:S(2)}, u32[]{:S(2)}) collective-permute-start(bf16[1,2,64,256]{3,2,1,0:T(8,128)(2,1)S(1)} %get-tuple-element.70), channel_id=1, source_target_pairs={{0,3},{1,2},{2,1},{3,0},{4,7},{5,6},{6,5},{7,4},{8,11},{9,10},{10,... | collective-permute-start | bytes 196616 | tf_op jit(solution)/shard_map/ppermute | solution.py:305
  20.4 0.7 %collective-permute-start.9 = (bf16[1,2,64,256]{3,2,1,0:T(8,128)(2,1)S(1)}, bf16[1,2,64,256]{3,2,1,0:T(8,128)(2,1)S(1)}, u32[]{:S(2)}, u32[]{:S(2)}) collective-permute-start(bf16[1,2,64,256]{3,2,1,0:T(8,128)(2,1)S(1)} %get-tuple-element.71), channel_id=1, source_target_pairs={{0,2},{1,3},{2,0},{3,1},{4,6},{5,7},{6,4},{7,5},{8,10},{9,11},{10,... | collective-permute-start | bytes 196616 | tf_op jit(solution)/shard_map/ppermute | solution.py:305
  21.0 0.0 collective-permute-start.10
  21.0 0.0 collective-permute-done.11.back_a
  21.0 0.0 collective-permute-done.12.back_b
  21.0 0.1 merge.1
  21.2 1.4 %collective-permute-start.13 = (bf16[1,2,64,256]{3,2,1,0:T(8,128)(2,1)S(1)}, bf16[1,2,64,256]{3,2,1,0:T(8,128)(2,1)S(1)}, u32[]{:S(2)}, u32[]{:S(2)}) collective-permute-start(bf16[1,2,64,256]{3,2,1,0:T(8,128)(2,1)S(1)} %get-tuple-element.79), channel_id=1, source_target_pairs={{0,2},{1,3},{2,0},{3,1},{4,6},{5,7},{6,4},{7,5},{8,10},{9,11},{10,... | collective-permute-start | bytes 196616 | tf_op jit(solution)/shard_map/ppermute | solution.py:305
  22.6 0.5 %collective-permute-start.14 = (bf16[1,2,64,256]{3,2,1,0:T(8,128)(2,1)S(1)}, bf16[1,2,64,256]{3,2,1,0:T(8,128)(2,1)S(1)}, u32[]{:S(2)}, u32[]{:S(2)}) collective-permute-start(bf16[1,2,64,256]{3,2,1,0:T(8,128)(2,1)S(1)} %get-tuple-element.80), channel_id=1, source_target_pairs={{0,3},{1,2},{2,1},{3,0},{4,7},{5,6},{6,5},{7,4},{8,11},{9,10},{10,... | collective-permute-start | bytes 196616 | tf_op jit(solution)/shard_map/ppermute | solution.py:305
  23.1 0.0 collective-permute-done.8.refs_1_
  23.1 0.4 %collective-permute-start.15 = (bf16[1,2,64,256]{3,2,1,0:T(8,128)(2,1)S(1)}, bf16[1,2,64,256]{3,2,1,0:T(8,128)(2,1)S(1)}, u32[]{:S(2)}, u32[]{:S(2)}) collective-permute-start(bf16[1,2,64,256]{3,2,1,0:T(8,128)(2,1)S(1)} %get-tuple-element.81), channel_id=1, source_target_pairs={{0,1},{1,0},{2,3},{3,2},{4,5},{5,4},{6,7},{7,6},{8,9},{9,8},{10,11... | collective-permute-start | bytes 196616 | tf_op jit(solution)/shard_map/ppermute | solution.py:305
  23.5 1.6 %collective-permute-done.9.refs_2_ = bf16[1,2,64,256]{3,2,1,0:T(8,128)(2,1)S(1)} collective-permute-done((bf16[1,2,64,256]{3,2,1,0:T(8,128)(2,1)S(1)}, bf16[1,2,64,256]{3,2,1,0:T(8,128)(2,1)S(1)}, u32[]{:S(2)}, u32[]{:S(2)}) %collective-permute-start.9) | collective-permute-done | bytes 65568 | tf_op jit(solution)/shard_map/ppermute | solution.py:305
  25.1 0.0 collective-permute-done.10.refs_3_
  25.1 0.7 %unpack.2 = (bf16[64,1024]{1,0:T(8,128)(2,1)}, bf16[64,1024]{1,0:T(8,128)(2,1)}) custom-call(bf16[1,2,64,256]{3,2,1,0:T(8,128)(2,1)S(1)} %get-tuple-element.69.refs_0_, bf16[1,2,64,256]{3,2,1,0:T(8,128)(2,1)S(1)} %collective-permute-done.8.refs_1_, bf16[1,2,64,256]{3,2,1,0:T(8,128)(2,1)S(1)} %collective-permute-done.9.refs_2_, ...), custom_call_target="tpu_custom_call" | custom-call | tf_op jit(solution)/shard_map/unpack/pallas_call | solution.py:24
  25.8 0.7 %collective-permute-done.13.refs_1_ = bf16[1,2,64,256]{3,2,1,0:T(8,128)(2,1)S(1)} collective-permute-done((bf16[1,2,64,256]{3,2,1,0:T(8,128)(2,1)S(1)}, bf16[1,2,64,256]{3,2,1,0:T(8,128)(2,1)S(1)}, u32[]{:S(2)}, u32[]{:S(2)}) %collective-permute-start.13) | collective-permute-done | bytes 65568 | tf_op jit(solution)/shard_map/ppermute | solution.py:305
  26.5 0.5 %collective-permute-done.14.refs_2_ = bf16[1,2,64,256]{3,2,1,0:T(8,128)(2,1)S(1)} collective-permute-done((bf16[1,2,64,256]{3,2,1,0:T(8,128)(2,1)S(1)}, bf16[1,2,64,256]{3,2,1,0:T(8,128)(2,1)S(1)}, u32[]{:S(2)}, u32[]{:S(2)}) %collective-permute-start.14) | collective-permute-done | bytes 65568 | tf_op jit(solution)/shard_map/ppermute | solution.py:305
  27.1 0.0 collective-permute-done.15.refs_3_
  27.1 0.7 %unpack.3 = (bf16[64,1024]{1,0:T(8,128)(2,1)}, bf16[64,1024]{1,0:T(8,128)(2,1)}) custom-call(bf16[1,2,64,256]{3,2,1,0:T(8,128)(2,1)S(1)} %get-tuple-element.78.refs_0_, bf16[1,2,64,256]{3,2,1,0:T(8,128)(2,1)S(1)} %collective-permute-done.13.refs_1_, bf16[1,2,64,256]{3,2,1,0:T(8,128)(2,1)S(1)} %collective-permute-done.14.refs_2_, ...), custom_call_target="tpu_custom_call" | custom-call | tf_op jit(solution)/shard_map/unpack/pallas_call | solution.py:24
  (2 shorter events, 0.1 us)
Async XLA Ops:
  1.6 4.1 %copy-start = (bf16[64,1024]{1,0:T(8,128)(2,1)S(1)}, bf16[64,1024]{1,0:T(8,128)(2,1)}, u32[]{:S(2)}) copy-start(bf16[64,1024]{1,0:T(8,128)(2,1)} %one.1) | copy-start | bytes 393220
  1.6 4.1 %copy-start.1 = (bf16[64,1024]{1,0:T(8,128)(2,1)S(1)}, bf16[64,1024]{1,0:T(8,128)(2,1)}, u32[]{:S(2)}) copy-start(bf16[64,1024]{1,0:T(8,128)(2,1)} %two.1) | copy-start | bytes 393220
  1.6 3.2 %copy-start.2 = (s32[8,8]{1,0:T(8,128)S(1)}, s32[8,8]{1,0:T(8,128)}, u32[]{:S(2)}) copy-start(s32[8,8]{1,0:T(8,128)} %nbr_ref.1) | copy-start | bytes 772
  1.6 6.1 %collective-permute-start = (bf16[1,2,64,256]{3,2,1,0:T(8,128)(2,1)S(1)}, bf16[1,2,64,256]{3,2,1,0:T(8,128)(2,1)S(1)}, u32[]{:S(2)}, u32[]{:S(2)}) collective-permute-start(bf16[1,2,64,256]{3,2,1,0:T(8,128)(2,1)S(1)} %get-tuple-element.46), channel_id=1, source_target_pairs={{0,2},{1,3},{2,0},{3,1},{4,6},{5,7},{6,4},{7,5},{8,10},{9,11},{10,... | collective-permute-start | bytes 196616 | tf_op jit(solution)/shard_map/ppermute | solution.py:305
  4.6 4.1 %collective-permute-start.1 = (bf16[1,2,64,256]{3,2,1,0:T(8,128)(2,1)S(1)}, bf16[1,2,64,256]{3,2,1,0:T(8,128)(2,1)S(1)}, u32[]{:S(2)}, u32[]{:S(2)}) collective-permute-start(bf16[1,2,64,256]{3,2,1,0:T(8,128)(2,1)S(1)} %get-tuple-element.47), channel_id=1, source_target_pairs={{0,3},{1,2},{2,1},{3,0},{4,7},{5,6},{6,5},{7,4},{8,11},{9,10},{10,... | collective-permute-start | bytes 196616 | tf_op jit(solution)/shard_map/ppermute | solution.py:305
  4.6 4.1 %collective-permute-start.2 = (bf16[1,2,64,256]{3,2,1,0:T(8,128)(2,1)S(1)}, bf16[1,2,64,256]{3,2,1,0:T(8,128)(2,1)S(1)}, u32[]{:S(2)}, u32[]{:S(2)}) collective-permute-start(bf16[1,2,64,256]{3,2,1,0:T(8,128)(2,1)S(1)} %get-tuple-element.48), channel_id=1, source_target_pairs={{0,1},{1,0},{2,3},{3,2},{4,5},{5,4},{6,7},{7,6},{8,9},{9,8},{10,11... | collective-permute-start | bytes 196616 | tf_op jit(solution)/shard_map/ppermute | solution.py:305
  5.7 4.8 %collective-permute-start.3 = (bf16[1,2,64,256]{3,2,1,0:T(8,128)(2,1)S(1)}, bf16[1,2,64,256]{3,2,1,0:T(8,128)(2,1)S(1)}, u32[]{:S(2)}, u32[]{:S(2)}) collective-permute-start(bf16[1,2,64,256]{3,2,1,0:T(8,128)(2,1)S(1)} %get-tuple-element.51), channel_id=1, source_target_pairs={{0,2},{1,3},{2,0},{3,1},{4,6},{5,7},{6,4},{7,5},{8,10},{9,11},{10,... | collective-permute-start | bytes 196616 | tf_op jit(solution)/shard_map/ppermute | solution.py:305
  7.8 4.3 %collective-permute-start.4 = (bf16[1,2,64,256]{3,2,1,0:T(8,128)(2,1)S(1)}, bf16[1,2,64,256]{3,2,1,0:T(8,128)(2,1)S(1)}, u32[]{:S(2)}, u32[]{:S(2)}) collective-permute-start(bf16[1,2,64,256]{3,2,1,0:T(8,128)(2,1)S(1)} %get-tuple-element.52), channel_id=1, source_target_pairs={{0,3},{1,2},{2,1},{3,0},{4,7},{5,6},{6,5},{7,4},{8,11},{9,10},{10,... | collective-permute-start | bytes 196616 | tf_op jit(solution)/shard_map/ppermute | solution.py:305
  7.8 4.3 %collective-permute-start.5 = (bf16[1,2,64,256]{3,2,1,0:T(8,128)(2,1)S(1)}, bf16[1,2,64,256]{3,2,1,0:T(8,128)(2,1)S(1)}, u32[]{:S(2)}, u32[]{:S(2)}) collective-permute-start(bf16[1,2,64,256]{3,2,1,0:T(8,128)(2,1)S(1)} %get-tuple-element.53), channel_id=1, source_target_pairs={{0,1},{1,0},{2,3},{3,2},{4,5},{5,4},{6,7},{7,6},{8,9},{9,8},{10,11... | collective-permute-start | bytes 196616 | tf_op jit(solution)/shard_map/ppermute | solution.py:305
  8.9 5.3 %collective-permute-start.6 = (bf16[2,128,256]{2,1,0:T(8,128)(2,1)S(1)}, bf16[2,128,256]{2,1,0:T(8,128)(2,1)S(1)}, u32[]{:S(2)}, u32[]{:S(2)}) collective-permute-start(bf16[2,128,256]{2,1,0:T(8,128)(2,1)S(1)} %get-tuple-element.57), channel_id=1, source_target_pairs={{0,4},{1,5},{2,6},{3,7},{4,0},{5,1},{6,2},{7,3},{8,12},{9,13},{10,... | collective-permute-start | bytes 393224 | tf_op jit(solution)/shard_map/ppermute | solution.py:346
  10.6 4.0 %collective-permute-start.7 = (bf16[2,128,256]{2,1,0:T(8,128)(2,1)S(1)}, bf16[2,128,256]{2,1,0:T(8,128)(2,1)S(1)}, u32[]{:S(2)}, u32[]{:S(2)}) collective-permute-start(bf16[2,128,256]{2,1,0:T(8,128)(2,1)S(1)} %get-tuple-element.63), channel_id=1, source_target_pairs={{0,1},{1,0},{2,3},{3,2},{4,8},{5,9},{6,10},{7,11},{8,4},{9,5},{10,... | collective-permute-start | bytes 393224 | tf_op jit(solution)/shard_map/ppermute | solution.py:346
  15.0 6.0 %collective-permute-start.11 = (bf16[2,128,256]{2,1,0:T(8,128)(2,1)S(1)}, bf16[2,128,256]{2,1,0:T(8,128)(2,1)S(1)}, u32[]{:S(2)}, u32[]{:S(2)}) collective-permute-start(bf16[2,128,256]{2,1,0:T(8,128)(2,1)S(1)} %get-tuple-element.76), channel_id=1, source_target_pairs={{0,4},{1,5},{2,6},{3,7},{4,0},{5,1},{6,2},{7,3},{8,12},{9,13},{10,... | collective-permute-start | bytes 393224 | tf_op jit(solution)/shard_map/ppermute | solution.py:401
  18.0 3.0 %collective-permute-start.12 = (bf16[2,128,256]{2,1,0:T(8,128)(2,1)S(1)}, bf16[2,128,256]{2,1,0:T(8,128)(2,1)S(1)}, u32[]{:S(2)}, u32[]{:S(2)}) collective-permute-start(bf16[2,128,256]{2,1,0:T(8,128)(2,1)S(1)} %get-tuple-element.77), channel_id=1, source_target_pairs={{0,1},{1,0},{2,3},{3,2},{4,8},{5,9},{6,10},{7,11},{8,4},{9,5},{10,... | collective-permute-start | bytes 393224 | tf_op jit(solution)/shard_map/ppermute | solution.py:401
  18.8 4.3 %collective-permute-start.8 = (bf16[1,2,64,256]{3,2,1,0:T(8,128)(2,1)S(1)}, bf16[1,2,64,256]{3,2,1,0:T(8,128)(2,1)S(1)}, u32[]{:S(2)}, u32[]{:S(2)}) collective-permute-start(bf16[1,2,64,256]{3,2,1,0:T(8,128)(2,1)S(1)} %get-tuple-element.70), channel_id=1, source_target_pairs={{0,3},{1,2},{2,1},{3,0},{4,7},{5,6},{6,5},{7,4},{8,11},{9,10},{10,... | collective-permute-start | bytes 196616 | tf_op jit(solution)/shard_map/ppermute | solution.py:305
  20.4 4.8 %collective-permute-start.9 = (bf16[1,2,64,256]{3,2,1,0:T(8,128)(2,1)S(1)}, bf16[1,2,64,256]{3,2,1,0:T(8,128)(2,1)S(1)}, u32[]{:S(2)}, u32[]{:S(2)}) collective-permute-start(bf16[1,2,64,256]{3,2,1,0:T(8,128)(2,1)S(1)} %get-tuple-element.71), channel_id=1, source_target_pairs={{0,2},{1,3},{2,0},{3,1},{4,6},{5,7},{6,4},{7,5},{8,10},{9,11},{10,... | collective-permute-start | bytes 196616 | tf_op jit(solution)/shard_map/ppermute | solution.py:305
  21.0 4.1 %collective-permute-start.10 = (bf16[1,2,64,256]{3,2,1,0:T(8,128)(2,1)S(1)}, bf16[1,2,64,256]{3,2,1,0:T(8,128)(2,1)S(1)}, u32[]{:S(2)}, u32[]{:S(2)}) collective-permute-start(bf16[1,2,64,256]{3,2,1,0:T(8,128)(2,1)S(1)} %get-tuple-element.72), channel_id=1, source_target_pairs={{0,1},{1,0},{2,3},{3,2},{4,5},{5,4},{6,7},{7,6},{8,9},{9,8},{10,11... | collective-permute-start | bytes 196616 | tf_op jit(solution)/shard_map/ppermute | solution.py:305
  21.2 5.3 %collective-permute-start.13 = (bf16[1,2,64,256]{3,2,1,0:T(8,128)(2,1)S(1)}, bf16[1,2,64,256]{3,2,1,0:T(8,128)(2,1)S(1)}, u32[]{:S(2)}, u32[]{:S(2)}) collective-permute-start(bf16[1,2,64,256]{3,2,1,0:T(8,128)(2,1)S(1)} %get-tuple-element.79), channel_id=1, source_target_pairs={{0,2},{1,3},{2,0},{3,1},{4,6},{5,7},{6,4},{7,5},{8,10},{9,11},{10,... | collective-permute-start | bytes 196616 | tf_op jit(solution)/shard_map/ppermute | solution.py:305
  22.6 4.5 %collective-permute-start.14 = (bf16[1,2,64,256]{3,2,1,0:T(8,128)(2,1)S(1)}, bf16[1,2,64,256]{3,2,1,0:T(8,128)(2,1)S(1)}, u32[]{:S(2)}, u32[]{:S(2)}) collective-permute-start(bf16[1,2,64,256]{3,2,1,0:T(8,128)(2,1)S(1)} %get-tuple-element.80), channel_id=1, source_target_pairs={{0,3},{1,2},{2,1},{3,0},{4,7},{5,6},{6,5},{7,4},{8,11},{9,10},{10,... | collective-permute-start | bytes 196616 | tf_op jit(solution)/shard_map/ppermute | solution.py:305
  23.1 4.0 %collective-permute-start.15 = (bf16[1,2,64,256]{3,2,1,0:T(8,128)(2,1)S(1)}, bf16[1,2,64,256]{3,2,1,0:T(8,128)(2,1)S(1)}, u32[]{:S(2)}, u32[]{:S(2)}) collective-permute-start(bf16[1,2,64,256]{3,2,1,0:T(8,128)(2,1)S(1)} %get-tuple-element.81), channel_id=1, source_target_pairs={{0,1},{1,0},{2,3},{3,2},{4,5},{5,4},{6,7},{7,6},{8,9},{9,8},{10,11... | collective-permute-start | bytes 196616 | tf_op jit(solution)/shard_map/ppermute | solution.py:305

commit v9 on v8

--- a/solution.py
+++ b/solution.py
@@ -181,8 +181,13 @@
         stat_ref[2:3, lanes] = jnp.sum(exps * grad_weights, 0, keepdims=True)
 
 
-def far_kernel(heads, owners, bias_ref, stat_ref, exps_ref, gw_ref, first_ref, query_down, query_across, grad_down, *refs):
-    grad_across, second_ref, w_ref, ds_ref, final_ref, far_a, far_b = refs
+def far_kernel(
+    heads, owners, places, bias_ref, stat_ref, exps_ref, gw_ref, first_ref, query_down, query_across, grad_down, *refs
+):
+    grad_across, near_exps_ref, near_gw_ref = refs[:3]
+    kv, slabs = refs[3 : heads + 3], refs[heads + 3 : heads + 5]
+    w_ref, ds_ref, final_ref, far_a, far_b, *early, near_out, own_w_ref, own_ds_ref = refs[heads + 5 :]
+    second_ref = slabs[1]
     patch, width = second_ref.shape[1:]
     queries = bias_ref.shape[1]
     node = lax.axis_index("node")
@@ -236,10 +241,16 @@
         w_ref[patch:, :] = jnp.zeros((patch, w_ref.shape[1]), LOW)
         ds_ref[patch:, :] = jnp.zeros((patch, ds_ref.shape[1]), LOW)
 
-
-def rest_kernel(heads, places, final_ref, exps_ref, gw_ref, far_w_ref, far_ds_ref, query_down, grad_down, *refs):
-    kv, far, outs = refs[:heads], refs[heads : heads + 2], refs[heads + 2 : -3]
-    near_out, w_ref, ds_ref = refs[-3:]
+    @pl.when(node == 0)
+    def _():
+        weights_of = final_ref, near_exps_ref, near_gw_ref, w_ref, ds_ref
+        rest(places, weights_of, (query_down, grad_down), kv, slabs, early, near_out, own_w_ref, own_ds_ref)
+
+
+def rest(places, weights_of, downs, kv, far, outs, near_out, w_ref, ds_ref):
+    heads = len(places)
+    final_ref, exps_ref, gw_ref, far_w_ref, far_ds_ref = weights_of
+    query_down, grad_down = downs
     rows, width = kv[0].shape[2:]
     queries = heads * rows
     keys_t, values_t = joined(kv, places, 0).T, joined(kv, places, 1).T
@@ -266,6 +277,22 @@
         near_out[d, 0], near_out[d, 1] = key_grad[span], value_grad[span]
 
 
+def rest_kernel(heads, places, final_ref, exps_ref, gw_ref, far_w_ref, far_ds_ref, query_down, grad_down, *refs):
+    kv, far, early = refs[:heads], refs[heads : heads + 2], refs[heads + 2 : 2 * heads + 3]
+    *outs, near_out, w_ref, ds_ref = refs[2 * heads + 3 :]
+    first = lax.axis_index("node") == 0
+
+    @pl.when(first)
+    def _():
+        for ref, out in zip(early, outs + [near_out]):
+            out[...] = ref[...]
+
+    @pl.when(jnp.logical_not(first))
+    def _():
+        weights_of = final_ref, exps_ref, gw_ref, far_w_ref, far_ds_ref
+        rest(places, weights_of, (query_down, grad_down), kv, far, outs, near_out, w_ref, ds_ref)
+
+
 def merge_kernel(heads, slot_ref, near, back_a, back_b, *outs):
     rows = near.shape[2]
     per_patch = back_a.shape[1] // rows
@@ -371,15 +398,20 @@
         sides[3],
         far[0],
     )
-    far_w, far_ds, final, *far_grads = call(
-        functools.partial(far_kernel, heads, owners),
+    far_w, far_ds, final, far_a, far_b, *early = call(
+        functools.partial(far_kernel, heads, owners, places),
         "far",
-        [table(other, LOW), table(other, LOW), table(2), slab, slab],
+        [table(other, LOW), table(other, LOW), table(2), slab, slab] + [block] * heads + [near_shape],
         bias,
         stats,
         *first,
         *sides,
-        far[1],
+        exps,
+        grad_weights,
+        *kv,
+        *far,
+        scratch=[pltpu.VMEM((own, lanes), LOW)] * 2,
+        limit=12,
         cost=work,
     )
     *mq, near = call(
@@ -395,10 +427,11 @@
         sides[2],
         *kv,
         *far,
+        *early,
         scratch=[pltpu.VMEM((own, lanes), LOW)] * 2,
         cost=work,
     )
-    back = [lax.ppermute(p, ("node", "head"), r) for p, r in zip(far_grads, routes)]
+    back = [lax.ppermute(p, ("node", "head"), r) for p, r in zip((far_a, far_b), routes)]
     mq = exchange(mq, downward)
     merged = call(functools.partial(merge_kernel, heads), "merge", [block] * heads, slots, near, *back)
     kv_grads = exchange(merged, order)

time: 28 us -> 27.7 us (0.989)
  starting transfers between devices: 14.6 us -> 13.7 us
  waiting for transfers between devices: 6.58 us -> 7.23 us
    ppermute x2, starting transfers between devices: 3 us -> 2.2 us  [shards(): lax.ppermute(p, ('node', 'head'), r)]
    ppermute x2, waiting for transfers between devices: 0.01 us -> 0.68 us  [shards(): lax.ppermute(p, ('node', 'head'), r)]
  transfers between devices with their start and end apart: 16 -> 16, of which waited for: 6 -> 7; matrix products, arithmetic and copies ran while one was open for 0% -> 0% of each run, Pallas kernels for 13% -> 11%
where the time goes in v9:
time: 27.7 us; the launch traced here: 27.5 us
  starting transfers between devices  13.7 us (49%)
  waiting for transfers between devices  7.23 us (26%)
  Pallas kernels  4.92 us (18%)
  local copies, waits for them, and re-layouts  0.92 us (3%)
  between operations  0.77 us (3%)
    ppermute x12, starting transfers between devices, exchange(): lax.ppermute(blocks[d], 'head', swaps[d])  9.82 us
    ppermute x12, waiting for transfers between devices, exchange(): lax.ppermute(blocks[d], 'head', swaps[d])  5.1 us
    pallas_call x11, Pallas kernels, call(): pl.pallas_call(kernel, out_shape=outs, in_specs=specs or [VMEM] * len(arg...  4.92 us
    ppermute x2, starting transfers between devices, shards(): lax.ppermute(p, ('node', 'head'), r)  2.2 us
    ppermute x2, starting transfers between devices, shards(): far = [lax.ppermute(p, ('node', 'head'), r) for p, r in zip(picked, routes)]  1.7 us
    ppermute x2, waiting for transfers between devices, shards(): far = [lax.ppermute(p, ('node', 'head'), r) for p, r in zip(picked, routes)]  1.45 us
    dynamic_slice x1, local copies, waits for them, and re-layouts, cut(): lax.dynamic_slice_in_dim(a, at, width, 1)  0.9 us
    ppermute x2, waiting for transfers between devices, shards(): lax.ppermute(p, ('node', 'head'), r)  0.68 us
  transfers between devices with their start and end apart: 16, of which 7 were waited for; matrix products, arithmetic and copies ran while one was open for 0% of the time, Pallas kernels for 11%

profile of v9, /device:TPU:0, one launch (start us, length us, event | category | flops | bytes accessed | tf_op | source)
XLA Modules:
  0.0 27.5 jit_solution(490923606179075544)
XLA Ops:
  0.7 0.9 %constant_dynamic-slice_fusion = (bf16[64,256]{1,0:T(8,128)(2,1)S(1)}, bf16[64,256]{1,0:T(8,128)(2,1)S(1)}, bf16[64,256]{1,0:T(8,128)(2,1)S(1)}, bf16[64,256]{1,...) fusion(bf16[64,1024]{1,0:T(8,128)(2,1)} %param.7, ...), kind=kLoop, calls=%fused_computation | loop fusion | bytes 524304 | tf_op jit(solution)/shard_map/dynamic_slice | solution.py:339
  1.6 0.0 copy-start
  1.6 0.0 copy-start.1
  1.6 0.0 copy-start.2
  1.6 3.0 %collective-permute-start = (bf16[1,2,64,256]{3,2,1,0:T(8,128)(2,1)S(1)}, bf16[1,2,64,256]{3,2,1,0:T(8,128)(2,1)S(1)}, u32[]{:S(2)}, u32[]{:S(2)}) collective-permute-start(bf16[1,2,64,256]{3,2,1,0:T(8,128)(2,1)S(1)} %get-tuple-element.51), channel_id=1, source_target_pairs={{0,2},{1,3},{2,0},{3,1},{4,6},{5,7},{6,4},{7,5},{8,10},{9,11},{10,... | collective-permute-start | bytes 196616 | tf_op jit(solution)/shard_map/ppermute | solution.py:332
  4.6 0.0 collective-permute-start.1
  4.6 0.2 collective-permute-start.2
  4.8 0.0 copy-done.2
  4.8 0.8 %prep.1 = (f32[6,256]{1,0:T(8,128)S(1)}, s32[4,256]{1,0:T(4,128)S(1)}) custom-call(s32[8,8]{1,0:T(8,128)S(1)} %copy-done.2, bf16[1,2,64,256]{3,2,1,0:T(8,128)(2,1)S(1)} %get-tuple-element.49.after_ref.refs_0_.refs_3_), custom_call_target="tpu_custom_call" | custom-call | tf_op jit(solution)/shard_map/prep/pallas_call | solution.py:24
  5.7 0.0 copy-done
  5.7 0.0 copy-done.1
  5.7 2.0 %collective-permute-start.3 = (bf16[1,2,64,256]{3,2,1,0:T(8,128)(2,1)S(1)}, bf16[1,2,64,256]{3,2,1,0:T(8,128)(2,1)S(1)}, u32[]{:S(2)}, u32[]{:S(2)}) collective-permute-start(bf16[1,2,64,256]{3,2,1,0:T(8,128)(2,1)S(1)} %get-tuple-element.56), channel_id=1, source_target_pairs={{0,2},{1,3},{2,0},{3,1},{4,6},{5,7},{6,4},{7,5},{8,10},{9,11},{10,... | collective-permute-start | bytes 196616 | tf_op jit(solution)/shard_map/ppermute | solution.py:332
  7.8 0.0 collective-permute-start.4
  7.8 0.0 collective-permute-done.refs_1_.refs_4_
  7.8 0.2 collective-permute-start.5
  8.0 0.8 %collective-permute-done.1.refs_2_.refs_5_ = bf16[1,2,64,256]{3,2,1,0:T(8,128)(2,1)S(1)} collective-permute-done((bf16[1,2,64,256]{3,2,1,0:T(8,128)(2,1)S(1)}, bf16[1,2,64,256]{3,2,1,0:T(8,128)(2,1)S(1)}, u32[]{:S(2)}, u32[]{:S(2)}) %collective-permute-start.1) | collective-permute-done | bytes 65568 | tf_op jit(solution)/shard_map/ppermute | solution.py:332
  8.8 0.0 collective-permute-done.2.refs_3_.refs_6_
  8.8 0.1 pick.1
  8.9 1.7 %collective-permute-start.6 = (bf16[2,128,256]{2,1,0:T(8,128)(2,1)S(1)}, bf16[2,128,256]{2,1,0:T(8,128)(2,1)S(1)}, u32[]{:S(2)}, u32[]{:S(2)}) collective-permute-start(bf16[2,128,256]{2,1,0:T(8,128)(2,1)S(1)} %get-tuple-element.62), channel_id=1, source_target_pairs={{0,4},{1,5},{2,6},{3,7},{4,0},{5,1},{6,2},{7,3},{8,12},{9,13},{10,... | collective-permute-start | bytes 393224 | tf_op jit(solution)/shard_map/ppermute | solution.py:373
  10.6 0.0 collective-permute-start.7
  10.6 0.0 collective-permute-done.3.refs_5_
  10.6 1.5 %collective-permute-done.4.refs_6_ = bf16[1,2,64,256]{3,2,1,0:T(8,128)(2,1)S(1)} collective-permute-done((bf16[1,2,64,256]{3,2,1,0:T(8,128)(2,1)S(1)}, bf16[1,2,64,256]{3,2,1,0:T(8,128)(2,1)S(1)}, u32[]{:S(2)}, u32[]{:S(2)}) %collective-permute-start.4) | collective-permute-done | bytes 65568 | tf_op jit(solution)/shard_map/ppermute | solution.py:332
  12.1 0.0 collective-permute-done.5.refs_7_
  12.1 0.7 %near.1 = (f32[256,1024]{1,0:T(8,128)S(1)}, f32[256,1024]{1,0:T(8,128)S(1)}, f32[3,1024]{1,0:T(4,128)S(1)}, bf16[1024,256]{1,0:T(8,128)(2,1)S(1)}, bf16[256,1024...) custom-call(f32[6,256]{1,0:T(8,128)S(1)} %get-tuple-element.50.bias_ref, ...), custom_call_target="tpu_custom_call" | custom-call | flops 1500000000 | bytes 1 | tf_op jit(solution)/shard_map/near/pallas_call | solution.py:24
  12.7 1.4 %collective-permute-done.6.keys_ref.refs_7_.refs_4_ = bf16[2,128,256]{2,1,0:T(8,128)(2,1)S(1)} collective-permute-done((bf16[2,128,256]{2,1,0:T(8,128)(2,1)S(1)}, bf16[2,128,256]{2,1,0:T(8,128)(2,1)S(1)}, u32[]{:S(2)}, u32[]{:S(2)}) %collective-permute-start.6) | collective-permute-done | bytes 131104 | tf_op jit(solution)/shard_map/ppermute | solution.py:373
  14.2 0.4 %first.1 = (f32[128,1024]{1,0:T(8,128)S(1)}, f32[128,1024]{1,0:T(8,128)S(1)}, f32[3,1024]{1,0:T(4,128)S(1)}) custom-call(f32[6,256]{1,0:T(8,128)S(1)} %get-tuple-element.50.bias_ref, bf16[256,1024]{1,0:T(8,128)(2,1)S(1)} %get-tuple-element.60.query_across, bf16[256,1024]{1,0:T(8,128)(2,1)S(1)} %get-tuple-element.61.grad_across.refs_0_, ...), custom_call_target="tpu_custom_call" | custom-call | tf_op jit(solution)/shard_map/first/pallas_call | solution.py:24
  14.6 0.0 collective-permute-done.7.refs_8_.refs_5_
  14.6 1.2 %far.1 = (bf16[256,1024]{1,0:T(8,128)(2,1)S(1)}, bf16[256,1024]{1,0:T(8,128)(2,1)S(1)}, f32[2,1024]{1,0:T(2,128)S(1)}, bf16[2,128,256]{2,1,0:T(8,128)(2,1)S(1)},...) custom-call(f32[6,256]{1,0:T(8,128)S(1)} %get-tuple-element.50.bias_, ...), custom_call_target="tpu_custom_call" | custom-call | flops 1500000000 | bytes 1 | tf_op jit(solution)/shard_map/far/pallas_call | solution.py:24
  15.8 2.2 %collective-permute-start.11 = (bf16[2,128,256]{2,1,0:T(8,128)(2,1)S(1)}, bf16[2,128,256]{2,1,0:T(8,128)(2,1)S(1)}, u32[]{:S(2)}, u32[]{:S(2)}) collective-permute-start(bf16[2,128,256]{2,1,0:T(8,128)(2,1)S(1)} %get-tuple-element.86), channel_id=1, source_target_pairs={{0,4},{1,5},{2,6},{3,7},{4,0},{5,1},{6,2},{7,3},{8,12},{9,13},{10,... | collective-permute-start | bytes 393224 | tf_op jit(solution)/shard_map/ppermute | solution.py:434
  18.0 0.0 collective-permute-start.12
  18.0 0.1 rest.1
  18.1 1.5 %collective-permute-start.8 = (bf16[1,2,64,256]{3,2,1,0:T(8,128)(2,1)S(1)}, bf16[1,2,64,256]{3,2,1,0:T(8,128)(2,1)S(1)}, u32[]{:S(2)}, u32[]{:S(2)}) collective-permute-start(bf16[1,2,64,256]{3,2,1,0:T(8,128)(2,1)S(1)} %get-tuple-element.80), channel_id=1, source_target_pairs={{0,3},{1,2},{2,1},{3,0},{4,7},{5,6},{6,5},{7,4},{8,11},{9,10},{10,... | collective-permute-start | bytes 196616 | tf_op jit(solution)/shard_map/ppermute | solution.py:332
  19.6 0.7 %collective-permute-start.9 = (bf16[1,2,64,256]{3,2,1,0:T(8,128)(2,1)S(1)}, bf16[1,2,64,256]{3,2,1,0:T(8,128)(2,1)S(1)}, u32[]{:S(2)}, u32[]{:S(2)}) collective-permute-start(bf16[1,2,64,256]{3,2,1,0:T(8,128)(2,1)S(1)} %get-tuple-element.81), channel_id=1, source_target_pairs={{0,2},{1,3},{2,0},{3,1},{4,6},{5,7},{6,4},{7,5},{8,10},{9,11},{10,... | collective-permute-start | bytes 196616 | tf_op jit(solution)/shard_map/ppermute | solution.py:332
  20.3 0.0 collective-permute-start.10
  20.3 0.7 %collective-permute-done.11.back_a = bf16[2,128,256]{2,1,0:T(8,128)(2,1)S(1)} collective-permute-done((bf16[2,128,256]{2,1,0:T(8,128)(2,1)S(1)}, bf16[2,128,256]{2,1,0:T(8,128)(2,1)S(1)}, u32[]{:S(2)}, u32[]{:S(2)}) %collective-permute-start.11) | collective-permute-done | bytes 131104 | tf_op jit(solution)/shard_map/ppermute | solution.py:434
  20.9 0.0 collective-permute-done.12.back_b
  20.9 0.1 merge.1
  21.1 1.5 %collective-permute-start.13 = (bf16[1,2,64,256]{3,2,1,0:T(8,128)(2,1)S(1)}, bf16[1,2,64,256]{3,2,1,0:T(8,128)(2,1)S(1)}, u32[]{:S(2)}, u32[]{:S(2)}) collective-permute-start(bf16[1,2,64,256]{3,2,1,0:T(8,128)(2,1)S(1)} %get-tuple-element.89), channel_id=1, source_target_pairs={{0,2},{1,3},{2,0},{3,1},{4,6},{5,7},{6,4},{7,5},{8,10},{9,11},{10,... | collective-permute-start | bytes 196616 | tf_op jit(solution)/shard_map/ppermute | solution.py:332
  22.6 0.0 collective-permute-start.14
  22.6 0.0 collective-permute-done.8.refs_1_
  22.6 0.7 %collective-permute-start.15 = (bf16[1,2,64,256]{3,2,1,0:T(8,128)(2,1)S(1)}, bf16[1,2,64,256]{3,2,1,0:T(8,128)(2,1)S(1)}, u32[]{:S(2)}, u32[]{:S(2)}) collective-permute-start(bf16[1,2,64,256]{3,2,1,0:T(8,128)(2,1)S(1)} %get-tuple-element.91), channel_id=1, source_target_pairs={{0,1},{1,0},{2,3},{3,2},{4,5},{5,4},{6,7},{7,6},{8,9},{9,8},{10,11... | collective-permute-start | bytes 196616 | tf_op jit(solution)/shard_map/ppermute | solution.py:332
  23.3 1.0 %collective-permute-done.9.refs_2_ = bf16[1,2,64,256]{3,2,1,0:T(8,128)(2,1)S(1)} collective-permute-done((bf16[1,2,64,256]{3,2,1,0:T(8,128)(2,1)S(1)}, bf16[1,2,64,256]{3,2,1,0:T(8,128)(2,1)S(1)}, u32[]{:S(2)}, u32[]{:S(2)}) %collective-permute-start.9) | collective-permute-done | bytes 65568 | tf_op jit(solution)/shard_map/ppermute | solution.py:332
  24.3 0.0 collective-permute-done.10.refs_3_
  24.4 0.7 %unpack.2 = (bf16[64,1024]{1,0:T(8,128)(2,1)}, bf16[64,1024]{1,0:T(8,128)(2,1)}) custom-call(bf16[1,2,64,256]{3,2,1,0:T(8,128)(2,1)S(1)} %get-tuple-element.79.refs_0_, bf16[1,2,64,256]{3,2,1,0:T(8,128)(2,1)S(1)} %collective-permute-done.8.refs_1_, bf16[1,2,64,256]{3,2,1,0:T(8,128)(2,1)S(1)} %collective-permute-done.9.refs_2_, ...), custom_call_target="tpu_custom_call" | custom-call | tf_op jit(solution)/shard_map/unpack/pallas_call | solution.py:24
  25.1 0.3 %collective-permute-done.13.refs_1_ = bf16[1,2,64,256]{3,2,1,0:T(8,128)(2,1)S(1)} collective-permute-done((bf16[1,2,64,256]{3,2,1,0:T(8,128)(2,1)S(1)}, bf16[1,2,64,256]{3,2,1,0:T(8,128)(2,1)S(1)}, u32[]{:S(2)}, u32[]{:S(2)}) %collective-permute-start.13) | collective-permute-done | bytes 65568 | tf_op jit(solution)/shard_map/ppermute | solution.py:332
  25.4 1.4 %collective-permute-done.14.refs_2_ = bf16[1,2,64,256]{3,2,1,0:T(8,128)(2,1)S(1)} collective-permute-done((bf16[1,2,64,256]{3,2,1,0:T(8,128)(2,1)S(1)}, bf16[1,2,64,256]{3,2,1,0:T(8,128)(2,1)S(1)}, u32[]{:S(2)}, u32[]{:S(2)}) %collective-permute-start.14) | collective-permute-done | bytes 65568 | tf_op jit(solution)/shard_map/ppermute | solution.py:332
  26.8 0.0 collective-permute-done.15.refs_3_
  26.8 0.7 %unpack.3 = (bf16[64,1024]{1,0:T(8,128)(2,1)}, bf16[64,1024]{1,0:T(8,128)(2,1)}) custom-call(bf16[1,2,64,256]{3,2,1,0:T(8,128)(2,1)S(1)} %get-tuple-element.88.refs_0_, bf16[1,2,64,256]{3,2,1,0:T(8,128)(2,1)S(1)} %collective-permute-done.13.refs_1_, bf16[1,2,64,256]{3,2,1,0:T(8,128)(2,1)S(1)} %collective-permute-done.14.refs_2_, ...), custom_call_target="tpu_custom_call" | custom-call | tf_op jit(solution)/shard_map/unpack/pallas_call | solution.py:24
  (2 shorter events, 0.1 us)
Async XLA Ops:
  1.6 4.1 %copy-start = (bf16[64,1024]{1,0:T(8,128)(2,1)S(1)}, bf16[64,1024]{1,0:T(8,128)(2,1)}, u32[]{:S(2)}) copy-start(bf16[64,1024]{1,0:T(8,128)(2,1)} %one.1) | copy-start | bytes 393220
  1.6 4.1 %copy-start.1 = (bf16[64,1024]{1,0:T(8,128)(2,1)S(1)}, bf16[64,1024]{1,0:T(8,128)(2,1)}, u32[]{:S(2)}) copy-start(bf16[64,1024]{1,0:T(8,128)(2,1)} %two.1) | copy-start | bytes 393220
  1.6 3.2 %copy-start.2 = (s32[8,8]{1,0:T(8,128)S(1)}, s32[8,8]{1,0:T(8,128)}, u32[]{:S(2)}) copy-start(s32[8,8]{1,0:T(8,128)} %nbr_ref.1) | copy-start | bytes 772
  1.6 6.1 %collective-permute-start = (bf16[1,2,64,256]{3,2,1,0:T(8,128)(2,1)S(1)}, bf16[1,2,64,256]{3,2,1,0:T(8,128)(2,1)S(1)}, u32[]{:S(2)}, u32[]{:S(2)}) collective-permute-start(bf16[1,2,64,256]{3,2,1,0:T(8,128)(2,1)S(1)} %get-tuple-element.51), channel_id=1, source_target_pairs={{0,2},{1,3},{2,0},{3,1},{4,6},{5,7},{6,4},{7,5},{8,10},{9,11},{10,... | collective-permute-start | bytes 196616 | tf_op jit(solution)/shard_map/ppermute | solution.py:332
  4.6 4.1 %collective-permute-start.1 = (bf16[1,2,64,256]{3,2,1,0:T(8,128)(2,1)S(1)}, bf16[1,2,64,256]{3,2,1,0:T(8,128)(2,1)S(1)}, u32[]{:S(2)}, u32[]{:S(2)}) collective-permute-start(bf16[1,2,64,256]{3,2,1,0:T(8,128)(2,1)S(1)} %get-tuple-element.52), channel_id=1, source_target_pairs={{0,3},{1,2},{2,1},{3,0},{4,7},{5,6},{6,5},{7,4},{8,11},{9,10},{10,... | collective-permute-start | bytes 196616 | tf_op jit(solution)/shard_map/ppermute | solution.py:332
  4.6 4.1 %collective-permute-start.2 = (bf16[1,2,64,256]{3,2,1,0:T(8,128)(2,1)S(1)}, bf16[1,2,64,256]{3,2,1,0:T(8,128)(2,1)S(1)}, u32[]{:S(2)}, u32[]{:S(2)}) collective-permute-start(bf16[1,2,64,256]{3,2,1,0:T(8,128)(2,1)S(1)} %get-tuple-element.53), channel_id=1, source_target_pairs={{0,1},{1,0},{2,3},{3,2},{4,5},{5,4},{6,7},{7,6},{8,9},{9,8},{10,11... | collective-permute-start | bytes 196616 | tf_op jit(solution)/shard_map/ppermute | solution.py:332
  5.7 4.8 %collective-permute-start.3 = (bf16[1,2,64,256]{3,2,1,0:T(8,128)(2,1)S(1)}, bf16[1,2,64,256]{3,2,1,0:T(8,128)(2,1)S(1)}, u32[]{:S(2)}, u32[]{:S(2)}) collective-permute-start(bf16[1,2,64,256]{3,2,1,0:T(8,128)(2,1)S(1)} %get-tuple-element.56), channel_id=1, source_target_pairs={{0,2},{1,3},{2,0},{3,1},{4,6},{5,7},{6,4},{7,5},{8,10},{9,11},{10,... | collective-permute-start | bytes 196616 | tf_op jit(solution)/shard_map/ppermute | solution.py:332
  7.8 4.3 %collective-permute-start.4 = (bf16[1,2,64,256]{3,2,1,0:T(8,128)(2,1)S(1)}, bf16[1,2,64,256]{3,2,1,0:T(8,128)(2,1)S(1)}, u32[]{:S(2)}, u32[]{:S(2)}) collective-permute-start(bf16[1,2,64,256]{3,2,1,0:T(8,128)(2,1)S(1)} %get-tuple-element.57), channel_id=1, source_target_pairs={{0,3},{1,2},{2,1},{3,0},{4,7},{5,6},{6,5},{7,4},{8,11},{9,10},{10,... | collective-permute-start | bytes 196616 | tf_op jit(solution)/shard_map/ppermute | solution.py:332
  7.8 4.3 %collective-permute-start.5 = (bf16[1,2,64,256]{3,2,1,0:T(8,128)(2,1)S(1)}, bf16[1,2,64,256]{3,2,1,0:T(8,128)(2,1)S(1)}, u32[]{:S(2)}, u32[]{:S(2)}) collective-permute-start(bf16[1,2,64,256]{3,2,1,0:T(8,128)(2,1)S(1)} %get-tuple-element.58), channel_id=1, source_target_pairs={{0,1},{1,0},{2,3},{3,2},{4,5},{5,4},{6,7},{7,6},{8,9},{9,8},{10,11... | collective-permute-start | bytes 196616 | tf_op jit(solution)/shard_map/ppermute | solution.py:332
  8.9 5.3 %collective-permute-start.6 = (bf16[2,128,256]{2,1,0:T(8,128)(2,1)S(1)}, bf16[2,128,256]{2,1,0:T(8,128)(2,1)S(1)}, u32[]{:S(2)}, u32[]{:S(2)}) collective-permute-start(bf16[2,128,256]{2,1,0:T(8,128)(2,1)S(1)} %get-tuple-element.62), channel_id=1, source_target_pairs={{0,4},{1,5},{2,6},{3,7},{4,0},{5,1},{6,2},{7,3},{8,12},{9,13},{10,... | collective-permute-start | bytes 393224 | tf_op jit(solution)/shard_map/ppermute | solution.py:373
  10.6 4.0 %collective-permute-start.7 = (bf16[2,128,256]{2,1,0:T(8,128)(2,1)S(1)}, bf16[2,128,256]{2,1,0:T(8,128)(2,1)S(1)}, u32[]{:S(2)}, u32[]{:S(2)}) collective-permute-start(bf16[2,128,256]{2,1,0:T(8,128)(2,1)S(1)} %get-tuple-element.70), channel_id=1, source_target_pairs={{0,1},{1,0},{2,3},{3,2},{4,8},{5,9},{6,10},{7,11},{8,4},{9,5},{10,... | collective-permute-start | bytes 393224 | tf_op jit(solution)/shard_map/ppermute | solution.py:373
  15.8 5.1 %collective-permute-start.11 = (bf16[2,128,256]{2,1,0:T(8,128)(2,1)S(1)}, bf16[2,128,256]{2,1,0:T(8,128)(2,1)S(1)}, u32[]{:S(2)}, u32[]{:S(2)}) collective-permute-start(bf16[2,128,256]{2,1,0:T(8,128)(2,1)S(1)} %get-tuple-element.86), channel_id=1, source_target_pairs={{0,4},{1,5},{2,6},{3,7},{4,0},{5,1},{6,2},{7,3},{8,12},{9,13},{10,... | collective-permute-start | bytes 393224 | tf_op jit(solution)/shard_map/ppermute | solution.py:434
  18.0 3.0 %collective-permute-start.12 = (bf16[2,128,256]{2,1,0:T(8,128)(2,1)S(1)}, bf16[2,128,256]{2,1,0:T(8,128)(2,1)S(1)}, u32[]{:S(2)}, u32[]{:S(2)}) collective-permute-start(bf16[2,128,256]{2,1,0:T(8,128)(2,1)S(1)} %get-tuple-element.87), channel_id=1, source_target_pairs={{0,1},{1,0},{2,3},{3,2},{4,8},{5,9},{6,10},{7,11},{8,4},{9,5},{10,... | collective-permute-start | bytes 393224 | tf_op jit(solution)/shard_map/ppermute | solution.py:434
  18.1 4.5 %collective-permute-start.8 = (bf16[1,2,64,256]{3,2,1,0:T(8,128)(2,1)S(1)}, bf16[1,2,64,256]{3,2,1,0:T(8,128)(2,1)S(1)}, u32[]{:S(2)}, u32[]{:S(2)}) collective-permute-start(bf16[1,2,64,256]{3,2,1,0:T(8,128)(2,1)S(1)} %get-tuple-element.80), channel_id=1, source_target_pairs={{0,3},{1,2},{2,1},{3,0},{4,7},{5,6},{6,5},{7,4},{8,11},{9,10},{10,... | collective-permute-start | bytes 196616 | tf_op jit(solution)/shard_map/ppermute | solution.py:332
  19.6 4.8 %collective-permute-start.9 = (bf16[1,2,64,256]{3,2,1,0:T(8,128)(2,1)S(1)}, bf16[1,2,64,256]{3,2,1,0:T(8,128)(2,1)S(1)}, u32[]{:S(2)}, u32[]{:S(2)}) collective-permute-start(bf16[1,2,64,256]{3,2,1,0:T(8,128)(2,1)S(1)} %get-tuple-element.81), channel_id=1, source_target_pairs={{0,2},{1,3},{2,0},{3,1},{4,6},{5,7},{6,4},{7,5},{8,10},{9,11},{10,... | collective-permute-start | bytes 196616 | tf_op jit(solution)/shard_map/ppermute | solution.py:332
  20.3 4.1 %collective-permute-start.10 = (bf16[1,2,64,256]{3,2,1,0:T(8,128)(2,1)S(1)}, bf16[1,2,64,256]{3,2,1,0:T(8,128)(2,1)S(1)}, u32[]{:S(2)}, u32[]{:S(2)}) collective-permute-start(bf16[1,2,64,256]{3,2,1,0:T(8,128)(2,1)S(1)} %get-tuple-element.82), channel_id=1, source_target_pairs={{0,1},{1,0},{2,3},{3,2},{4,5},{5,4},{6,7},{7,6},{8,9},{9,8},{10,11... | collective-permute-start | bytes 196616 | tf_op jit(solution)/shard_map/ppermute | solution.py:332
  21.1 4.3 %collective-permute-start.13 = (bf16[1,2,64,256]{3,2,1,0:T(8,128)(2,1)S(1)}, bf16[1,2,64,256]{3,2,1,0:T(8,128)(2,1)S(1)}, u32[]{:S(2)}, u32[]{:S(2)}) collective-permute-start(bf16[1,2,64,256]{3,2,1,0:T(8,128)(2,1)S(1)} %get-tuple-element.89), channel_id=1, source_target_pairs={{0,2},{1,3},{2,0},{3,1},{4,6},{5,7},{6,4},{7,5},{8,10},{9,11},{10,... | collective-permute-start | bytes 196616 | tf_op jit(solution)/shard_map/ppermute | solution.py:332
  22.6 4.3 %collective-permute-start.14 = (bf16[1,2,64,256]{3,2,1,0:T(8,128)(2,1)S(1)}, bf16[1,2,64,256]{3,2,1,0:T(8,128)(2,1)S(1)}, u32[]{:S(2)}, u32[]{:S(2)}) collective-permute-start(bf16[1,2,64,256]{3,2,1,0:T(8,128)(2,1)S(1)} %get-tuple-element.90), channel_id=1, source_target_pairs={{0,3},{1,2},{2,1},{3,0},{4,7},{5,6},{6,5},{7,4},{8,11},{9,10},{10,... | collective-permute-start | bytes 196616 | tf_op jit(solution)/shard_map/ppermute | solution.py:332
  22.6 4.2 %collective-permute-start.15 = (bf16[1,2,64,256]{3,2,1,0:T(8,128)(2,1)S(1)}, bf16[1,2,64,256]{3,2,1,0:T(8,128)(2,1)S(1)}, u32[]{:S(2)}, u32[]{:S(2)}) collective-permute-start(bf16[1,2,64,256]{3,2,1,0:T(8,128)(2,1)S(1)} %get-tuple-element.91), channel_id=1, source_target_pairs={{0,1},{1,0},{2,3},{3,2},{4,5},{5,4},{6,7},{7,6},{8,9},{9,8},{10,11... | collective-permute-start | bytes 196616 | tf_op jit(solution)/shard_map/ppermute | solution.py:332

commit v10 on v9

--- a/solution.py
+++ b/solution.py
@@ -274,7 +274,7 @@
     for d, out in enumerate(outs):
         span = slice(d * rows, (d + 1) * rows)
         out[0, 0], out[0, 1] = mixed[span], qgrad[span]
-        near_out[d, 0], near_out[d, 1] = key_grad[span], value_grad[span]
+        near_out[d, 0], near_out[d, 1] = key_grad[span].astype(LOW), value_grad[span].astype(LOW)
 
 
 def rest_kernel(heads, places, final_ref, exps_ref, gw_ref, far_w_ref, far_ds_ref, query_down, grad_down, *refs):
@@ -298,7 +298,7 @@
     per_patch = back_a.shape[1] // rows
     me = lax.axis_index("head")
     for d in range(heads):
-        total = near[d]
+        total = near[d].astype(jnp.float32)
         part = lax.rem(me ^ d, per_patch)
         for s, back in enumerate((back_a, back_b)):
             slot = slot_ref[pl.ds(s * per_patch + part, 1), :]
@@ -350,7 +350,7 @@
     block = jax.ShapeDtypeStruct((1, 2, rows, width), LOW)
     order, downward = far_first(heads), [0] + list(range(heads - 1, 0, -1))
     places = [(order.index(d), 0) for d in range(heads)]
-    near_shape = jax.ShapeDtypeStruct((heads, 2, rows, width), jnp.float32)
+    near_shape = jax.ShapeDtypeStruct((heads, 2, rows, width), LOW)
     slab = jax.ShapeDtypeStruct((2, patch, width), LOW)
     whole = jax.ShapeDtypeStruct((rows, features), LOW)
     routes = pair_routes(owners, heads)

time: 27.7 us -> 27.8 us (level)
  no operation moved by 1% of the time
where the time goes in v10:
time: 27.8 us; the launch traced here: 27.6 us
  starting transfers between devices  13.7 us (49%)
  waiting for transfers between devices  7.25 us (26%)
  Pallas kernels  4.91 us (18%)
  local copies, waits for them, and re-layouts  0.92 us (3%)
  between operations  0.78 us (3%)
    ppermute x12, starting transfers between devices, exchange(): lax.ppermute(blocks[d], 'head', swaps[d])  9.82 us
    ppermute x12, waiting for transfers between devices, exchange(): lax.ppermute(blocks[d], 'head', swaps[d])  5.1 us
    pallas_call x11, Pallas kernels, call(): pl.pallas_call(kernel, out_shape=outs, in_specs=specs or [VMEM] * len(arg...  4.91 us
    ppermute x2, starting transfers between devices, shards(): lax.ppermute(p, ('node', 'head'), r)  2.2 us
    ppermute x2, starting transfers between devices, shards(): far = [lax.ppermute(p, ('node', 'head'), r) for p, r in zip(picked, routes)]  1.7 us
    ppermute x2, waiting for transfers between devices, shards(): far = [lax.ppermute(p, ('node', 'head'), r) for p, r in zip(picked, routes)]  1.45 us
    dynamic_slice x1, local copies, waits for them, and re-layouts, cut(): lax.dynamic_slice_in_dim(a, at, width, 1)  0.9 us
    ppermute x2, waiting for transfers between devices, shards(): lax.ppermute(p, ('node', 'head'), r)  0.7 us
  transfers between devices with their start and end apart: 16, of which 7 were waited for; matrix products, arithmetic and copies ran while one was open for 0% of the time, Pallas kernels for 11%

profile of v10, /device:TPU:0, one launch (start us, length us, event | category | flops | bytes accessed | tf_op | source)
XLA Modules:
  0.0 27.6 jit_solution(1426074720429992109)
XLA Ops:
  0.7 0.9 %constant_dynamic-slice_fusion = (bf16[64,256]{1,0:T(8,128)(2,1)S(1)}, bf16[64,256]{1,0:T(8,128)(2,1)S(1)}, bf16[64,256]{1,0:T(8,128)(2,1)S(1)}, bf16[64,256]{1,...) fusion(bf16[64,1024]{1,0:T(8,128)(2,1)} %param.7, ...), kind=kLoop, calls=%fused_computation | loop fusion | bytes 524304 | tf_op jit(solution)/shard_map/dynamic_slice | solution.py:339
  1.6 0.0 copy-start
  1.6 0.0 copy-start.1
  1.6 0.0 copy-start.2
  1.6 3.0 %collective-permute-start = (bf16[1,2,64,256]{3,2,1,0:T(8,128)(2,1)S(1)}, bf16[1,2,64,256]{3,2,1,0:T(8,128)(2,1)S(1)}, u32[]{:S(2)}, u32[]{:S(2)}) collective-permute-start(bf16[1,2,64,256]{3,2,1,0:T(8,128)(2,1)S(1)} %get-tuple-element.51), channel_id=1, source_target_pairs={{0,2},{1,3},{2,0},{3,1},{4,6},{5,7},{6,4},{7,5},{8,10},{9,11},{10,... | collective-permute-start | bytes 196616 | tf_op jit(solution)/shard_map/ppermute | solution.py:332
  4.6 0.0 collective-permute-start.1
  4.6 0.2 collective-permute-start.2
  4.8 0.0 copy-done.2
  4.8 0.8 %prep.1 = (f32[6,256]{1,0:T(8,128)S(1)}, s32[4,256]{1,0:T(4,128)S(1)}) custom-call(s32[8,8]{1,0:T(8,128)S(1)} %copy-done.2, bf16[1,2,64,256]{3,2,1,0:T(8,128)(2,1)S(1)} %get-tuple-element.49.after_ref.refs_0_.refs_3_), custom_call_target="tpu_custom_call" | custom-call | tf_op jit(solution)/shard_map/prep/pallas_call | solution.py:24
  5.7 0.0 copy-done
  5.7 0.0 copy-done.1
  5.7 2.0 %collective-permute-start.3 = (bf16[1,2,64,256]{3,2,1,0:T(8,128)(2,1)S(1)}, bf16[1,2,64,256]{3,2,1,0:T(8,128)(2,1)S(1)}, u32[]{:S(2)}, u32[]{:S(2)}) collective-permute-start(bf16[1,2,64,256]{3,2,1,0:T(8,128)(2,1)S(1)} %get-tuple-element.56), channel_id=1, source_target_pairs={{0,2},{1,3},{2,0},{3,1},{4,6},{5,7},{6,4},{7,5},{8,10},{9,11},{10,... | collective-permute-start | bytes 196616 | tf_op jit(solution)/shard_map/ppermute | solution.py:332
  7.8 0.0 collective-permute-start.4
  7.8 0.0 collective-permute-done.refs_1_.refs_4_
  7.8 0.2 collective-permute-start.5
  8.0 0.8 %collective-permute-done.1.refs_2_.refs_5_ = bf16[1,2,64,256]{3,2,1,0:T(8,128)(2,1)S(1)} collective-permute-done((bf16[1,2,64,256]{3,2,1,0:T(8,128)(2,1)S(1)}, bf16[1,2,64,256]{3,2,1,0:T(8,128)(2,1)S(1)}, u32[]{:S(2)}, u32[]{:S(2)}) %collective-permute-start.1) | collective-permute-done | bytes 65568 | tf_op jit(solution)/shard_map/ppermute | solution.py:332
  8.8 0.0 collective-permute-done.2.refs_3_.refs_6_
  8.8 0.1 pick.1
  8.9 1.7 %collective-permute-start.6 = (bf16[2,128,256]{2,1,0:T(8,128)(2,1)S(1)}, bf16[2,128,256]{2,1,0:T(8,128)(2,1)S(1)}, u32[]{:S(2)}, u32[]{:S(2)}) collective-permute-start(bf16[2,128,256]{2,1,0:T(8,128)(2,1)S(1)} %get-tuple-element.62), channel_id=1, source_target_pairs={{0,4},{1,5},{2,6},{3,7},{4,0},{5,1},{6,2},{7,3},{8,12},{9,13},{10,... | collective-permute-start | bytes 393224 | tf_op jit(solution)/shard_map/ppermute | solution.py:373
  10.6 0.0 collective-permute-start.7
  10.6 0.0 collective-permute-done.3.refs_5_
  10.6 1.5 %collective-permute-done.4.refs_6_ = bf16[1,2,64,256]{3,2,1,0:T(8,128)(2,1)S(1)} collective-permute-done((bf16[1,2,64,256]{3,2,1,0:T(8,128)(2,1)S(1)}, bf16[1,2,64,256]{3,2,1,0:T(8,128)(2,1)S(1)}, u32[]{:S(2)}, u32[]{:S(2)}) %collective-permute-start.4) | collective-permute-done | bytes 65568 | tf_op jit(solution)/shard_map/ppermute | solution.py:332
  12.1 0.0 collective-permute-done.5.refs_7_
  12.1 0.7 %near.1 = (f32[256,1024]{1,0:T(8,128)S(1)}, f32[256,1024]{1,0:T(8,128)S(1)}, f32[3,1024]{1,0:T(4,128)S(1)}, bf16[1024,256]{1,0:T(8,128)(2,1)S(1)}, bf16[256,1024...) custom-call(f32[6,256]{1,0:T(8,128)S(1)} %get-tuple-element.50.bias_ref, ...), custom_call_target="tpu_custom_call" | custom-call | flops 1500000000 | bytes 1 | tf_op jit(solution)/shard_map/near/pallas_call | solution.py:24
  12.7 1.4 %collective-permute-done.6.keys_ref.refs_7_.refs_4_ = bf16[2,128,256]{2,1,0:T(8,128)(2,1)S(1)} collective-permute-done((bf16[2,128,256]{2,1,0:T(8,128)(2,1)S(1)}, bf16[2,128,256]{2,1,0:T(8,128)(2,1)S(1)}, u32[]{:S(2)}, u32[]{:S(2)}) %collective-permute-start.6) | collective-permute-done | bytes 131104 | tf_op jit(solution)/shard_map/ppermute | solution.py:373
  14.2 0.4 %first.1 = (f32[128,1024]{1,0:T(8,128)S(1)}, f32[128,1024]{1,0:T(8,128)S(1)}, f32[3,1024]{1,0:T(4,128)S(1)}) custom-call(f32[6,256]{1,0:T(8,128)S(1)} %get-tuple-element.50.bias_ref, bf16[256,1024]{1,0:T(8,128)(2,1)S(1)} %get-tuple-element.60.query_across, bf16[256,1024]{1,0:T(8,128)(2,1)S(1)} %get-tuple-element.61.grad_across.refs_0_, ...), custom_call_target="tpu_custom_call" | custom-call | tf_op jit(solution)/shard_map/first/pallas_call | solution.py:24
  14.6 0.0 collective-permute-done.7.refs_8_.refs_5_
  14.6 1.2 %far.1 = (bf16[256,1024]{1,0:T(8,128)(2,1)S(1)}, bf16[256,1024]{1,0:T(8,128)(2,1)S(1)}, f32[2,1024]{1,0:T(2,128)S(1)}, bf16[2,128,256]{2,1,0:T(8,128)(2,1)S(1)},...) custom-call(f32[6,256]{1,0:T(8,128)S(1)} %get-tuple-element.50.bias_, ...), custom_call_target="tpu_custom_call" | custom-call | flops 1500000000 | bytes 1 | tf_op jit(solution)/shard_map/far/pallas_call | solution.py:24
  15.8 2.2 %collective-permute-start.11 = (bf16[2,128,256]{2,1,0:T(8,128)(2,1)S(1)}, bf16[2,128,256]{2,1,0:T(8,128)(2,1)S(1)}, u32[]{:S(2)}, u32[]{:S(2)}) collective-permute-start(bf16[2,128,256]{2,1,0:T(8,128)(2,1)S(1)} %get-tuple-element.86), channel_id=1, source_target_pairs={{0,4},{1,5},{2,6},{3,7},{4,0},{5,1},{6,2},{7,3},{8,12},{9,13},{10,... | collective-permute-start | bytes 393224 | tf_op jit(solution)/shard_map/ppermute | solution.py:434
  18.0 0.0 collective-permute-start.12
  18.0 1.5 %collective-permute-start.8 = (bf16[1,2,64,256]{3,2,1,0:T(8,128)(2,1)S(1)}, bf16[1,2,64,256]{3,2,1,0:T(8,128)(2,1)S(1)}, u32[]{:S(2)}, u32[]{:S(2)}) collective-permute-start(bf16[1,2,64,256]{3,2,1,0:T(8,128)(2,1)S(1)} %get-tuple-element.80), channel_id=1, source_target_pairs={{0,3},{1,2},{2,1},{3,0},{4,7},{5,6},{6,5},{7,4},{8,11},{9,10},{10,... | collective-permute-start | bytes 196616 | tf_op jit(solution)/shard_map/ppermute | solution.py:332
  19.6 0.7 %collective-permute-start.9 = (bf16[1,2,64,256]{3,2,1,0:T(8,128)(2,1)S(1)}, bf16[1,2,64,256]{3,2,1,0:T(8,128)(2,1)S(1)}, u32[]{:S(2)}, u32[]{:S(2)}) collective-permute-start(bf16[1,2,64,256]{3,2,1,0:T(8,128)(2,1)S(1)} %get-tuple-element.81), channel_id=1, source_target_pairs={{0,2},{1,3},{2,0},{3,1},{4,6},{5,7},{6,4},{7,5},{8,10},{9,11},{10,... | collective-permute-start | bytes 196616 | tf_op jit(solution)/shard_map/ppermute | solution.py:332
  20.2 0.0 collective-permute-start.10
  20.3 0.7 %collective-permute-done.11.back_a = bf16[2,128,256]{2,1,0:T(8,128)(2,1)S(1)} collective-permute-done((bf16[2,128,256]{2,1,0:T(8,128)(2,1)S(1)}, bf16[2,128,256]{2,1,0:T(8,128)(2,1)S(1)}, u32[]{:S(2)}, u32[]{:S(2)}) %collective-permute-start.11) | collective-permute-done | bytes 131104 | tf_op jit(solution)/shard_map/ppermute | solution.py:434
  20.9 0.0 collective-permute-done.12.back_b
  20.9 0.1 merge.1
  21.1 1.5 %collective-permute-start.13 = (bf16[1,2,64,256]{3,2,1,0:T(8,128)(2,1)S(1)}, bf16[1,2,64,256]{3,2,1,0:T(8,128)(2,1)S(1)}, u32[]{:S(2)}, u32[]{:S(2)}) collective-permute-start(bf16[1,2,64,256]{3,2,1,0:T(8,128)(2,1)S(1)} %get-tuple-element.89), channel_id=1, source_target_pairs={{0,2},{1,3},{2,0},{3,1},{4,6},{5,7},{6,4},{7,5},{8,10},{9,11},{10,... | collective-permute-start | bytes 196616 | tf_op jit(solution)/shard_map/ppermute | solution.py:332
  22.6 0.0 collective-permute-start.14
  22.6 0.0 collective-permute-done.8.refs_1_
  22.6 0.7 %collective-permute-start.15 = (bf16[1,2,64,256]{3,2,1,0:T(8,128)(2,1)S(1)}, bf16[1,2,64,256]{3,2,1,0:T(8,128)(2,1)S(1)}, u32[]{:S(2)}, u32[]{:S(2)}) collective-permute-start(bf16[1,2,64,256]{3,2,1,0:T(8,128)(2,1)S(1)} %get-tuple-element.91), channel_id=1, source_target_pairs={{0,1},{1,0},{2,3},{3,2},{4,5},{5,4},{6,7},{7,6},{8,9},{9,8},{10,11... | collective-permute-start | bytes 196616 | tf_op jit(solution)/shard_map/ppermute | solution.py:332
  23.3 1.0 %collective-permute-done.9.refs_2_ = bf16[1,2,64,256]{3,2,1,0:T(8,128)(2,1)S(1)} collective-permute-done((bf16[1,2,64,256]{3,2,1,0:T(8,128)(2,1)S(1)}, bf16[1,2,64,256]{3,2,1,0:T(8,128)(2,1)S(1)}, u32[]{:S(2)}, u32[]{:S(2)}) %collective-permute-start.9) | collective-permute-done | bytes 65568 | tf_op jit(solution)/shard_map/ppermute | solution.py:332
  24.3 0.0 collective-permute-done.10.refs_3_
  24.3 0.7 %unpack.2 = (bf16[64,1024]{1,0:T(8,128)(2,1)}, bf16[64,1024]{1,0:T(8,128)(2,1)}) custom-call(bf16[1,2,64,256]{3,2,1,0:T(8,128)(2,1)S(1)} %get-tuple-element.79.refs_0_, bf16[1,2,64,256]{3,2,1,0:T(8,128)(2,1)S(1)} %collective-permute-done.8.refs_1_, bf16[1,2,64,256]{3,2,1,0:T(8,128)(2,1)S(1)} %collective-permute-done.9.refs_2_, ...), custom_call_target="tpu_custom_call" | custom-call | tf_op jit(solution)/shard_map/unpack/pallas_call | solution.py:24
  25.0 0.4 %collective-permute-done.13.refs_1_ = bf16[1,2,64,256]{3,2,1,0:T(8,128)(2,1)S(1)} collective-permute-done((bf16[1,2,64,256]{3,2,1,0:T(8,128)(2,1)S(1)}, bf16[1,2,64,256]{3,2,1,0:T(8,128)(2,1)S(1)}, u32[]{:S(2)}, u32[]{:S(2)}) %collective-permute-start.13) | collective-permute-done | bytes 65568 | tf_op jit(solution)/shard_map/ppermute | solution.py:332
  25.4 1.4 %collective-permute-done.14.refs_2_ = bf16[1,2,64,256]{3,2,1,0:T(8,128)(2,1)S(1)} collective-permute-done((bf16[1,2,64,256]{3,2,1,0:T(8,128)(2,1)S(1)}, bf16[1,2,64,256]{3,2,1,0:T(8,128)(2,1)S(1)}, u32[]{:S(2)}, u32[]{:S(2)}) %collective-permute-start.14) | collective-permute-done | bytes 65568 | tf_op jit(solution)/shard_map/ppermute | solution.py:332
  26.8 0.0 collective-permute-done.15.refs_3_
  26.8 0.7 %unpack.3 = (bf16[64,1024]{1,0:T(8,128)(2,1)}, bf16[64,1024]{1,0:T(8,128)(2,1)}) custom-call(bf16[1,2,64,256]{3,2,1,0:T(8,128)(2,1)S(1)} %get-tuple-element.88.refs_0_, bf16[1,2,64,256]{3,2,1,0:T(8,128)(2,1)S(1)} %collective-permute-done.13.refs_1_, bf16[1,2,64,256]{3,2,1,0:T(8,128)(2,1)S(1)} %collective-permute-done.14.refs_2_, ...), custom_call_target="tpu_custom_call" | custom-call | tf_op jit(solution)/shard_map/unpack/pallas_call | solution.py:24
  (3 shorter events, 0.1 us)
Async XLA Ops:
  1.6 4.1 %copy-start = (bf16[64,1024]{1,0:T(8,128)(2,1)S(1)}, bf16[64,1024]{1,0:T(8,128)(2,1)}, u32[]{:S(2)}) copy-start(bf16[64,1024]{1,0:T(8,128)(2,1)} %one.1) | copy-start | bytes 393220
  1.6 4.1 %copy-start.1 = (bf16[64,1024]{1,0:T(8,128)(2,1)S(1)}, bf16[64,1024]{1,0:T(8,128)(2,1)}, u32[]{:S(2)}) copy-start(bf16[64,1024]{1,0:T(8,128)(2,1)} %two.1) | copy-start | bytes 393220
  1.6 3.2 %copy-start.2 = (s32[8,8]{1,0:T(8,128)S(1)}, s32[8,8]{1,0:T(8,128)}, u32[]{:S(2)}) copy-start(s32[8,8]{1,0:T(8,128)} %nbr_ref.1) | copy-start | bytes 772
  1.6 6.1 %collective-permute-start = (bf16[1,2,64,256]{3,2,1,0:T(8,128)(2,1)S(1)}, bf16[1,2,64,256]{3,2,1,0:T(8,128)(2,1)S(1)}, u32[]{:S(2)}, u32[]{:S(2)}) collective-permute-start(bf16[1,2,64,256]{3,2,1,0:T(8,128)(2,1)S(1)} %get-tuple-element.51), channel_id=1, source_target_pairs={{0,2},{1,3},{2,0},{3,1},{4,6},{5,7},{6,4},{7,5},{8,10},{9,11},{10,... | collective-permute-start | bytes 196616 | tf_op jit(solution)/shard_map/ppermute | solution.py:332
  4.6 4.1 %collective-permute-start.1 = (bf16[1,2,64,256]{3,2,1,0:T(8,128)(2,1)S(1)}, bf16[1,2,64,256]{3,2,1,0:T(8,128)(2,1)S(1)}, u32[]{:S(2)}, u32[]{:S(2)}) collective-permute-start(bf16[1,2,64,256]{3,2,1,0:T(8,128)(2,1)S(1)} %get-tuple-element.52), channel_id=1, source_target_pairs={{0,3},{1,2},{2,1},{3,0},{4,7},{5,6},{6,5},{7,4},{8,11},{9,10},{10,... | collective-permute-start | bytes 196616 | tf_op jit(solution)/shard_map/ppermute | solution.py:332
  4.6 4.1 %collective-permute-start.2 = (bf16[1,2,64,256]{3,2,1,0:T(8,128)(2,1)S(1)}, bf16[1,2,64,256]{3,2,1,0:T(8,128)(2,1)S(1)}, u32[]{:S(2)}, u32[]{:S(2)}) collective-permute-start(bf16[1,2,64,256]{3,2,1,0:T(8,128)(2,1)S(1)} %get-tuple-element.53), channel_id=1, source_target_pairs={{0,1},{1,0},{2,3},{3,2},{4,5},{5,4},{6,7},{7,6},{8,9},{9,8},{10,11... | collective-permute-start | bytes 196616 | tf_op jit(solution)/shard_map/ppermute | solution.py:332
  5.7 4.8 %collective-permute-start.3 = (bf16[1,2,64,256]{3,2,1,0:T(8,128)(2,1)S(1)}, bf16[1,2,64,256]{3,2,1,0:T(8,128)(2,1)S(1)}, u32[]{:S(2)}, u32[]{:S(2)}) collective-permute-start(bf16[1,2,64,256]{3,2,1,0:T(8,128)(2,1)S(1)} %get-tuple-element.56), channel_id=1, source_target_pairs={{0,2},{1,3},{2,0},{3,1},{4,6},{5,7},{6,4},{7,5},{8,10},{9,11},{10,... | collective-permute-start | bytes 196616 | tf_op jit(solution)/shard_map/ppermute | solution.py:332
  7.8 4.3 %collective-permute-start.4 = (bf16[1,2,64,256]{3,2,1,0:T(8,128)(2,1)S(1)}, bf16[1,2,64,256]{3,2,1,0:T(8,128)(2,1)S(1)}, u32[]{:S(2)}, u32[]{:S(2)}) collective-permute-start(bf16[1,2,64,256]{3,2,1,0:T(8,128)(2,1)S(1)} %get-tuple-element.57), channel_id=1, source_target_pairs={{0,3},{1,2},{2,1},{3,0},{4,7},{5,6},{6,5},{7,4},{8,11},{9,10},{10,... | collective-permute-start | bytes 196616 | tf_op jit(solution)/shard_map/ppermute | solution.py:332
  7.8 4.3 %collective-permute-start.5 = (bf16[1,2,64,256]{3,2,1,0:T(8,128)(2,1)S(1)}, bf16[1,2,64,256]{3,2,1,0:T(8,128)(2,1)S(1)}, u32[]{:S(2)}, u32[]{:S(2)}) collective-permute-start(bf16[1,2,64,256]{3,2,1,0:T(8,128)(2,1)S(1)} %get-tuple-element.58), channel_id=1, source_target_pairs={{0,1},{1,0},{2,3},{3,2},{4,5},{5,4},{6,7},{7,6},{8,9},{9,8},{10,11... | collective-permute-start | bytes 196616 | tf_op jit(solution)/shard_map/ppermute | solution.py:332
  8.9 5.3 %collective-permute-start.6 = (bf16[2,128,256]{2,1,0:T(8,128)(2,1)S(1)}, bf16[2,128,256]{2,1,0:T(8,128)(2,1)S(1)}, u32[]{:S(2)}, u32[]{:S(2)}) collective-permute-start(bf16[2,128,256]{2,1,0:T(8,128)(2,1)S(1)} %get-tuple-element.62), channel_id=1, source_target_pairs={{0,4},{1,5},{2,6},{3,7},{4,0},{5,1},{6,2},{7,3},{8,12},{9,13},{10,... | collective-permute-start | bytes 393224 | tf_op jit(solution)/shard_map/ppermute | solution.py:373
  10.6 4.0 %collective-permute-start.7 = (bf16[2,128,256]{2,1,0:T(8,128)(2,1)S(1)}, bf16[2,128,256]{2,1,0:T(8,128)(2,1)S(1)}, u32[]{:S(2)}, u32[]{:S(2)}) collective-permute-start(bf16[2,128,256]{2,1,0:T(8,128)(2,1)S(1)} %get-tuple-element.70), channel_id=1, source_target_pairs={{0,1},{1,0},{2,3},{3,2},{4,8},{5,9},{6,10},{7,11},{8,4},{9,5},{10,... | collective-permute-start | bytes 393224 | tf_op jit(solution)/shard_map/ppermute | solution.py:373
  15.8 5.1 %collective-permute-start.11 = (bf16[2,128,256]{2,1,0:T(8,128)(2,1)S(1)}, bf16[2,128,256]{2,1,0:T(8,128)(2,1)S(1)}, u32[]{:S(2)}, u32[]{:S(2)}) collective-permute-start(bf16[2,128,256]{2,1,0:T(8,128)(2,1)S(1)} %get-tuple-element.86), channel_id=1, source_target_pairs={{0,4},{1,5},{2,6},{3,7},{4,0},{5,1},{6,2},{7,3},{8,12},{9,13},{10,... | collective-permute-start | bytes 393224 | tf_op jit(solution)/shard_map/ppermute | solution.py:434
  18.0 3.0 %collective-permute-start.12 = (bf16[2,128,256]{2,1,0:T(8,128)(2,1)S(1)}, bf16[2,128,256]{2,1,0:T(8,128)(2,1)S(1)}, u32[]{:S(2)}, u32[]{:S(2)}) collective-permute-start(bf16[2,128,256]{2,1,0:T(8,128)(2,1)S(1)} %get-tuple-element.87), channel_id=1, source_target_pairs={{0,1},{1,0},{2,3},{3,2},{4,8},{5,9},{6,10},{7,11},{8,4},{9,5},{10,... | collective-permute-start | bytes 393224 | tf_op jit(solution)/shard_map/ppermute | solution.py:434
  18.0 4.5 %collective-permute-start.8 = (bf16[1,2,64,256]{3,2,1,0:T(8,128)(2,1)S(1)}, bf16[1,2,64,256]{3,2,1,0:T(8,128)(2,1)S(1)}, u32[]{:S(2)}, u32[]{:S(2)}) collective-permute-start(bf16[1,2,64,256]{3,2,1,0:T(8,128)(2,1)S(1)} %get-tuple-element.80), channel_id=1, source_target_pairs={{0,3},{1,2},{2,1},{3,0},{4,7},{5,6},{6,5},{7,4},{8,11},{9,10},{10,... | collective-permute-start | bytes 196616 | tf_op jit(solution)/shard_map/ppermute | solution.py:332
  19.6 4.7 %collective-permute-start.9 = (bf16[1,2,64,256]{3,2,1,0:T(8,128)(2,1)S(1)}, bf16[1,2,64,256]{3,2,1,0:T(8,128)(2,1)S(1)}, u32[]{:S(2)}, u32[]{:S(2)}) collective-permute-start(bf16[1,2,64,256]{3,2,1,0:T(8,128)(2,1)S(1)} %get-tuple-element.81), channel_id=1, source_target_pairs={{0,2},{1,3},{2,0},{3,1},{4,6},{5,7},{6,4},{7,5},{8,10},{9,11},{10,... | collective-permute-start | bytes 196616 | tf_op jit(solution)/shard_map/ppermute | solution.py:332
  20.2 4.1 %collective-permute-start.10 = (bf16[1,2,64,256]{3,2,1,0:T(8,128)(2,1)S(1)}, bf16[1,2,64,256]{3,2,1,0:T(8,128)(2,1)S(1)}, u32[]{:S(2)}, u32[]{:S(2)}) collective-permute-start(bf16[1,2,64,256]{3,2,1,0:T(8,128)(2,1)S(1)} %get-tuple-element.82), channel_id=1, source_target_pairs={{0,1},{1,0},{2,3},{3,2},{4,5},{5,4},{6,7},{7,6},{8,9},{9,8},{10,11... | collective-permute-start | bytes 196616 | tf_op jit(solution)/shard_map/ppermute | solution.py:332
  21.1 4.3 %collective-permute-start.13 = (bf16[1,2,64,256]{3,2,1,0:T(8,128)(2,1)S(1)}, bf16[1,2,64,256]{3,2,1,0:T(8,128)(2,1)S(1)}, u32[]{:S(2)}, u32[]{:S(2)}) collective-permute-start(bf16[1,2,64,256]{3,2,1,0:T(8,128)(2,1)S(1)} %get-tuple-element.89), channel_id=1, source_target_pairs={{0,2},{1,3},{2,0},{3,1},{4,6},{5,7},{6,4},{7,5},{8,10},{9,11},{10,... | collective-permute-start | bytes 196616 | tf_op jit(solution)/shard_map/ppermute | solution.py:332
  22.6 4.2 %collective-permute-start.14 = (bf16[1,2,64,256]{3,2,1,0:T(8,128)(2,1)S(1)}, bf16[1,2,64,256]{3,2,1,0:T(8,128)(2,1)S(1)}, u32[]{:S(2)}, u32[]{:S(2)}) collective-permute-start(bf16[1,2,64,256]{3,2,1,0:T(8,128)(2,1)S(1)} %get-tuple-element.90), channel_id=1, source_target_pairs={{0,3},{1,2},{2,1},{3,0},{4,7},{5,6},{6,5},{7,4},{8,11},{9,10},{10,... | collective-permute-start | bytes 196616 | tf_op jit(solution)/shard_map/ppermute | solution.py:332
  22.6 4.2 %collective-permute-start.15 = (bf16[1,2,64,256]{3,2,1,0:T(8,128)(2,1)S(1)}, bf16[1,2,64,256]{3,2,1,0:T(8,128)(2,1)S(1)}, u32[]{:S(2)}, u32[]{:S(2)}) collective-permute-start(bf16[1,2,64,256]{3,2,1,0:T(8,128)(2,1)S(1)} %get-tuple-element.91), channel_id=1, source_target_pairs={{0,1},{1,0},{2,3},{3,2},{4,5},{5,4},{6,7},{7,6},{8,9},{9,8},{10,11... | collective-permute-start | bytes 196616 | tf_op jit(solution)/shard_map/ppermute | solution.py:332

commit v11 on v10

--- a/solution.py
+++ b/solution.py
@@ -113,14 +113,14 @@
     arrays, outs = refs[:-2], refs[-2:]
     rows = arrays[0].shape[2]
     per_patch = outs[0].shape[1] // rows
-    blocks = [arrays[a][j].astype(jnp.float32) for a, j in places]
+    blocks = [arrays[a][j] for a, j in places]
     for s, out in enumerate(outs):
         for t in range(per_patch):
             slot = slot_ref[s * per_patch + t : s * per_patch + t + 1, :]
             value = blocks[0]
             for d in range(1, heads):
-                value = jnp.where((slot == d)[None], blocks[d], value)
-            out[:, t * rows : (t + 1) * rows, :] = value.astype(LOW)
+                value = jnp.where(jnp.broadcast_to(slot == d, value.shape[1:])[None], blocks[d], value)
+            out[:, t * rows : (t + 1) * rows, :] = value
 
 
 def spread(bias_ref, first, sizes):

time: 27.8 us -> 27.7 us (level)
  no operation moved by 1% of the time
where the time goes in v11:
time: 27.7 us; the launch traced here: 27.5 us
  starting transfers between devices  13.7 us (49%)
  waiting for transfers between devices  7.25 us (26%)
  Pallas kernels  4.85 us (18%)
  local copies, waits for them, and re-layouts  0.92 us (3%)
  between operations  0.78 us (3%)
    ppermute x12, starting transfers between devices, exchange(): lax.ppermute(blocks[d], 'head', swaps[d])  9.82 us
    ppermute x12, waiting for transfers between devices, exchange(): lax.ppermute(blocks[d], 'head', swaps[d])  5.16 us
    pallas_call x11, Pallas kernels, call(): pl.pallas_call(kernel, out_shape=outs, in_specs=specs or [VMEM] * len(arg...  4.85 us
    ppermute x2, starting transfers between devices, shards(): lax.ppermute(p, ('node', 'head'), r)  2.2 us
    ppermute x2, starting transfers between devices, shards(): far = [lax.ppermute(p, ('node', 'head'), r) for p, r in zip(picked, routes)]  1.7 us
    ppermute x2, waiting for transfers between devices, shards(): far = [lax.ppermute(p, ('node', 'head'), r) for p, r in zip(picked, routes)]  1.39 us
    dynamic_slice x1, local copies, waits for them, and re-layouts, cut(): lax.dynamic_slice_in_dim(a, at, width, 1)  0.9 us
    ppermute x2, waiting for transfers between devices, shards(): lax.ppermute(p, ('node', 'head'), r)  0.7 us
  transfers between devices with their start and end apart: 16, of which 7 were waited for; matrix products, arithmetic and copies ran while one was open for 0% of the time, Pallas kernels for 11%

profile of v11, /device:TPU:0, one launch (start us, length us, event | category | flops | bytes accessed | tf_op | source)
XLA Modules:
  0.0 27.5 jit_solution(18246578642933391269)
XLA Ops:
  0.7 0.9 %constant_dynamic-slice_fusion = (bf16[64,256]{1,0:T(8,128)(2,1)S(1)}, bf16[64,256]{1,0:T(8,128)(2,1)S(1)}, bf16[64,256]{1,0:T(8,128)(2,1)S(1)}, bf16[64,256]{1,...) fusion(bf16[64,1024]{1,0:T(8,128)(2,1)} %param.7, ...), kind=kLoop, calls=%fused_computation | loop fusion | bytes 524304 | tf_op jit(solution)/shard_map/dynamic_slice | solution.py:339
  1.6 0.0 copy-start
  1.6 0.0 copy-start.1
  1.6 0.0 copy-start.2
  1.6 3.0 %collective-permute-start = (bf16[1,2,64,256]{3,2,1,0:T(8,128)(2,1)S(1)}, bf16[1,2,64,256]{3,2,1,0:T(8,128)(2,1)S(1)}, u32[]{:S(2)}, u32[]{:S(2)}) collective-permute-start(bf16[1,2,64,256]{3,2,1,0:T(8,128)(2,1)S(1)} %get-tuple-element.51), channel_id=1, source_target_pairs={{0,2},{1,3},{2,0},{3,1},{4,6},{5,7},{6,4},{7,5},{8,10},{9,11},{10,... | collective-permute-start | bytes 196616 | tf_op jit(solution)/shard_map/ppermute | solution.py:332
  4.6 0.0 collective-permute-start.1
  4.6 0.2 collective-permute-start.2
  4.8 0.0 copy-done.2
  4.8 0.8 %prep.1 = (f32[6,256]{1,0:T(8,128)S(1)}, s32[4,256]{1,0:T(4,128)S(1)}) custom-call(s32[8,8]{1,0:T(8,128)S(1)} %copy-done.2, bf16[1,2,64,256]{3,2,1,0:T(8,128)(2,1)S(1)} %get-tuple-element.49.after_ref.refs_0_.refs_3_), custom_call_target="tpu_custom_call" | custom-call | tf_op jit(solution)/shard_map/prep/pallas_call | solution.py:24
  5.7 0.0 copy-done
  5.7 0.0 copy-done.1
  5.7 2.0 %collective-permute-start.3 = (bf16[1,2,64,256]{3,2,1,0:T(8,128)(2,1)S(1)}, bf16[1,2,64,256]{3,2,1,0:T(8,128)(2,1)S(1)}, u32[]{:S(2)}, u32[]{:S(2)}) collective-permute-start(bf16[1,2,64,256]{3,2,1,0:T(8,128)(2,1)S(1)} %get-tuple-element.56), channel_id=1, source_target_pairs={{0,2},{1,3},{2,0},{3,1},{4,6},{5,7},{6,4},{7,5},{8,10},{9,11},{10,... | collective-permute-start | bytes 196616 | tf_op jit(solution)/shard_map/ppermute | solution.py:332
  7.8 0.0 collective-permute-start.4
  7.8 0.0 collective-permute-done.refs_1_.refs_4_
  7.8 0.2 collective-permute-start.5
  8.0 0.8 %collective-permute-done.1.refs_2_.refs_5_ = bf16[1,2,64,256]{3,2,1,0:T(8,128)(2,1)S(1)} collective-permute-done((bf16[1,2,64,256]{3,2,1,0:T(8,128)(2,1)S(1)}, bf16[1,2,64,256]{3,2,1,0:T(8,128)(2,1)S(1)}, u32[]{:S(2)}, u32[]{:S(2)}) %collective-permute-start.1) | collective-permute-done | bytes 65568 | tf_op jit(solution)/shard_map/ppermute | solution.py:332
  8.8 0.0 collective-permute-done.2.refs_3_.refs_6_
  8.8 1.7 %collective-permute-start.6 = (bf16[2,128,256]{2,1,0:T(8,128)(2,1)S(1)}, bf16[2,128,256]{2,1,0:T(8,128)(2,1)S(1)}, u32[]{:S(2)}, u32[]{:S(2)}) collective-permute-start(bf16[2,128,256]{2,1,0:T(8,128)(2,1)S(1)} %get-tuple-element.62), channel_id=1, source_target_pairs={{0,4},{1,5},{2,6},{3,7},{4,0},{5,1},{6,2},{7,3},{8,12},{9,13},{10,... | collective-permute-start | bytes 393224 | tf_op jit(solution)/shard_map/ppermute | solution.py:373
  10.5 0.0 collective-permute-start.7
  10.5 0.0 collective-permute-done.3.refs_5_
  10.5 1.5 %collective-permute-done.4.refs_6_ = bf16[1,2,64,256]{3,2,1,0:T(8,128)(2,1)S(1)} collective-permute-done((bf16[1,2,64,256]{3,2,1,0:T(8,128)(2,1)S(1)}, bf16[1,2,64,256]{3,2,1,0:T(8,128)(2,1)S(1)}, u32[]{:S(2)}, u32[]{:S(2)}) %collective-permute-start.4) | collective-permute-done | bytes 65568 | tf_op jit(solution)/shard_map/ppermute | solution.py:332
  12.1 0.0 collective-permute-done.5.refs_7_
  12.1 0.7 %near.1 = (f32[256,1024]{1,0:T(8,128)S(1)}, f32[256,1024]{1,0:T(8,128)S(1)}, f32[3,1024]{1,0:T(4,128)S(1)}, bf16[1024,256]{1,0:T(8,128)(2,1)S(1)}, bf16[256,1024...) custom-call(f32[6,256]{1,0:T(8,128)S(1)} %get-tuple-element.50.bias_ref, ...), custom_call_target="tpu_custom_call" | custom-call | flops 1500000000 | bytes 1 | tf_op jit(solution)/shard_map/near/pallas_call | solution.py:24
  12.7 1.4 %collective-permute-done.6.keys_ref.refs_7_.refs_4_ = bf16[2,128,256]{2,1,0:T(8,128)(2,1)S(1)} collective-permute-done((bf16[2,128,256]{2,1,0:T(8,128)(2,1)S(1)}, bf16[2,128,256]{2,1,0:T(8,128)(2,1)S(1)}, u32[]{:S(2)}, u32[]{:S(2)}) %collective-permute-start.6) | collective-permute-done | bytes 131104 | tf_op jit(solution)/shard_map/ppermute | solution.py:373
  14.1 0.4 %first.1 = (f32[128,1024]{1,0:T(8,128)S(1)}, f32[128,1024]{1,0:T(8,128)S(1)}, f32[3,1024]{1,0:T(4,128)S(1)}) custom-call(f32[6,256]{1,0:T(8,128)S(1)} %get-tuple-element.50.bias_ref, bf16[256,1024]{1,0:T(8,128)(2,1)S(1)} %get-tuple-element.60.query_across, bf16[256,1024]{1,0:T(8,128)(2,1)S(1)} %get-tuple-element.61.grad_across.refs_0_, ...), custom_call_target="tpu_custom_call" | custom-call | tf_op jit(solution)/shard_map/first/pallas_call | solution.py:24
  14.5 0.0 collective-permute-done.7.refs_8_.refs_5_
  14.5 1.2 %far.1 = (bf16[256,1024]{1,0:T(8,128)(2,1)S(1)}, bf16[256,1024]{1,0:T(8,128)(2,1)S(1)}, f32[2,1024]{1,0:T(2,128)S(1)}, bf16[2,128,256]{2,1,0:T(8,128)(2,1)S(1)},...) custom-call(f32[6,256]{1,0:T(8,128)S(1)} %get-tuple-element.50.bias_, ...), custom_call_target="tpu_custom_call" | custom-call | flops 1500000000 | bytes 1 | tf_op jit(solution)/shard_map/far/pallas_call | solution.py:24
  15.7 2.2 %collective-permute-start.11 = (bf16[2,128,256]{2,1,0:T(8,128)(2,1)S(1)}, bf16[2,128,256]{2,1,0:T(8,128)(2,1)S(1)}, u32[]{:S(2)}, u32[]{:S(2)}) collective-permute-start(bf16[2,128,256]{2,1,0:T(8,128)(2,1)S(1)} %get-tuple-element.86), channel_id=1, source_target_pairs={{0,4},{1,5},{2,6},{3,7},{4,0},{5,1},{6,2},{7,3},{8,12},{9,13},{10,... | collective-permute-start | bytes 393224 | tf_op jit(solution)/shard_map/ppermute | solution.py:434
  17.9 0.0 collective-permute-start.12
  18.0 1.5 %collective-permute-start.8 = (bf16[1,2,64,256]{3,2,1,0:T(8,128)(2,1)S(1)}, bf16[1,2,64,256]{3,2,1,0:T(8,128)(2,1)S(1)}, u32[]{:S(2)}, u32[]{:S(2)}) collective-permute-start(bf16[1,2,64,256]{3,2,1,0:T(8,128)(2,1)S(1)} %get-tuple-element.80), channel_id=1, source_target_pairs={{0,3},{1,2},{2,1},{3,0},{4,7},{5,6},{6,5},{7,4},{8,11},{9,10},{10,... | collective-permute-start | bytes 196616 | tf_op jit(solution)/shard_map/ppermute | solution.py:332
  19.5 0.7 %collective-permute-start.9 = (bf16[1,2,64,256]{3,2,1,0:T(8,128)(2,1)S(1)}, bf16[1,2,64,256]{3,2,1,0:T(8,128)(2,1)S(1)}, u32[]{:S(2)}, u32[]{:S(2)}) collective-permute-start(bf16[1,2,64,256]{3,2,1,0:T(8,128)(2,1)S(1)} %get-tuple-element.81), channel_id=1, source_target_pairs={{0,2},{1,3},{2,0},{3,1},{4,6},{5,7},{6,4},{7,5},{8,10},{9,11},{10,... | collective-permute-start | bytes 196616 | tf_op jit(solution)/shard_map/ppermute | solution.py:332
  20.2 0.0 collective-permute-start.10
  20.2 0.7 %collective-permute-done.11.back_a = bf16[2,128,256]{2,1,0:T(8,128)(2,1)S(1)} collective-permute-done((bf16[2,128,256]{2,1,0:T(8,128)(2,1)S(1)}, bf16[2,128,256]{2,1,0:T(8,128)(2,1)S(1)}, u32[]{:S(2)}, u32[]{:S(2)}) %collective-permute-start.11) | collective-permute-done | bytes 131104 | tf_op jit(solution)/shard_map/ppermute | solution.py:434
  20.9 0.0 collective-permute-done.12.back_b
  20.9 0.1 merge.1
  21.0 1.5 %collective-permute-start.13 = (bf16[1,2,64,256]{3,2,1,0:T(8,128)(2,1)S(1)}, bf16[1,2,64,256]{3,2,1,0:T(8,128)(2,1)S(1)}, u32[]{:S(2)}, u32[]{:S(2)}) collective-permute-start(bf16[1,2,64,256]{3,2,1,0:T(8,128)(2,1)S(1)} %get-tuple-element.89), channel_id=1, source_target_pairs={{0,2},{1,3},{2,0},{3,1},{4,6},{5,7},{6,4},{7,5},{8,10},{9,11},{10,... | collective-permute-start | bytes 196616 | tf_op jit(solution)/shard_map/ppermute | solution.py:332
  22.5 0.0 collective-permute-start.14
  22.5 0.0 collective-permute-done.8.refs_1_
  22.5 0.7 %collective-permute-start.15 = (bf16[1,2,64,256]{3,2,1,0:T(8,128)(2,1)S(1)}, bf16[1,2,64,256]{3,2,1,0:T(8,128)(2,1)S(1)}, u32[]{:S(2)}, u32[]{:S(2)}) collective-permute-start(bf16[1,2,64,256]{3,2,1,0:T(8,128)(2,1)S(1)} %get-tuple-element.91), channel_id=1, source_target_pairs={{0,1},{1,0},{2,3},{3,2},{4,5},{5,4},{6,7},{7,6},{8,9},{9,8},{10,11... | collective-permute-start | bytes 196616 | tf_op jit(solution)/shard_map/ppermute | solution.py:332
  23.3 1.0 %collective-permute-done.9.refs_2_ = bf16[1,2,64,256]{3,2,1,0:T(8,128)(2,1)S(1)} collective-permute-done((bf16[1,2,64,256]{3,2,1,0:T(8,128)(2,1)S(1)}, bf16[1,2,64,256]{3,2,1,0:T(8,128)(2,1)S(1)}, u32[]{:S(2)}, u32[]{:S(2)}) %collective-permute-start.9) | collective-permute-done | bytes 65568 | tf_op jit(solution)/shard_map/ppermute | solution.py:332
  24.3 0.0 collective-permute-done.10.refs_3_
  24.3 0.7 %unpack.2 = (bf16[64,1024]{1,0:T(8,128)(2,1)}, bf16[64,1024]{1,0:T(8,128)(2,1)}) custom-call(bf16[1,2,64,256]{3,2,1,0:T(8,128)(2,1)S(1)} %get-tuple-element.79.refs_0_, bf16[1,2,64,256]{3,2,1,0:T(8,128)(2,1)S(1)} %collective-permute-done.8.refs_1_, bf16[1,2,64,256]{3,2,1,0:T(8,128)(2,1)S(1)} %collective-permute-done.9.refs_2_, ...), custom_call_target="tpu_custom_call" | custom-call | tf_op jit(solution)/shard_map/unpack/pallas_call | solution.py:24
  25.0 0.4 %collective-permute-done.13.refs_1_ = bf16[1,2,64,256]{3,2,1,0:T(8,128)(2,1)S(1)} collective-permute-done((bf16[1,2,64,256]{3,2,1,0:T(8,128)(2,1)S(1)}, bf16[1,2,64,256]{3,2,1,0:T(8,128)(2,1)S(1)}, u32[]{:S(2)}, u32[]{:S(2)}) %collective-permute-start.13) | collective-permute-done | bytes 65568 | tf_op jit(solution)/shard_map/ppermute | solution.py:332
  25.4 1.4 %collective-permute-done.14.refs_2_ = bf16[1,2,64,256]{3,2,1,0:T(8,128)(2,1)S(1)} collective-permute-done((bf16[1,2,64,256]{3,2,1,0:T(8,128)(2,1)S(1)}, bf16[1,2,64,256]{3,2,1,0:T(8,128)(2,1)S(1)}, u32[]{:S(2)}, u32[]{:S(2)}) %collective-permute-start.14) | collective-permute-done | bytes 65568 | tf_op jit(solution)/shard_map/ppermute | solution.py:332
  26.8 0.0 collective-permute-done.15.refs_3_
  26.8 0.7 %unpack.3 = (bf16[64,1024]{1,0:T(8,128)(2,1)}, bf16[64,1024]{1,0:T(8,128)(2,1)}) custom-call(bf16[1,2,64,256]{3,2,1,0:T(8,128)(2,1)S(1)} %get-tuple-element.88.refs_0_, bf16[1,2,64,256]{3,2,1,0:T(8,128)(2,1)S(1)} %collective-permute-done.13.refs_1_, bf16[1,2,64,256]{3,2,1,0:T(8,128)(2,1)S(1)} %collective-permute-done.14.refs_2_, ...), custom_call_target="tpu_custom_call" | custom-call | tf_op jit(solution)/shard_map/unpack/pallas_call | solution.py:24
  (4 shorter events, 0.2 us)
Async XLA Ops:
  1.6 4.1 %copy-start = (bf16[64,1024]{1,0:T(8,128)(2,1)S(1)}, bf16[64,1024]{1,0:T(8,128)(2,1)}, u32[]{:S(2)}) copy-start(bf16[64,1024]{1,0:T(8,128)(2,1)} %one.1) | copy-start | bytes 393220
  1.6 4.1 %copy-start.1 = (bf16[64,1024]{1,0:T(8,128)(2,1)S(1)}, bf16[64,1024]{1,0:T(8,128)(2,1)}, u32[]{:S(2)}) copy-start(bf16[64,1024]{1,0:T(8,128)(2,1)} %two.1) | copy-start | bytes 393220
  1.6 3.2 %copy-start.2 = (s32[8,8]{1,0:T(8,128)S(1)}, s32[8,8]{1,0:T(8,128)}, u32[]{:S(2)}) copy-start(s32[8,8]{1,0:T(8,128)} %nbr_ref.1) | copy-start | bytes 772
  1.6 6.1 %collective-permute-start = (bf16[1,2,64,256]{3,2,1,0:T(8,128)(2,1)S(1)}, bf16[1,2,64,256]{3,2,1,0:T(8,128)(2,1)S(1)}, u32[]{:S(2)}, u32[]{:S(2)}) collective-permute-start(bf16[1,2,64,256]{3,2,1,0:T(8,128)(2,1)S(1)} %get-tuple-element.51), channel_id=1, source_target_pairs={{0,2},{1,3},{2,0},{3,1},{4,6},{5,7},{6,4},{7,5},{8,10},{9,11},{10,... | collective-permute-start | bytes 196616 | tf_op jit(solution)/shard_map/ppermute | solution.py:332
  4.6 4.1 %collective-permute-start.1 = (bf16[1,2,64,256]{3,2,1,0:T(8,128)(2,1)S(1)}, bf16[1,2,64,256]{3,2,1,0:T(8,128)(2,1)S(1)}, u32[]{:S(2)}, u32[]{:S(2)}) collective-permute-start(bf16[1,2,64,256]{3,2,1,0:T(8,128)(2,1)S(1)} %get-tuple-element.52), channel_id=1, source_target_pairs={{0,3},{1,2},{2,1},{3,0},{4,7},{5,6},{6,5},{7,4},{8,11},{9,10},{10,... | collective-permute-start | bytes 196616 | tf_op jit(solution)/shard_map/ppermute | solution.py:332
  4.6 4.1 %collective-permute-start.2 = (bf16[1,2,64,256]{3,2,1,0:T(8,128)(2,1)S(1)}, bf16[1,2,64,256]{3,2,1,0:T(8,128)(2,1)S(1)}, u32[]{:S(2)}, u32[]{:S(2)}) collective-permute-start(bf16[1,2,64,256]{3,2,1,0:T(8,128)(2,1)S(1)} %get-tuple-element.53), channel_id=1, source_target_pairs={{0,1},{1,0},{2,3},{3,2},{4,5},{5,4},{6,7},{7,6},{8,9},{9,8},{10,11... | collective-permute-start | bytes 196616 | tf_op jit(solution)/shard_map/ppermute | solution.py:332
  5.7 4.8 %collective-permute-start.3 = (bf16[1,2,64,256]{3,2,1,0:T(8,128)(2,1)S(1)}, bf16[1,2,64,256]{3,2,1,0:T(8,128)(2,1)S(1)}, u32[]{:S(2)}, u32[]{:S(2)}) collective-permute-start(bf16[1,2,64,256]{3,2,1,0:T(8,128)(2,1)S(1)} %get-tuple-element.56), channel_id=1, source_target_pairs={{0,2},{1,3},{2,0},{3,1},{4,6},{5,7},{6,4},{7,5},{8,10},{9,11},{10,... | collective-permute-start | bytes 196616 | tf_op jit(solution)/shard_map/ppermute | solution.py:332
  7.8 4.3 %collective-permute-start.4 = (bf16[1,2,64,256]{3,2,1,0:T(8,128)(2,1)S(1)}, bf16[1,2,64,256]{3,2,1,0:T(8,128)(2,1)S(1)}, u32[]{:S(2)}, u32[]{:S(2)}) collective-permute-start(bf16[1,2,64,256]{3,2,1,0:T(8,128)(2,1)S(1)} %get-tuple-element.57), channel_id=1, source_target_pairs={{0,3},{1,2},{2,1},{3,0},{4,7},{5,6},{6,5},{7,4},{8,11},{9,10},{10,... | collective-permute-start | bytes 196616 | tf_op jit(solution)/shard_map/ppermute | solution.py:332
  7.8 4.3 %collective-permute-start.5 = (bf16[1,2,64,256]{3,2,1,0:T(8,128)(2,1)S(1)}, bf16[1,2,64,256]{3,2,1,0:T(8,128)(2,1)S(1)}, u32[]{:S(2)}, u32[]{:S(2)}) collective-permute-start(bf16[1,2,64,256]{3,2,1,0:T(8,128)(2,1)S(1)} %get-tuple-element.58), channel_id=1, source_target_pairs={{0,1},{1,0},{2,3},{3,2},{4,5},{5,4},{6,7},{7,6},{8,9},{9,8},{10,11... | collective-permute-start | bytes 196616 | tf_op jit(solution)/shard_map/ppermute | solution.py:332
  8.8 5.3 %collective-permute-start.6 = (bf16[2,128,256]{2,1,0:T(8,128)(2,1)S(1)}, bf16[2,128,256]{2,1,0:T(8,128)(2,1)S(1)}, u32[]{:S(2)}, u32[]{:S(2)}) collective-permute-start(bf16[2,128,256]{2,1,0:T(8,128)(2,1)S(1)} %get-tuple-element.62), channel_id=1, source_target_pairs={{0,4},{1,5},{2,6},{3,7},{4,0},{5,1},{6,2},{7,3},{8,12},{9,13},{10,... | collective-permute-start | bytes 393224 | tf_op jit(solution)/shard_map/ppermute | solution.py:373
  10.5 4.0 %collective-permute-start.7 = (bf16[2,128,256]{2,1,0:T(8,128)(2,1)S(1)}, bf16[2,128,256]{2,1,0:T(8,128)(2,1)S(1)}, u32[]{:S(2)}, u32[]{:S(2)}) collective-permute-start(bf16[2,128,256]{2,1,0:T(8,128)(2,1)S(1)} %get-tuple-element.70), channel_id=1, source_target_pairs={{0,1},{1,0},{2,3},{3,2},{4,8},{5,9},{6,10},{7,11},{8,4},{9,5},{10,... | collective-permute-start | bytes 393224 | tf_op jit(solution)/shard_map/ppermute | solution.py:373
  15.7 5.1 %collective-permute-start.11 = (bf16[2,128,256]{2,1,0:T(8,128)(2,1)S(1)}, bf16[2,128,256]{2,1,0:T(8,128)(2,1)S(1)}, u32[]{:S(2)}, u32[]{:S(2)}) collective-permute-start(bf16[2,128,256]{2,1,0:T(8,128)(2,1)S(1)} %get-tuple-element.86), channel_id=1, source_target_pairs={{0,4},{1,5},{2,6},{3,7},{4,0},{5,1},{6,2},{7,3},{8,12},{9,13},{10,... | collective-permute-start | bytes 393224 | tf_op jit(solution)/shard_map/ppermute | solution.py:434
  17.9 3.0 %collective-permute-start.12 = (bf16[2,128,256]{2,1,0:T(8,128)(2,1)S(1)}, bf16[2,128,256]{2,1,0:T(8,128)(2,1)S(1)}, u32[]{:S(2)}, u32[]{:S(2)}) collective-permute-start(bf16[2,128,256]{2,1,0:T(8,128)(2,1)S(1)} %get-tuple-element.87), channel_id=1, source_target_pairs={{0,1},{1,0},{2,3},{3,2},{4,8},{5,9},{6,10},{7,11},{8,4},{9,5},{10,... | collective-permute-start | bytes 393224 | tf_op jit(solution)/shard_map/ppermute | solution.py:434
  18.0 4.6 %collective-permute-start.8 = (bf16[1,2,64,256]{3,2,1,0:T(8,128)(2,1)S(1)}, bf16[1,2,64,256]{3,2,1,0:T(8,128)(2,1)S(1)}, u32[]{:S(2)}, u32[]{:S(2)}) collective-permute-start(bf16[1,2,64,256]{3,2,1,0:T(8,128)(2,1)S(1)} %get-tuple-element.80), channel_id=1, source_target_pairs={{0,3},{1,2},{2,1},{3,0},{4,7},{5,6},{6,5},{7,4},{8,11},{9,10},{10,... | collective-permute-start | bytes 196616 | tf_op jit(solution)/shard_map/ppermute | solution.py:332
  19.5 4.7 %collective-permute-start.9 = (bf16[1,2,64,256]{3,2,1,0:T(8,128)(2,1)S(1)}, bf16[1,2,64,256]{3,2,1,0:T(8,128)(2,1)S(1)}, u32[]{:S(2)}, u32[]{:S(2)}) collective-permute-start(bf16[1,2,64,256]{3,2,1,0:T(8,128)(2,1)S(1)} %get-tuple-element.81), channel_id=1, source_target_pairs={{0,2},{1,3},{2,0},{3,1},{4,6},{5,7},{6,4},{7,5},{8,10},{9,11},{10,... | collective-permute-start | bytes 196616 | tf_op jit(solution)/shard_map/ppermute | solution.py:332
  20.2 4.1 %collective-permute-start.10 = (bf16[1,2,64,256]{3,2,1,0:T(8,128)(2,1)S(1)}, bf16[1,2,64,256]{3,2,1,0:T(8,128)(2,1)S(1)}, u32[]{:S(2)}, u32[]{:S(2)}) collective-permute-start(bf16[1,2,64,256]{3,2,1,0:T(8,128)(2,1)S(1)} %get-tuple-element.82), channel_id=1, source_target_pairs={{0,1},{1,0},{2,3},{3,2},{4,5},{5,4},{6,7},{7,6},{8,9},{9,8},{10,11... | collective-permute-start | bytes 196616 | tf_op jit(solution)/shard_map/ppermute | solution.py:332
  21.0 4.3 %collective-permute-start.13 = (bf16[1,2,64,256]{3,2,1,0:T(8,128)(2,1)S(1)}, bf16[1,2,64,256]{3,2,1,0:T(8,128)(2,1)S(1)}, u32[]{:S(2)}, u32[]{:S(2)}) collective-permute-start(bf16[1,2,64,256]{3,2,1,0:T(8,128)(2,1)S(1)} %get-tuple-element.89), channel_id=1, source_target_pairs={{0,2},{1,3},{2,0},{3,1},{4,6},{5,7},{6,4},{7,5},{8,10},{9,11},{10,... | collective-permute-start | bytes 196616 | tf_op jit(solution)/shard_map/ppermute | solution.py:332
  22.5 4.2 %collective-permute-start.14 = (bf16[1,2,64,256]{3,2,1,0:T(8,128)(2,1)S(1)}, bf16[1,2,64,256]{3,2,1,0:T(8,128)(2,1)S(1)}, u32[]{:S(2)}, u32[]{:S(2)}) collective-permute-start(bf16[1,2,64,256]{3,2,1,0:T(8,128)(2,1)S(1)} %get-tuple-element.90), channel_id=1, source_target_pairs={{0,3},{1,2},{2,1},{3,0},{4,7},{5,6},{6,5},{7,4},{8,11},{9,10},{10,... | collective-permute-start | bytes 196616 | tf_op jit(solution)/shard_map/ppermute | solution.py:332
  22.5 4.2 %collective-permute-start.15 = (bf16[1,2,64,256]{3,2,1,0:T(8,128)(2,1)S(1)}, bf16[1,2,64,256]{3,2,1,0:T(8,128)(2,1)S(1)}, u32[]{:S(2)}, u32[]{:S(2)}) collective-permute-start(bf16[1,2,64,256]{3,2,1,0:T(8,128)(2,1)S(1)} %get-tuple-element.91), channel_id=1, source_target_pairs={{0,1},{1,0},{2,3},{3,2},{4,5},{5,4},{6,7},{7,6},{8,9},{9,8},{10,11... | collective-permute-start | bytes 196616 | tf_op jit(solution)/shard_map/ppermute | solution.py:332
